TPU v7x, 32 devices: a whole 2x2x4 slice. The times are simulated.
32 devices in a mesh: groups: 2 (over x), dev: 16 (over z, y, core).
Axes of the slice: x: 2, y: 2, z: 4, core: 2. Of those that a mesh axis runs over, the one named last changes fastest.
Arguments:
- image_rows: bfloat16 [512, 2560], P(('groups', 'dev')), parts along dimension 0, may hold values from -6 to 6
- text_hidden: bfloat16 [512, 4096], P('groups', 'dev'), parts along dimension 0, may hold values from -6 to 6
- caption_weight: bfloat16 [4096, 2560], P('dev'), may hold values from -0.09375 to 0.09375
- mod_scale: float32 [2560], replicated, may hold values from 0.5 to 1.5
- mod_shift: float32 [2560], replicated, may hold values from -3 to 3
- router_weight: float32 [2560, 4], replicated, may hold values from -0.125 to 0.125
- image_experts: int32 [512, 2], P(('groups', 'dev')), parts along dimension 0, may hold values from 0 to 3, all different within a row; in each aligned block of 16 rows (0 to 15, 16 to 31, ...) at most 12 rows name the same one
- caption_experts: int32 [512, 2], P(('groups', 'dev')), parts along dimension 0, may hold values from 0 to 3, all different within a row; in each aligned block of 16 rows (0 to 15, 16 to 31, ...) at most 9 rows name the same one
- prompt_lengths: int32 [4], P('groups'), parts along dimension 0, may hold values from 1 to 128, as said below
- w_gate: bfloat16 [2560, 27648], P(None, 'dev'), may hold values from -0.125 to 0.125
- w_up: bfloat16 [2560, 27648], P(None, 'dev'), may hold values from -0.125 to 0.125
- w_down: bfloat16 [27648, 2560], P('dev'), may hold values from -0.078125 to 0.078125
Outputs:
- image_out: bfloat16 [512, 2560], P(('groups', 'dev')), parts along dimension 0
- caption_out: bfloat16 [512, 2560], P(('groups', 'dev')), parts along dimension 0
There are 2 independent parts, one for each index of `groups`. A program takes and returns all parts, laid end to end along the dimension named above; an argument that names none is the same for every part. Nothing has to cross between parts.
Inputs may be any that keep to these rules, and one draw needn't show every extreme that they name: `image_experts`: in each aligned block of 16 rows (the rows of one device) no expert is named by more than 12 rows, a bound that some block reaches; a row names two different experts. `caption_experts`: in each aligned block of 16 rows (the rows of one device) no expert is named by more than 9 rows, a bound that some block reaches; a row names two different experts. `prompt_lengths`: one prompt has exactly 128 live tokens.
All inputs are finite; a program needn't handle non-finite values.
Results may differ from a plain program's by a relative error of at most 0.018.
Values may be sent and summed in bfloat16 or wider, within the bound.
No kernel may reach another device: no remote copies, remote signals or barrier semaphores. Data moves between devices by JAX's collectives and lax.ppermute only.
A program may use at most 128 MiB of HBM per device.

v0:
```python
import jax
import jax.numpy as jnp
from jax import lax
from jax.sharding import PartitionSpec as P

PLEN = 128


def modulate(inputs, mod_scale, mod_shift):
    values = inputs.astype(jnp.float32)
    center = values - jnp.mean(values, axis=1, keepdims=True)
    spread = jnp.mean(center * center, axis=1, keepdims=True)
    return (center * lax.rsqrt(spread + 1e-06) * mod_scale + mod_shift).astype(jnp.bfloat16)


def route_weights(normed, router_weight, chosen):
    logits = jnp.dot(normed.astype(jnp.float32), router_weight, precision=lax.Precision.HIGHEST)
    expert_ids = jnp.arange(router_weight.shape[1], dtype=jnp.int32)
    first_logit = jnp.sum(jnp.where(chosen[:, 0:1] == expert_ids[None, :], logits, 0.0), axis=1)
    second_logit = jnp.sum(jnp.where(chosen[:, 1:2] == expert_ids[None, :], logits, 0.0), axis=1)
    return (jax.nn.sigmoid(first_logit - second_logit), jax.nn.sigmoid(second_logit - first_logit))


def slot_tables(normed, chosen, active_rows, router_weight, capacity):
    weight_first, weight_second = route_weights(normed, router_weight, chosen)
    expert_ids = jnp.arange(router_weight.shape[1], dtype=jnp.int32)
    match_first = chosen[:, 0:1] == expert_ids[None, :]
    match_second = chosen[:, 1:2] == expert_ids[None, :]
    routed = (match_first | match_second).astype(jnp.int32) * active_rows[:, None]
    ordinal = jnp.cumsum(routed, axis=0) - routed
    slot_ids = jnp.arange(capacity, dtype=jnp.int32)
    placed = (ordinal[:, :, None] == slot_ids[None, None, :]) & (routed[:, :, None] > 0)
    mixing = weight_first[:, None] * match_first + weight_second[:, None] * match_second
    scatter_table = jnp.transpose(placed, (1, 2, 0)).astype(jnp.bfloat16)
    gather_table = jnp.transpose(placed.astype(jnp.float32) * mixing[:, :, None], (1, 2, 0))
    bucket = jnp.einsum(
        "ecr,rd->ecd", scatter_table, normed, preferred_element_type=jnp.float32
    ).astype(jnp.bfloat16)
    return (bucket, gather_table)


def expert_rows(received, w_gate, w_up, w_down):
    sources, slot_count, features = received.shape
    flattened = received.reshape(sources * slot_count, features)
    gate_proj = jnp.dot(flattened, w_gate, preferred_element_type=jnp.float32)
    up_proj = jnp.dot(flattened, w_up, preferred_element_type=jnp.float32)
    hidden = (jax.nn.silu(gate_proj) * up_proj).astype(jnp.bfloat16)
    partial_value = jnp.dot(hidden, w_down, preferred_element_type=jnp.float32).astype(jnp.bfloat16)
    return partial_value.reshape(sources, slot_count, features)


def regroup(returned, experts):
    sources, slot_count, features = returned.shape
    return jnp.sum(
        returned.reshape(experts, sources // experts, slot_count, features).astype(jnp.float32),
        axis=1,
    )


def combine(gather_table, expert_out):
    return jnp.einsum(
        "ecr,ecd->rd", gather_table, expert_out, precision=lax.Precision.HIGHEST
    ).astype(jnp.bfloat16)


def local(
    image_rows,
    text_hidden,
    caption_weight,
    mod_scale,
    mod_shift,
    router_weight,
    image_experts,
    caption_experts,
    prompt_lengths,
    w_gate,
    w_up,
    w_down,
):
    devices = lax.axis_size("dev")
    my_index = lax.axis_index("dev")
    experts = router_weight.shape[1]
    sharing = devices // experts
    caption_rows = text_hidden.shape[0] // devices
    caption_cap = caption_rows // 2 + 1
    image_cap = image_rows.shape[0] * 3 // 4
    image_normed = modulate(image_rows, mod_scale, mod_shift)
    image_active = jnp.ones((image_rows.shape[0],), jnp.int32)
    image_bucket, image_table = slot_tables(
        image_normed, image_experts, image_active, router_weight, image_cap
    )
    caption = lax.psum_scatter(
        jnp.dot(text_hidden, caption_weight, preferred_element_type=jnp.float32),
        "dev",
        scatter_dimension=0,
        tiled=True,
    ).astype(jnp.bfloat16)
    position = my_index * caption_rows + jnp.arange(caption_rows, dtype=jnp.int32)
    prompt_ids = position // PLEN
    prompt_range = jnp.arange(prompt_lengths.shape[0], dtype=jnp.int32)
    lengths = jnp.sum(
        jnp.where(prompt_ids[:, None] == prompt_range[None, :], prompt_lengths[None, :], 0), axis=1
    )
    caption_active = (position % PLEN < lengths).astype(jnp.int32)
    caption_normed = modulate(caption, mod_scale, mod_shift)
    caption_bucket, caption_table = slot_tables(
        caption_normed, caption_experts, caption_active, router_weight, caption_cap
    )
    joint_bucket = jnp.concatenate((image_bucket, caption_bucket), axis=1)
    returned = lax.all_to_all(
        expert_rows(
            lax.all_to_all(
                jnp.repeat(joint_bucket, sharing, axis=0),
                "dev",
                split_axis=0,
                concat_axis=0,
                tiled=True,
            ),
            w_gate,
            w_up,
            w_down,
        ),
        "dev",
        split_axis=0,
        concat_axis=0,
        tiled=True,
    )
    expert_out = regroup(returned, experts)
    image_result = expert_out[:, :image_cap]
    caption_result = expert_out[:, image_cap:]
    image_out = combine(image_table, image_result)
    caption_out = combine(caption_table, caption_result)
    return (image_out, caption_out)


def solution(mesh):
    in_specs = (
        P(("groups", "dev"), None),
        P("groups", "dev"),
        P("dev", None),
        P(),
        P(),
        P(),
        P(("groups", "dev"), None),
        P(("groups", "dev"), None),
        P("groups"),
        P(None, "dev"),
        P(None, "dev"),
        P("dev", None),
    )
    out_specs = (P(("groups", "dev"), None), P(("groups", "dev"), None))
    return jax.shard_map(local, mesh=mesh, in_specs=in_specs, out_specs=out_specs, check_vma=False)
```

profile of v0, /device:TPU:13, one launch (start us, length us, event | category | flops | bytes accessed | tf_op | source)
XLA Modules:
  0.0 217.7 jit_solution(2446653484651180623)
XLA Ops:
  7.2 0.0 copy-start
  7.2 0.0 copy-start.6
  7.2 0.0 copy-start.8
  7.2 0.0 copy-start.7
  7.2 0.0 copy-start.2
  7.2 0.0 reduce-scatter.2.cloned.1.call-start
  7.3 1.2 copy-done
  8.5 2.9 %fusion.52 = f32[256,2560]{1,0:T(8,128)} fusion(bf16[256,256]{1,0:T(8,128)(2,1)} %param.13, bf16[256,2560]{1,0:T(8,128)(2,1)S(1)} %copy-done), kind=kOutput, calls=%fused_computation.98 | convolution fusion | flops 335544320 | bytes 4063232 | tf_op jit(solution)/shard_map/dot_general | solution.py:93
  11.4 0.0 copy-start.3
  11.4 0.0 copy-start.4
  11.4 0.0 reduce-scatter.2.cloned.1.call-update
  11.4 0.0 copy-done.6
  11.5 0.1 copy.44
  11.6 0.1 copy.45
  11.7 0.0 copy-done.8
  11.7 0.1 fusion.45
  11.8 0.0 copy-done.7
  11.8 0.1 copy.47
  11.9 0.1 copy.48
  12.0 0.0 copy-done.2
  12.0 0.1 convert_reduce_fusion.2
  12.2 0.2 fusion.13
  12.4 0.0 copy-done.3
  12.5 0.0 copy-done.4
  12.5 0.4 convolution_convert_fusion.2
  12.8 61.9 %reduce-scatter.2.cloned.1.call-done = f32[16,2560]{1,0:T(8,128)} async-done(((f32[256,2560]{1,0:T(8,128)}), f32[16,2560]{1,0:T(8,128)}) %reduce-scatter.2.cloned.1.call-update) | async-done | bytes 163856 | tf_op jit(solution)/shard_map/reduce_scatter | solution.py:92
  74.7 1.0 convert_reduce_fusion.1
  75.8 1.1 fusion.9
  76.9 1.0 fusion.12
  77.9 0.3 convolution_convert_fusion.1
  78.3 0.1 pad_maximum_fusion
  78.4 0.1 broadcast_in_dim.27
  78.5 51.0 %all_to_all.10 = bf16[16,21,2560]{2,1,0:T(8,128)(2,1)S(1)} all-to-all(bf16[16,21,2560]{2,1,0:T(8,128)(2,1)S(1)} %bitcast.40), channel_id=1, replica_groups=mesh['groups'=2,'dev'=16] {'dev'}, dimensions={0} | all-to-all | bytes 3440640 | tf_op jit(solution)/shard_map/all_to_all | solution.py:112
  129.5 1.5 reshape.567
  131.0 0.0 copy-start.1
  131.0 8.9 %fusion.53 = f32[336,1728]{1,0:T(8,128)} fusion(bf16[336,2560]{1,0:T(8,128)(2,1)} %reshape.567, bf16[2560,1728]{0,1:T(8,128)(2,1)} %param.21), kind=kOutput, calls=%fused_computation.99 | convolution fusion | flops 2972712960 | bytes 12890112 | tf_op jit(solution)/shard_map/dot_general | solution.py:45
  139.9 0.0 copy-done.1
  139.9 15.1 %convolution_convert_fusion = bf16[336,2560]{1,0:T(8,128)(2,1)} fusion(bf16[1728,2560]{1,0:T(8,128)(2,1)} %param.23, bf16[336,2560]{1,0:T(8,128)(2,1)S(1)} %copy-done.1, bf16[2560,1728]{0,1:T(8,128)(2,1)} %param.22, f32[336,1728]{1,0:T(8,128)} %fusion.53), kind=kOutput, calls=%fused_computation | convolution fusion | flops 5949769728 | bytes 23457792 | tf_op jit(solution)/shard_map/dot_general | solution.py:48
  155.0 2.7 %reshape.568 = bf16[16,21,2560]{2,1,0:T(8,128)(2,1)} reshape(bf16[336,2560]{1,0:T(8,128)(2,1)} %convolution_convert_fusion) | data formatting | bytes 3440640 | tf_op jit(solution)/shard_map/reshape | solution.py:49
  157.7 0.0 copy-start.5
  157.7 5.2 %all-to-all-start.1 = ((bf16[16,21,2560]{2,1,0:T(8,128)(2,1)}), bf16[16,21,2560]{2,1,0:T(8,128)(2,1)S(1)}, u32[]{:S(2)}, u32[]{:S(2)}) async-start(bf16[16,21,2560]{2,1,0:T(8,128)(2,1)} %reshape.568), calls=%async_computation.2 | async-start | bytes 3932160 | tf_op jit(solution)/shard_map/all_to_all | solution.py:110
  162.9 0.0 copy-done.5
  162.9 0.3 select_reduce_fusion.3
  163.2 0.2 select_reduce_fusion.1
  163.5 44.0 %all-to-all-done.1 = bf16[16,21,2560]{2,1,0:T(8,128)(2,1)S(1)} async-done(((bf16[16,21,2560]{2,1,0:T(8,128)(2,1)}), bf16[16,21,2560]{2,1,0:T(8,128)(2,1)S(1)}, u32[]{:S(2)}, u32[]{:S(2)}) %all-to-all-start.1) | async-done | bytes 1720352 | tf_op jit(solution)/shard_map/all_to_all | solution.py:110
  207.5 0.3 convert_reduce_fusion
  207.8 1.5 fusion.1
  209.4 1.5 fusion
  (20 shorter events, 0.2 us)
Async XLA Ops:
  7.2 1.3 copy-start
  7.2 4.3 %copy-start.6 = (s32[16,2]{0,1:T(2,128)S(1)}, s32[16,2]{0,1:T(2,128)}, u32[]{:S(2)}) copy-start(s32[16,2]{0,1:T(2,128)} %param.18) | copy-start | bytes 388
  7.2 4.5 %copy-start.8 = (s32[2]{0:T(128)S(1)}, s32[2]{0:T(128)}, u32[]{:S(2)}) copy-start(s32[2]{0:T(128)} %param.20) | copy-start | bytes 28
  7.2 4.6 %copy-start.7 = (s32[16,2]{0,1:T(2,128)S(1)}, s32[16,2]{0,1:T(2,128)}, u32[]{:S(2)}) copy-start(s32[16,2]{0,1:T(2,128)} %param.19) | copy-start | bytes 388
  7.2 4.8 %copy-start.2 = (bf16[16,2560]{1,0:T(8,128)(2,1)S(1)}, bf16[16,2560]{1,0:T(8,128)(2,1)}, u32[]{:S(2)}) copy-start(bf16[16,2560]{1,0:T(8,128)(2,1)} %param.12) | copy-start | bytes 245764
  7.2 67.5 %reduce-scatter.2.cloned.1.call-start = ((), (), s32[]{:S(2)}) async-start(), calls=%async_computation.3 | async-start | bytes 2785280 | tf_op jit(solution)/shard_map/reduce_scatter | solution.py:92
  11.4 1.0 copy-start.3
  11.4 1.1 copy-start.4
  131.0 8.9 %copy-start.1 = (bf16[336,2560]{1,0:T(8,128)(2,1)S(1)}, bf16[336,2560]{1,0:T(8,128)(2,1)}, u32[]{:S(2)}) copy-start(bf16[336,2560]{1,0:T(8,128)(2,1)} %reshape.567) | copy-start | bytes 5160964
  157.7 5.2 %copy-start.5 = (f32[2560,4]{0,1:T(4,128)S(1)}, f32[2560,4]{0,1:T(4,128)}, u32[]{:S(2)}) copy-start(f32[2560,4]{0,1:T(4,128)} %param.17) | copy-start | bytes 122884
  157.7 49.8 %all-to-all-start.1 = ((bf16[16,21,2560]{2,1,0:T(8,128)(2,1)}), bf16[16,21,2560]{2,1,0:T(8,128)(2,1)S(1)}, u32[]{:S(2)}, u32[]{:S(2)}) async-start(bf16[16,21,2560]{2,1,0:T(8,128)(2,1)} %reshape.568), calls=%async_computation.2 | async-start | bytes 3932160 | tf_op jit(solution)/shard_map/all_to_all | solution.py:110
Sparse Core Ops, SparseCore 0:
  11.8 62.8 reduce-scatter.1
where the time goes:
time: 218 us
  waiting for transfers between devices  106 us (49%)
  blocking collectives  51 us (23%)
  matrix products  31.2 us (14%)
  between operations  14.3 us (7%)
  local copies, waits for them, and re-layouts  5.95 us (3%)
  starting transfers between devices  5.24 us (2%)
  other arithmetic  4.26 us (2%)
    reduce_scatter x1, waiting for transfers between devices, local(): lax.psum_scatter(jnp.dot(text_hidden, caption_weight, preferred_element_t...  61.9 us
    all_to_all x1, blocking collectives, local(): lax.all_to_all(jnp.repeat(joint_bucket, sharing, axis=0), 'dev', split_ax...  51 us
    all_to_all x1, waiting for transfers between devices, local(): lax.all_to_all(expert_rows(lax.all_to_all(jnp.repeat(joint_bucket, sharin...  44 us
    dot_general x1, matrix products, expert_rows(): jnp.dot(hidden, w_down, preferred_element_type=jnp.float32)  15.1 us
    dot_general x1, matrix products, expert_rows(): gate_proj = jnp.dot(flattened, w_gate, preferred_element_type=jnp.float32)  8.89 us
    all_to_all x1, starting transfers between devices, local(): lax.all_to_all(expert_rows(lax.all_to_all(jnp.repeat(joint_bucket, sharin...  5.2 us
  transfers between devices with their start and end apart: 2, of which 2 were waited for; matrix products, arithmetic and copies ran while one was open for 1% of the time, Pallas kernels for 0%

commit v1 on v0

v1 whole, which is shorter than its diff:
```python
import jax
import jax.numpy as jnp
from jax import lax
from jax.sharding import PartitionSpec as P

PLEN = 128


def modulate(inputs, mod_scale, mod_shift):
    values = inputs.astype(jnp.float32)
    center = values - jnp.mean(values, axis=1, keepdims=True)
    spread = jnp.mean(center * center, axis=1, keepdims=True)
    return (center * lax.rsqrt(spread + 1e-06) * mod_scale + mod_shift).astype(jnp.bfloat16)


def route_weights(normed, router_weight, chosen):
    logits = jnp.dot(normed.astype(jnp.float32), router_weight, precision=lax.Precision.HIGHEST)
    expert_ids = jnp.arange(router_weight.shape[1], dtype=jnp.int32)
    first_logit = jnp.sum(jnp.where(chosen[:, 0:1] == expert_ids[None, :], logits, 0.0), axis=1)
    second_logit = jnp.sum(jnp.where(chosen[:, 1:2] == expert_ids[None, :], logits, 0.0), axis=1)
    return (jax.nn.sigmoid(first_logit - second_logit), jax.nn.sigmoid(second_logit - first_logit))


class Grid:
    def __init__(self, devices, experts):
        self.experts = experts
        self.pairs = devices // experts // 2
        index = lax.axis_index("dev")
        self.index = index
        self.expert = index // (self.pairs * 2)
        self.pair = (index // 2) % self.pairs
        self.core = index % 2

    def send(self, value, axis, step):
        moves = []
        for expert in range(self.experts):
            for pair in range(self.pairs):
                for core in range(2):
                    to = [expert, pair, core]
                    to[axis] = (to[axis] + step) % (self.experts, self.pairs, 2)[axis]
                    moves.append(
                        (
                            (expert * self.pairs + pair) * 2 + core,
                            (to[0] * self.pairs + to[1]) * 2 + to[2],
                        )
                    )
        return lax.ppermute(value, "dev", moves)


def slots(normed, chosen, active_rows, router_weight, capacity, grid):
    weight_first, weight_second = route_weights(normed, router_weight, chosen)
    experts = grid.experts
    expert_ids = (grid.expert + jnp.arange(experts, dtype=jnp.int32)) % experts
    match_first = chosen[:, 0:1] == expert_ids[None, :]
    match_second = chosen[:, 1:2] == expert_ids[None, :]
    routed = (match_first | match_second).astype(jnp.int32) * active_rows[:, None]
    ordinal = jnp.cumsum(routed, axis=0) - routed
    slot_ids = jnp.arange(capacity, dtype=jnp.int32)
    placed = (ordinal[:, :, None] == slot_ids[None, None, :]) & (routed[:, :, None] > 0)
    mixing = weight_first[:, None] * match_first + weight_second[:, None] * match_second
    scatter_table = jnp.transpose(placed, (1, 2, 0)).astype(jnp.bfloat16)
    gather_table = jnp.transpose(placed.astype(jnp.float32) * mixing[:, :, None], (1, 2, 0))
    buckets = [
        jnp.dot(scatter_table[k], normed, preferred_element_type=jnp.float32).astype(jnp.bfloat16)
        for k in range(experts)
    ]
    return (buckets, gather_table)


def dispatch(buckets, grid):
    held = [buckets[0]] + [grid.send(buckets[k], 0, k) for k in range(1, grid.experts)]
    block = jnp.concatenate(held, axis=0)
    block = jnp.concatenate(
        [block] + [grid.send(block, 1, k) for k in range(1, grid.pairs)], axis=0
    )
    return (block, grid.send(block, 2, 1))


def expert_rows(own, other, w_gate, w_up, w_down):
    rows = jnp.concatenate([own, other], axis=0)
    gate_proj = jnp.dot(rows, w_gate, preferred_element_type=jnp.float32)
    up_proj = jnp.dot(rows, w_up, preferred_element_type=jnp.float32)
    hidden = (jax.nn.silu(gate_proj) * up_proj).astype(jnp.bfloat16)
    out = jnp.dot(hidden, w_down, preferred_element_type=jnp.float32).astype(jnp.bfloat16)
    return (out[: own.shape[0]], out[own.shape[0] :])


def give_back(own, other, grid):
    total = own.astype(jnp.float32) + grid.send(other, 2, 1).astype(jnp.float32)
    total = total.astype(jnp.bfloat16)
    rows = total.shape[0] // grid.pairs
    parts = [total[k * rows : (k + 1) * rows] for k in range(grid.pairs)]
    total = parts[0].astype(jnp.float32)
    for k in range(1, grid.pairs):
        total = total + grid.send(parts[k], 1, -k).astype(jnp.float32)
    total = total.astype(jnp.bfloat16)
    rows = rows // grid.experts
    parts = [total[k * rows : (k + 1) * rows] for k in range(grid.experts)]
    return jnp.stack(
        [parts[0]] + [grid.send(parts[k], 0, -k) for k in range(1, grid.experts)], axis=0
    )


def combine(gather_table, expert_out):
    return jnp.einsum(
        "ecr,ecd->rd",
        gather_table,
        expert_out.astype(jnp.float32),
        precision=lax.Precision.HIGHEST,
    ).astype(jnp.bfloat16)


def project(text_hidden, caption_weight, grid):
    rows = text_hidden.shape[0] // (grid.experts * grid.pairs * 2)
    text = text_hidden.reshape(grid.experts, grid.pairs, 2, rows, text_hidden.shape[1])
    text = jnp.roll(text, -grid.expert, axis=0)
    text = jnp.roll(text, -grid.pair, axis=1)
    text = jnp.roll(text, -grid.core, axis=2)
    text = jnp.transpose(text, (2, 1, 0, 3, 4)).reshape(2, -1, text_hidden.shape[1])
    other = jnp.dot(text[1], caption_weight, preferred_element_type=jnp.float32)
    own = jnp.dot(text[0], caption_weight, preferred_element_type=jnp.float32)
    total = own + grid.send(other.astype(jnp.bfloat16), 2, 1).astype(jnp.float32)
    rows_pair = rows * grid.experts
    parts = [total[k * rows_pair : (k + 1) * rows_pair] for k in range(grid.pairs)]
    total = parts[0]
    for k in range(1, grid.pairs):
        total = total + grid.send(parts[k].astype(jnp.bfloat16), 1, k).astype(jnp.float32)
    parts = [total[k * rows : (k + 1) * rows] for k in range(grid.experts)]
    total = parts[0]
    for k in range(1, grid.experts):
        total = total + grid.send(parts[k].astype(jnp.bfloat16), 0, k).astype(jnp.float32)
    return total.astype(jnp.bfloat16)


def local(
    image_rows,
    text_hidden,
    caption_weight,
    mod_scale,
    mod_shift,
    router_weight,
    image_experts,
    caption_experts,
    prompt_lengths,
    w_gate,
    w_up,
    w_down,
):
    devices = lax.axis_size("dev")
    experts = router_weight.shape[1]
    grid = Grid(devices, experts)
    caption_rows = text_hidden.shape[0] // devices
    caption_cap = caption_rows // 2 + 1
    image_cap = image_rows.shape[0] * 3 // 4

    caption = project(text_hidden, caption_weight, grid)

    image_normed = modulate(image_rows, mod_scale, mod_shift)
    image_active = jnp.ones((image_rows.shape[0],), jnp.int32)
    image_buckets, image_table = slots(
        image_normed, image_experts, image_active, router_weight, image_cap, grid
    )
    image_own, image_other = dispatch(image_buckets, grid)
    image_back = give_back(
        *expert_rows(image_own, image_other, w_gate, w_up, w_down), grid
    )
    image_out = combine(image_table, image_back)

    position = grid.index * caption_rows + jnp.arange(caption_rows, dtype=jnp.int32)
    prompt_ids = position // PLEN
    prompt_range = jnp.arange(prompt_lengths.shape[0], dtype=jnp.int32)
    lengths = jnp.sum(
        jnp.where(prompt_ids[:, None] == prompt_range[None, :], prompt_lengths[None, :], 0), axis=1
    )
    caption_active = (position % PLEN < lengths).astype(jnp.int32)
    caption_normed = modulate(caption, mod_scale, mod_shift)
    caption_buckets, caption_table = slots(
        caption_normed, caption_experts, caption_active, router_weight, caption_cap, grid
    )
    caption_own, caption_other = dispatch(caption_buckets, grid)
    caption_back = give_back(
        *expert_rows(caption_own, caption_other, w_gate, w_up, w_down), grid
    )
    caption_out = combine(caption_table, caption_back)
    return (image_out, caption_out)


def solution(mesh):
    in_specs = (
        P(("groups", "dev"), None),
        P("groups", "dev"),
        P("dev", None),
        P(),
        P(),
        P(),
        P(("groups", "dev"), None),
        P(("groups", "dev"), None),
        P("groups"),
        P(None, "dev"),
        P(None, "dev"),
        P("dev", None),
    )
    out_specs = (P(("groups", "dev"), None), P(("groups", "dev"), None))
    return jax.shard_map(local, mesh=mesh, in_specs=in_specs, out_specs=out_specs, check_vma=False)
```

time: 218 us -> 130 us (0.60)
  the two profiles are of different devices: /device:TPU:13 before, /device:TPU:0 now
where the time goes in v1:
time: 130 us; the launch traced here: 129 us
  matrix products  43.4 us (33%)
  waiting for transfers between devices  34.7 us (27%)
  starting transfers between devices  31.2 us (24%)
  local copies, waits for them, and re-layouts  14.8 us (11%)
  other arithmetic  4.04 us (3%)
    ppermute x25, waiting for transfers between devices, send(): return lax.ppermute(value, 'dev', moves)  34.7 us
    ppermute x25, starting transfers between devices, send(): return lax.ppermute(value, 'dev', moves)  31.2 us
    dot_general x2, matrix products, expert_rows(): jnp.dot(hidden, w_down, preferred_element_type=jnp.float32)  24.1 us
    dot_general x2, matrix products, expert_rows(): gate_proj = jnp.dot(rows, w_gate, preferred_element_type=jnp.float32)  14 us
    concatenate x2, local copies, waits for them, and re-layouts, dispatch(): jnp.concatenate([block] + [grid.send(block, 1, k) for k in range(1, grid....  6.09 us
    concatenate x2, local copies, waits for them, and re-layouts, expert_rows(): rows = jnp.concatenate([own, other], axis=0)  5.14 us
    slice x2, local copies, waits for them, and re-layouts, expert_rows(): return (out[:own.shape[0]], out[own.shape[0]:])  2.89 us
  transfers between devices with their start and end apart: 25, of which 13 were waited for; matrix products, arithmetic and copies ran while one was open for 43% of the time, Pallas kernels for 0%

profile of v1, /device:TPU:0, one launch (start us, length us, event | category | flops | bytes accessed | tf_op | source)
XLA Modules:
  0.0 129.3 jit_solution(11306835156319654259)
XLA Ops:
  0.7 1.0 fusion.36
  2.0 0.3 convolution_convert_fusion.2
  2.4 0.5 collective-permute-start.10
  3.3 0.1 convert_reduce_fusion.1
  4.0 0.6 collective-permute-done.10
  4.6 0.3 convert_add_fusion
  5.0 3.0 %collective-permute-start.11 = (bf16[64,2560]{1,0:T(8,128)(2,1)S(1)}, bf16[64,2560]{1,0:T(8,128)(2,1)S(1)}, u32[]{:S(2)}, u32[]{:S(2)}) collective-permute-start(bf16[64,2560]{1,0:T(8,128)(2,1)S(1)} %slice.233), channel_id=1, source_target_pairs={{0,2},{1,3},{2,0},{3,1},{4,6},{5,7},{6,4},{7,5},{8,10},{9,11},{10,... | collective-permute-start | bytes 983048 | tf_op jit(solution)/shard_map/ppermute | solution.py:47
  8.0 0.2 fusion.26
  8.3 7.7 %collective-permute-done.11 = bf16[64,2560]{1,0:T(8,128)(2,1)S(1)} collective-permute-done((bf16[64,2560]{1,0:T(8,128)(2,1)S(1)}, bf16[64,2560]{1,0:T(8,128)(2,1)S(1)}, u32[]{:S(2)}, u32[]{:S(2)}) %collective-permute-start.11) | collective-permute-done | bytes 327712 | tf_op jit(solution)/shard_map/ppermute | solution.py:47
  16.1 1.8 %collective-permute-start.12 = (bf16[16,2560]{1,0:T(8,128)(2,1)S(1)}, bf16[16,2560]{1,0:T(8,128)(2,1)S(1)}, u32[]{:S(2)}, u32[]{:S(2)}) collective-permute-start(bf16[16,2560]{1,0:T(8,128)(2,1)S(1)} %get-tuple-element.12), channel_id=1, source_target_pairs={{0,4},{1,5},{2,6},{3,7},{4,8},{5,9},{6,10},{7,11},{8,12},{9,13},{1... | collective-permute-start | bytes 245768 | tf_op jit(solution)/shard_map/ppermute | solution.py:47
  18.0 2.6 %collective-permute-start.13 = (bf16[16,2560]{1,0:T(8,128)(2,1)S(1)}, bf16[16,2560]{1,0:T(8,128)(2,1)S(1)}, u32[]{:S(2)}, u32[]{:S(2)}) collective-permute-start(bf16[16,2560]{1,0:T(8,128)(2,1)S(1)} %get-tuple-element.14), channel_id=1, source_target_pairs={{0,8},{1,9},{2,10},{3,11},{4,12},{5,13},{6,14},{7,15},{8,0},{9,1},... | collective-permute-start | bytes 245768 | tf_op jit(solution)/shard_map/ppermute | solution.py:47
  20.6 1.3 %collective-permute-start.14 = (bf16[16,2560]{1,0:T(8,128)(2,1)S(1)}, bf16[16,2560]{1,0:T(8,128)(2,1)S(1)}, u32[]{:S(2)}, u32[]{:S(2)}) collective-permute-start(bf16[16,2560]{1,0:T(8,128)(2,1)S(1)} %get-tuple-element.13), channel_id=1, source_target_pairs={{0,12},{1,13},{2,14},{3,15},{4,0},{5,1},{6,2},{7,3},{8,4},{9,5},{1... | collective-permute-start | bytes 245768 | tf_op jit(solution)/shard_map/ppermute | solution.py:47
  21.9 1.5 %collective-permute-done.12 = bf16[16,2560]{1,0:T(8,128)(2,1)S(1)} collective-permute-done((bf16[16,2560]{1,0:T(8,128)(2,1)S(1)}, bf16[16,2560]{1,0:T(8,128)(2,1)S(1)}, u32[]{:S(2)}, u32[]{:S(2)}) %collective-permute-start.12) | collective-permute-done | bytes 81952 | tf_op jit(solution)/shard_map/ppermute | solution.py:47
  23.4 2.5 %collective-permute-done.13 = bf16[16,2560]{1,0:T(8,128)(2,1)S(1)} collective-permute-done((bf16[16,2560]{1,0:T(8,128)(2,1)S(1)}, bf16[16,2560]{1,0:T(8,128)(2,1)S(1)}, u32[]{:S(2)}, u32[]{:S(2)}) %collective-permute-start.13) | collective-permute-done | bytes 81952 | tf_op jit(solution)/shard_map/ppermute | solution.py:47
  25.9 0.2 convert_reduce_fusion
  26.1 0.2 fusion.22
  26.3 0.1 fusion.25
  26.4 0.2 convolution_convert_fusion.5
  26.7 0.2 convolution_convert_fusion.4
  26.9 0.2 convolution_convert_fusion.3
  27.1 0.2 convolution_convert_fusion.6
  27.3 0.2 select_reduce_fusion.1
  27.5 0.2 select_reduce_fusion.3
  27.8 0.2 convolution_convert_fusion.8
  28.0 0.2 convolution_convert_fusion.7
  28.2 0.2 convolution_convert_fusion.9
  28.4 0.2 convolution_convert_fusion.10
  28.6 1.9 %collective-permute-start.15 = (bf16[9,2560]{1,0:T(8,128)(2,1)S(1)}, bf16[9,2560]{1,0:T(8,128)(2,1)S(1)}, u32[]{:S(2)}, u32[]{:S(2)}) collective-permute-start(bf16[9,2560]{1,0:T(8,128)(2,1)S(1)} %convolution_convert_fusion.5), channel_id=1, source_target_pairs={{0,4},{1,5},{2,6},{3,7},{4,8},{5,9},{6,10},{7,11},{8,12},{9,13},{1... | collective-permute-start | bytes 138248 | tf_op jit(solution)/shard_map/ppermute | solution.py:47
  30.5 1.8 %collective-permute-start.16 = (bf16[9,2560]{1,0:T(8,128)(2,1)S(1)}, bf16[9,2560]{1,0:T(8,128)(2,1)S(1)}, u32[]{:S(2)}, u32[]{:S(2)}) collective-permute-start(bf16[9,2560]{1,0:T(8,128)(2,1)S(1)} %convolution_convert_fusion.4), channel_id=1, source_target_pairs={{0,8},{1,9},{2,10},{3,11},{4,12},{5,13},{6,14},{7,15},{8,0},{9,1},... | collective-permute-start | bytes 138248 | tf_op jit(solution)/shard_map/ppermute | solution.py:47
  32.3 0.6 collective-permute-start.17
  33.0 1.5 %collective-permute-start.1 = (bf16[12,2560]{1,0:T(8,128)(2,1)S(1)}, bf16[12,2560]{1,0:T(8,128)(2,1)S(1)}, u32[]{:S(2)}, u32[]{:S(2)}) collective-permute-start(bf16[12,2560]{1,0:T(8,128)(2,1)S(1)} %convolution_convert_fusion.8), channel_id=1, source_target_pairs={{0,8},{1,9},{2,10},{3,11},{4,12},{5,13},{6,14},{7,15},{8,0},{9,1},... | collective-permute-start | bytes 184328 | tf_op jit(solution)/shard_map/ppermute | solution.py:47
  34.5 2.2 %collective-permute-start.2 = (bf16[12,2560]{1,0:T(8,128)(2,1)S(1)}, bf16[12,2560]{1,0:T(8,128)(2,1)S(1)}, u32[]{:S(2)}, u32[]{:S(2)}) collective-permute-start(bf16[12,2560]{1,0:T(8,128)(2,1)S(1)} %convolution_convert_fusion.7), channel_id=1, source_target_pairs={{0,12},{1,13},{2,14},{3,15},{4,0},{5,1},{6,2},{7,3},{8,4},{9,5},{1... | collective-permute-start | bytes 184328 | tf_op jit(solution)/shard_map/ppermute | solution.py:47
  36.8 0.2 collective-permute-start
  37.0 1.7 %collective-permute-done.16 = bf16[9,2560]{1,0:T(8,128)(2,1)S(1)} collective-permute-done((bf16[9,2560]{1,0:T(8,128)(2,1)S(1)}, bf16[9,2560]{1,0:T(8,128)(2,1)S(1)}, u32[]{:S(2)}, u32[]{:S(2)}) %collective-permute-start.16) | collective-permute-done | bytes 46112 | tf_op jit(solution)/shard_map/ppermute | solution.py:47
  38.8 1.6 %collective-permute-start.18 = (bf16[36,2560]{1,0:T(8,128)(2,1)S(1)}, bf16[36,2560]{1,0:T(8,128)(2,1)S(1)}, u32[]{:S(2)}, u32[]{:S(2)}) collective-permute-start(bf16[36,2560]{1,0:T(8,128)(2,1)S(1)} %pad_maximum_fusion.1), channel_id=1, source_target_pairs={{0,2},{1,3},{2,0},{3,1},{4,6},{5,7},{6,4},{7,5},{8,10},{9,11},{10,... | collective-permute-start | bytes 552968 | tf_op jit(solution)/shard_map/ppermute | solution.py:47
  40.4 4.4 %collective-permute-done.1 = bf16[12,2560]{1,0:T(8,128)(2,1)S(1)} collective-permute-done((bf16[12,2560]{1,0:T(8,128)(2,1)S(1)}, bf16[12,2560]{1,0:T(8,128)(2,1)S(1)}, u32[]{:S(2)}, u32[]{:S(2)}) %collective-permute-start.1) | collective-permute-done | bytes 61472 | tf_op jit(solution)/shard_map/ppermute | solution.py:47
  44.9 0.8 pad_maximum_fusion
  45.6 1.5 %collective-permute-start.3 = (bf16[48,2560]{1,0:T(8,128)(2,1)}, bf16[48,2560]{1,0:T(8,128)(2,1)S(1)}, u32[]{:S(2)}, u32[]{:S(2)}) collective-permute-start(bf16[48,2560]{1,0:T(8,128)(2,1)} %pad_maximum_fusion), channel_id=1, source_target_pairs={{0,2},{1,3},{2,0},{3,1},{4,6},{5,7},{6,4},{7,5},{8,10},{9,11},{10,... | collective-permute-start | bytes 737288 | tf_op jit(solution)/shard_map/ppermute | solution.py:47
  47.2 1.0 concatenate.41
  48.3 5.0 %collective-permute-done.3 = bf16[48,2560]{1,0:T(8,128)(2,1)S(1)} collective-permute-done((bf16[48,2560]{1,0:T(8,128)(2,1)}, bf16[48,2560]{1,0:T(8,128)(2,1)S(1)}, u32[]{:S(2)}, u32[]{:S(2)}) %collective-permute-start.3) | collective-permute-done | bytes 245792 | tf_op jit(solution)/shard_map/ppermute | solution.py:47
  53.3 5.1 %concatenate.35 = bf16[96,2560]{1,0:T(8,128)(2,1)} concatenate(bf16[12,2560]{1,0:T(8,128)(2,1)S(1)} %convolution_convert_fusion.10, bf16[12,2560]{1,0:T(8,128)(2,1)S(1)} %collective-permute-done, bf16[12,2560]{1,0:T(8,128)(2,1)S(1)} %collective-permute-done.1, bf16[12,2560]{1,0:T(8,128)(2,1)S(1)} %collective-permute-done.2, bf16[48,2560]{1,0:T(8,128)(2,1)S(1)} %collective-permute-done.3), dimensions={0} | concatenate | bytes 983040 | tf_op jit(solution)/shard_map/concatenate | solution.py:73
  58.5 1.0 concatenate.42
  59.6 6.5 %fusion.66 = f32[144,1728]{1,0:T(8,128)S(1)} fusion(bf16[144,2560]{1,0:T(8,128)(2,1)S(1)} %concatenate.42, bf16[2560,1728]{0,1:T(8,128)(2,1)} %param.21), kind=kOutput, calls=%fused_computation.151 | convolution fusion | flops 1274019840 | bytes 10579968 | tf_op jit(solution)/shard_map/dot_general | solution.py:81
  66.0 11.6 %convolution_convert_fusion.1 = bf16[144,2560]{1,0:T(8,128)(2,1)} fusion(bf16[1728,2560]{1,0:T(8,128)(2,1)} %param.23, f32[144,1728]{1,0:T(8,128)S(1)} %fusion.66, bf16[144,2560]{1,0:T(8,128)(2,1)S(1)} %concatenate.42, bf16[2560,1728]{0,1:T(8,128)(2,1)} %param.22), kind=kOutput, calls=%fused_computation.1 | convolution fusion | flops 2549901312 | bytes 20164608 | tf_op jit(solution)/shard_map/dot_general | solution.py:84
  77.6 1.7 %slice.191 = bf16[72,2560]{1,0:T(8,128)(2,1)} slice(bf16[144,2560]{1,0:T(8,128)(2,1)} %convolution_convert_fusion.1), slice={[72:144], [0:2560]} | slice | bytes 737280 | tf_op jit(solution)/shard_map/slice | solution.py:85
  79.4 0.5 collective-permute-start.20
  79.9 4.1 %concatenate.36 = bf16[192,2560]{1,0:T(8,128)(2,1)S(1)} concatenate(bf16[12,2560]{1,0:T(8,128)(2,1)S(1)} %convolution_convert_fusion.10, bf16[12,2560]{1,0:T(8,128)(2,1)} %copy-done.5, bf16[12,2560]{1,0:T(8,128)(2,1)S(1)} %copy-done.3, bf16[12,2560]{1,0:T(8,128)(2,1)} %copy-done.4, bf16[48,2560]{1,0:T(8,128)(2,1)S(1)} %collective-permute-done.3, ...), dimensions={0} | concatenate | bytes 1966080 | tf_op jit(solution)/shard_map/concatenate | solution.py:80
  84.0 7.6 %fusion.65 = f32[192,1728]{1,0:T(8,128)} fusion(bf16[192,2560]{1,0:T(8,128)(2,1)S(1)} %concatenate.36, bf16[2560,1728]{0,1:T(8,128)(2,1)} %param.21), kind=kOutput, calls=%fused_computation.150 | convolution fusion | flops 1698693120 | bytes 11157504 | tf_op jit(solution)/shard_map/dot_general | solution.py:81
  91.7 1.4 %collective-permute-start.21 = (bf16[36,2560]{1,0:T(8,128)(2,1)S(1)}, bf16[36,2560]{1,0:T(8,128)(2,1)S(1)}, u32[]{:S(2)}, u32[]{:S(2)}) collective-permute-start(bf16[36,2560]{1,0:T(8,128)(2,1)S(1)} %slice.193), channel_id=1, source_target_pairs={{0,2},{1,3},{2,0},{3,1},{4,6},{5,7},{6,4},{7,5},{8,10},{9,11},{10,... | collective-permute-start | bytes 552968 | tf_op jit(solution)/shard_map/ppermute | solution.py:47
  93.1 12.5 %convolution_convert_fusion = bf16[192,2560]{1,0:T(8,128)(2,1)} fusion(bf16[1728,2560]{1,0:T(8,128)(2,1)} %param.23, f32[192,1728]{1,0:T(8,128)} %fusion.65, bf16[192,2560]{1,0:T(8,128)(2,1)S(1)} %concatenate.36, bf16[2560,1728]{0,1:T(8,128)(2,1)} %param.22), kind=kOutput, calls=%fused_computation | convolution fusion | flops 3399868416 | bytes 20987904 | tf_op jit(solution)/shard_map/dot_general | solution.py:84
  105.6 1.1 slice.171
  106.9 1.8 %collective-permute-done.5 = bf16[96,2560]{1,0:T(8,128)(2,1)S(1)} collective-permute-done((bf16[96,2560]{1,0:T(8,128)(2,1)S(1)}, bf16[96,2560]{1,0:T(8,128)(2,1)S(1)}, u32[]{:S(2)}, u32[]{:S(2)}) %collective-permute-start.5) | collective-permute-done | bytes 491552 | tf_op jit(solution)/shard_map/ppermute | solution.py:47
  108.9 0.8 collective-permute-start.6
  109.7 2.7 %collective-permute-start.22 = (bf16[9,2560]{1,0:T(8,128)(2,1)S(1)}, bf16[9,2560]{1,0:T(8,128)(2,1)S(1)}, u32[]{:S(2)}, u32[]{:S(2)}) collective-permute-start(bf16[9,2560]{1,0:T(8,128)(2,1)S(1)} %get-tuple-element.22), channel_id=1, source_target_pairs={{0,12},{1,13},{2,14},{3,15},{4,0},{5,1},{6,2},{7,3},{8,4},{9,5},{1... | collective-permute-start | bytes 138248 | tf_op jit(solution)/shard_map/ppermute | solution.py:47
  112.4 1.1 collective-permute-start.23
  113.5 3.4 %collective-permute-done.6 = bf16[48,2560]{1,0:T(8,128)(2,1)S(1)} collective-permute-done((bf16[48,2560]{1,0:T(8,128)(2,1)S(1)}, bf16[48,2560]{1,0:T(8,128)(2,1)S(1)}, u32[]{:S(2)}, u32[]{:S(2)}) %collective-permute-start.6) | collective-permute-done | bytes 245792 | tf_op jit(solution)/shard_map/ppermute | solution.py:47
  117.1 2.3 %collective-permute-start.9 = (bf16[12,2560]{1,0:T(8,128)(2,1)S(1)}, bf16[12,2560]{1,0:T(8,128)(2,1)S(1)}, u32[]{:S(2)}, u32[]{:S(2)}) collective-permute-start(bf16[12,2560]{1,0:T(8,128)(2,1)S(1)} %get-tuple-element.16), channel_id=1, source_target_pairs={{0,4},{1,5},{2,6},{3,7},{4,8},{5,9},{6,10},{7,11},{8,12},{9,13},{1... | collective-permute-start | bytes 184328 | tf_op jit(solution)/shard_map/ppermute | solution.py:47
  119.4 1.5 %collective-permute-start.7 = (bf16[12,2560]{1,0:T(8,128)(2,1)S(1)}, bf16[12,2560]{1,0:T(8,128)(2,1)S(1)}, u32[]{:S(2)}, u32[]{:S(2)}) collective-permute-start(bf16[12,2560]{1,0:T(8,128)(2,1)S(1)} %get-tuple-element.18), channel_id=1, source_target_pairs={{0,12},{1,13},{2,14},{3,15},{4,0},{5,1},{6,2},{7,3},{8,4},{9,5},{1... | collective-permute-start | bytes 184328 | tf_op jit(solution)/shard_map/ppermute | solution.py:47
  120.9 1.3 collective-permute-done.23
  122.2 1.2 fusion.1
  123.4 0.5 collective-permute-done.9
  123.9 0.7 collective-permute-done.7
  124.6 3.5 %collective-permute-done.8 = bf16[12,2560]{1,0:T(8,128)(2,1)S(1)} collective-permute-done((bf16[12,2560]{1,0:T(8,128)(2,1)S(1)}, bf16[12,2560]{1,0:T(8,128)(2,1)S(1)}, u32[]{:S(2)}, u32[]{:S(2)}) %collective-permute-start.8) | collective-permute-done | bytes 61472 | tf_op jit(solution)/shard_map/ppermute | solution.py:47
  128.1 1.2 fusion
  (87 shorter events, 2.3 us)
Async XLA Ops:
  0.6 1.4 %copy-start = (bf16[256,2560]{1,0:T(8,128)(2,1)S(1)}, bf16[256,2560]{1,0:T(8,128)(2,1)}, u32[]{:S(2)}) copy-start(bf16[256,2560]{1,0:T(8,128)(2,1)} %param.14) | copy-start | bytes 3932164
  1.8 1.1 copy-start.13
  1.8 1.2 copy-start.11
  1.8 1.2 copy-start.12
  1.9 1.4 %copy-start.7 = (bf16[16,2560]{1,0:T(8,128)(2,1)S(1)}, bf16[16,2560]{1,0:T(8,128)(2,1)}, u32[]{:S(2)}) copy-start(bf16[16,2560]{1,0:T(8,128)(2,1)} %param.12) | copy-start | bytes 245764
  2.4 2.2 %collective-permute-start.10 = (bf16[128,2560]{1,0:T(8,128)(2,1)S(1)}, bf16[128,2560]{1,0:T(8,128)(2,1)S(1)}, u32[]{:S(2)}, u32[]{:S(2)}) collective-permute-start(bf16[128,2560]{1,0:T(8,128)(2,1)S(1)} %convolution_convert_fusion.2), channel_id=1, source_target_pairs={{0,1},{1,0},{2,3},{3,2},{4,5},{5,4},{6,7},{7,6},{8,9},{9,8},{10,11... | collective-permute-start | bytes 1966088 | tf_op jit(solution)/shard_map/ppermute | solution.py:47
  5.0 11.0 %collective-permute-start.11 = (bf16[64,2560]{1,0:T(8,128)(2,1)S(1)}, bf16[64,2560]{1,0:T(8,128)(2,1)S(1)}, u32[]{:S(2)}, u32[]{:S(2)}) collective-permute-start(bf16[64,2560]{1,0:T(8,128)(2,1)S(1)} %slice.233), channel_id=1, source_target_pairs={{0,2},{1,3},{2,0},{3,1},{4,6},{5,7},{6,4},{7,5},{8,10},{9,11},{10,... | collective-permute-start | bytes 983048 | tf_op jit(solution)/shard_map/ppermute | solution.py:47
  8.3 18.0 %copy-start.9 = (f32[2560]{0:T(1024)S(1)}, f32[2560]{0:T(1024)}, u32[]{:S(2)}) copy-start(f32[2560]{0:T(1024)} %param.16) | copy-start | bytes 30724
  8.3 18.0 %copy-start.10 = (f32[2560]{0:T(1024)S(1)}, f32[2560]{0:T(1024)}, u32[]{:S(2)}) copy-start(f32[2560]{0:T(1024)} %param.15) | copy-start | bytes 30724
  16.1 11.2 %copy-start.8 = (f32[2560,4]{0,1:T(4,128)S(1)}, f32[2560,4]{0,1:T(4,128)}, u32[]{:S(2)}) copy-start(f32[2560,4]{0,1:T(4,128)} %param.17) | copy-start | bytes 122884
  16.1 7.3 %collective-permute-start.12 = (bf16[16,2560]{1,0:T(8,128)(2,1)S(1)}, bf16[16,2560]{1,0:T(8,128)(2,1)S(1)}, u32[]{:S(2)}, u32[]{:S(2)}) collective-permute-start(bf16[16,2560]{1,0:T(8,128)(2,1)S(1)} %get-tuple-element.12), channel_id=1, source_target_pairs={{0,4},{1,5},{2,6},{3,7},{4,8},{5,9},{6,10},{7,11},{8,12},{9,13},{1... | collective-permute-start | bytes 245768 | tf_op jit(solution)/shard_map/ppermute | solution.py:47
  18.0 8.0 %collective-permute-start.13 = (bf16[16,2560]{1,0:T(8,128)(2,1)S(1)}, bf16[16,2560]{1,0:T(8,128)(2,1)S(1)}, u32[]{:S(2)}, u32[]{:S(2)}) collective-permute-start(bf16[16,2560]{1,0:T(8,128)(2,1)S(1)} %get-tuple-element.14), channel_id=1, source_target_pairs={{0,8},{1,9},{2,10},{3,11},{4,12},{5,13},{6,14},{7,15},{8,0},{9,1},... | collective-permute-start | bytes 245768 | tf_op jit(solution)/shard_map/ppermute | solution.py:47
  20.6 5.3 %collective-permute-start.14 = (bf16[16,2560]{1,0:T(8,128)(2,1)S(1)}, bf16[16,2560]{1,0:T(8,128)(2,1)S(1)}, u32[]{:S(2)}, u32[]{:S(2)}) collective-permute-start(bf16[16,2560]{1,0:T(8,128)(2,1)S(1)} %get-tuple-element.13), channel_id=1, source_target_pairs={{0,12},{1,13},{2,14},{3,15},{4,0},{5,1},{6,2},{7,3},{8,4},{9,5},{1... | collective-permute-start | bytes 245768 | tf_op jit(solution)/shard_map/ppermute | solution.py:47
  28.6 8.1 %collective-permute-start.15 = (bf16[9,2560]{1,0:T(8,128)(2,1)S(1)}, bf16[9,2560]{1,0:T(8,128)(2,1)S(1)}, u32[]{:S(2)}, u32[]{:S(2)}) collective-permute-start(bf16[9,2560]{1,0:T(8,128)(2,1)S(1)} %convolution_convert_fusion.5), channel_id=1, source_target_pairs={{0,4},{1,5},{2,6},{3,7},{4,8},{5,9},{6,10},{7,11},{8,12},{9,13},{1... | collective-permute-start | bytes 138248 | tf_op jit(solution)/shard_map/ppermute | solution.py:47
  30.5 8.2 %collective-permute-start.16 = (bf16[9,2560]{1,0:T(8,128)(2,1)S(1)}, bf16[9,2560]{1,0:T(8,128)(2,1)S(1)}, u32[]{:S(2)}, u32[]{:S(2)}) collective-permute-start(bf16[9,2560]{1,0:T(8,128)(2,1)S(1)} %convolution_convert_fusion.4), channel_id=1, source_target_pairs={{0,8},{1,9},{2,10},{3,11},{4,12},{5,13},{6,14},{7,15},{8,0},{9,1},... | collective-permute-start | bytes 138248 | tf_op jit(solution)/shard_map/ppermute | solution.py:47
  32.3 6.4 %collective-permute-start.17 = (bf16[9,2560]{1,0:T(8,128)(2,1)S(1)}, bf16[9,2560]{1,0:T(8,128)(2,1)S(1)}, u32[]{:S(2)}, u32[]{:S(2)}) collective-permute-start(bf16[9,2560]{1,0:T(8,128)(2,1)S(1)} %convolution_convert_fusion.3), channel_id=1, source_target_pairs={{0,12},{1,13},{2,14},{3,15},{4,0},{5,1},{6,2},{7,3},{8,4},{9,5},{1... | collective-permute-start | bytes 138248 | tf_op jit(solution)/shard_map/ppermute | solution.py:47
  33.0 11.9 %collective-permute-start.1 = (bf16[12,2560]{1,0:T(8,128)(2,1)S(1)}, bf16[12,2560]{1,0:T(8,128)(2,1)S(1)}, u32[]{:S(2)}, u32[]{:S(2)}) collective-permute-start(bf16[12,2560]{1,0:T(8,128)(2,1)S(1)} %convolution_convert_fusion.8), channel_id=1, source_target_pairs={{0,8},{1,9},{2,10},{3,11},{4,12},{5,13},{6,14},{7,15},{8,0},{9,1},... | collective-permute-start | bytes 184328 | tf_op jit(solution)/shard_map/ppermute | solution.py:47
  34.5 10.3 %collective-permute-start.2 = (bf16[12,2560]{1,0:T(8,128)(2,1)S(1)}, bf16[12,2560]{1,0:T(8,128)(2,1)S(1)}, u32[]{:S(2)}, u32[]{:S(2)}) collective-permute-start(bf16[12,2560]{1,0:T(8,128)(2,1)S(1)} %convolution_convert_fusion.7), channel_id=1, source_target_pairs={{0,12},{1,13},{2,14},{3,15},{4,0},{5,1},{6,2},{7,3},{8,4},{9,5},{1... | collective-permute-start | bytes 184328 | tf_op jit(solution)/shard_map/ppermute | solution.py:47
  36.8 8.1 %collective-permute-start = (bf16[12,2560]{1,0:T(8,128)(2,1)S(1)}, bf16[12,2560]{1,0:T(8,128)(2,1)S(1)}, u32[]{:S(2)}, u32[]{:S(2)}) collective-permute-start(bf16[12,2560]{1,0:T(8,128)(2,1)S(1)} %convolution_convert_fusion.9), channel_id=1, source_target_pairs={{0,4},{1,5},{2,6},{3,7},{4,8},{5,9},{6,10},{7,11},{8,12},{9,13},{1... | collective-permute-start | bytes 184328 | tf_op jit(solution)/shard_map/ppermute | solution.py:47
  38.8 8.4 %collective-permute-start.18 = (bf16[36,2560]{1,0:T(8,128)(2,1)S(1)}, bf16[36,2560]{1,0:T(8,128)(2,1)S(1)}, u32[]{:S(2)}, u32[]{:S(2)}) collective-permute-start(bf16[36,2560]{1,0:T(8,128)(2,1)S(1)} %pad_maximum_fusion.1), channel_id=1, source_target_pairs={{0,2},{1,3},{2,0},{3,1},{4,6},{5,7},{6,4},{7,5},{8,10},{9,11},{10,... | collective-permute-start | bytes 552968 | tf_op jit(solution)/shard_map/ppermute | solution.py:47
  44.8 13.6 %copy-start.2 = (bf16[12,2560]{1,0:T(8,128)(2,1)}, bf16[12,2560]{1,0:T(8,128)(2,1)S(1)}, u32[]{:S(2)}) copy-start(bf16[12,2560]{1,0:T(8,128)(2,1)S(1)} %collective-permute-done.1) | copy-start | bytes 184324
  44.9 13.6 %copy-start.4 = (bf16[12,2560]{1,0:T(8,128)(2,1)}, bf16[12,2560]{1,0:T(8,128)(2,1)S(1)}, u32[]{:S(2)}) copy-start(bf16[12,2560]{1,0:T(8,128)(2,1)S(1)} %collective-permute-done.2) | copy-start | bytes 184324
  44.9 13.6 %copy-start.5 = (bf16[12,2560]{1,0:T(8,128)(2,1)}, bf16[12,2560]{1,0:T(8,128)(2,1)S(1)}, u32[]{:S(2)}) copy-start(bf16[12,2560]{1,0:T(8,128)(2,1)S(1)} %collective-permute-done) | copy-start | bytes 184324
  45.6 7.7 %collective-permute-start.3 = (bf16[48,2560]{1,0:T(8,128)(2,1)}, bf16[48,2560]{1,0:T(8,128)(2,1)S(1)}, u32[]{:S(2)}, u32[]{:S(2)}) collective-permute-start(bf16[48,2560]{1,0:T(8,128)(2,1)} %pad_maximum_fusion), channel_id=1, source_target_pairs={{0,2},{1,3},{2,0},{3,1},{4,6},{5,7},{6,4},{7,5},{8,10},{9,11},{10,... | collective-permute-start | bytes 737288 | tf_op jit(solution)/shard_map/ppermute | solution.py:47
  48.1 10.4 %collective-permute-start.19 = (bf16[72,2560]{1,0:T(8,128)(2,1)S(1)}, bf16[72,2560]{1,0:T(8,128)(2,1)S(1)}, u32[]{:S(2)}, u32[]{:S(2)}) collective-permute-start(bf16[72,2560]{1,0:T(8,128)(2,1)S(1)} %concatenate.41), channel_id=1, source_target_pairs={{0,1},{1,0},{2,3},{3,2},{4,5},{5,4},{6,7},{7,6},{8,9},{9,8},{10,11... | collective-permute-start | bytes 1105928 | tf_op jit(solution)/shard_map/ppermute | solution.py:47
  58.5 21.4 %collective-permute-start.4 = (bf16[96,2560]{1,0:T(8,128)(2,1)}, bf16[96,2560]{1,0:T(8,128)(2,1)}, u32[]{:S(2)}, u32[]{:S(2)}) collective-permute-start(bf16[96,2560]{1,0:T(8,128)(2,1)} %concatenate.35), channel_id=1, source_target_pairs={{0,1},{1,0},{2,3},{3,2},{4,5},{5,4},{6,7},{7,6},{8,9},{9,8},{10,11... | collective-permute-start | bytes 1474568 | tf_op jit(solution)/shard_map/ppermute | solution.py:47
  66.0 13.8 %copy-start.3 = (bf16[12,2560]{1,0:T(8,128)(2,1)S(1)}, bf16[12,2560]{1,0:T(8,128)(2,1)}, u32[]{:S(2)}) copy-start(bf16[12,2560]{1,0:T(8,128)(2,1)} %copy-done.2) | copy-start | bytes 184324
  79.4 12.2 %collective-permute-start.20 = (bf16[72,2560]{1,0:T(8,128)(2,1)}, bf16[72,2560]{1,0:T(8,128)(2,1)S(1)}, u32[]{:S(2)}, u32[]{:S(2)}) collective-permute-start(bf16[72,2560]{1,0:T(8,128)(2,1)} %slice.191), channel_id=1, source_target_pairs={{0,1},{1,0},{2,3},{3,2},{4,5},{5,4},{6,7},{7,6},{8,9},{9,8},{10,11... | collective-permute-start | bytes 1105928 | tf_op jit(solution)/shard_map/ppermute | solution.py:47
  84.0 7.6 %copy-start.6 = (bf16[144,2560]{1,0:T(8,128)(2,1)S(1)}, bf16[144,2560]{1,0:T(8,128)(2,1)}, u32[]{:S(2)}) copy-start(bf16[144,2560]{1,0:T(8,128)(2,1)} %convolution_convert_fusion.1) | copy-start | bytes 2211844
  91.7 15.2 %collective-permute-start.21 = (bf16[36,2560]{1,0:T(8,128)(2,1)S(1)}, bf16[36,2560]{1,0:T(8,128)(2,1)S(1)}, u32[]{:S(2)}, u32[]{:S(2)}) collective-permute-start(bf16[36,2560]{1,0:T(8,128)(2,1)S(1)} %slice.193), channel_id=1, source_target_pairs={{0,2},{1,3},{2,0},{3,1},{4,6},{5,7},{6,4},{7,5},{8,10},{9,11},{10,... | collective-permute-start | bytes 552968 | tf_op jit(solution)/shard_map/ppermute | solution.py:47
  105.6 3.1 %copy-start.1 = (bf16[192,2560]{1,0:T(8,128)(2,1)S(1)}, bf16[192,2560]{1,0:T(8,128)(2,1)}, u32[]{:S(2)}) copy-start(bf16[192,2560]{1,0:T(8,128)(2,1)} %convolution_convert_fusion) | copy-start | bytes 2949124
  106.8 1.9 %collective-permute-start.5 = (bf16[96,2560]{1,0:T(8,128)(2,1)S(1)}, bf16[96,2560]{1,0:T(8,128)(2,1)S(1)}, u32[]{:S(2)}, u32[]{:S(2)}) collective-permute-start(bf16[96,2560]{1,0:T(8,128)(2,1)S(1)} %slice.171), channel_id=1, source_target_pairs={{0,1},{1,0},{2,3},{3,2},{4,5},{5,4},{6,7},{7,6},{8,9},{9,8},{10,11... | collective-permute-start | bytes 1474568 | tf_op jit(solution)/shard_map/ppermute | solution.py:47
  108.9 8.1 %collective-permute-start.6 = (bf16[48,2560]{1,0:T(8,128)(2,1)S(1)}, bf16[48,2560]{1,0:T(8,128)(2,1)S(1)}, u32[]{:S(2)}, u32[]{:S(2)}) collective-permute-start(bf16[48,2560]{1,0:T(8,128)(2,1)S(1)} %slice.173), channel_id=1, source_target_pairs={{0,2},{1,3},{2,0},{3,1},{4,6},{5,7},{6,4},{7,5},{8,10},{9,11},{10,... | collective-permute-start | bytes 737288 | tf_op jit(solution)/shard_map/ppermute | solution.py:47
  109.7 11.2 %collective-permute-start.22 = (bf16[9,2560]{1,0:T(8,128)(2,1)S(1)}, bf16[9,2560]{1,0:T(8,128)(2,1)S(1)}, u32[]{:S(2)}, u32[]{:S(2)}) collective-permute-start(bf16[9,2560]{1,0:T(8,128)(2,1)S(1)} %get-tuple-element.22), channel_id=1, source_target_pairs={{0,12},{1,13},{2,14},{3,15},{4,0},{5,1},{6,2},{7,3},{8,4},{9,5},{1... | collective-permute-start | bytes 138248 | tf_op jit(solution)/shard_map/ppermute | solution.py:47
  112.4 9.8 %collective-permute-start.23 = (bf16[9,2560]{1,0:T(8,128)(2,1)S(1)}, bf16[9,2560]{1,0:T(8,128)(2,1)S(1)}, u32[]{:S(2)}, u32[]{:S(2)}) collective-permute-start(bf16[9,2560]{1,0:T(8,128)(2,1)S(1)} %get-tuple-element.21), channel_id=1, source_target_pairs={{0,8},{1,9},{2,10},{3,11},{4,12},{5,13},{6,14},{7,15},{8,0},{9,1},... | collective-permute-start | bytes 138248 | tf_op jit(solution)/shard_map/ppermute | solution.py:47
  113.5 8.7 %collective-permute-start.24 = (bf16[9,2560]{1,0:T(8,128)(2,1)S(1)}, bf16[9,2560]{1,0:T(8,128)(2,1)S(1)}, u32[]{:S(2)}, u32[]{:S(2)}) collective-permute-start(bf16[9,2560]{1,0:T(8,128)(2,1)S(1)} %get-tuple-element.20), channel_id=1, source_target_pairs={{0,4},{1,5},{2,6},{3,7},{4,8},{5,9},{6,10},{7,11},{8,12},{9,13},{1... | collective-permute-start | bytes 138248 | tf_op jit(solution)/shard_map/ppermute | solution.py:47
  117.1 6.9 %collective-permute-start.9 = (bf16[12,2560]{1,0:T(8,128)(2,1)S(1)}, bf16[12,2560]{1,0:T(8,128)(2,1)S(1)}, u32[]{:S(2)}, u32[]{:S(2)}) collective-permute-start(bf16[12,2560]{1,0:T(8,128)(2,1)S(1)} %get-tuple-element.16), channel_id=1, source_target_pairs={{0,4},{1,5},{2,6},{3,7},{4,8},{5,9},{6,10},{7,11},{8,12},{9,13},{1... | collective-permute-start | bytes 184328 | tf_op jit(solution)/shard_map/ppermute | solution.py:47
  119.4 5.2 %collective-permute-start.7 = (bf16[12,2560]{1,0:T(8,128)(2,1)S(1)}, bf16[12,2560]{1,0:T(8,128)(2,1)S(1)}, u32[]{:S(2)}, u32[]{:S(2)}) collective-permute-start(bf16[12,2560]{1,0:T(8,128)(2,1)S(1)} %get-tuple-element.18), channel_id=1, source_target_pairs={{0,12},{1,13},{2,14},{3,15},{4,0},{5,1},{6,2},{7,3},{8,4},{9,5},{1... | collective-permute-start | bytes 184328 | tf_op jit(solution)/shard_map/ppermute | solution.py:47
  120.9 7.2 %collective-permute-start.8 = (bf16[12,2560]{1,0:T(8,128)(2,1)S(1)}, bf16[12,2560]{1,0:T(8,128)(2,1)S(1)}, u32[]{:S(2)}, u32[]{:S(2)}) collective-permute-start(bf16[12,2560]{1,0:T(8,128)(2,1)S(1)} %get-tuple-element.17), channel_id=1, source_target_pairs={{0,8},{1,9},{2,10},{3,11},{4,12},{5,13},{6,14},{7,15},{8,0},{9,1},... | collective-permute-start | bytes 184328 | tf_op jit(solution)/shard_map/ppermute | solution.py:47

commit v2 on v1

v2 whole, which is shorter than its diff:
```python
import functools

import jax
import jax.numpy as jnp
from jax import lax
from jax.experimental import pallas as pl
from jax.experimental.pallas import tpu as pltpu
from jax.sharding import PartitionSpec as P

PLEN = 128
VMEM = pl.BlockSpec(memory_space=pltpu.VMEM)
HIDDEN_STEP = 512
FEATURE_STEP = 512


class Grid:
    def __init__(self, devices, experts):
        self.experts = experts
        self.pairs = devices // experts // 2
        index = lax.axis_index("dev")
        self.index = index
        self.expert = index // (self.pairs * 2)
        self.pair = (index // 2) % self.pairs
        self.core = index % 2

    def send(self, value, axis, step):
        moves = []
        for expert in range(self.experts):
            for pair in range(self.pairs):
                for core in range(2):
                    to = [expert, pair, core]
                    to[axis] = (to[axis] + step) % (self.experts, self.pairs, 2)[axis]
                    moves.append(
                        (
                            (expert * self.pairs + pair) * 2 + core,
                            (to[0] * self.pairs + to[1]) * 2 + to[2],
                        )
                    )
        return lax.ppermute(value, "dev", moves)


class Packing:
    def __init__(self, cap, features):
        best = None
        for chunks in range(1, features // 128 + 1):
            if features % (128 * chunks):
                continue
            rows = -(-cap * chunks // 16) * 16
            cost = rows * (features // chunks)
            if best is None or cost < best[0]:
                best = (cost, chunks, rows)
        _, self.chunks, self.rows = best
        self.cap = cap
        self.width = features // self.chunks


def route_weights(normed, router_weight, chosen):
    logits = jnp.dot(normed.astype(jnp.float32), router_weight, precision=lax.Precision.HIGHEST)
    expert_ids = jnp.arange(router_weight.shape[1], dtype=jnp.int32)
    first_logit = jnp.sum(jnp.where(chosen[:, 0:1] == expert_ids[None, :], logits, 0.0), axis=1)
    second_logit = jnp.sum(jnp.where(chosen[:, 1:2] == expert_ids[None, :], logits, 0.0), axis=1)
    return (jax.nn.sigmoid(first_logit - second_logit), jax.nn.sigmoid(second_logit - first_logit))


def tables(chosen, active, packing, grid):
    experts, rows = grid.experts, chosen.shape[0]
    relative = (chosen - grid.expert) % experts
    expert_ids = jnp.arange(experts, dtype=jnp.int32)
    routed = jnp.any(relative[:, :, None] == expert_ids, axis=1) & active[:, None]
    counts = routed.astype(jnp.int32)
    slot = jnp.cumsum(counts, axis=0) - counts
    offset = jnp.arange(packing.chunks, dtype=jnp.int32) * packing.cap
    place = jnp.arange(packing.rows, dtype=jnp.int32)
    into = (place[None, :, None, None] == offset[None, None, :, None] + slot.T[:, None, None, :]) & (
        routed.T[:, None, None, :]
    )
    into = into.reshape(experts * packing.rows, packing.chunks * rows).astype(jnp.bfloat16)
    own_slot = jnp.sum(
        jnp.where(relative[:, :, None] == expert_ids, slot[:, None, :], 0), axis=2
    )
    spot = (relative * packing.rows + own_slot).T
    back = (
        spot[:, None, :, None] + offset[None, :, None, None]
        == jnp.arange(experts * packing.rows, dtype=jnp.int32)
    ) & active[None, None, :, None]
    back = back.reshape(2 * packing.chunks * rows, experts * packing.rows).astype(jnp.bfloat16)
    return (into, back)


def modulate_kernel(packing, experts, count, into_ref, scale_ref, shift_ref, *refs):
    value_refs, out_refs = refs[:count], refs[count:]
    values = value_refs[0][...].astype(jnp.float32)
    for ref in value_refs[1:]:
        values = values + ref[...].astype(jnp.float32)
    values = values.astype(jnp.bfloat16).astype(jnp.float32)
    center = values - jnp.mean(values, axis=1, keepdims=True)
    spread = jnp.mean(center * center, axis=1, keepdims=True)
    normed = center * lax.rsqrt(spread + 1e-06) * scale_ref[...] + shift_ref[...]
    normed = normed.astype(jnp.bfloat16)
    out_refs[0][...] = normed
    width = packing.width
    stacked = jnp.concatenate(
        [normed[:, j * width : (j + 1) * width] for j in range(packing.chunks)], axis=0
    )
    packed = jnp.dot(into_ref[...], stacked, preferred_element_type=jnp.float32)
    for k in range(experts):
        out_refs[1 + k][...] = packed[k * packing.rows : (k + 1) * packing.rows].astype(
            jnp.bfloat16
        )


def modulate(parts, into, mod_scale, mod_shift, packing, experts):
    rows, features = parts[0].shape
    outs = [jax.ShapeDtypeStruct((rows, features), jnp.bfloat16)]
    outs += [jax.ShapeDtypeStruct((packing.rows, packing.width), jnp.bfloat16)] * experts
    results = pl.pallas_call(
        functools.partial(modulate_kernel, packing, experts, len(parts)),
        out_shape=outs,
        in_specs=[VMEM] * (3 + len(parts)),
        out_specs=[VMEM] * len(outs),
        compiler_params=pltpu.CompilerParams(vmem_limit_bytes=8 << 20),
        name="modulate",
    )(into, mod_scale.reshape(1, -1), mod_shift.reshape(1, -1), *parts)
    return (results[0], list(results[1:]))


def cuts(total, step):
    return [(start, min(start + step, total)) for start in range(0, total, step)]


def expert_kernel(
    packing,
    own_ref,
    other_ref,
    gate_hbm,
    up_hbm,
    down_hbm,
    own_out,
    other_out,
    gate_ref,
    up_ref,
    down_ref,
    rows_ref,
    sems,
):
    features, units = gate_hbm.shape
    feature_cuts, unit_cuts = cuts(features, FEATURE_STEP), cuts(units, HIDDEN_STEP)
    copies = []
    for lo, hi in feature_cuts:
        copies.append((gate_hbm.at[lo:hi], gate_ref.at[lo:hi]))
        copies.append((up_hbm.at[lo:hi], up_ref.at[lo:hi]))
    for lo, hi in unit_cuts:
        copies.append((down_hbm.at[lo:hi], down_ref.at[lo:hi]))
    copies = [
        pltpu.make_async_copy(source, target, sems.at[i])
        for i, (source, target) in enumerate(copies)
    ]
    for copy in copies:
        copy.start()

    cap, chunks, width = packing.cap, packing.chunks, packing.width
    blocks = own_ref.shape[0] // packing.rows * 2
    group = 16
    row_at = lax.broadcasted_iota(jnp.int32, (group * cap, group * packing.rows), 0)
    place = lax.broadcasted_iota(jnp.int32, (group * cap, group * packing.rows), 1)
    source_row = (row_at // cap) * packing.rows + row_at % cap
    packed = jnp.concatenate([own_ref[...], other_ref[...]], axis=0)
    for g in range(blocks // group):
        part = packed[g * group * packing.rows : (g + 1) * group * packing.rows]
        for j in range(chunks):
            pick = jnp.where(place == source_row + j * cap, 1.0, 0.0).astype(jnp.bfloat16)
            rows_ref[g * group * cap : (g + 1) * group * cap, j * width : (j + 1) * width] = (
                jnp.dot(pick, part, preferred_element_type=jnp.float32).astype(jnp.bfloat16)
            )

    gate, up = None, None
    for i, (lo, hi) in enumerate(feature_cuts):
        rows = rows_ref[:, lo:hi]
        copies[2 * i].wait()
        term = jnp.dot(rows, gate_ref[lo:hi, :], preferred_element_type=jnp.float32)
        gate = term if gate is None else gate + term
        copies[2 * i + 1].wait()
        term = jnp.dot(rows, up_ref[lo:hi, :], preferred_element_type=jnp.float32)
        up = term if up is None else up + term
    hidden = (gate * jax.nn.sigmoid(gate) * up).astype(jnp.bfloat16)
    total = None
    for i, (lo, hi) in enumerate(unit_cuts):
        copies[2 * len(feature_cuts) + i].wait()
        term = jnp.dot(hidden[:, lo:hi], down_ref[lo:hi, :], preferred_element_type=jnp.float32)
        total = term if total is None else total + term
    total = total.astype(jnp.bfloat16)

    place = lax.broadcasted_iota(jnp.int32, (group * packing.rows, group * cap), 0)
    row_at = lax.broadcasted_iota(jnp.int32, (group * packing.rows, group * cap), 1)
    target = (row_at // cap) * packing.rows + row_at % cap
    results = []
    for g in range(blocks // group):
        packed = None
        for j in range(chunks):
            put = jnp.where(place == target + j * cap, 1.0, 0.0).astype(jnp.bfloat16)
            term = jnp.dot(
                put,
                total[g * group * cap : (g + 1) * group * cap, j * width : (j + 1) * width],
                preferred_element_type=jnp.float32,
            )
            packed = term if packed is None else packed + term
        results.append(packed.astype(jnp.bfloat16))
    packed = results[0] if len(results) == 1 else jnp.concatenate(results, axis=0)
    own_out[...] = packed[: own_out.shape[0]]
    other_out[...] = packed[own_out.shape[0] :]


def expert_rows(own, other, w_gate, w_up, w_down, packing):
    features, units = w_gate.shape
    blocks = own.shape[0] // packing.rows * 2
    rows = blocks * packing.cap
    copies = 2 * len(cuts(features, FEATURE_STEP)) + len(cuts(units, HIDDEN_STEP))
    return pl.pallas_call(
        functools.partial(expert_kernel, packing),
        out_shape=[jax.ShapeDtypeStruct(own.shape, jnp.bfloat16)] * 2,
        in_specs=[VMEM, VMEM] + [pl.BlockSpec(memory_space=pl.ANY)] * 3,
        out_specs=[VMEM, VMEM],
        scratch_shapes=[
            pltpu.VMEM((features, units), jnp.bfloat16),
            pltpu.VMEM((features, units), jnp.bfloat16),
            pltpu.VMEM((units, features), jnp.bfloat16),
            pltpu.VMEM((rows, features), jnp.bfloat16),
            pltpu.SemaphoreType.DMA((copies,)),
        ],
        compiler_params=pltpu.CompilerParams(vmem_limit_bytes=48 << 20),
        cost_estimate=pl.CostEstimate(
            flops=6 * rows * features * units,
            bytes_accessed=6 * features * units,
            transcendentals=rows * units,
        ),
        name="experts",
    )(own, other, w_gate, w_up, w_down)


def combine_kernel(packing, back_ref, first_ref, second_ref, *refs):
    block_refs, out_ref = refs[:-1], refs[-1]
    rows = out_ref.shape[0]
    blocks = jnp.concatenate([ref[...] for ref in block_refs], axis=0)
    picked = jnp.dot(back_ref[...], blocks, preferred_element_type=jnp.float32)
    half = packing.chunks * rows
    for j in range(packing.chunks):
        first = picked[j * rows : (j + 1) * rows]
        second = picked[half + j * rows : half + (j + 1) * rows]
        out_ref[:, j * packing.width : (j + 1) * packing.width] = (
            first_ref[...] * first + second_ref[...] * second
        ).astype(jnp.bfloat16)


def combine(back, weights, blocks, packing, rows, features):
    first, second = weights
    return pl.pallas_call(
        functools.partial(combine_kernel, packing),
        out_shape=jax.ShapeDtypeStruct((rows, features), jnp.bfloat16),
        in_specs=[VMEM] * (3 + len(blocks)),
        out_specs=VMEM,
        compiler_params=pltpu.CompilerParams(vmem_limit_bytes=8 << 20),
        name="combine",
    )(back, first[:, None], second[:, None], *blocks)


def dispatch(blocks, grid):
    held = [blocks[0]] + [grid.send(blocks[k], 0, k) for k in range(1, grid.experts)]
    block = jnp.concatenate(held, axis=0)
    block = jnp.concatenate(
        [block] + [grid.send(block, 1, k) for k in range(1, grid.pairs)], axis=0
    )
    return (block, grid.send(block, 2, 1))


def give_back(own, other, grid):
    total = own.astype(jnp.float32) + grid.send(other, 2, 1).astype(jnp.float32)
    rows = total.shape[0] // grid.pairs
    parts = [total[k * rows : (k + 1) * rows] for k in range(grid.pairs)]
    total = parts[0]
    for k in range(1, grid.pairs):
        total = total + grid.send(parts[k].astype(jnp.bfloat16), 1, -k).astype(jnp.float32)
    total = total.astype(jnp.bfloat16)
    rows = rows // grid.experts
    parts = [total[k * rows : (k + 1) * rows] for k in range(grid.experts)]
    return [parts[0]] + [grid.send(parts[k], 0, -k) for k in range(1, grid.experts)]


def project(text_hidden, caption_weight, grid):
    rows = text_hidden.shape[0] // (grid.experts * grid.pairs * 2)
    text = text_hidden.reshape(grid.experts, grid.pairs, 2, rows, text_hidden.shape[1])
    text = jnp.roll(text, -grid.expert, axis=0)
    text = jnp.roll(text, -grid.pair, axis=1)
    text = jnp.roll(text, -grid.core, axis=2)
    text = jnp.transpose(text, (2, 1, 0, 3, 4)).reshape(2, -1, text_hidden.shape[1])
    other = jnp.dot(text[1], caption_weight, preferred_element_type=jnp.float32)
    own = jnp.dot(text[0], caption_weight, preferred_element_type=jnp.float32)
    total = own + grid.send(other.astype(jnp.bfloat16), 2, 1).astype(jnp.float32)
    rows_pair = rows * grid.experts
    parts = [total[k * rows_pair : (k + 1) * rows_pair] for k in range(grid.pairs)]
    total = parts[0]
    for k in range(1, grid.pairs):
        total = total + grid.send(parts[k].astype(jnp.bfloat16), 1, k).astype(jnp.float32)
    parts = [total[k * rows : (k + 1) * rows] for k in range(grid.experts)]
    return [parts[0]] + [
        grid.send(parts[k].astype(jnp.bfloat16), 0, k) for k in range(1, grid.experts)
    ]


def local(
    image_rows,
    text_hidden,
    caption_weight,
    mod_scale,
    mod_shift,
    router_weight,
    image_experts,
    caption_experts,
    prompt_lengths,
    w_gate,
    w_up,
    w_down,
):
    devices = lax.axis_size("dev")
    features, experts = router_weight.shape
    grid = Grid(devices, experts)
    caption_rows = text_hidden.shape[0] // devices
    caption_packing = Packing(caption_rows // 2 + 1, features)
    image_packing = Packing(image_rows.shape[0] * 3 // 4, features)
    position = grid.index * caption_rows + jnp.arange(caption_rows, dtype=jnp.int32)
    prompt_ids = position // PLEN
    prompt_range = jnp.arange(prompt_lengths.shape[0], dtype=jnp.int32)
    lengths = jnp.sum(
        jnp.where(prompt_ids[:, None] == prompt_range[None, :], prompt_lengths[None, :], 0), axis=1
    )
    caption_active = position % PLEN < lengths
    image_active = jnp.ones((image_rows.shape[0],), jnp.bool_)

    def block(parts, chosen, active, packing):
        into, back = tables(chosen, active, packing, grid)
        normed, blocks = modulate(parts, into, mod_scale, mod_shift, packing, experts)
        own, other = dispatch(blocks, grid)
        own, other = expert_rows(own, other, w_gate, w_up, w_down, packing)
        weights = route_weights(normed, router_weight, chosen)
        blocks = give_back(own, other, grid)
        return combine(back, weights, blocks, packing, chosen.shape[0], features)

    caption = project(text_hidden, caption_weight, grid)
    image_out = block([image_rows], image_experts, image_active, image_packing)
    caption_out = block(caption, caption_experts, caption_active, caption_packing)
    return (image_out, caption_out)


def solution(mesh):
    in_specs = (
        P(("groups", "dev"), None),
        P("groups", "dev"),
        P("dev", None),
        P(),
        P(),
        P(),
        P(("groups", "dev"), None),
        P(("groups", "dev"), None),
        P("groups"),
        P(None, "dev"),
        P(None, "dev"),
        P("dev", None),
    )
    out_specs = (P(("groups", "dev"), None), P(("groups", "dev"), None))
    return jax.shard_map(local, mesh=mesh, in_specs=in_specs, out_specs=out_specs, check_vma=False)
```

time: 130 us -> 122 us (0.938)
  matrix products: 43.4 us -> 1.11 us
  Pallas kernels: 0 us -> 25.9 us
  local copies, waits for them, and re-layouts: 14.8 us -> 31.1 us
  waiting for transfers between devices: 34.7 us -> 26.8 us
  starting transfers between devices: 31.2 us -> 28.7 us
  other arithmetic: 4.04 us -> 6.17 us
    dot_general x14 -> x0, matrix products: 42.3 us -> none  [the longest x2 24.1 us: expert_rows(): jnp.dot(hidden, w_down, preferred_element_type=jnp.float32)]
    unnamed x28 -> x36, local copies, waits for them, and re-layouts: 0.08 us -> 26.5 us
    pallas_call x0 -> x6, Pallas kernels: none -> 25.9 us  [the longest x2 23.4 us: expert_rows(): pl.pallas_call(functools.partial(expert_kernel, packing), out_shape=[jax....]
    ppermute x25, waiting for transfers between devices: 34.7 us -> 26.8 us  [send(): return lax.ppermute(value, 'dev', moves)]
    concatenate x2, local copies, waits for them, and re-layouts: 6.09 us -> 0.04 us  [dispatch(): jnp.concatenate([block] + [grid.send(block, 1, k) for k in range(1, grid....]
    concatenate x2 -> x0, local copies, waits for them, and re-layouts: 5.14 us -> none  [expert_rows(): rows = jnp.concatenate([own, other], axis=0)]
    slice x3 -> x2, local copies, waits for them, and re-layouts: 2.9 us -> 0.04 us  [give_back(): parts = [total[k * rows:(k + 1) * rows] for k in range(grid.experts)]]
    ppermute x25, starting transfers between devices: 31.2 us -> 28.7 us  [send(): return lax.ppermute(value, 'dev', moves)]
  transfers between devices with their start and end apart: 25 -> 25, of which waited for: 13 -> 10; matrix products, arithmetic and copies ran while one was open for 43% -> 29% of each run, Pallas kernels for 0% -> 21%
where the time goes in v2:
time: 122 us; the launch traced here: 121 us
  local copies, waits for them, and re-layouts  31.1 us (25%)
  starting transfers between devices  28.7 us (24%)
  waiting for transfers between devices  26.8 us (22%)
  Pallas kernels  25.9 us (21%)
  other arithmetic  6.17 us (5%)
  between operations  1.37 us (1%)
    ppermute x25, starting transfers between devices, send(): return lax.ppermute(value, 'dev', moves)  28.7 us
    ppermute x25, waiting for transfers between devices, send(): return lax.ppermute(value, 'dev', moves)  26.8 us
    unnamed x36, local copies, waits for them, and re-layouts  26.5 us
    pallas_call x2, Pallas kernels, expert_rows(): pl.pallas_call(functools.partial(expert_kernel, packing), out_shape=[jax....  23.4 us
  transfers between devices with their start and end apart: 25, of which 10 were waited for; matrix products, arithmetic and copies ran while one was open for 29% of the time, Pallas kernels for 21%

profile of v2, /device:TPU:0, one launch (start us, length us, event | category | flops | bytes accessed | tf_op | source)
XLA Modules:
  0.0 121.2 jit_solution(15089186412861413477)
XLA Ops:
  0.7 1.0 fusion.7
  2.1 0.3 convolution_convert_fusion
  2.4 0.5 collective-permute-start.10
  3.1 0.1 copy.77
  3.3 0.1 eq.209
  3.5 0.1 eq.210
  3.8 0.1 and.132
  3.9 0.1 copy.82
  4.1 0.1 and_convert_fusion.1.into_ref
  4.2 0.4 modulate.2
  4.6 2.7 %collective-permute-start = (bf16[48,640]{1,0:T(8,128)(2,1)S(1)}, bf16[48,640]{1,0:T(8,128)(2,1)}, u32[]{:S(2)}, u32[]{:S(2)}) collective-permute-start(bf16[48,640]{1,0:T(8,128)(2,1)S(1)} %get-tuple-element.18), channel_id=1, source_target_pairs={{0,4},{1,5},{2,6},{3,7},{4,8},{5,9},{6,10},{7,11},{8,12},{9,13},{1... | collective-permute-start | bytes 184328 | tf_op jit(solution)/shard_map/ppermute | solution.py:39
  7.3 2.6 %collective-permute-start.1 = (bf16[48,640]{1,0:T(8,128)(2,1)S(1)}, bf16[48,640]{1,0:T(8,128)(2,1)S(1)}, u32[]{:S(2)}, u32[]{:S(2)}) collective-permute-start(bf16[48,640]{1,0:T(8,128)(2,1)S(1)} %get-tuple-element.19), channel_id=1, source_target_pairs={{0,8},{1,9},{2,10},{3,11},{4,12},{5,13},{6,14},{7,15},{8,0},{9,1},... | collective-permute-start | bytes 184328 | tf_op jit(solution)/shard_map/ppermute | solution.py:39
  9.8 1.3 %collective-permute-start.2 = (bf16[48,640]{1,0:T(8,128)(2,1)S(1)}, bf16[48,640]{1,0:T(8,128)(2,1)S(1)}, u32[]{:S(2)}, u32[]{:S(2)}) collective-permute-start(bf16[48,640]{1,0:T(8,128)(2,1)S(1)} %get-tuple-element.20), channel_id=1, source_target_pairs={{0,12},{1,13},{2,14},{3,15},{4,0},{5,1},{6,2},{7,3},{8,4},{9,5},{1... | collective-permute-start | bytes 184328 | tf_op jit(solution)/shard_map/ppermute | solution.py:39
  11.2 0.1 copy.87
  11.5 0.7 bitcast_subtract_fusion
  13.0 0.1 fusion.8.back_ref
  13.1 0.1 fusion.3.back_ref
  13.2 0.6 slice_bitcast_fusion.1
  13.8 0.1 eq.230
  13.9 0.1 eq.231
  14.2 0.8 and.144
  14.9 0.1 and.145
  15.1 0.1 copy.91
  15.2 12.7 %copy.83.gate_hbm = bf16[2560,1728]{1,0:T(8,128)(2,1)} copy(bf16[2560,1728]{0,1:T(8,128)(2,1)} %param.21) | data formatting | bytes 17694720 | tf_op args[9]
  27.9 12.8 %copy.84.up_hbm = bf16[2560,1728]{1,0:T(8,128)(2,1)} copy(bf16[2560,1728]{0,1:T(8,128)(2,1)} %param.22) | data formatting | bytes 17694720 | tf_op args[10]
  40.9 0.9 pad_maximum_fusion
  41.7 1.6 %collective-permute-start.3 = (bf16[192,640]{1,0:T(8,128)(2,1)S(1)}, bf16[192,640]{1,0:T(8,128)(2,1)S(1)}, u32[]{:S(2)}, u32[]{:S(2)}) collective-permute-start(bf16[192,640]{1,0:T(8,128)(2,1)S(1)} %pad_maximum_fusion), channel_id=1, source_target_pairs={{0,2},{1,3},{2,0},{3,1},{4,6},{5,7},{6,4},{7,5},{8,10},{9,11},{10,... | collective-permute-start | bytes 737288 | tf_op jit(solution)/shard_map/ppermute | solution.py:39
  43.3 0.8 constant_dynamic-update-slice_fusion.3
  44.1 0.3 convert_add_fusion
  44.5 0.6 collective-permute-start.11
  45.1 5.5 %collective-permute-done.3 = bf16[192,640]{1,0:T(8,128)(2,1)S(1)} collective-permute-done((bf16[192,640]{1,0:T(8,128)(2,1)S(1)}, bf16[192,640]{1,0:T(8,128)(2,1)S(1)}, u32[]{:S(2)}, u32[]{:S(2)}) %collective-permute-start.3) | collective-permute-done | bytes 245792 | tf_op jit(solution)/shard_map/ppermute | solution.py:39
  50.8 5.5 %collective-permute-done.11 = bf16[64,2560]{1,0:T(8,128)(2,1)S(1)} collective-permute-done((bf16[64,2560]{1,0:T(8,128)(2,1)S(1)}, bf16[64,2560]{1,0:T(8,128)(2,1)S(1)}, u32[]{:S(2)}, u32[]{:S(2)}) %collective-permute-start.11) | collective-permute-done | bytes 327712 | tf_op jit(solution)/shard_map/ppermute | solution.py:39
  56.4 0.8 collective-permute-start.12
  57.2 0.3 collective-permute-start.13
  57.5 2.8 %collective-permute-start.14 = (bf16[16,2560]{1,0:T(8,128)(2,1)S(1)}, bf16[16,2560]{1,0:T(8,128)(2,1)S(1)}, u32[]{:S(2)}, u32[]{:S(2)}) collective-permute-start(bf16[16,2560]{1,0:T(8,128)(2,1)S(1)} %get-tuple-element.38), channel_id=1, source_target_pairs={{0,12},{1,13},{2,14},{3,15},{4,0},{5,1},{6,2},{7,3},{8,4},{9,5},{1... | collective-permute-start | bytes 245768 | tf_op jit(solution)/shard_map/ppermute | solution.py:39
  60.3 12.2 %experts.2 = (bf16[384,640]{1,0:T(8,128)(2,1)S(1)}, bf16[384,640]{1,0:T(8,128)(2,1)S(1)}) custom-call(bf16[384,640]{1,0:T(8,128)(2,1)S(1)} %constant_dynamic-update-slice_fusion.own_ref, bf16[384,640]{1,0:T(8,128)(2,1)S(1)} %collective-permute-done.4.other_ref, bf16[2560,1728]{1,0:T(8,128)(2,1)} %copy.83.gate_hbm, bf16[2560,1728]{1,0:T(8,128)(2,1)} %copy.84.up_hbm, ...), custom_call_target="tpu_custom_call" | custom-call | flops 5096079360 | bytes 26542080 | tf_op jit(solution)/shard_map/experts/pallas_call | solution.py:218
  72.7 0.4 modulate.3
  73.1 0.6 collective-permute-start.15
  73.7 1.5 %collective-permute-start.16 = (bf16[48,512]{1,0:T(8,128)(2,1)S(1)}, bf16[48,512]{1,0:T(8,128)(2,1)S(1)}, u32[]{:S(2)}, u32[]{:S(2)}) collective-permute-start(bf16[48,512]{1,0:T(8,128)(2,1)S(1)} %get-tuple-element.26), channel_id=1, source_target_pairs={{0,8},{1,9},{2,10},{3,11},{4,12},{5,13},{6,14},{7,15},{8,0},{9,1},... | collective-permute-start | bytes 147464 | tf_op jit(solution)/shard_map/ppermute | solution.py:39
  75.3 2.8 %collective-permute-start.17 = (bf16[48,512]{1,0:T(8,128)(2,1)S(1)}, bf16[48,512]{1,0:T(8,128)(2,1)S(1)}, u32[]{:S(2)}, u32[]{:S(2)}) collective-permute-start(bf16[48,512]{1,0:T(8,128)(2,1)S(1)} %get-tuple-element.27), channel_id=1, source_target_pairs={{0,12},{1,13},{2,14},{3,15},{4,0},{5,1},{6,2},{7,3},{8,4},{9,5},{1... | collective-permute-start | bytes 147464 | tf_op jit(solution)/shard_map/ppermute | solution.py:39
  78.1 1.3 %collective-permute-done.15 = bf16[48,512]{1,0:T(8,128)(2,1)S(1)} collective-permute-done((bf16[48,512]{1,0:T(8,128)(2,1)S(1)}, bf16[48,512]{1,0:T(8,128)(2,1)S(1)}, u32[]{:S(2)}, u32[]{:S(2)}) %collective-permute-start.15) | collective-permute-done | bytes 49184 | tf_op jit(solution)/shard_map/ppermute | solution.py:39
  79.4 1.7 %collective-permute-done.16 = bf16[48,512]{1,0:T(8,128)(2,1)S(1)} collective-permute-done((bf16[48,512]{1,0:T(8,128)(2,1)S(1)}, bf16[48,512]{1,0:T(8,128)(2,1)S(1)}, u32[]{:S(2)}, u32[]{:S(2)}) %collective-permute-start.16) | collective-permute-done | bytes 49184 | tf_op jit(solution)/shard_map/ppermute | solution.py:39
  81.1 1.6 %collective-permute-start.18 = (bf16[192,512]{1,0:T(8,128)(2,1)S(1)}, bf16[192,512]{1,0:T(8,128)(2,1)S(1)}, u32[]{:S(2)}, u32[]{:S(2)}) collective-permute-start(bf16[192,512]{1,0:T(8,128)(2,1)S(1)} %pad_maximum_fusion.1), channel_id=1, source_target_pairs={{0,2},{1,3},{2,0},{3,1},{4,6},{5,7},{6,4},{7,5},{8,10},{9,11},{10,... | collective-permute-start | bytes 589832 | tf_op jit(solution)/shard_map/ppermute | solution.py:39
  82.7 4.5 %collective-permute-done.18 = bf16[192,512]{1,0:T(8,128)(2,1)S(1)} collective-permute-done((bf16[192,512]{1,0:T(8,128)(2,1)S(1)}, bf16[192,512]{1,0:T(8,128)(2,1)S(1)}, u32[]{:S(2)}, u32[]{:S(2)}) %collective-permute-start.18) | collective-permute-done | bytes 196640 | tf_op jit(solution)/shard_map/ppermute | solution.py:39
  87.4 0.2 select_reduce_fusion.4
  87.7 0.1 convert_add_fusion.1
  87.8 0.7 slice.139
  88.5 1.5 %collective-permute-start.6 = (bf16[192,640]{1,0:T(8,128)(2,1)}, bf16[192,640]{1,0:T(8,128)(2,1)}, u32[]{:S(2)}, u32[]{:S(2)}) collective-permute-start(bf16[192,640]{1,0:T(8,128)(2,1)} %slice.139), channel_id=1, source_target_pairs={{0,2},{1,3},{2,0},{3,1},{4,6},{5,7},{6,4},{7,5},{8,10},{9,11},{10,... | collective-permute-start | bytes 737288 | tf_op jit(solution)/shard_map/ppermute | solution.py:39
  90.0 11.2 %experts.3 = (bf16[384,512]{1,0:T(8,128)(2,1)S(1)}, bf16[384,512]{1,0:T(8,128)(2,1)S(1)}) custom-call(bf16[384,512]{1,0:T(8,128)(2,1)S(1)} %constant_dynamic-update-slice_fusion.5.own_ref, bf16[384,512]{1,0:T(8,128)(2,1)S(1)} %collective-permute-done.19.other_ref, bf16[2560,1728]{1,0:T(8,128)(2,1)} %copy.83.gate_hbm, bf16[2560,1728]{1,0:T(8,128)(2,1)} %copy.84.up_hbm, ...), custom_call_target="tpu_custom_call" | custom-call | flops 3822059520 | bytes 26542080 | tf_op jit(solution)/shard_map/experts/pallas_call | solution.py:218
  101.2 0.3 collective-permute-start.20
  101.6 0.2 select_reduce_fusion.2
  101.9 1.0 fusion
  102.9 0.2 collective-permute-done.20
  103.1 1.1 convert_add_fusion.2
  104.2 0.7 collective-permute-start.21
  105.0 2.5 %collective-permute-start.7 = (bf16[48,640]{1,0:T(8,128)(2,1)S(1)}, bf16[48,640]{1,0:T(8,128)(2,1)S(1)}, u32[]{:S(2)}, u32[]{:S(2)}) collective-permute-start(bf16[48,640]{1,0:T(8,128)(2,1)S(1)} %get-tuple-element.43), channel_id=1, source_target_pairs={{0,12},{1,13},{2,14},{3,15},{4,0},{5,1},{6,2},{7,3},{8,4},{9,5},{1... | collective-permute-start | bytes 184328 | tf_op jit(solution)/shard_map/ppermute | solution.py:39
  107.5 0.6 collective-permute-start.8
  108.1 3.2 %collective-permute-done.21 = bf16[192,512]{1,0:T(8,128)(2,1)S(1)} collective-permute-done((bf16[192,512]{1,0:T(8,128)(2,1)S(1)}, bf16[192,512]{1,0:T(8,128)(2,1)S(1)}, u32[]{:S(2)}, u32[]{:S(2)}) %collective-permute-start.21) | collective-permute-done | bytes 196640 | tf_op jit(solution)/shard_map/ppermute | solution.py:39
  111.4 2.5 %collective-permute-start.22 = (bf16[48,512]{1,0:T(8,128)(2,1)S(1)}, bf16[48,512]{1,0:T(8,128)(2,1)S(1)}, u32[]{:S(2)}, u32[]{:S(2)}) collective-permute-start(bf16[48,512]{1,0:T(8,128)(2,1)S(1)} %get-tuple-element.47), channel_id=1, source_target_pairs={{0,12},{1,13},{2,14},{3,15},{4,0},{5,1},{6,2},{7,3},{8,4},{9,5},{1... | collective-permute-start | bytes 147464 | tf_op jit(solution)/shard_map/ppermute | solution.py:39
  113.9 0.6 collective-permute-start.23
  114.7 0.9 combine.2
  115.6 3.3 %collective-permute-done.23.refs_2_ = bf16[48,512]{1,0:T(8,128)(2,1)S(1)} collective-permute-done((bf16[48,512]{1,0:T(8,128)(2,1)S(1)}, bf16[48,512]{1,0:T(8,128)(2,1)S(1)}, u32[]{:S(2)}, u32[]{:S(2)}) %collective-permute-start.23) | collective-permute-done | bytes 49184 | tf_op jit(solution)/shard_map/ppermute | solution.py:39
  118.9 1.4 %collective-permute-done.24.refs_3_ = bf16[48,512]{1,0:T(8,128)(2,1)S(1)} collective-permute-done((bf16[48,512]{1,0:T(8,128)(2,1)S(1)}, bf16[48,512]{1,0:T(8,128)(2,1)S(1)}, u32[]{:S(2)}, u32[]{:S(2)}) %collective-permute-start.24) | collective-permute-done | bytes 49184 | tf_op jit(solution)/shard_map/ppermute | solution.py:39
  120.3 0.8 combine.3
  (114 shorter events, 3.0 us)
Async XLA Ops:
  0.6 1.4 %copy-start = (bf16[256,2560]{1,0:T(8,128)(2,1)S(1)}, bf16[256,2560]{1,0:T(8,128)(2,1)}, u32[]{:S(2)}) copy-start(bf16[256,2560]{1,0:T(8,128)(2,1)} %param.14) | copy-start | bytes 3932164
  1.9 1.1 copy-start.3
  1.9 1.2 copy-start.4
  1.9 1.2 copy-start.7
  1.9 1.2 copy-start.8
  2.0 2.1 %copy-start.1 = (bf16[16,2560]{1,0:T(8,128)(2,1)S(1)}, bf16[16,2560]{1,0:T(8,128)(2,1)}, u32[]{:S(2)}) copy-start(bf16[16,2560]{1,0:T(8,128)(2,1)} %refs_0_.1) | copy-start | bytes 245764
  2.1 9.3 %copy-start.12 = (s32[2]{0:T(128)S(1)}, s32[2]{0:T(128)}, u32[]{:S(2)}) copy-start(s32[2]{0:T(128)} %param.20) | copy-start | bytes 28
  2.4 41.7 %collective-permute-start.10 = (bf16[128,2560]{1,0:T(8,128)(2,1)S(1)}, bf16[128,2560]{1,0:T(8,128)(2,1)S(1)}, u32[]{:S(2)}, u32[]{:S(2)}) collective-permute-start(bf16[128,2560]{1,0:T(8,128)(2,1)S(1)} %convolution_convert_fusion), channel_id=1, source_target_pairs={{0,1},{1,0},{2,3},{3,2},{4,5},{5,4},{6,7},{7,6},{8,9},{9,8},{10,11... | collective-permute-start | bytes 1966088 | tf_op jit(solution)/shard_map/ppermute | solution.py:39
  3.0 1.0 copy-start.5
  4.6 36.2 %collective-permute-start = (bf16[48,640]{1,0:T(8,128)(2,1)S(1)}, bf16[48,640]{1,0:T(8,128)(2,1)}, u32[]{:S(2)}, u32[]{:S(2)}) collective-permute-start(bf16[48,640]{1,0:T(8,128)(2,1)S(1)} %get-tuple-element.18), channel_id=1, source_target_pairs={{0,4},{1,5},{2,6},{3,7},{4,8},{5,9},{6,10},{7,11},{8,12},{9,13},{1... | collective-permute-start | bytes 184328 | tf_op jit(solution)/shard_map/ppermute | solution.py:39
  7.3 33.6 %collective-permute-start.1 = (bf16[48,640]{1,0:T(8,128)(2,1)S(1)}, bf16[48,640]{1,0:T(8,128)(2,1)S(1)}, u32[]{:S(2)}, u32[]{:S(2)}) collective-permute-start(bf16[48,640]{1,0:T(8,128)(2,1)S(1)} %get-tuple-element.19), channel_id=1, source_target_pairs={{0,8},{1,9},{2,10},{3,11},{4,12},{5,13},{6,14},{7,15},{8,0},{9,1},... | collective-permute-start | bytes 184328 | tf_op jit(solution)/shard_map/ppermute | solution.py:39
  9.8 31.0 %collective-permute-start.2 = (bf16[48,640]{1,0:T(8,128)(2,1)S(1)}, bf16[48,640]{1,0:T(8,128)(2,1)S(1)}, u32[]{:S(2)}, u32[]{:S(2)}) collective-permute-start(bf16[48,640]{1,0:T(8,128)(2,1)S(1)} %get-tuple-element.20), channel_id=1, source_target_pairs={{0,12},{1,13},{2,14},{3,15},{4,0},{5,1},{6,2},{7,3},{8,4},{9,5},{1... | collective-permute-start | bytes 184328 | tf_op jit(solution)/shard_map/ppermute | solution.py:39
  27.9 12.8 %copy-start.6 = (s32[192]{0:T(256)S(1)}, s32[192]{0:T(256)}, u32[]{:S(2)}) copy-start(s32[192]{0:T(256)} %copy-done.5) | copy-start | bytes 2308
  41.7 8.9 %collective-permute-start.3 = (bf16[192,640]{1,0:T(8,128)(2,1)S(1)}, bf16[192,640]{1,0:T(8,128)(2,1)S(1)}, u32[]{:S(2)}, u32[]{:S(2)}) collective-permute-start(bf16[192,640]{1,0:T(8,128)(2,1)S(1)} %pad_maximum_fusion), channel_id=1, source_target_pairs={{0,2},{1,3},{2,0},{3,1},{4,6},{5,7},{6,4},{7,5},{8,10},{9,11},{10,... | collective-permute-start | bytes 737288 | tf_op jit(solution)/shard_map/ppermute | solution.py:39
  44.5 11.7 %collective-permute-start.11 = (bf16[64,2560]{1,0:T(8,128)(2,1)S(1)}, bf16[64,2560]{1,0:T(8,128)(2,1)S(1)}, u32[]{:S(2)}, u32[]{:S(2)}) collective-permute-start(bf16[64,2560]{1,0:T(8,128)(2,1)S(1)} %slice.138), channel_id=1, source_target_pairs={{0,2},{1,3},{2,0},{3,1},{4,6},{5,7},{6,4},{7,5},{8,10},{9,11},{10,... | collective-permute-start | bytes 983048 | tf_op jit(solution)/shard_map/ppermute | solution.py:39
  50.7 9.6 %collective-permute-start.4 = (bf16[384,640]{1,0:T(8,128)(2,1)S(1)}, bf16[384,640]{1,0:T(8,128)(2,1)S(1)}, u32[]{:S(2)}, u32[]{:S(2)}) collective-permute-start(bf16[384,640]{1,0:T(8,128)(2,1)S(1)} %constant_dynamic-update-slice_fusion.own_ref), channel_id=1, source_target_pairs={{0,1},{1,0},{2,3},{3,2},{4,5},{5,4},{6,7},{7,6},{8,9},{9,8},{10,11... | collective-permute-start | bytes 1474568 | tf_op jit(solution)/shard_map/ppermute | solution.py:39
  56.4 16.3 %collective-permute-start.12 = (bf16[16,2560]{1,0:T(8,128)(2,1)S(1)}, bf16[16,2560]{1,0:T(8,128)(2,1)S(1)}, u32[]{:S(2)}, u32[]{:S(2)}) collective-permute-start(bf16[16,2560]{1,0:T(8,128)(2,1)S(1)} %get-tuple-element.40), channel_id=1, source_target_pairs={{0,4},{1,5},{2,6},{3,7},{4,8},{5,9},{6,10},{7,11},{8,12},{9,13},{1... | collective-permute-start | bytes 245768 | tf_op jit(solution)/shard_map/ppermute | solution.py:39
  57.2 15.5 %collective-permute-start.13 = (bf16[16,2560]{1,0:T(8,128)(2,1)S(1)}, bf16[16,2560]{1,0:T(8,128)(2,1)S(1)}, u32[]{:S(2)}, u32[]{:S(2)}) collective-permute-start(bf16[16,2560]{1,0:T(8,128)(2,1)S(1)} %get-tuple-element.39), channel_id=1, source_target_pairs={{0,8},{1,9},{2,10},{3,11},{4,12},{5,13},{6,14},{7,15},{8,0},{9,1},... | collective-permute-start | bytes 245768 | tf_op jit(solution)/shard_map/ppermute | solution.py:39
  57.5 15.2 %collective-permute-start.14 = (bf16[16,2560]{1,0:T(8,128)(2,1)S(1)}, bf16[16,2560]{1,0:T(8,128)(2,1)S(1)}, u32[]{:S(2)}, u32[]{:S(2)}) collective-permute-start(bf16[16,2560]{1,0:T(8,128)(2,1)S(1)} %get-tuple-element.38), channel_id=1, source_target_pairs={{0,12},{1,13},{2,14},{3,15},{4,0},{5,1},{6,2},{7,3},{8,4},{9,5},{1... | collective-permute-start | bytes 245768 | tf_op jit(solution)/shard_map/ppermute | solution.py:39
  72.5 14.9 %copy-start.9 = (s32[16,2]{0,1:T(2,128)S(1)}, s32[16,2]{0,1:T(2,128)}, u32[]{:S(2)}) copy-start(s32[16,2]{0,1:T(2,128)} %param.18) | copy-start | bytes 388
  72.5 14.9 %copy-start.2 = (f32[2560,4]{0,1:T(4,128)S(1)}, f32[2560,4]{0,1:T(4,128)}, u32[]{:S(2)}) copy-start(f32[2560,4]{0,1:T(4,128)} %param.17) | copy-start | bytes 122884
  72.5 15.1 %collective-permute-start.5 = (bf16[384,640]{1,0:T(8,128)(2,1)S(1)}, bf16[384,640]{1,0:T(8,128)(2,1)S(1)}, u32[]{:S(2)}, u32[]{:S(2)}) collective-permute-start(bf16[384,640]{1,0:T(8,128)(2,1)S(1)} %get-tuple-element.22), channel_id=1, source_target_pairs={{0,1},{1,0},{2,3},{3,2},{4,5},{5,4},{6,7},{7,6},{8,9},{9,8},{10,11... | collective-permute-start | bytes 1474568 | tf_op jit(solution)/shard_map/ppermute | solution.py:39
  73.1 6.3 %collective-permute-start.15 = (bf16[48,512]{1,0:T(8,128)(2,1)S(1)}, bf16[48,512]{1,0:T(8,128)(2,1)S(1)}, u32[]{:S(2)}, u32[]{:S(2)}) collective-permute-start(bf16[48,512]{1,0:T(8,128)(2,1)S(1)} %get-tuple-element.25), channel_id=1, source_target_pairs={{0,4},{1,5},{2,6},{3,7},{4,8},{5,9},{6,10},{7,11},{8,12},{9,13},{1... | collective-permute-start | bytes 147464 | tf_op jit(solution)/shard_map/ppermute | solution.py:39
  73.7 7.4 %collective-permute-start.16 = (bf16[48,512]{1,0:T(8,128)(2,1)S(1)}, bf16[48,512]{1,0:T(8,128)(2,1)S(1)}, u32[]{:S(2)}, u32[]{:S(2)}) collective-permute-start(bf16[48,512]{1,0:T(8,128)(2,1)S(1)} %get-tuple-element.26), channel_id=1, source_target_pairs={{0,8},{1,9},{2,10},{3,11},{4,12},{5,13},{6,14},{7,15},{8,0},{9,1},... | collective-permute-start | bytes 147464 | tf_op jit(solution)/shard_map/ppermute | solution.py:39
  75.3 5.9 %collective-permute-start.17 = (bf16[48,512]{1,0:T(8,128)(2,1)S(1)}, bf16[48,512]{1,0:T(8,128)(2,1)S(1)}, u32[]{:S(2)}, u32[]{:S(2)}) collective-permute-start(bf16[48,512]{1,0:T(8,128)(2,1)S(1)} %get-tuple-element.27), channel_id=1, source_target_pairs={{0,12},{1,13},{2,14},{3,15},{4,0},{5,1},{6,2},{7,3},{8,4},{9,5},{1... | collective-permute-start | bytes 147464 | tf_op jit(solution)/shard_map/ppermute | solution.py:39
  81.1 6.2 %collective-permute-start.18 = (bf16[192,512]{1,0:T(8,128)(2,1)S(1)}, bf16[192,512]{1,0:T(8,128)(2,1)S(1)}, u32[]{:S(2)}, u32[]{:S(2)}) collective-permute-start(bf16[192,512]{1,0:T(8,128)(2,1)S(1)} %pad_maximum_fusion.1), channel_id=1, source_target_pairs={{0,2},{1,3},{2,0},{3,1},{4,6},{5,7},{6,4},{7,5},{8,10},{9,11},{10,... | collective-permute-start | bytes 589832 | tf_op jit(solution)/shard_map/ppermute | solution.py:39
  87.3 2.7 %collective-permute-start.19 = (bf16[384,512]{1,0:T(8,128)(2,1)S(1)}, bf16[384,512]{1,0:T(8,128)(2,1)S(1)}, u32[]{:S(2)}, u32[]{:S(2)}) collective-permute-start(bf16[384,512]{1,0:T(8,128)(2,1)S(1)} %constant_dynamic-update-slice_fusion.5.own_ref), channel_id=1, source_target_pairs={{0,1},{1,0},{2,3},{3,2},{4,5},{5,4},{6,7},{7,6},{8,9},{9,8},{10,11... | collective-permute-start | bytes 1179656 | tf_op jit(solution)/shard_map/ppermute | solution.py:39
  88.5 13.1 %copy-start.10 = (s32[16]{0:T(128)S(1)}, s32[16]{0:T(128)}, u32[]{:S(2)}) copy-start(s32[16]{0:T(128)} %get-tuple-element.53) | copy-start | bytes 196
  88.5 13.1 %copy-start.11 = (s32[16]{0:T(128)S(1)}, s32[16]{0:T(128)}, u32[]{:S(2)}) copy-start(s32[16]{0:T(128)} %get-tuple-element.54) | copy-start | bytes 196
  88.5 13.4 %collective-permute-start.6 = (bf16[192,640]{1,0:T(8,128)(2,1)}, bf16[192,640]{1,0:T(8,128)(2,1)}, u32[]{:S(2)}, u32[]{:S(2)}) collective-permute-start(bf16[192,640]{1,0:T(8,128)(2,1)} %slice.139), channel_id=1, source_target_pairs={{0,2},{1,3},{2,0},{3,1},{4,6},{5,7},{6,4},{7,5},{8,10},{9,11},{10,... | collective-permute-start | bytes 737288 | tf_op jit(solution)/shard_map/ppermute | solution.py:39
  101.2 1.9 %collective-permute-start.20 = (bf16[384,512]{1,0:T(8,128)(2,1)S(1)}, bf16[384,512]{1,0:T(8,128)(2,1)}, u32[]{:S(2)}, u32[]{:S(2)}) collective-permute-start(bf16[384,512]{1,0:T(8,128)(2,1)S(1)} %get-tuple-element.29), channel_id=1, source_target_pairs={{0,1},{1,0},{2,3},{3,2},{4,5},{5,4},{6,7},{7,6},{8,9},{9,8},{10,11... | collective-permute-start | bytes 1179656 | tf_op jit(solution)/shard_map/ppermute | solution.py:39
  104.2 7.1 %collective-permute-start.21 = (bf16[192,512]{1,0:T(8,128)(2,1)S(1)}, bf16[192,512]{1,0:T(8,128)(2,1)S(1)}, u32[]{:S(2)}, u32[]{:S(2)}) collective-permute-start(bf16[192,512]{1,0:T(8,128)(2,1)S(1)} %slice.140), channel_id=1, source_target_pairs={{0,2},{1,3},{2,0},{3,1},{4,6},{5,7},{6,4},{7,5},{8,10},{9,11},{10,... | collective-permute-start | bytes 589832 | tf_op jit(solution)/shard_map/ppermute | solution.py:39
  105.0 9.5 %collective-permute-start.7 = (bf16[48,640]{1,0:T(8,128)(2,1)S(1)}, bf16[48,640]{1,0:T(8,128)(2,1)S(1)}, u32[]{:S(2)}, u32[]{:S(2)}) collective-permute-start(bf16[48,640]{1,0:T(8,128)(2,1)S(1)} %get-tuple-element.43), channel_id=1, source_target_pairs={{0,12},{1,13},{2,14},{3,15},{4,0},{5,1},{6,2},{7,3},{8,4},{9,5},{1... | collective-permute-start | bytes 184328 | tf_op jit(solution)/shard_map/ppermute | solution.py:39
  107.5 7.2 %collective-permute-start.8 = (bf16[48,640]{1,0:T(8,128)(2,1)S(1)}, bf16[48,640]{1,0:T(8,128)(2,1)S(1)}, u32[]{:S(2)}, u32[]{:S(2)}) collective-permute-start(bf16[48,640]{1,0:T(8,128)(2,1)S(1)} %get-tuple-element.42), channel_id=1, source_target_pairs={{0,8},{1,9},{2,10},{3,11},{4,12},{5,13},{6,14},{7,15},{8,0},{9,1},... | collective-permute-start | bytes 184328 | tf_op jit(solution)/shard_map/ppermute | solution.py:39
  108.0 6.7 %collective-permute-start.9 = (bf16[48,640]{1,0:T(8,128)(2,1)S(1)}, bf16[48,640]{1,0:T(8,128)(2,1)S(1)}, u32[]{:S(2)}, u32[]{:S(2)}) collective-permute-start(bf16[48,640]{1,0:T(8,128)(2,1)S(1)} %get-tuple-element.41), channel_id=1, source_target_pairs={{0,4},{1,5},{2,6},{3,7},{4,8},{5,9},{6,10},{7,11},{8,12},{9,13},{1... | collective-permute-start | bytes 184328 | tf_op jit(solution)/shard_map/ppermute | solution.py:39
  111.4 4.2 %collective-permute-start.22 = (bf16[48,512]{1,0:T(8,128)(2,1)S(1)}, bf16[48,512]{1,0:T(8,128)(2,1)S(1)}, u32[]{:S(2)}, u32[]{:S(2)}) collective-permute-start(bf16[48,512]{1,0:T(8,128)(2,1)S(1)} %get-tuple-element.47), channel_id=1, source_target_pairs={{0,12},{1,13},{2,14},{3,15},{4,0},{5,1},{6,2},{7,3},{8,4},{9,5},{1... | collective-permute-start | bytes 147464 | tf_op jit(solution)/shard_map/ppermute | solution.py:39
  113.9 5.1 %collective-permute-start.23 = (bf16[48,512]{1,0:T(8,128)(2,1)S(1)}, bf16[48,512]{1,0:T(8,128)(2,1)S(1)}, u32[]{:S(2)}, u32[]{:S(2)}) collective-permute-start(bf16[48,512]{1,0:T(8,128)(2,1)S(1)} %get-tuple-element.46), channel_id=1, source_target_pairs={{0,8},{1,9},{2,10},{3,11},{4,12},{5,13},{6,14},{7,15},{8,0},{9,1},... | collective-permute-start | bytes 147464 | tf_op jit(solution)/shard_map/ppermute | solution.py:39
  114.5 5.9 %collective-permute-start.24 = (bf16[48,512]{1,0:T(8,128)(2,1)S(1)}, bf16[48,512]{1,0:T(8,128)(2,1)S(1)}, u32[]{:S(2)}, u32[]{:S(2)}) collective-permute-start(bf16[48,512]{1,0:T(8,128)(2,1)S(1)} %get-tuple-element.45), channel_id=1, source_target_pairs={{0,4},{1,5},{2,6},{3,7},{4,8},{5,9},{6,10},{7,11},{8,12},{9,13},{1... | collective-permute-start | bytes 147464 | tf_op jit(solution)/shard_map/ppermute | solution.py:39

commit v3 on v2

v3 whole, which is shorter than its diff:
```python
import functools

import jax
import jax.numpy as jnp
from jax import lax
from jax.experimental import pallas as pl
from jax.experimental.pallas import tpu as pltpu
from jax.sharding import PartitionSpec as P

PLEN = 128
VMEM = pl.BlockSpec(memory_space=pltpu.VMEM)
SMEM = pl.BlockSpec(memory_space=pltpu.SMEM)
ANY = pl.BlockSpec(memory_space=pl.ANY)
UNIT_STEP = 256


class Grid:
    def __init__(self, devices, experts):
        self.experts = experts
        self.pairs = devices // experts // 2
        index = lax.axis_index("dev")
        self.index = index
        self.expert = index // (self.pairs * 2)
        self.pair = (index // 2) % self.pairs
        self.core = index % 2

    def send(self, value, axis, step):
        moves = []
        for expert in range(self.experts):
            for pair in range(self.pairs):
                for core in range(2):
                    to = [expert, pair, core]
                    to[axis] = (to[axis] + step) % (self.experts, self.pairs, 2)[axis]
                    moves.append(
                        (
                            (expert * self.pairs + pair) * 2 + core,
                            (to[0] * self.pairs + to[1]) * 2 + to[2],
                        )
                    )
        return lax.ppermute(value, "dev", moves)


class Packing:
    def __init__(self, cap, features):
        best = None
        for chunks in range(1, features // 128 + 1):
            if features % (128 * chunks):
                continue
            rows = -(-cap * chunks // 16) * 16
            cost = rows * (features // chunks)
            if best is None or cost < best[0]:
                best = (cost, chunks, rows)
        _, self.chunks, self.rows = best
        self.cap = cap
        self.width = features // self.chunks


def inner_index(experts):
    devices = lax.axis_size("dev")
    index = lax.axis_index("dev")
    return index, index // (devices // experts)


def live(position, lengths_ref):
    prompt = position // PLEN
    length = jnp.zeros_like(position)
    for p in range(lengths_ref.shape[0]):
        length = jnp.where(prompt == p, lengths_ref[p], length)
    return position % PLEN < length


def modulate_kernel(packing, experts, count, prompts, *refs):
    lengths_ref, chosen_ref, scale_ref, shift_ref = refs[:4]
    value_refs, out_refs = refs[4 : 4 + count], refs[len(refs) - 1 - experts :]
    index, own_expert = inner_index(experts)
    rows = value_refs[0].shape[0]
    relative = lax.rem(chosen_ref[...] + (experts - own_expert), experts)
    expert_at = lax.broadcasted_iota(jnp.int32, (experts, rows), 0)
    routed = (relative[0:1] == expert_at) | (relative[1:2] == expert_at)
    if prompts:
        position = index * rows + lax.broadcasted_iota(jnp.int32, (experts, rows), 1)
        routed = routed & live(position, lengths_ref)
    before = lax.broadcasted_iota(jnp.int32, (rows, rows), 0) < lax.broadcasted_iota(
        jnp.int32, (rows, rows), 1
    )
    slot = jnp.dot(
        routed.astype(jnp.float32), before.astype(jnp.float32), preferred_element_type=jnp.float32
    )
    slot = jnp.where(routed, slot, -1024.0)

    values = value_refs[0][...].astype(jnp.float32)
    for ref in value_refs[1:]:
        values = values + ref[...].astype(jnp.float32)
    values = values.astype(jnp.bfloat16).astype(jnp.float32)
    center = values - jnp.mean(values, axis=1, keepdims=True)
    spread = jnp.mean(center * center, axis=1, keepdims=True)
    normed = center * lax.rsqrt(spread + 1e-06) * scale_ref[...] + shift_ref[...]
    normed = normed.astype(jnp.bfloat16)
    out_refs[0][...] = normed

    place = lax.broadcasted_iota(jnp.int32, (packing.rows, rows), 0).astype(jnp.float32)
    packed = None
    for j in range(packing.chunks):
        into = jnp.concatenate(
            [
                jnp.where(place - float(j * packing.cap) == slot[k : k + 1], 1.0, 0.0)
                for k in range(experts)
            ],
            axis=0,
        ).astype(jnp.bfloat16)
        term = jnp.dot(
            into,
            normed[:, j * packing.width : (j + 1) * packing.width],
            preferred_element_type=jnp.float32,
        )
        packed = term if packed is None else packed + term
    for k in range(experts):
        out_refs[1 + k][...] = packed[k * packing.rows : (k + 1) * packing.rows].astype(
            jnp.bfloat16
        )


def modulate(parts, chosen, lengths, mod_scale, mod_shift, packing, experts, prompts, after):
    rows, features = parts[0].shape
    outs = [jax.ShapeDtypeStruct((rows, features), jnp.bfloat16)]
    outs += [jax.ShapeDtypeStruct((packing.rows, packing.width), jnp.bfloat16)] * experts
    results = pl.pallas_call(
        functools.partial(modulate_kernel, packing, experts, len(parts), prompts),
        out_shape=outs,
        in_specs=[SMEM] + [VMEM] * (3 + len(parts)) + [ANY] * len(after),
        out_specs=[VMEM] * len(outs),
        compiler_params=pltpu.CompilerParams(vmem_limit_bytes=8 << 20),
        name="modulate",
    )(lengths, chosen.T, mod_scale.reshape(1, -1), mod_shift.reshape(1, -1), *parts, *after)
    return (results[0], list(results[1:]))


def route_kernel(packing, experts, prompts, lengths_ref, chosen_ref, normed_ref, router_ref, spot_ref, weight_ref):
    index, own_expert = inner_index(experts)
    rows = normed_ref.shape[0]
    chosen = chosen_ref[...]
    relative = lax.rem(chosen + (experts - own_expert), experts)
    expert_at = lax.broadcasted_iota(jnp.int32, (rows, experts), 1)
    routed = (relative[:, 0:1] == expert_at) | (relative[:, 1:2] == expert_at)
    active = None
    if prompts:
        position = index * rows + lax.broadcasted_iota(jnp.int32, (rows, experts), 0)
        active = live(position, lengths_ref)
        routed = routed & active
    before = lax.broadcasted_iota(jnp.int32, (rows, rows), 1) < lax.broadcasted_iota(
        jnp.int32, (rows, rows), 0
    )
    slot = jnp.dot(
        before.astype(jnp.float32), routed.astype(jnp.float32), preferred_element_type=jnp.float32
    )
    normed = normed_ref[...].astype(jnp.float32)
    logits = [
        jnp.sum(normed * router_ref[k : k + 1, :], axis=1, keepdims=True) for k in range(experts)
    ]
    picked = []
    for t in range(2):
        mine = relative[:, t : t + 1] == expert_at
        own_slot = jnp.sum(jnp.where(mine, slot, 0.0), axis=1, keepdims=True)
        spot = relative[:, t : t + 1].astype(jnp.float32) * float(packing.rows) + own_slot
        if active is not None:
            spot = jnp.where(active[:, 0:1], spot, -65536.0)
        spot_ref[:, t : t + 1] = spot
        logit = jnp.zeros((rows, 1), jnp.float32)
        for k in range(experts):
            logit = jnp.where(chosen[:, t : t + 1] == k, logits[k], logit)
        picked.append(logit)
    weight_ref[:, 0:1] = jax.nn.sigmoid(picked[0] - picked[1])
    weight_ref[:, 1:2] = jax.nn.sigmoid(picked[1] - picked[0])


def route(normed, chosen, lengths, router_weight, packing, prompts):
    rows = normed.shape[0]
    return pl.pallas_call(
        functools.partial(route_kernel, packing, router_weight.shape[1], prompts),
        out_shape=[jax.ShapeDtypeStruct((rows, 2), jnp.float32)] * 2,
        in_specs=[SMEM] + [VMEM] * 3,
        out_specs=[VMEM] * 2,
        compiler_params=pltpu.CompilerParams(vmem_limit_bytes=8 << 20),
        name="route",
    )(lengths, chosen, normed, router_weight.T)


def cuts(total, step):
    return [(start, min(start + step, total)) for start in range(0, total, step)]


def expert_kernel(packing, count, after, *refs):
    row_refs = refs[:count]
    gate_hbm, up_hbm, down_hbm = refs[count : count + 3]
    out_refs = refs[count + 3 + after : 2 * count + 3 + after]
    gate_ref, up_ref, down_ref, rows_ref, total_ref, sems = refs[2 * count + 3 + after :]
    units = gate_hbm.shape[0]
    unit_cuts = cuts(units, UNIT_STEP)
    copies = []
    for i, (lo, hi) in enumerate(unit_cuts):
        for t, (source, target) in enumerate(
            ((gate_hbm, gate_ref), (up_hbm, up_ref), (down_hbm, down_ref))
        ):
            copies.append(
                pltpu.make_async_copy(source.at[lo:hi], target.at[lo:hi], sems.at[3 * i + t])
            )
    for copy in copies:
        copy.start()

    cap, chunks, width, high = packing.cap, packing.chunks, packing.width, packing.rows
    per_ref = row_refs[0].shape[0] // high
    blocks = count * per_ref
    group = 16
    row_at = lax.broadcasted_iota(jnp.int32, (group * cap, group * high), 0)
    place = lax.broadcasted_iota(jnp.int32, (group * cap, group * high), 1)
    source_row = (row_at // cap) * high + row_at % cap
    packed = jnp.concatenate([ref[...] for ref in row_refs], axis=0)
    for g in range(blocks // group):
        part = packed[g * group * high : (g + 1) * group * high]
        for j in range(chunks):
            pick = jnp.where(place == source_row + j * cap, 1.0, 0.0).astype(jnp.bfloat16)
            rows_ref[g * group * cap : (g + 1) * group * cap, j * width : (j + 1) * width] = (
                jnp.dot(pick, part, preferred_element_type=jnp.float32).astype(jnp.bfloat16)
            )

    def down(i, hidden):
        lo, hi = unit_cuts[i]
        copies[3 * i + 2].wait()
        term = jnp.dot(hidden, down_ref[lo:hi, :], preferred_element_type=jnp.float32)
        if i == 0:
            total_ref[...] = term
        else:
            total_ref[...] += term

    hidden = None
    for i, (lo, hi) in enumerate(unit_cuts):
        contract = (((1,), (1,)), ((), ()))
        rows = rows_ref[...]
        copies[3 * i].wait()
        gate = lax.dot_general(
            rows, gate_ref[lo:hi, :], contract, preferred_element_type=jnp.float32
        )
        copies[3 * i + 1].wait()
        up = lax.dot_general(rows, up_ref[lo:hi, :], contract, preferred_element_type=jnp.float32)
        if i > 0:
            down(i - 1, hidden)
        hidden = (gate * jax.nn.sigmoid(gate) * up).astype(jnp.bfloat16)
    down(len(unit_cuts) - 1, hidden)
    total = total_ref[...].astype(jnp.bfloat16)

    place = lax.broadcasted_iota(jnp.int32, (group * high, group * cap), 0)
    row_at = lax.broadcasted_iota(jnp.int32, (group * high, group * cap), 1)
    target = (row_at // cap) * high + row_at % cap
    per_group = group // per_ref
    for g in range(blocks // group):
        packed = None
        for j in range(chunks):
            put = jnp.where(place == target + j * cap, 1.0, 0.0).astype(jnp.bfloat16)
            term = jnp.dot(
                put,
                total[g * group * cap : (g + 1) * group * cap, j * width : (j + 1) * width],
                preferred_element_type=jnp.float32,
            )
            packed = term if packed is None else packed + term
        packed = packed.astype(jnp.bfloat16)
        for i in range(per_group):
            out_refs[g * per_group + i][...] = packed[i * per_ref * high : (i + 1) * per_ref * high]


def expert_rows(arrays, w_gate, w_up, w_down, packing, after):
    features, units = w_gate.shape
    rows = len(arrays) * (arrays[0].shape[0] // packing.rows) * packing.cap
    return pl.pallas_call(
        functools.partial(expert_kernel, packing, len(arrays), len(after)),
        out_shape=[jax.ShapeDtypeStruct(arrays[0].shape, jnp.bfloat16)] * len(arrays),
        in_specs=[VMEM] * len(arrays) + [ANY] * (3 + len(after)),
        out_specs=[VMEM] * len(arrays),
        scratch_shapes=[
            pltpu.VMEM((units, features), jnp.bfloat16),
            pltpu.VMEM((units, features), jnp.bfloat16),
            pltpu.VMEM((units, features), jnp.bfloat16),
            pltpu.VMEM((rows, features), jnp.bfloat16),
            pltpu.VMEM((rows, features), jnp.float32),
            pltpu.SemaphoreType.DMA((3 * len(cuts(units, UNIT_STEP)),)),
        ],
        compiler_params=pltpu.CompilerParams(vmem_limit_bytes=48 << 20),
        cost_estimate=pl.CostEstimate(
            flops=6 * rows * features * units,
            bytes_accessed=6 * features * units,
            transcendentals=rows * units,
        ),
        name="experts",
    )(*arrays, w_gate.T, w_up.T, w_down, *after)


def combine_kernel(packing, spot_ref, weight_ref, *refs):
    block_refs, out_ref = refs[:-1], refs[-1]
    rows = out_ref.shape[0]
    blocks = jnp.concatenate([ref[...] for ref in block_refs], axis=0)
    place = lax.broadcasted_iota(jnp.int32, (rows, blocks.shape[0]), 1).astype(jnp.float32)
    picks = [
        jnp.where(place - float(j * packing.cap) == spot_ref[:, t : t + 1], 1.0, 0.0)
        for t in range(2)
        for j in range(packing.chunks)
    ]
    if rows % 16 == 0:
        table = jnp.concatenate(picks, axis=0).astype(jnp.bfloat16)
        picked = jnp.dot(table, blocks, preferred_element_type=jnp.float32)
        picked = [picked[i * rows : (i + 1) * rows] for i in range(len(picks))]
    else:
        picked = [
            jnp.dot(pick.astype(jnp.bfloat16), blocks, preferred_element_type=jnp.float32)
            for pick in picks
        ]
    for j in range(packing.chunks):
        out_ref[:, j * packing.width : (j + 1) * packing.width] = (
            weight_ref[:, 0:1] * picked[j] + weight_ref[:, 1:2] * picked[packing.chunks + j]
        ).astype(jnp.bfloat16)


def combine(spot, weights, blocks, packing, rows, features):
    return pl.pallas_call(
        functools.partial(combine_kernel, packing),
        out_shape=jax.ShapeDtypeStruct((rows, features), jnp.bfloat16),
        in_specs=[VMEM] * (2 + len(blocks)),
        out_specs=VMEM,
        compiler_params=pltpu.CompilerParams(vmem_limit_bytes=8 << 20),
        name="combine",
    )(spot, weights, *blocks)


def dispatch(blocks, grid):
    first = jnp.concatenate(
        [blocks[0]] + [grid.send(blocks[k], 0, k) for k in range(1, grid.experts)], axis=0
    )
    own = [first] + [grid.send(first, 1, k) for k in range(1, grid.pairs)]
    return own + [grid.send(value, 2, 1) for value in own]


def give_back(results, grid):
    own, other = results[: grid.pairs], results[grid.pairs :]
    sums = []
    for k in list(range(1, grid.pairs)) + [0]:
        sums.append(own[k].astype(jnp.float32) + grid.send(other[k], 2, 1).astype(jnp.float32))
    total = sums[-1]
    for k in range(1, grid.pairs):
        total = total + grid.send(sums[k - 1].astype(jnp.bfloat16), 1, -k).astype(jnp.float32)
    total = total.astype(jnp.bfloat16)
    rows = total.shape[0] // grid.experts
    parts = [total[k * rows : (k + 1) * rows] for k in range(grid.experts)]
    return [parts[0]] + [grid.send(parts[k], 0, -k) for k in range(1, grid.experts)]


def project(text_hidden, caption_weight, grid):
    rows = text_hidden.shape[0] // (grid.experts * grid.pairs * 2)
    text = text_hidden.reshape(grid.experts, grid.pairs, 2, rows, text_hidden.shape[1])
    text = jnp.roll(text, -grid.expert, axis=0)
    text = jnp.roll(text, -grid.pair, axis=1)
    text = jnp.roll(text, -grid.core, axis=2)
    text = jnp.transpose(text, (2, 1, 0, 3, 4)).reshape(2, -1, text_hidden.shape[1])
    other = jnp.dot(text[1], caption_weight, preferred_element_type=jnp.float32)
    own = jnp.dot(text[0], caption_weight, preferred_element_type=jnp.float32)
    total = own + grid.send(other.astype(jnp.bfloat16), 2, 1).astype(jnp.float32)
    rows_pair = rows * grid.experts
    parts = [total[k * rows_pair : (k + 1) * rows_pair] for k in range(grid.pairs)]
    total = parts[0]
    crossing = [part.astype(jnp.bfloat16) for part in parts[1:]]
    for k in range(1, grid.pairs):
        total = total + grid.send(crossing[k - 1], 1, k).astype(jnp.float32)
    parts = [total[k * rows : (k + 1) * rows] for k in range(grid.experts)]
    terms = [parts[0]] + [
        grid.send(parts[k].astype(jnp.bfloat16), 0, k) for k in range(1, grid.experts)
    ]
    return (terms, crossing)


def local(
    image_rows,
    text_hidden,
    caption_weight,
    mod_scale,
    mod_shift,
    router_weight,
    image_experts,
    caption_experts,
    prompt_lengths,
    w_gate,
    w_up,
    w_down,
):
    devices = lax.axis_size("dev")
    features, experts = router_weight.shape
    grid = Grid(devices, experts)
    image_packing = Packing(image_rows.shape[0] * 3 // 4, features)
    caption_packing = Packing(text_hidden.shape[0] // devices // 2 + 1, features)

    terms, crossing = project(text_hidden, caption_weight, grid)
    caption_normed, caption_blocks = modulate(
        terms, caption_experts, prompt_lengths, mod_scale, mod_shift,
        caption_packing, experts, True, [],
    )
    image_normed, image_blocks = modulate(
        [image_rows], image_experts, prompt_lengths, mod_scale, mod_shift,
        image_packing, experts, False, crossing[:1],
    )

    def finish(normed, blocks, chosen, packing, prompts, after):
        arrays = dispatch(blocks, grid)
        spot, weights = route(normed, chosen, prompt_lengths, router_weight, packing, prompts)
        results = expert_rows(arrays, w_gate, w_up, w_down, packing, after + [spot])
        blocks = give_back(results, grid)
        return combine(spot, weights, blocks, packing, chosen.shape[0], features)

    image_out = finish(
        image_normed, image_blocks, image_experts, image_packing, False, caption_blocks[:1]
    )
    caption_out = finish(
        caption_normed, caption_blocks, caption_experts, caption_packing, True, []
    )
    return (image_out, caption_out)


def solution(mesh):
    in_specs = (
        P(("groups", "dev"), None),
        P("groups", "dev"),
        P("dev", None),
        P(),
        P(),
        P(),
        P(("groups", "dev"), None),
        P(("groups", "dev"), None),
        P("groups"),
        P(None, "dev"),
        P(None, "dev"),
        P("dev", None),
    )
    out_specs = (P(("groups", "dev"), None), P(("groups", "dev"), None))
    return jax.shard_map(local, mesh=mesh, in_specs=in_specs, out_specs=out_specs, check_vma=False)
```

time: 122 us -> 99.4 us (0.81)
  local copies, waits for them, and re-layouts: 31.1 us -> 0.43 us
  Pallas kernels: 25.9 us -> 40.8 us
  other arithmetic: 6.17 us -> 1.57 us
  waiting for transfers between devices: 26.8 us -> 24.9 us
    unnamed x36 -> x24, local copies, waits for them, and re-layouts: 26.5 us -> 0.26 us
    pallas_call x2 -> x4, Pallas kernels: 23.4 us -> 36.7 us  [the longest x2 35 us: expert_rows(): pl.pallas_call(functools.partial(expert_kernel, packing, len(arrays), len...]
    ppermute x25 -> x29, waiting for transfers between devices: 26.8 us -> 24.9 us  [send(): return lax.ppermute(value, 'dev', moves)]
    add x6 -> x0, other arithmetic: 1.49 us -> none  [the longest x2 1.2 us: give_back(): total = own.astype(jnp.float32) + grid.send(other, 2, 1).astype(jnp.float32)]
    pallas_call x2, Pallas kernels: 0.84 us -> 2.31 us  [modulate(): pl.pallas_call(functools.partial(modulate_kernel, packing, experts, len(p...]
    and x8 -> x0, local copies, waits for them, and re-layouts: 1.43 us -> none  [the longest x6 1.34 us: tables(): (place[None, :, None, None] == offset[None, None, :, None] + slot.T[:, No...]
    eq x10 -> x0, local copies, waits for them, and re-layouts: 1.39 us -> none  [the longest x8 0.79 us: tables(): place[None, :, None, None]]
    ppermute x25 -> x29, starting transfers between devices: 28.7 us -> 29.7 us  [send(): return lax.ppermute(value, 'dev', moves)]
  transfers between devices with their start and end apart: 25 -> 29, of which waited for: 10 -> 14; matrix products, arithmetic and copies ran while one was open for 29% -> 1% of each run, Pallas kernels for 21% -> 40%
where the time goes in v3:
time: 99.4 us; the launch traced here: 99.2 us
  Pallas kernels  40.8 us (41%)
  starting transfers between devices  29.7 us (30%)
  waiting for transfers between devices  24.9 us (25%)
  other arithmetic  1.57 us (2%)
  between operations  1.08 us (1%)
    pallas_call x2, Pallas kernels, expert_rows(): pl.pallas_call(functools.partial(expert_kernel, packing, len(arrays), len...  35 us
    ppermute x29, starting transfers between devices, send(): return lax.ppermute(value, 'dev', moves)  29.7 us
    ppermute x29, waiting for transfers between devices, send(): return lax.ppermute(value, 'dev', moves)  24.9 us
    pallas_call x2, Pallas kernels, modulate(): pl.pallas_call(functools.partial(modulate_kernel, packing, experts, len(p...  2.31 us
  transfers between devices with their start and end apart: 29, of which 14 were waited for; matrix products, arithmetic and copies ran while one was open for 1% of the time, Pallas kernels for 40%

profile of v3, /device:TPU:0, one launch (start us, length us, event | category | flops | bytes accessed | tf_op | source)
XLA Modules:
  0.0 99.2 jit_solution(17440548778349320648)
XLA Ops:
  0.6 0.0 copy-start
  0.7 1.0 %fusion.3 = bf16[4,2,2,16,256]{4,3,2,1,0:T(8,128)(2,1)S(1)} fusion(s32[]{:T(128)S(6)} %select_n.52, bf16[4,2,2,16,256]{4,3,2,1,0:T(8,128)(2,1)} %bitcast.24), kind=kLoop, calls=%fused_computation.17 | loop fusion | flops 65536 | bytes 262148 | tf_op jit(solution)/shard_map/jit(_roll_dynamic)/concatenate | solution.py:357
  1.8 0.1 fusion.2
  1.9 0.1 fusion.1
  1.9 0.0 copy-start.6
  2.0 0.0 copy-start.7
  2.0 0.0 copy-done
  2.0 0.3 convolution_convert_fusion
  2.4 0.5 collective-permute-start
  2.9 1.7 %collective-permute-done = bf16[128,2560]{1,0:T(8,128)(2,1)S(1)} collective-permute-done((bf16[128,2560]{1,0:T(8,128)(2,1)S(1)}, bf16[128,2560]{1,0:T(8,128)(2,1)S(1)}, u32[]{:S(2)}, u32[]{:S(2)}) %collective-permute-start) | collective-permute-done | bytes 655392 | tf_op jit(solution)/shard_map/ppermute | solution.py:40
  4.6 0.3 convert_add_fusion
  5.0 3.0 %collective-permute-start.7 = (bf16[64,2560]{1,0:T(8,128)(2,1)S(1)}, bf16[64,2560]{1,0:T(8,128)(2,1)S(1)}, u32[]{:S(2)}, u32[]{:S(2)}) collective-permute-start(bf16[64,2560]{1,0:T(8,128)(2,1)S(1)} %slice.88.refs_5_), channel_id=1, source_target_pairs={{0,2},{1,3},{2,0},{3,1},{4,6},{5,7},{6,4},{7,5},{8,10},{9,11},{10,... | collective-permute-start | bytes 983048 | tf_op jit(solution)/shard_map/ppermute | solution.py:40
  8.0 1.1 %modulate.2 = (bf16[16,2560]{1,0:T(8,128)(2,1)S(1)}, bf16[48,640]{1,0:T(8,128)(2,1)S(1)}, bf16[48,640]{1,0:T(8,128)(2,1)S(1)}, bf16[48,640]{1,0:T(8,128)(2,1)S(1)}, bf16[48,640]{1,0:T(8,128)(2,1)S(1)}) custom-call(s32[2]{0:T(128)S(1)} %copy-done.3, s32[2,16]{1,0:T(2,128)S(1)} %bitcast.16, f32[1,2560]{1,0:T(1,128)S(1)} %reshape.20.refs_2_, ...), custom_call_target="tpu_custom_call" | custom-call | tf_op jit(solution)/shard_map/modulate/pallas_call | solution.py:127
  9.1 1.6 %collective-permute-start.1 = (bf16[48,640]{1,0:T(8,128)(2,1)S(1)}, bf16[48,640]{1,0:T(8,128)(2,1)S(1)}, u32[]{:S(2)}, u32[]{:S(2)}) collective-permute-start(bf16[48,640]{1,0:T(8,128)(2,1)S(1)} %get-tuple-element.28), channel_id=1, source_target_pairs={{0,4},{1,5},{2,6},{3,7},{4,8},{5,9},{6,10},{7,11},{8,12},{9,13},{1... | collective-permute-start | bytes 184328 | tf_op jit(solution)/shard_map/ppermute | solution.py:40
  10.7 2.6 %collective-permute-start.2 = (bf16[48,640]{1,0:T(8,128)(2,1)S(1)}, bf16[48,640]{1,0:T(8,128)(2,1)S(1)}, u32[]{:S(2)}, u32[]{:S(2)}) collective-permute-start(bf16[48,640]{1,0:T(8,128)(2,1)S(1)} %get-tuple-element.29), channel_id=1, source_target_pairs={{0,8},{1,9},{2,10},{3,11},{4,12},{5,13},{6,14},{7,15},{8,0},{9,1},... | collective-permute-start | bytes 184328 | tf_op jit(solution)/shard_map/ppermute | solution.py:40
  13.3 1.3 %collective-permute-start.3 = (bf16[48,640]{1,0:T(8,128)(2,1)S(1)}, bf16[48,640]{1,0:T(8,128)(2,1)S(1)}, u32[]{:S(2)}, u32[]{:S(2)}) collective-permute-start(bf16[48,640]{1,0:T(8,128)(2,1)S(1)} %get-tuple-element.30), channel_id=1, source_target_pairs={{0,12},{1,13},{2,14},{3,15},{4,0},{5,1},{6,2},{7,3},{8,4},{9,5},{1... | collective-permute-start | bytes 184328 | tf_op jit(solution)/shard_map/ppermute | solution.py:40
  14.7 0.9 collective-permute-done.1
  15.6 2.3 %collective-permute-done.2 = bf16[48,640]{1,0:T(8,128)(2,1)S(1)} collective-permute-done((bf16[48,640]{1,0:T(8,128)(2,1)S(1)}, bf16[48,640]{1,0:T(8,128)(2,1)S(1)}, u32[]{:S(2)}, u32[]{:S(2)}) %collective-permute-start.2) | collective-permute-done | bytes 61472 | tf_op jit(solution)/shard_map/ppermute | solution.py:40
  17.9 0.0 copy-start.1
  17.9 0.0 copy-start.5
  18.0 0.6 collective-permute-start.4
  18.6 0.1 fusion.4
  18.7 2.9 %collective-permute-start.10 = (bf16[16,2560]{1,0:T(8,128)(2,1)S(1)}, bf16[16,2560]{1,0:T(8,128)(2,1)S(1)}, u32[]{:S(2)}, u32[]{:S(2)}) collective-permute-start(bf16[16,2560]{1,0:T(8,128)(2,1)S(1)} %get-tuple-element.48), channel_id=1, source_target_pairs={{0,12},{1,13},{2,14},{3,15},{4,0},{5,1},{6,2},{7,3},{8,4},{9,5},{1... | collective-permute-start | bytes 245768 | tf_op jit(solution)/shard_map/ppermute | solution.py:40
  21.6 0.6 collective-permute-start.9
  22.3 0.1 copy.20.chosen_ref
  22.3 0.8 route.2
  23.2 0.0 collective-permute-start.5
  23.2 1.4 %collective-permute-done.4.refs_1_ = bf16[192,640]{1,0:T(8,128)(2,1)S(1)} collective-permute-done((bf16[192,640]{1,0:T(8,128)(2,1)S(1)}, bf16[192,640]{1,0:T(8,128)(2,1)S(1)}, u32[]{:S(2)}, u32[]{:S(2)}) %collective-permute-start.4) | collective-permute-done | bytes 245792 | tf_op jit(solution)/shard_map/ppermute | solution.py:40
  24.7 3.3 %collective-permute-done.8.refs_5_ = bf16[16,2560]{1,0:T(8,128)(2,1)S(1)} collective-permute-done((bf16[16,2560]{1,0:T(8,128)(2,1)S(1)}, bf16[16,2560]{1,0:T(8,128)(2,1)S(1)}, u32[]{:S(2)}, u32[]{:S(2)}) %collective-permute-start.8) | collective-permute-done | bytes 81952 | tf_op jit(solution)/shard_map/ppermute | solution.py:40
  28.0 1.5 %collective-permute-done.9.refs_6_ = bf16[16,2560]{1,0:T(8,128)(2,1)S(1)} collective-permute-done((bf16[16,2560]{1,0:T(8,128)(2,1)S(1)}, bf16[16,2560]{1,0:T(8,128)(2,1)S(1)}, u32[]{:S(2)}, u32[]{:S(2)}) %collective-permute-start.9) | collective-permute-done | bytes 81952 | tf_op jit(solution)/shard_map/ppermute | solution.py:40
  29.4 1.2 %modulate.3 = (bf16[16,2560]{1,0:T(8,128)(2,1)S(1)}, bf16[48,512]{1,0:T(8,128)(2,1)S(1)}, bf16[48,512]{1,0:T(8,128)(2,1)S(1)}, bf16[48,512]{1,0:T(8,128)(2,1)S(1)}, bf16[48,512]{1,0:T(8,128)(2,1)S(1)}) custom-call(s32[2]{0:T(128)S(1)} %copy-done.3, s32[2,16]{1,0:T(2,128)S(1)} %bitcast.17, f32[1,2560]{1,0:T(1,128)S(1)} %reshape.20.refs_2_, ...), custom_call_target="tpu_custom_call" | custom-call | tf_op jit(solution)/shard_map/modulate/pallas_call | solution.py:127
  30.6 0.1 collective-permute-start.17
  30.7 2.6 %collective-permute-start.18 = (bf16[48,512]{1,0:T(8,128)(2,1)S(1)}, bf16[48,512]{1,0:T(8,128)(2,1)S(1)}, u32[]{:S(2)}, u32[]{:S(2)}) collective-permute-start(bf16[48,512]{1,0:T(8,128)(2,1)S(1)} %get-tuple-element.40), channel_id=1, source_target_pairs={{0,8},{1,9},{2,10},{3,11},{4,12},{5,13},{6,14},{7,15},{8,0},{9,1},... | collective-permute-start | bytes 147464 | tf_op jit(solution)/shard_map/ppermute | solution.py:40
  33.3 1.4 %collective-permute-start.19 = (bf16[48,512]{1,0:T(8,128)(2,1)S(1)}, bf16[48,512]{1,0:T(8,128)(2,1)S(1)}, u32[]{:S(2)}, u32[]{:S(2)}) collective-permute-start(bf16[48,512]{1,0:T(8,128)(2,1)S(1)} %get-tuple-element.41), channel_id=1, source_target_pairs={{0,12},{1,13},{2,14},{3,15},{4,0},{5,1},{6,2},{7,3},{8,4},{9,5},{1... | collective-permute-start | bytes 147464 | tf_op jit(solution)/shard_map/ppermute | solution.py:40
  34.7 1.8 %collective-permute-done.17 = bf16[48,512]{1,0:T(8,128)(2,1)S(1)} collective-permute-done((bf16[48,512]{1,0:T(8,128)(2,1)S(1)}, bf16[48,512]{1,0:T(8,128)(2,1)S(1)}, u32[]{:S(2)}, u32[]{:S(2)}) %collective-permute-start.17) | collective-permute-done | bytes 49184 | tf_op jit(solution)/shard_map/ppermute | solution.py:40
  36.6 18.4 %experts.2 = (bf16[192,640]{1,0:T(8,128)(2,1)S(1)}, bf16[192,640]{1,0:T(8,128)(2,1)S(1)}, bf16[192,640]{1,0:T(8,128)(2,1)S(1)}, bf16[192,640]{1,0:T(8,128)(2,1)S(1)}) custom-call(bf16[192,640]{1,0:T(8,128)(2,1)S(1)} %constant_dynamic-update-slice_fusion.refs_0_, bf16[192,640]{1,0:T(8,128)(2,1)S(1)} %collective-permute-done.4.refs_1_, ...), custom_call_target="tpu_custom_call" | custom-call | flops 5096079360 | bytes 26542080 | tf_op jit(solution)/shard_map/experts/pallas_call | solution.py:273
  55.0 0.1 collective-permute-start.12
  55.1 1.2 %collective-permute-start.20 = (bf16[192,512]{1,0:T(8,128)(2,1)S(1)}, bf16[192,512]{1,0:T(8,128)(2,1)S(1)}, u32[]{:S(2)}, u32[]{:S(2)}) collective-permute-start(bf16[192,512]{1,0:T(8,128)(2,1)S(1)} %constant_dynamic-update-slice_fusion.4.refs_0_), channel_id=1, source_target_pairs={{0,2},{1,3},{2,0},{3,1},{4,6},{5,7},{6,4},{7,5},{8,10},{9,11},{10,... | collective-permute-start | bytes 589832 | tf_op jit(solution)/shard_map/ppermute | solution.py:40
  56.3 0.1 copy.21.chosen_ref
  56.3 0.8 route.3
  57.2 0.2 collective-permute-start.21
  57.4 0.3 collective-permute-start.11
  57.7 4.7 %collective-permute-done.20.refs_1_ = bf16[192,512]{1,0:T(8,128)(2,1)S(1)} collective-permute-done((bf16[192,512]{1,0:T(8,128)(2,1)S(1)}, bf16[192,512]{1,0:T(8,128)(2,1)S(1)}, u32[]{:S(2)}, u32[]{:S(2)}) %collective-permute-start.20) | collective-permute-done | bytes 196640 | tf_op jit(solution)/shard_map/ppermute | solution.py:40
  62.4 0.1 add_convert_fusion.1
  62.5 1.2 %collective-permute-start.13 = (bf16[192,640]{1,0:T(8,128)(2,1)S(1)}, bf16[192,640]{1,0:T(8,128)(2,1)S(1)}, u32[]{:S(2)}, u32[]{:S(2)}) collective-permute-start(bf16[192,640]{1,0:T(8,128)(2,1)S(1)} %add_convert_fusion.1), channel_id=1, source_target_pairs={{0,2},{1,3},{2,0},{3,1},{4,6},{5,7},{6,4},{7,5},{8,10},{9,11},{10,... | collective-permute-start | bytes 737288 | tf_op jit(solution)/shard_map/ppermute | solution.py:40
  63.7 0.2 collective-permute-done.22.refs_3_
  63.9 16.7 %experts.3 = (bf16[192,512]{1,0:T(8,128)(2,1)S(1)}, bf16[192,512]{1,0:T(8,128)(2,1)S(1)}, bf16[192,512]{1,0:T(8,128)(2,1)S(1)}, bf16[192,512]{1,0:T(8,128)(2,1)S(1)}) custom-call(bf16[192,512]{1,0:T(8,128)(2,1)S(1)} %constant_dynamic-update-slice_fusion.4.refs_0_, bf16[192,512]{1,0:T(8,128)(2,1)S(1)} %collective-permute-done.20.refs_1_, ...), custom_call_target="tpu_custom_call" | custom-call | flops 3822059520 | bytes 26542080 | tf_op jit(solution)/shard_map/experts/pallas_call | solution.py:273
  80.5 0.2 collective-permute-start.24
  80.7 0.4 collective-permute-start.23
  81.1 0.1 add_convert_fusion
  81.2 0.8 collective-permute-done.24
  82.0 0.1 add_convert_fusion.3
  82.1 1.2 %collective-permute-start.25 = (bf16[192,512]{1,0:T(8,128)(2,1)S(1)}, bf16[192,512]{1,0:T(8,128)(2,1)S(1)}, u32[]{:S(2)}, u32[]{:S(2)}) collective-permute-start(bf16[192,512]{1,0:T(8,128)(2,1)S(1)} %add_convert_fusion.3), channel_id=1, source_target_pairs={{0,2},{1,3},{2,0},{3,1},{4,6},{5,7},{6,4},{7,5},{8,10},{9,11},{10,... | collective-permute-start | bytes 589832 | tf_op jit(solution)/shard_map/ppermute | solution.py:40
  83.3 3.2 %collective-permute-start.14 = (bf16[48,640]{1,0:T(8,128)(2,1)S(1)}, bf16[48,640]{1,0:T(8,128)(2,1)S(1)}, u32[]{:S(2)}, u32[]{:S(2)}) collective-permute-start(bf16[48,640]{1,0:T(8,128)(2,1)S(1)} %get-tuple-element.53), channel_id=1, source_target_pairs={{0,12},{1,13},{2,14},{3,15},{4,0},{5,1},{6,2},{7,3},{8,4},{9,5},{1... | collective-permute-start | bytes 184328 | tf_op jit(solution)/shard_map/ppermute | solution.py:40
  86.5 0.7 collective-permute-start.16
  87.1 2.0 %collective-permute-done.25 = bf16[192,512]{1,0:T(8,128)(2,1)S(1)} collective-permute-done((bf16[192,512]{1,0:T(8,128)(2,1)S(1)}, bf16[192,512]{1,0:T(8,128)(2,1)S(1)}, u32[]{:S(2)}, u32[]{:S(2)}) %collective-permute-start.25) | collective-permute-done | bytes 196640 | tf_op jit(solution)/shard_map/ppermute | solution.py:40
  89.1 0.1 add_convert_fusion.2
  89.2 3.2 %collective-permute-start.26 = (bf16[48,512]{1,0:T(8,128)(2,1)S(1)}, bf16[48,512]{1,0:T(8,128)(2,1)S(1)}, u32[]{:S(2)}, u32[]{:S(2)}) collective-permute-start(bf16[48,512]{1,0:T(8,128)(2,1)S(1)} %get-tuple-element.57), channel_id=1, source_target_pairs={{0,12},{1,13},{2,14},{3,15},{4,0},{5,1},{6,2},{7,3},{8,4},{9,5},{1... | collective-permute-start | bytes 147464 | tf_op jit(solution)/shard_map/ppermute | solution.py:40
  92.4 0.6 collective-permute-start.28
  93.0 0.9 combine.2
  93.9 0.2 collective-permute-done.26.refs_1_
  94.1 3.2 %collective-permute-done.27.refs_2_ = bf16[48,512]{1,0:T(8,128)(2,1)S(1)} collective-permute-done((bf16[48,512]{1,0:T(8,128)(2,1)S(1)}, bf16[48,512]{1,0:T(8,128)(2,1)S(1)}, u32[]{:S(2)}, u32[]{:S(2)}) %collective-permute-start.27) | collective-permute-done | bytes 49184 | tf_op jit(solution)/shard_map/ppermute | solution.py:40
  97.4 0.9 collective-permute-done.28.refs_3_
  98.3 0.9 combine.3
  (48 shorter events, 0.3 us)
Async XLA Ops:
  0.6 1.4 %copy-start = (bf16[256,2560]{1,0:T(8,128)(2,1)S(1)}, bf16[256,2560]{1,0:T(8,128)(2,1)}, u32[]{:S(2)}) copy-start(bf16[256,2560]{1,0:T(8,128)(2,1)} %param.14) | copy-start | bytes 3932164
  1.9 0.9 copy-start.6
  2.0 1.0 copy-start.7
  2.4 2.2 %collective-permute-start = (bf16[128,2560]{1,0:T(8,128)(2,1)S(1)}, bf16[128,2560]{1,0:T(8,128)(2,1)S(1)}, u32[]{:S(2)}, u32[]{:S(2)}) collective-permute-start(bf16[128,2560]{1,0:T(8,128)(2,1)S(1)} %convolution_convert_fusion), channel_id=1, source_target_pairs={{0,1},{1,0},{2,3},{3,2},{4,5},{5,4},{6,7},{7,6},{8,9},{9,8},{10,11... | collective-permute-start | bytes 1966088 | tf_op jit(solution)/shard_map/ppermute | solution.py:40
  4.6 3.4 %copy-start.2 = (bf16[16,2560]{1,0:T(8,128)(2,1)S(1)}, bf16[16,2560]{1,0:T(8,128)(2,1)}, u32[]{:S(2)}) copy-start(bf16[16,2560]{1,0:T(8,128)(2,1)} %refs_4_.1) | copy-start | bytes 245764
  4.6 3.4 %copy-start.3 = (s32[2]{0:T(128)S(1)}, s32[2]{0:T(128)}, u32[]{:S(2)}) copy-start(s32[2]{0:T(128)} %lengths_ref.3) | copy-start | bytes 28
  4.6 3.4 %copy-start.4 = (s32[16,2]{0,1:T(2,128)S(1)}, s32[16,2]{0,1:T(2,128)}, u32[]{:S(2)}) copy-start(s32[16,2]{0,1:T(2,128)} %param.18) | copy-start | bytes 388
  5.0 13.6 %collective-permute-start.7 = (bf16[64,2560]{1,0:T(8,128)(2,1)S(1)}, bf16[64,2560]{1,0:T(8,128)(2,1)S(1)}, u32[]{:S(2)}, u32[]{:S(2)}) collective-permute-start(bf16[64,2560]{1,0:T(8,128)(2,1)S(1)} %slice.88.refs_5_), channel_id=1, source_target_pairs={{0,2},{1,3},{2,0},{3,1},{4,6},{5,7},{6,4},{7,5},{8,10},{9,11},{10,... | collective-permute-start | bytes 983048 | tf_op jit(solution)/shard_map/ppermute | solution.py:40
  9.1 6.5 %collective-permute-start.1 = (bf16[48,640]{1,0:T(8,128)(2,1)S(1)}, bf16[48,640]{1,0:T(8,128)(2,1)S(1)}, u32[]{:S(2)}, u32[]{:S(2)}) collective-permute-start(bf16[48,640]{1,0:T(8,128)(2,1)S(1)} %get-tuple-element.28), channel_id=1, source_target_pairs={{0,4},{1,5},{2,6},{3,7},{4,8},{5,9},{6,10},{7,11},{8,12},{9,13},{1... | collective-permute-start | bytes 184328 | tf_op jit(solution)/shard_map/ppermute | solution.py:40
  10.7 7.1 %collective-permute-start.2 = (bf16[48,640]{1,0:T(8,128)(2,1)S(1)}, bf16[48,640]{1,0:T(8,128)(2,1)S(1)}, u32[]{:S(2)}, u32[]{:S(2)}) collective-permute-start(bf16[48,640]{1,0:T(8,128)(2,1)S(1)} %get-tuple-element.29), channel_id=1, source_target_pairs={{0,8},{1,9},{2,10},{3,11},{4,12},{5,13},{6,14},{7,15},{8,0},{9,1},... | collective-permute-start | bytes 184328 | tf_op jit(solution)/shard_map/ppermute | solution.py:40
  13.3 4.6 %collective-permute-start.3 = (bf16[48,640]{1,0:T(8,128)(2,1)S(1)}, bf16[48,640]{1,0:T(8,128)(2,1)S(1)}, u32[]{:S(2)}, u32[]{:S(2)}) collective-permute-start(bf16[48,640]{1,0:T(8,128)(2,1)S(1)} %get-tuple-element.30), channel_id=1, source_target_pairs={{0,12},{1,13},{2,14},{3,15},{4,0},{5,1},{6,2},{7,3},{8,4},{9,5},{1... | collective-permute-start | bytes 184328 | tf_op jit(solution)/shard_map/ppermute | solution.py:40
  17.9 4.4 %copy-start.1 = (f32[2560,4]{0,1:T(4,128)S(1)}, f32[2560,4]{0,1:T(4,128)}, u32[]{:S(2)}) copy-start(f32[2560,4]{0,1:T(4,128)} %param.17) | copy-start | bytes 122884
  17.9 11.5 %copy-start.5 = (s32[16,2]{0,1:T(2,128)S(1)}, s32[16,2]{0,1:T(2,128)}, u32[]{:S(2)}) copy-start(s32[16,2]{0,1:T(2,128)} %param.19) | copy-start | bytes 388
  18.0 6.7 %collective-permute-start.4 = (bf16[192,640]{1,0:T(8,128)(2,1)S(1)}, bf16[192,640]{1,0:T(8,128)(2,1)S(1)}, u32[]{:S(2)}, u32[]{:S(2)}) collective-permute-start(bf16[192,640]{1,0:T(8,128)(2,1)S(1)} %constant_dynamic-update-slice_fusion.refs_0_), channel_id=1, source_target_pairs={{0,2},{1,3},{2,0},{3,1},{4,6},{5,7},{6,4},{7,5},{8,10},{9,11},{10,... | collective-permute-start | bytes 737288 | tf_op jit(solution)/shard_map/ppermute | solution.py:40
  18.7 5.9 %collective-permute-start.10 = (bf16[16,2560]{1,0:T(8,128)(2,1)S(1)}, bf16[16,2560]{1,0:T(8,128)(2,1)S(1)}, u32[]{:S(2)}, u32[]{:S(2)}) collective-permute-start(bf16[16,2560]{1,0:T(8,128)(2,1)S(1)} %get-tuple-element.48), channel_id=1, source_target_pairs={{0,12},{1,13},{2,14},{3,15},{4,0},{5,1},{6,2},{7,3},{8,4},{9,5},{1... | collective-permute-start | bytes 245768 | tf_op jit(solution)/shard_map/ppermute | solution.py:40
  21.6 6.3 %collective-permute-start.8 = (bf16[16,2560]{1,0:T(8,128)(2,1)S(1)}, bf16[16,2560]{1,0:T(8,128)(2,1)S(1)}, u32[]{:S(2)}, u32[]{:S(2)}) collective-permute-start(bf16[16,2560]{1,0:T(8,128)(2,1)S(1)} %get-tuple-element.50), channel_id=1, source_target_pairs={{0,4},{1,5},{2,6},{3,7},{4,8},{5,9},{6,10},{7,11},{8,12},{9,13},{1... | collective-permute-start | bytes 245768 | tf_op jit(solution)/shard_map/ppermute | solution.py:40
  21.6 7.8 %collective-permute-start.9 = (bf16[16,2560]{1,0:T(8,128)(2,1)S(1)}, bf16[16,2560]{1,0:T(8,128)(2,1)S(1)}, u32[]{:S(2)}, u32[]{:S(2)}) collective-permute-start(bf16[16,2560]{1,0:T(8,128)(2,1)S(1)} %get-tuple-element.49), channel_id=1, source_target_pairs={{0,8},{1,9},{2,10},{3,11},{4,12},{5,13},{6,14},{7,15},{8,0},{9,1},... | collective-permute-start | bytes 245768 | tf_op jit(solution)/shard_map/ppermute | solution.py:40
  23.2 13.4 %collective-permute-start.5 = (bf16[192,640]{1,0:T(8,128)(2,1)S(1)}, bf16[192,640]{1,0:T(8,128)(2,1)S(1)}, u32[]{:S(2)}, u32[]{:S(2)}) collective-permute-start(bf16[192,640]{1,0:T(8,128)(2,1)S(1)} %constant_dynamic-update-slice_fusion.refs_0_), channel_id=1, source_target_pairs={{0,1},{1,0},{2,3},{3,2},{4,5},{5,4},{6,7},{7,6},{8,9},{9,8},{10,11... | collective-permute-start | bytes 737288 | tf_op jit(solution)/shard_map/ppermute | solution.py:40
  24.6 12.0 %collective-permute-start.6 = (bf16[192,640]{1,0:T(8,128)(2,1)S(1)}, bf16[192,640]{1,0:T(8,128)(2,1)S(1)}, u32[]{:S(2)}, u32[]{:S(2)}) collective-permute-start(bf16[192,640]{1,0:T(8,128)(2,1)S(1)} %collective-permute-done.4.refs_1_), channel_id=1, source_target_pairs={{0,1},{1,0},{2,3},{3,2},{4,5},{5,4},{6,7},{7,6},{8,9},{9,8},{10,11... | collective-permute-start | bytes 737288 | tf_op jit(solution)/shard_map/ppermute | solution.py:40
  30.6 5.9 %collective-permute-start.17 = (bf16[48,512]{1,0:T(8,128)(2,1)S(1)}, bf16[48,512]{1,0:T(8,128)(2,1)S(1)}, u32[]{:S(2)}, u32[]{:S(2)}) collective-permute-start(bf16[48,512]{1,0:T(8,128)(2,1)S(1)} %get-tuple-element.39), channel_id=1, source_target_pairs={{0,4},{1,5},{2,6},{3,7},{4,8},{5,9},{6,10},{7,11},{8,12},{9,13},{1... | collective-permute-start | bytes 147464 | tf_op jit(solution)/shard_map/ppermute | solution.py:40
  30.7 5.9 %collective-permute-start.18 = (bf16[48,512]{1,0:T(8,128)(2,1)S(1)}, bf16[48,512]{1,0:T(8,128)(2,1)S(1)}, u32[]{:S(2)}, u32[]{:S(2)}) collective-permute-start(bf16[48,512]{1,0:T(8,128)(2,1)S(1)} %get-tuple-element.40), channel_id=1, source_target_pairs={{0,8},{1,9},{2,10},{3,11},{4,12},{5,13},{6,14},{7,15},{8,0},{9,1},... | collective-permute-start | bytes 147464 | tf_op jit(solution)/shard_map/ppermute | solution.py:40
  33.3 21.8 %collective-permute-start.19 = (bf16[48,512]{1,0:T(8,128)(2,1)S(1)}, bf16[48,512]{1,0:T(8,128)(2,1)S(1)}, u32[]{:S(2)}, u32[]{:S(2)}) collective-permute-start(bf16[48,512]{1,0:T(8,128)(2,1)S(1)} %get-tuple-element.41), channel_id=1, source_target_pairs={{0,12},{1,13},{2,14},{3,15},{4,0},{5,1},{6,2},{7,3},{8,4},{9,5},{1... | collective-permute-start | bytes 147464 | tf_op jit(solution)/shard_map/ppermute | solution.py:40
  55.0 7.5 %collective-permute-start.12 = (bf16[192,640]{1,0:T(8,128)(2,1)S(1)}, bf16[192,640]{1,0:T(8,128)(2,1)S(1)}, u32[]{:S(2)}, u32[]{:S(2)}) collective-permute-start(bf16[192,640]{1,0:T(8,128)(2,1)S(1)} %get-tuple-element.35), channel_id=1, source_target_pairs={{0,1},{1,0},{2,3},{3,2},{4,5},{5,4},{6,7},{7,6},{8,9},{9,8},{10,11... | collective-permute-start | bytes 737288 | tf_op jit(solution)/shard_map/ppermute | solution.py:40
  55.1 7.3 %collective-permute-start.20 = (bf16[192,512]{1,0:T(8,128)(2,1)S(1)}, bf16[192,512]{1,0:T(8,128)(2,1)S(1)}, u32[]{:S(2)}, u32[]{:S(2)}) collective-permute-start(bf16[192,512]{1,0:T(8,128)(2,1)S(1)} %constant_dynamic-update-slice_fusion.4.refs_0_), channel_id=1, source_target_pairs={{0,2},{1,3},{2,0},{3,1},{4,6},{5,7},{6,4},{7,5},{8,10},{9,11},{10,... | collective-permute-start | bytes 589832 | tf_op jit(solution)/shard_map/ppermute | solution.py:40
  57.2 6.5 %collective-permute-start.21 = (bf16[192,512]{1,0:T(8,128)(2,1)S(1)}, bf16[192,512]{1,0:T(8,128)(2,1)S(1)}, u32[]{:S(2)}, u32[]{:S(2)}) collective-permute-start(bf16[192,512]{1,0:T(8,128)(2,1)S(1)} %constant_dynamic-update-slice_fusion.4.refs_0_), channel_id=1, source_target_pairs={{0,1},{1,0},{2,3},{3,2},{4,5},{5,4},{6,7},{7,6},{8,9},{9,8},{10,11... | collective-permute-start | bytes 589832 | tf_op jit(solution)/shard_map/ppermute | solution.py:40
  57.4 23.7 %collective-permute-start.11 = (bf16[192,640]{1,0:T(8,128)(2,1)S(1)}, bf16[192,640]{1,0:T(8,128)(2,1)S(1)}, u32[]{:S(2)}, u32[]{:S(2)}) collective-permute-start(bf16[192,640]{1,0:T(8,128)(2,1)S(1)} %get-tuple-element.33), channel_id=1, source_target_pairs={{0,1},{1,0},{2,3},{3,2},{4,5},{5,4},{6,7},{7,6},{8,9},{9,8},{10,11... | collective-permute-start | bytes 737288 | tf_op jit(solution)/shard_map/ppermute | solution.py:40
  62.4 1.4 %collective-permute-start.22 = (bf16[192,512]{1,0:T(8,128)(2,1)S(1)}, bf16[192,512]{1,0:T(8,128)(2,1)S(1)}, u32[]{:S(2)}, u32[]{:S(2)}) collective-permute-start(bf16[192,512]{1,0:T(8,128)(2,1)S(1)} %collective-permute-done.20.refs_1_), channel_id=1, source_target_pairs={{0,1},{1,0},{2,3},{3,2},{4,5},{5,4},{6,7},{7,6},{8,9},{9,8},{10,11... | collective-permute-start | bytes 589832 | tf_op jit(solution)/shard_map/ppermute | solution.py:40
  62.5 18.6 %collective-permute-start.13 = (bf16[192,640]{1,0:T(8,128)(2,1)S(1)}, bf16[192,640]{1,0:T(8,128)(2,1)S(1)}, u32[]{:S(2)}, u32[]{:S(2)}) collective-permute-start(bf16[192,640]{1,0:T(8,128)(2,1)S(1)} %add_convert_fusion.1), channel_id=1, source_target_pairs={{0,2},{1,3},{2,0},{3,1},{4,6},{5,7},{6,4},{7,5},{8,10},{9,11},{10,... | collective-permute-start | bytes 737288 | tf_op jit(solution)/shard_map/ppermute | solution.py:40
  80.5 1.5 %collective-permute-start.24 = (bf16[192,512]{1,0:T(8,128)(2,1)S(1)}, bf16[192,512]{1,0:T(8,128)(2,1)S(1)}, u32[]{:S(2)}, u32[]{:S(2)}) collective-permute-start(bf16[192,512]{1,0:T(8,128)(2,1)S(1)} %get-tuple-element.45), channel_id=1, source_target_pairs={{0,1},{1,0},{2,3},{3,2},{4,5},{5,4},{6,7},{7,6},{8,9},{9,8},{10,11... | collective-permute-start | bytes 589832 | tf_op jit(solution)/shard_map/ppermute | solution.py:40
  80.7 6.4 %collective-permute-start.23 = (bf16[192,512]{1,0:T(8,128)(2,1)S(1)}, bf16[192,512]{1,0:T(8,128)(2,1)S(1)}, u32[]{:S(2)}, u32[]{:S(2)}) collective-permute-start(bf16[192,512]{1,0:T(8,128)(2,1)S(1)} %get-tuple-element.43), channel_id=1, source_target_pairs={{0,1},{1,0},{2,3},{3,2},{4,5},{5,4},{6,7},{7,6},{8,9},{9,8},{10,11... | collective-permute-start | bytes 589832 | tf_op jit(solution)/shard_map/ppermute | solution.py:40
  82.1 7.0 %collective-permute-start.25 = (bf16[192,512]{1,0:T(8,128)(2,1)S(1)}, bf16[192,512]{1,0:T(8,128)(2,1)S(1)}, u32[]{:S(2)}, u32[]{:S(2)}) collective-permute-start(bf16[192,512]{1,0:T(8,128)(2,1)S(1)} %add_convert_fusion.3), channel_id=1, source_target_pairs={{0,2},{1,3},{2,0},{3,1},{4,6},{5,7},{6,4},{7,5},{8,10},{9,11},{10,... | collective-permute-start | bytes 589832 | tf_op jit(solution)/shard_map/ppermute | solution.py:40
  83.3 9.1 %collective-permute-start.14 = (bf16[48,640]{1,0:T(8,128)(2,1)S(1)}, bf16[48,640]{1,0:T(8,128)(2,1)S(1)}, u32[]{:S(2)}, u32[]{:S(2)}) collective-permute-start(bf16[48,640]{1,0:T(8,128)(2,1)S(1)} %get-tuple-element.53), channel_id=1, source_target_pairs={{0,12},{1,13},{2,14},{3,15},{4,0},{5,1},{6,2},{7,3},{8,4},{9,5},{1... | collective-permute-start | bytes 184328 | tf_op jit(solution)/shard_map/ppermute | solution.py:40
  86.5 6.6 %collective-permute-start.15 = (bf16[48,640]{1,0:T(8,128)(2,1)S(1)}, bf16[48,640]{1,0:T(8,128)(2,1)S(1)}, u32[]{:S(2)}, u32[]{:S(2)}) collective-permute-start(bf16[48,640]{1,0:T(8,128)(2,1)S(1)} %get-tuple-element.52), channel_id=1, source_target_pairs={{0,8},{1,9},{2,10},{3,11},{4,12},{5,13},{6,14},{7,15},{8,0},{9,1},... | collective-permute-start | bytes 184328 | tf_op jit(solution)/shard_map/ppermute | solution.py:40
  86.5 6.6 %collective-permute-start.16 = (bf16[48,640]{1,0:T(8,128)(2,1)S(1)}, bf16[48,640]{1,0:T(8,128)(2,1)S(1)}, u32[]{:S(2)}, u32[]{:S(2)}) collective-permute-start(bf16[48,640]{1,0:T(8,128)(2,1)S(1)} %get-tuple-element.51), channel_id=1, source_target_pairs={{0,4},{1,5},{2,6},{3,7},{4,8},{5,9},{6,10},{7,11},{8,12},{9,13},{1... | collective-permute-start | bytes 184328 | tf_op jit(solution)/shard_map/ppermute | solution.py:40
  89.2 4.9 %collective-permute-start.26 = (bf16[48,512]{1,0:T(8,128)(2,1)S(1)}, bf16[48,512]{1,0:T(8,128)(2,1)S(1)}, u32[]{:S(2)}, u32[]{:S(2)}) collective-permute-start(bf16[48,512]{1,0:T(8,128)(2,1)S(1)} %get-tuple-element.57), channel_id=1, source_target_pairs={{0,12},{1,13},{2,14},{3,15},{4,0},{5,1},{6,2},{7,3},{8,4},{9,5},{1... | collective-permute-start | bytes 147464 | tf_op jit(solution)/shard_map/ppermute | solution.py:40
  92.4 5.0 %collective-permute-start.27 = (bf16[48,512]{1,0:T(8,128)(2,1)S(1)}, bf16[48,512]{1,0:T(8,128)(2,1)S(1)}, u32[]{:S(2)}, u32[]{:S(2)}) collective-permute-start(bf16[48,512]{1,0:T(8,128)(2,1)S(1)} %get-tuple-element.56), channel_id=1, source_target_pairs={{0,8},{1,9},{2,10},{3,11},{4,12},{5,13},{6,14},{7,15},{8,0},{9,1},... | collective-permute-start | bytes 147464 | tf_op jit(solution)/shard_map/ppermute | solution.py:40
  92.4 5.9 %collective-permute-start.28 = (bf16[48,512]{1,0:T(8,128)(2,1)S(1)}, bf16[48,512]{1,0:T(8,128)(2,1)S(1)}, u32[]{:S(2)}, u32[]{:S(2)}) collective-permute-start(bf16[48,512]{1,0:T(8,128)(2,1)S(1)} %get-tuple-element.55), channel_id=1, source_target_pairs={{0,4},{1,5},{2,6},{3,7},{4,8},{5,9},{6,10},{7,11},{8,12},{9,13},{1... | collective-permute-start | bytes 147464 | tf_op jit(solution)/shard_map/ppermute | solution.py:40

commit v4 on v3

v4 whole, which is shorter than its diff:
```python
import functools

import jax
import jax.numpy as jnp
from jax import lax
from jax.experimental import pallas as pl
from jax.experimental.pallas import tpu as pltpu
from jax.sharding import PartitionSpec as P

PLEN = 128
VMEM = pl.BlockSpec(memory_space=pltpu.VMEM)
SMEM = pl.BlockSpec(memory_space=pltpu.SMEM)
ANY = pl.BlockSpec(memory_space=pl.ANY)
UNIT_STEP = 256


class Grid:
    def __init__(self, devices, experts):
        self.experts = experts
        self.pairs = devices // experts // 2
        index = lax.axis_index("dev")
        self.pair = (index // 2) % self.pairs
        self.core = index % 2

    def send(self, value, axis, step):
        moves = []
        for expert in range(self.experts):
            for pair in range(self.pairs):
                for core in range(2):
                    to = [expert, pair, core]
                    to[axis] = (to[axis] + step) % (self.experts, self.pairs, 2)[axis]
                    moves.append(
                        (
                            (expert * self.pairs + pair) * 2 + core,
                            (to[0] * self.pairs + to[1]) * 2 + to[2],
                        )
                    )
        return lax.ppermute(value, "dev", moves)

    def exchange(self, value):
        sharing = self.pairs * 2
        groups = [[e * sharing + i for e in range(self.experts)] for i in range(sharing)]
        return lax.all_to_all(
            value, "dev", split_axis=0, concat_axis=0, axis_index_groups=groups, tiled=True
        )


class Packing:
    def __init__(self, cap, features):
        best = None
        for chunks in range(1, features // 128 + 1):
            if features % (128 * chunks):
                continue
            rows = -(-cap * chunks // 16) * 16
            cost = rows * (features // chunks)
            if best is None or cost < best[0]:
                best = (cost, chunks, rows)
        _, self.chunks, self.rows = best
        self.cap = cap
        self.width = features // self.chunks


def live(position, lengths_ref):
    prompt = position // PLEN
    length = jnp.zeros_like(position)
    for p in range(lengths_ref.shape[0]):
        length = jnp.where(prompt == p, lengths_ref[p], length)
    return position % PLEN < length


def place_kernel(packing, prompts, lengths_ref, across_ref, down_ref, slot_ref, spot_ref):
    experts, rows = slot_ref.shape
    dead = -65536.0
    first_row = lax.axis_index("dev") * rows

    def order(dim):
        ids = [lax.broadcasted_iota(jnp.int32, (rows, rows), d) for d in (dim, 1 - dim)]
        return (ids[0] < ids[1]).astype(jnp.float32)

    expert_at = lax.broadcasted_iota(jnp.int32, (experts, rows), 0)
    routed = (across_ref[0:1, :] == expert_at) | (across_ref[1:2, :] == expert_at)
    if prompts:
        row = lax.broadcasted_iota(jnp.int32, (experts, rows), 1)
        routed = routed & live(first_row + row, lengths_ref)
    slot = jnp.dot(routed.astype(jnp.float32), order(0), preferred_element_type=jnp.float32)
    slot_ref[...] = jnp.where(routed, slot, dead)

    expert_at = lax.broadcasted_iota(jnp.int32, (rows, experts), 1)
    routed = (down_ref[:, 0:1] == expert_at) | (down_ref[:, 1:2] == expert_at)
    if prompts:
        row = lax.broadcasted_iota(jnp.int32, (rows, experts), 0)
        routed = routed & live(first_row + row, lengths_ref)
    slot = jnp.dot(order(1), routed.astype(jnp.float32), preferred_element_type=jnp.float32)
    spot = expert_at.astype(jnp.float32) * float(packing.rows) + slot
    spot = jnp.where(routed, spot, dead)
    for t in range(2):
        mine = down_ref[:, t : t + 1] == expert_at
        spot_ref[:, t : t + 1] = jnp.sum(jnp.where(mine, spot, 0.0), axis=1, keepdims=True)


def place(chosen, lengths, experts, packing, prompts):
    rows = chosen.shape[0]
    return pl.pallas_call(
        functools.partial(place_kernel, packing, prompts),
        out_shape=[
            jax.ShapeDtypeStruct((experts, rows), jnp.float32),
            jax.ShapeDtypeStruct((rows, 2), jnp.float32),
        ],
        in_specs=[SMEM] + [VMEM] * 2,
        out_specs=[VMEM] * 2,
        compiler_params=pltpu.CompilerParams(vmem_limit_bytes=8 << 20),
        name="place",
    )(lengths, chosen.T, chosen)


def modulate_kernel(packing, experts, slot_ref, scale_ref, shift_ref, value_ref, *refs):
    normed_ref, packed_ref = refs[-2:]
    rows = normed_ref.shape[0]
    values = value_ref[0].astype(jnp.float32)
    for k in range(1, value_ref.shape[0]):
        values = values + value_ref[k].astype(jnp.float32)
    values = values.astype(jnp.bfloat16).astype(jnp.float32)
    center = values - jnp.mean(values, axis=1, keepdims=True)
    spread = jnp.mean(center * center, axis=1, keepdims=True)
    normed = center * lax.rsqrt(spread + 1e-06) * scale_ref[...] + shift_ref[...]
    normed = normed.astype(jnp.bfloat16)
    normed_ref[...] = normed

    place = lax.broadcasted_iota(jnp.int32, (packing.rows, rows), 0).astype(jnp.float32)
    packed = None
    for j in range(packing.chunks):
        into = jnp.concatenate(
            [
                jnp.where(place - float(j * packing.cap) == slot_ref[k : k + 1, :], 1.0, 0.0)
                for k in range(experts)
            ],
            axis=0,
        ).astype(jnp.bfloat16)
        term = jnp.dot(
            into,
            normed[:, j * packing.width : (j + 1) * packing.width],
            preferred_element_type=jnp.float32,
        )
        packed = term if packed is None else packed + term
    packed_ref[...] = packed.astype(jnp.bfloat16)
def modulate(terms, slot, mod_scale, mod_shift, packing, experts, after):
    _, rows, features = terms.shape
    return pl.pallas_call(
        functools.partial(modulate_kernel, packing, experts),
        out_shape=[
            jax.ShapeDtypeStruct((rows, features), jnp.bfloat16),
            jax.ShapeDtypeStruct((experts * packing.rows, packing.width), jnp.bfloat16),
        ],
        in_specs=[VMEM] * 4 + [ANY] * len(after),
        out_specs=[VMEM] * 2,
        compiler_params=pltpu.CompilerParams(vmem_limit_bytes=8 << 20),
        name="modulate",
    )(slot, mod_scale.reshape(1, -1), mod_shift.reshape(1, -1), terms, *after)


def route_kernel(chosen_ref, normed_ref, router_ref, weight_ref):
    normed = normed_ref[...].astype(jnp.float32)
    logits = [
        jnp.sum(normed * router_ref[k : k + 1, :], axis=1, keepdims=True)
        for k in range(router_ref.shape[0])
    ]
    picked = []
    for t in range(2):
        logit = jnp.zeros_like(logits[0])
        for k, value in enumerate(logits):
            logit = jnp.where(chosen_ref[:, t : t + 1] == k, value, logit)
        picked.append(logit)
    weight_ref[:, 0:1] = jax.nn.sigmoid(picked[0] - picked[1])
    weight_ref[:, 1:2] = jax.nn.sigmoid(picked[1] - picked[0])


def route(normed, chosen, router_weight):
    return pl.pallas_call(
        route_kernel,
        out_shape=jax.ShapeDtypeStruct(chosen.shape, jnp.float32),
        in_specs=[VMEM] * 3,
        out_specs=VMEM,
        compiler_params=pltpu.CompilerParams(vmem_limit_bytes=8 << 20),
        name="route",
    )(chosen, normed, router_weight.T)


def cuts(total, step):
    return [(start, min(start + step, total)) for start in range(0, total, step)]


def expert_kernel(packing, count, after, *refs):
    row_refs = refs[:count]
    gate_hbm, up_hbm, down_hbm = refs[count : count + 3]
    out_refs = refs[count + 3 + after : 2 * count + 3 + after]
    gate_ref, up_ref, down_ref, rows_ref, total_ref, sems = refs[2 * count + 3 + after :]
    rows = total_ref.shape[0]
    units = gate_hbm.shape[0]
    unit_cuts = cuts(units, UNIT_STEP)
    copies = []
    for i, (lo, hi) in enumerate(unit_cuts):
        for t, (source, target) in enumerate(
            ((gate_hbm, gate_ref), (up_hbm, up_ref), (down_hbm, down_ref))
        ):
            copies.append(
                pltpu.make_async_copy(source.at[lo:hi], target.at[lo:hi], sems.at[3 * i + t])
            )
    for copy in copies:
        copy.start()

    cap, chunks, width, high = packing.cap, packing.chunks, packing.width, packing.rows
    per_ref = row_refs[0].shape[0] // high
    blocks = count * per_ref
    group = 16
    row_at = lax.broadcasted_iota(jnp.int32, (group * cap, group * high), 0)
    place = lax.broadcasted_iota(jnp.int32, (group * cap, group * high), 1)
    source_row = (row_at // cap) * high + row_at % cap
    packed = jnp.concatenate([ref[...] for ref in row_refs], axis=0)
    spare = rows_ref.shape[1] - rows
    for j in range(chunks):
        pick = jnp.where(place == source_row + j * cap, 1.0, 0.0).astype(jnp.bfloat16)
        parts = [
            jnp.dot(
                pick,
                packed[g * group * high : (g + 1) * group * high],
                preferred_element_type=jnp.float32,
            )
            for g in range(blocks // group)
        ]
        if spare:
            parts.append(jnp.zeros((spare, width), jnp.float32))
        part = jnp.concatenate(parts, axis=0)
        rows_ref[j * width : (j + 1) * width, :] = part.T.astype(jnp.bfloat16)

    def down(i, hidden):
        lo, hi = unit_cuts[i]
        copies[3 * i + 2].wait()
        term = jnp.dot(hidden, down_ref[lo:hi, :], preferred_element_type=jnp.float32)
        if i == 0:
            total_ref[...] = term
        else:
            total_ref[...] += term

    hidden = None
    for i, (lo, hi) in enumerate(unit_cuts):
        copies[3 * i].wait()
        gate = jnp.dot(gate_ref[lo:hi, :], rows_ref[...], preferred_element_type=jnp.float32)
        copies[3 * i + 1].wait()
        up = jnp.dot(up_ref[lo:hi, :], rows_ref[...], preferred_element_type=jnp.float32)
        if i > 0:
            down(i - 1, hidden)
        hidden = (gate * jax.nn.sigmoid(gate) * up).T[0:rows].astype(jnp.bfloat16)
    down(len(unit_cuts) - 1, hidden)
    total = total_ref[...].astype(jnp.bfloat16)

    place = lax.broadcasted_iota(jnp.int32, (group * high, group * cap), 0)
    row_at = lax.broadcasted_iota(jnp.int32, (group * high, group * cap), 1)
    target = (row_at // cap) * high + row_at % cap
    per_group = group // per_ref
    for g in range(blocks // group):
        packed = None
        for j in range(chunks):
            put = jnp.where(place == target + j * cap, 1.0, 0.0).astype(jnp.bfloat16)
            term = jnp.dot(
                put,
                total[g * group * cap : (g + 1) * group * cap, j * width : (j + 1) * width],
                preferred_element_type=jnp.float32,
            )
            packed = term if packed is None else packed + term
        packed = packed.astype(jnp.bfloat16)
        for i in range(per_group):
            out_refs[g * per_group + i][...] = packed[i * per_ref * high : (i + 1) * per_ref * high]


def expert_rows(arrays, w_gate, w_up, w_down, packing, after):
    features, units = w_gate.shape
    rows = len(arrays) * (arrays[0].shape[0] // packing.rows) * packing.cap
    return pl.pallas_call(
        functools.partial(expert_kernel, packing, len(arrays), len(after)),
        out_shape=[jax.ShapeDtypeStruct(arrays[0].shape, jnp.bfloat16)] * len(arrays),
        in_specs=[VMEM] * len(arrays) + [ANY] * (3 + len(after)),
        out_specs=[VMEM] * len(arrays),
        scratch_shapes=[
            pltpu.VMEM((units, features), jnp.bfloat16),
            pltpu.VMEM((units, features), jnp.bfloat16),
            pltpu.VMEM((units, features), jnp.bfloat16),
            pltpu.VMEM((features, -(-rows // 128) * 128), jnp.bfloat16),
            pltpu.VMEM((rows, features), jnp.float32),
            pltpu.SemaphoreType.DMA((3 * len(cuts(units, UNIT_STEP)),)),
        ],
        compiler_params=pltpu.CompilerParams(vmem_limit_bytes=48 << 20),
        cost_estimate=pl.CostEstimate(
            flops=6 * rows * features * units,
            bytes_accessed=6 * features * units,
            transcendentals=rows * units,
        ),
        name="experts",
    )(*arrays, w_gate.T, w_up.T, w_down, *after)


def combine_kernel(packing, spot_ref, weight_ref, block_ref, out_ref):
    rows = out_ref.shape[0]
    blocks = block_ref[...]
    place = lax.broadcasted_iota(jnp.int32, (rows, blocks.shape[0]), 1).astype(jnp.float32)
    picks = [
        jnp.where(place - float(j * packing.cap) == spot_ref[:, t : t + 1], 1.0, 0.0)
        for t in range(2)
        for j in range(packing.chunks)
    ]
    if rows % 16 == 0:
        table = jnp.concatenate(picks, axis=0).astype(jnp.bfloat16)
        picked = jnp.dot(table, blocks, preferred_element_type=jnp.float32)
        picked = [picked[i * rows : (i + 1) * rows] for i in range(len(picks))]
    else:
        picked = [
            jnp.dot(pick.astype(jnp.bfloat16), blocks, preferred_element_type=jnp.float32)
            for pick in picks
        ]
    for j in range(packing.chunks):
        out_ref[:, j * packing.width : (j + 1) * packing.width] = (
            weight_ref[:, 0:1] * picked[j] + weight_ref[:, 1:2] * picked[packing.chunks + j]
        ).astype(jnp.bfloat16)


def combine(spot, weights, blocks, packing, rows, features):
    return pl.pallas_call(
        functools.partial(combine_kernel, packing),
        out_shape=jax.ShapeDtypeStruct((rows, features), jnp.bfloat16),
        in_specs=[VMEM] * 3,
        out_specs=VMEM,
        compiler_params=pltpu.CompilerParams(vmem_limit_bytes=8 << 20),
        name="combine",
    )(spot, weights, blocks)


def dispatch(blocks, grid):
    first = grid.exchange(blocks)
    own = [first] + [grid.send(first, 1, k) for k in range(1, grid.pairs)]
    return own + [grid.send(value, 2, 1) for value in own]


def give_back(results, grid):
    own, other = results[: grid.pairs], results[grid.pairs :]
    sums = []
    for k in list(range(1, grid.pairs)) + [0]:
        sums.append(own[k].astype(jnp.float32) + grid.send(other[k], 2, 1).astype(jnp.float32))
    total = sums[-1]
    for k in range(1, grid.pairs):
        total = total + grid.send(sums[k - 1].astype(jnp.bfloat16), 1, -k).astype(jnp.float32)
    return grid.exchange(total.astype(jnp.bfloat16))


def project(text_hidden, caption_weight, grid):
    rows = text_hidden.shape[0] // (grid.experts * grid.pairs * 2)
    text = text_hidden.reshape(grid.experts, grid.pairs, 2, rows, text_hidden.shape[1])
    text = jnp.roll(text, -grid.pair, axis=1)
    text = jnp.roll(text, -grid.core, axis=2)
    text = jnp.transpose(text, (2, 1, 0, 3, 4)).reshape(2, -1, text_hidden.shape[1])
    other = jnp.dot(text[1], caption_weight, preferred_element_type=jnp.float32)
    own = jnp.dot(text[0], caption_weight, preferred_element_type=jnp.float32)
    total = own + grid.send(other.astype(jnp.bfloat16), 2, 1).astype(jnp.float32)
    rows_pair = rows * grid.experts
    parts = [total[k * rows_pair : (k + 1) * rows_pair] for k in range(grid.pairs)]
    total = parts[0]
    crossing = [part.astype(jnp.bfloat16) for part in parts[1:]]
    for k in range(1, grid.pairs):
        total = total + grid.send(crossing[k - 1], 1, k).astype(jnp.float32)
    terms = grid.exchange(total.astype(jnp.bfloat16))
    return (terms.reshape(grid.experts, rows, -1), crossing)


def local(
    image_rows,
    text_hidden,
    caption_weight,
    mod_scale,
    mod_shift,
    router_weight,
    image_experts,
    caption_experts,
    prompt_lengths,
    w_gate,
    w_up,
    w_down,
):
    devices = lax.axis_size("dev")
    features, experts = router_weight.shape
    grid = Grid(devices, experts)
    image_packing = Packing(image_rows.shape[0] * 3 // 4, features)
    caption_packing = Packing(text_hidden.shape[0] // devices // 2 + 1, features)

    terms, crossing = project(text_hidden, caption_weight, grid)
    image_slot, image_spot = place(image_experts, prompt_lengths, experts, image_packing, False)
    caption_slot, caption_spot = place(
        caption_experts, prompt_lengths, experts, caption_packing, True
    )
    caption_normed, caption_blocks = modulate(
        terms, caption_slot, mod_scale, mod_shift, caption_packing, experts, []
    )
    image_normed, image_blocks = modulate(
        image_rows[None], image_slot, mod_scale, mod_shift, image_packing, experts, crossing[:1]
    )

    def finish(normed, blocks, chosen, spot, packing, after):
        arrays = dispatch(blocks, grid)
        weights = route(normed, chosen, router_weight)
        results = expert_rows(arrays, w_gate, w_up, w_down, packing, after + [weights])
        blocks = give_back(results, grid)
        return combine(spot, weights, blocks, packing, chosen.shape[0], features)

    image_out = finish(
        image_normed, image_blocks, image_experts, image_spot, image_packing, [caption_blocks]
    )
    caption_out = finish(
        caption_normed, caption_blocks, caption_experts, caption_spot, caption_packing, []
    )
    return (image_out, caption_out)


def solution(mesh):
    in_specs = (
        P(("groups", "dev"), None),
        P("groups", "dev"),
        P("dev", None),
        P(),
        P(),
        P(),
        P(("groups", "dev"), None),
        P(("groups", "dev"), None),
        P("groups"),
        P(None, "dev"),
        P(None, "dev"),
        P("dev", None),
    )
    out_specs = (P(("groups", "dev"), None), P(("groups", "dev"), None))
    return jax.shard_map(local, mesh=mesh, in_specs=in_specs, out_specs=out_specs, check_vma=False)
```

time: 99.4 us -> 127 us (1.28)
  waiting for transfers between devices: 24.9 us -> 48.8 us
  other arithmetic: 1.57 us -> 3.55 us
  starting transfers between devices: 29.7 us -> 31.1 us
    all_to_all x0 -> x5, waiting for transfers between devices: none -> 23.2 us  [exchange(): lax.all_to_all(value, 'dev', split_axis=0, concat_axis=0, axis_index_grou...]
    all_to_all x0 -> x5, starting transfers between devices: none -> 20.4 us  [exchange(): lax.all_to_all(value, 'dev', split_axis=0, concat_axis=0, axis_index_grou...]
    ppermute x29 -> x14, starting transfers between devices: 29.7 us -> 10.7 us  [send(): return lax.ppermute(value, 'dev', moves)]
    convert_element_type x2 -> x3, other arithmetic: 0.19 us -> 2.31 us  [the longest x2 1.53 us: give_back(): return grid.exchange(total.astype(jnp.bfloat16))]
    ppermute x29 -> x14, waiting for transfers between devices: 24.9 us -> 25.7 us  [send(): return lax.ppermute(value, 'dev', moves)]
    pallas_call x4 -> x6, Pallas kernels: 3.97 us -> 4.62 us  [the longest x2 2.6 us: modulate(): pl.pallas_call(functools.partial(modulate_kernel, packing, experts), out_...]
  transfers between devices with their start and end apart: 29 -> 19, of which waited for: 14 -> 9; matrix products, arithmetic and copies ran while one was open for 1% -> 1% of each run, Pallas kernels for 40% -> 31%
where the time goes in v4:
time: 127 us; the launch traced here: 126 us
  waiting for transfers between devices  48.8 us (38%)
  Pallas kernels  40.4 us (32%)
  starting transfers between devices  31.1 us (24%)
  other arithmetic  3.55 us (3%)
    pallas_call x2, Pallas kernels, expert_rows(): pl.pallas_call(functools.partial(expert_kernel, packing, len(arrays), len...  34 us
    ppermute x14, waiting for transfers between devices, send(): return lax.ppermute(value, 'dev', moves)  25.7 us
    all_to_all x5, waiting for transfers between devices, exchange(): lax.all_to_all(value, 'dev', split_axis=0, concat_axis=0, axis_index_grou...  23.2 us
    all_to_all x5, starting transfers between devices, exchange(): lax.all_to_all(value, 'dev', split_axis=0, concat_axis=0, axis_index_grou...  20.4 us
    ppermute x14, starting transfers between devices, send(): return lax.ppermute(value, 'dev', moves)  10.7 us
    pallas_call x2, Pallas kernels, modulate(): pl.pallas_call(functools.partial(modulate_kernel, packing, experts), out_...  2.6 us
  transfers between devices with their start and end apart: 19, of which 9 were waited for; matrix products, arithmetic and copies ran while one was open for 1% of the time, Pallas kernels for 31%

profile of v4, /device:TPU:0, one launch (start us, length us, event | category | flops | bytes accessed | tf_op | source)
XLA Modules:
  0.0 125.9 jit_solution(11900882655145778796)
XLA Ops:
  0.6 0.0 copy-start
  0.7 1.1 fusion.3
  1.8 0.1 fusion.2
  1.9 0.1 copy-done
  2.0 0.3 convolution_convert_fusion
  2.4 0.5 collective-permute-start
  2.9 1.7 %collective-permute-done = bf16[128,2560]{1,0:T(8,128)(2,1)S(1)} collective-permute-done((bf16[128,2560]{1,0:T(8,128)(2,1)S(1)}, bf16[128,2560]{1,0:T(8,128)(2,1)S(1)}, u32[]{:S(2)}, u32[]{:S(2)}) %collective-permute-start) | collective-permute-done | bytes 655392 | tf_op jit(solution)/shard_map/ppermute | solution.py:38
  4.6 0.3 convert_add_fusion
  5.0 0.0 copy-start.6
  5.0 0.0 copy-start.7
  5.0 0.0 copy-start.3
  5.0 0.0 copy-start.5
  5.0 0.0 copy-start.2
  5.1 0.0 copy-start.4
  5.1 3.0 %collective-permute-start.4 = (bf16[64,2560]{1,0:T(8,128)(2,1)S(1)}, bf16[64,2560]{1,0:T(8,128)(2,1)S(1)}, u32[]{:S(2)}, u32[]{:S(2)}) collective-permute-start(bf16[64,2560]{1,0:T(8,128)(2,1)S(1)} %slice.27.refs_0_), channel_id=1, source_target_pairs={{0,2},{1,3},{2,0},{3,1},{4,6},{5,7},{6,4},{7,5},{8,10},{9,11},{10,... | collective-permute-start | bytes 983048 | tf_op jit(solution)/shard_map/ppermute | solution.py:38
  8.0 8.0 %collective-permute-done.4 = bf16[64,2560]{1,0:T(8,128)(2,1)S(1)} collective-permute-done((bf16[64,2560]{1,0:T(8,128)(2,1)S(1)}, bf16[64,2560]{1,0:T(8,128)(2,1)S(1)}, u32[]{:S(2)}, u32[]{:S(2)}) %collective-permute-start.4) | collective-permute-done | bytes 327712 | tf_op jit(solution)/shard_map/ppermute | solution.py:38
  16.0 0.8 fusion
  16.8 5.2 %all-to-all-start.1 = ((bf16[4,16,2560]{2,1,0:T(8,128)(2,1)}), bf16[4,16,2560]{2,1,0:T(8,128)(2,1)S(1)}, u32[]{:S(2)}, u32[]{:S(2)}) async-start(bf16[4,16,2560]{2,1,0:T(8,128)(2,1)} %bitcast.12), calls=%async_computation.1 | async-start | bytes 655360 | tf_op jit(solution)/shard_map/all_to_all | solution.py:43
  22.1 0.1 copy.22.down_ref.chosen_ref
  22.2 0.8 place.2
  23.0 1.3 %modulate.2 = (bf16[16,2560]{1,0:T(8,128)(2,1)S(1)}, bf16[192,640]{1,0:T(8,128)(2,1)}) custom-call(f32[4,16]{1,0:T(4,128)S(1)} %get-tuple-element.19.slot_ref, f32[1,2560]{1,0:T(1,128)S(1)} %reshape.32.scale_ref, f32[1,2560]{1,0:T(1,128)S(1)} %reshape.33.shift_ref, bf16[1,16,2560]{2,1,0:T(8,128)(2,1)S(1)} %bitcast.34, bf16[64,2560]{1,0:T(8,128)(2,1)S(1)} %slice.27.refs_0_), custom_call_target="tpu_custom_call" | custom-call | tf_op jit(solution)/shard_map/modulate/pallas_call | solution.py:148
  24.3 7.5 %all-to-all-done.1.value_ref = bf16[4,16,2560]{2,1,0:T(8,128)(2,1)S(1)} async-done(((bf16[4,16,2560]{2,1,0:T(8,128)(2,1)}), bf16[4,16,2560]{2,1,0:T(8,128)(2,1)S(1)}, u32[]{:S(2)}, u32[]{:S(2)}) %all-to-all-start.1) | async-done | bytes 327712 | tf_op jit(solution)/shard_map/all_to_all | solution.py:43
  31.8 3.4 %all-to-all-start = ((bf16[4,48,640]{2,1,0:T(8,128)(2,1)}), bf16[4,48,640]{2,1,0:T(8,128)(2,1)S(1)}, u32[]{:S(2)}, u32[]{:S(2)}) async-start(bf16[4,48,640]{2,1,0:T(8,128)(2,1)} %bitcast.7), calls=%async_computation | async-start | bytes 491520 | tf_op jit(solution)/shard_map/all_to_all | solution.py:43
  35.2 0.1 copy.26.down_ref.chosen_ref
  35.3 0.8 place.3
  36.1 1.3 %modulate.3 = (bf16[16,2560]{1,0:T(8,128)(2,1)S(1)}, bf16[192,512]{1,0:T(8,128)(2,1)}) custom-call(f32[4,16]{1,0:T(4,128)S(1)} %get-tuple-element.22.slot_ref, f32[1,2560]{1,0:T(1,128)S(1)} %reshape.32.scale_ref, f32[1,2560]{1,0:T(1,128)S(1)} %reshape.33.shift_ref, bf16[4,16,2560]{2,1,0:T(8,128)(2,1)S(1)} %all-to-all-done.1.value_ref), custom_call_target="tpu_custom_call" | custom-call | tf_op jit(solution)/shard_map/modulate/pallas_call | solution.py:148
  37.4 4.4 %all-to-all-done = bf16[4,48,640]{2,1,0:T(8,128)(2,1)S(1)} async-done(((bf16[4,48,640]{2,1,0:T(8,128)(2,1)}), bf16[4,48,640]{2,1,0:T(8,128)(2,1)S(1)}, u32[]{:S(2)}, u32[]{:S(2)}) %all-to-all-start) | async-done | bytes 245792 | tf_op jit(solution)/shard_map/all_to_all | solution.py:43
  41.8 3.5 %all-to-all-start.3 = ((bf16[4,48,512]{2,1,0:T(8,128)(2,1)}), bf16[4,48,512]{2,1,0:T(8,128)(2,1)S(1)}, u32[]{:S(2)}, u32[]{:S(2)}) async-start(bf16[4,48,512]{2,1,0:T(8,128)(2,1)} %bitcast.15), calls=%async_computation.3 | async-start | bytes 393216 | tf_op jit(solution)/shard_map/all_to_all | solution.py:43
  45.3 1.6 %collective-permute-start.1 = (bf16[192,640]{1,0:T(8,128)(2,1)S(1)}, bf16[192,640]{1,0:T(8,128)(2,1)S(1)}, u32[]{:S(2)}, u32[]{:S(2)}) collective-permute-start(bf16[192,640]{1,0:T(8,128)(2,1)S(1)} %bitcast.24), channel_id=1, source_target_pairs={{0,2},{1,3},{2,0},{3,1},{4,6},{5,7},{6,4},{7,5},{8,10},{9,11},{10,... | collective-permute-start | bytes 737288 | tf_op jit(solution)/shard_map/ppermute | solution.py:38
  47.0 0.0 collective-permute-start.2
  47.0 4.6 %collective-permute-done.1.refs_1_ = bf16[192,640]{1,0:T(8,128)(2,1)S(1)} collective-permute-done((bf16[192,640]{1,0:T(8,128)(2,1)S(1)}, bf16[192,640]{1,0:T(8,128)(2,1)S(1)}, u32[]{:S(2)}, u32[]{:S(2)}) %collective-permute-start.1) | collective-permute-done | bytes 245792 | tf_op jit(solution)/shard_map/ppermute | solution.py:38
  51.6 0.0 collective-permute-start.3
  51.6 0.0 all-to-all-done.3
  51.6 1.5 %collective-permute-start.8 = (bf16[192,512]{1,0:T(8,128)(2,1)S(1)}, bf16[192,512]{1,0:T(8,128)(2,1)S(1)}, u32[]{:S(2)}, u32[]{:S(2)}) collective-permute-start(bf16[192,512]{1,0:T(8,128)(2,1)S(1)} %bitcast.28), channel_id=1, source_target_pairs={{0,2},{1,3},{2,0},{3,1},{4,6},{5,7},{6,4},{7,5},{8,10},{9,11},{10,... | collective-permute-start | bytes 589832 | tf_op jit(solution)/shard_map/ppermute | solution.py:38
  53.2 0.2 route.2.refs_8_.weight_ref
  53.4 0.2 route.3.refs_7_.weight_ref
  53.6 0.3 collective-permute-start.9
  53.8 5.1 %collective-permute-done.8.refs_1_ = bf16[192,512]{1,0:T(8,128)(2,1)S(1)} collective-permute-done((bf16[192,512]{1,0:T(8,128)(2,1)S(1)}, bf16[192,512]{1,0:T(8,128)(2,1)S(1)}, u32[]{:S(2)}, u32[]{:S(2)}) %collective-permute-start.8) | collective-permute-done | bytes 196640 | tf_op jit(solution)/shard_map/ppermute | solution.py:38
  58.9 0.0 collective-permute-start.10
  58.9 17.5 %experts.2 = (bf16[192,640]{1,0:T(8,128)(2,1)S(1)}, bf16[192,640]{1,0:T(8,128)(2,1)S(1)}, bf16[192,640]{1,0:T(8,128)(2,1)S(1)}, bf16[192,640]{1,0:T(8,128)(2,1)S(1)}) custom-call(bf16[192,640]{1,0:T(8,128)(2,1)S(1)} %bitcast.26, bf16[192,640]{1,0:T(8,128)(2,1)S(1)} %collective-permute-done.1.refs_1_, bf16[192,640]{1,0:T(8,128)(2,1)S(1)} %collective-permute-done.2.refs_2_, ...), custom_call_target="tpu_custom_call" | custom-call | flops 5096079360 | bytes 26542080 | tf_op jit(solution)/shard_map/experts/pallas_call | solution.py:278
  76.5 0.6 collective-permute-start.6
  77.1 0.1 collective-permute-start.5
  77.1 0.0 collective-permute-done.9.refs_2_
  77.1 0.0 collective-permute-done.10.refs_3_
  77.1 16.5 %experts.3 = (bf16[192,512]{1,0:T(8,128)(2,1)S(1)}, bf16[192,512]{1,0:T(8,128)(2,1)S(1)}, bf16[192,512]{1,0:T(8,128)(2,1)S(1)}, bf16[192,512]{1,0:T(8,128)(2,1)S(1)}) custom-call(bf16[192,512]{1,0:T(8,128)(2,1)S(1)} %bitcast.30, bf16[192,512]{1,0:T(8,128)(2,1)S(1)} %collective-permute-done.8.refs_1_, bf16[192,512]{1,0:T(8,128)(2,1)S(1)} %collective-permute-done.9.refs_2_, ...), custom_call_target="tpu_custom_call" | custom-call | flops 3822059520 | bytes 26542080 | tf_op jit(solution)/shard_map/experts/pallas_call | solution.py:278
  93.6 0.5 collective-permute-start.12
  94.1 0.0 collective-permute-done.6
  94.1 0.1 add_convert_fusion.1
  94.2 1.6 %collective-permute-start.7 = (bf16[192,640]{1,0:T(8,128)(2,1)S(1)}, bf16[192,640]{1,0:T(8,128)(2,1)S(1)}, u32[]{:S(2)}, u32[]{:S(2)}) collective-permute-start(bf16[192,640]{1,0:T(8,128)(2,1)S(1)} %add_convert_fusion.1), channel_id=1, source_target_pairs={{0,2},{1,3},{2,0},{3,1},{4,6},{5,7},{6,4},{7,5},{8,10},{9,11},{10,... | collective-permute-start | bytes 737288 | tf_op jit(solution)/shard_map/ppermute | solution.py:38
  95.8 0.0 collective-permute-start.11
  95.8 0.0 collective-permute-done.12
  95.8 0.1 add_convert_fusion.3
  95.9 1.0 collective-permute-start.13
  96.9 6.2 %collective-permute-done.7 = bf16[192,640]{1,0:T(8,128)(2,1)S(1)} collective-permute-done((bf16[192,640]{1,0:T(8,128)(2,1)S(1)}, bf16[192,640]{1,0:T(8,128)(2,1)S(1)}, u32[]{:S(2)}, u32[]{:S(2)}) %collective-permute-start.7) | collective-permute-done | bytes 245792 | tf_op jit(solution)/shard_map/ppermute | solution.py:38
  103.1 0.8 add_convert_fusion
  103.9 4.9 %all-to-all-start.2 = ((bf16[4,48,640]{2,1,0:T(8,128)(2,1)}), bf16[4,48,640]{2,1,0:T(8,128)(2,1)S(1)}, u32[]{:S(2)}, u32[]{:S(2)}) async-start(bf16[4,48,640]{2,1,0:T(8,128)(2,1)} %bitcast.13), calls=%async_computation.2 | async-start | bytes 491520 | tf_op jit(solution)/shard_map/all_to_all | solution.py:43
  108.7 0.0 collective-permute-done.11
  108.7 0.0 collective-permute-done.13
  108.7 0.7 add_convert_fusion.2
  109.5 5.9 %all-to-all-done.2 = bf16[4,48,640]{2,1,0:T(8,128)(2,1)S(1)} async-done(((bf16[4,48,640]{2,1,0:T(8,128)(2,1)}), bf16[4,48,640]{2,1,0:T(8,128)(2,1)S(1)}, u32[]{:S(2)}, u32[]{:S(2)}) %all-to-all-start.2) | async-done | bytes 245792 | tf_op jit(solution)/shard_map/all_to_all | solution.py:43
  115.4 3.4 %all-to-all-start.4 = ((bf16[4,48,512]{2,1,0:T(8,128)(2,1)}), bf16[4,48,512]{2,1,0:T(8,128)(2,1)S(1)}, u32[]{:S(2)}, u32[]{:S(2)}) async-start(bf16[4,48,512]{2,1,0:T(8,128)(2,1)} %bitcast.17), calls=%async_computation.4 | async-start | bytes 393216 | tf_op jit(solution)/shard_map/all_to_all | solution.py:43
  118.8 0.9 combine.2
  119.7 5.4 %all-to-all-done.4 = bf16[4,48,512]{2,1,0:T(8,128)(2,1)S(1)} async-done(((bf16[4,48,512]{2,1,0:T(8,128)(2,1)}), bf16[4,48,512]{2,1,0:T(8,128)(2,1)S(1)}, u32[]{:S(2)}, u32[]{:S(2)}) %all-to-all-start.4) | async-done | bytes 196640 | tf_op jit(solution)/shard_map/all_to_all | solution.py:43
  125.0 0.9 combine.3
  (17 shorter events, 0.1 us)
Async XLA Ops:
  0.6 1.4 %copy-start = (bf16[256,2560]{1,0:T(8,128)(2,1)S(1)}, bf16[256,2560]{1,0:T(8,128)(2,1)}, u32[]{:S(2)}) copy-start(bf16[256,2560]{1,0:T(8,128)(2,1)} %param.14) | copy-start | bytes 3932164
  2.4 2.2 %collective-permute-start = (bf16[128,2560]{1,0:T(8,128)(2,1)S(1)}, bf16[128,2560]{1,0:T(8,128)(2,1)S(1)}, u32[]{:S(2)}, u32[]{:S(2)}) collective-permute-start(bf16[128,2560]{1,0:T(8,128)(2,1)S(1)} %convolution_convert_fusion), channel_id=1, source_target_pairs={{0,1},{1,0},{2,3},{3,2},{4,5},{5,4},{6,7},{7,6},{8,9},{9,8},{10,11... | collective-permute-start | bytes 1966088 | tf_op jit(solution)/shard_map/ppermute | solution.py:38
  5.0 17.1 %copy-start.6 = (f32[2560]{0:T(1024)S(1)}, f32[2560]{0:T(1024)}, u32[]{:S(2)}) copy-start(f32[2560]{0:T(1024)} %param.15) | copy-start | bytes 30724
  5.0 17.1 %copy-start.7 = (f32[2560]{0:T(1024)S(1)}, f32[2560]{0:T(1024)}, u32[]{:S(2)}) copy-start(f32[2560]{0:T(1024)} %param.16) | copy-start | bytes 30724
  5.0 17.1 %copy-start.3 = (s32[16,2]{0,1:T(2,128)S(1)}, s32[16,2]{0,1:T(2,128)}, u32[]{:S(2)}) copy-start(s32[16,2]{0,1:T(2,128)} %param.18) | copy-start | bytes 388
  5.0 17.2 %copy-start.5 = (s32[2]{0:T(128)S(1)}, s32[2]{0:T(128)}, u32[]{:S(2)}) copy-start(s32[2]{0:T(128)} %lengths_ref.3) | copy-start | bytes 28
  5.0 18.0 %copy-start.2 = (bf16[16,2560]{1,0:T(8,128)(2,1)S(1)}, bf16[16,2560]{1,0:T(8,128)(2,1)}, u32[]{:S(2)}) copy-start(bf16[16,2560]{1,0:T(8,128)(2,1)} %param.12) | copy-start | bytes 245764
  5.1 30.1 %copy-start.4 = (s32[16,2]{0,1:T(2,128)S(1)}, s32[16,2]{0,1:T(2,128)}, u32[]{:S(2)}) copy-start(s32[16,2]{0,1:T(2,128)} %param.19) | copy-start | bytes 388
  5.1 11.0 %collective-permute-start.4 = (bf16[64,2560]{1,0:T(8,128)(2,1)S(1)}, bf16[64,2560]{1,0:T(8,128)(2,1)S(1)}, u32[]{:S(2)}, u32[]{:S(2)}) collective-permute-start(bf16[64,2560]{1,0:T(8,128)(2,1)S(1)} %slice.27.refs_0_), channel_id=1, source_target_pairs={{0,2},{1,3},{2,0},{3,1},{4,6},{5,7},{6,4},{7,5},{8,10},{9,11},{10,... | collective-permute-start | bytes 983048 | tf_op jit(solution)/shard_map/ppermute | solution.py:38
  16.8 36.3 %copy-start.1 = (f32[2560,4]{0,1:T(4,128)S(1)}, f32[2560,4]{0,1:T(4,128)}, u32[]{:S(2)}) copy-start(f32[2560,4]{0,1:T(4,128)} %param.17) | copy-start | bytes 122884
  16.8 15.0 %all-to-all-start.1 = ((bf16[4,16,2560]{2,1,0:T(8,128)(2,1)}), bf16[4,16,2560]{2,1,0:T(8,128)(2,1)S(1)}, u32[]{:S(2)}, u32[]{:S(2)}) async-start(bf16[4,16,2560]{2,1,0:T(8,128)(2,1)} %bitcast.12), calls=%async_computation.1 | async-start | bytes 655360 | tf_op jit(solution)/shard_map/all_to_all | solution.py:43
  31.8 10.0 %all-to-all-start = ((bf16[4,48,640]{2,1,0:T(8,128)(2,1)}), bf16[4,48,640]{2,1,0:T(8,128)(2,1)S(1)}, u32[]{:S(2)}, u32[]{:S(2)}) async-start(bf16[4,48,640]{2,1,0:T(8,128)(2,1)} %bitcast.7), calls=%async_computation | async-start | bytes 491520 | tf_op jit(solution)/shard_map/all_to_all | solution.py:43
  41.8 9.8 %all-to-all-start.3 = ((bf16[4,48,512]{2,1,0:T(8,128)(2,1)}), bf16[4,48,512]{2,1,0:T(8,128)(2,1)S(1)}, u32[]{:S(2)}, u32[]{:S(2)}) async-start(bf16[4,48,512]{2,1,0:T(8,128)(2,1)} %bitcast.15), calls=%async_computation.3 | async-start | bytes 393216 | tf_op jit(solution)/shard_map/all_to_all | solution.py:43
  45.3 6.3 %collective-permute-start.1 = (bf16[192,640]{1,0:T(8,128)(2,1)S(1)}, bf16[192,640]{1,0:T(8,128)(2,1)S(1)}, u32[]{:S(2)}, u32[]{:S(2)}) collective-permute-start(bf16[192,640]{1,0:T(8,128)(2,1)S(1)} %bitcast.24), channel_id=1, source_target_pairs={{0,2},{1,3},{2,0},{3,1},{4,6},{5,7},{6,4},{7,5},{8,10},{9,11},{10,... | collective-permute-start | bytes 737288 | tf_op jit(solution)/shard_map/ppermute | solution.py:38
  47.0 12.0 %collective-permute-start.2 = (bf16[192,640]{1,0:T(8,128)(2,1)S(1)}, bf16[192,640]{1,0:T(8,128)(2,1)S(1)}, u32[]{:S(2)}, u32[]{:S(2)}) collective-permute-start(bf16[192,640]{1,0:T(8,128)(2,1)S(1)} %bitcast.25), channel_id=1, source_target_pairs={{0,1},{1,0},{2,3},{3,2},{4,5},{5,4},{6,7},{7,6},{8,9},{9,8},{10,11... | collective-permute-start | bytes 737288 | tf_op jit(solution)/shard_map/ppermute | solution.py:38
  51.6 7.3 %collective-permute-start.3 = (bf16[192,640]{1,0:T(8,128)(2,1)S(1)}, bf16[192,640]{1,0:T(8,128)(2,1)S(1)}, u32[]{:S(2)}, u32[]{:S(2)}) collective-permute-start(bf16[192,640]{1,0:T(8,128)(2,1)S(1)} %collective-permute-done.1.refs_1_), channel_id=1, source_target_pairs={{0,1},{1,0},{2,3},{3,2},{4,5},{5,4},{6,7},{7,6},{8,9},{9,8},{10,11... | collective-permute-start | bytes 737288 | tf_op jit(solution)/shard_map/ppermute | solution.py:38
  51.6 7.3 %collective-permute-start.8 = (bf16[192,512]{1,0:T(8,128)(2,1)S(1)}, bf16[192,512]{1,0:T(8,128)(2,1)S(1)}, u32[]{:S(2)}, u32[]{:S(2)}) collective-permute-start(bf16[192,512]{1,0:T(8,128)(2,1)S(1)} %bitcast.28), channel_id=1, source_target_pairs={{0,2},{1,3},{2,0},{3,1},{4,6},{5,7},{6,4},{7,5},{8,10},{9,11},{10,... | collective-permute-start | bytes 589832 | tf_op jit(solution)/shard_map/ppermute | solution.py:38
  53.6 23.6 %collective-permute-start.9 = (bf16[192,512]{1,0:T(8,128)(2,1)S(1)}, bf16[192,512]{1,0:T(8,128)(2,1)S(1)}, u32[]{:S(2)}, u32[]{:S(2)}) collective-permute-start(bf16[192,512]{1,0:T(8,128)(2,1)S(1)} %bitcast.29), channel_id=1, source_target_pairs={{0,1},{1,0},{2,3},{3,2},{4,5},{5,4},{6,7},{7,6},{8,9},{9,8},{10,11... | collective-permute-start | bytes 589832 | tf_op jit(solution)/shard_map/ppermute | solution.py:38
  58.9 18.2 %collective-permute-start.10 = (bf16[192,512]{1,0:T(8,128)(2,1)S(1)}, bf16[192,512]{1,0:T(8,128)(2,1)S(1)}, u32[]{:S(2)}, u32[]{:S(2)}) collective-permute-start(bf16[192,512]{1,0:T(8,128)(2,1)S(1)} %collective-permute-done.8.refs_1_), channel_id=1, source_target_pairs={{0,1},{1,0},{2,3},{3,2},{4,5},{5,4},{6,7},{7,6},{8,9},{9,8},{10,11... | collective-permute-start | bytes 589832 | tf_op jit(solution)/shard_map/ppermute | solution.py:38
  76.5 17.7 %collective-permute-start.6 = (bf16[192,640]{1,0:T(8,128)(2,1)S(1)}, bf16[192,640]{1,0:T(8,128)(2,1)S(1)}, u32[]{:S(2)}, u32[]{:S(2)}) collective-permute-start(bf16[192,640]{1,0:T(8,128)(2,1)S(1)} %get-tuple-element.27), channel_id=1, source_target_pairs={{0,1},{1,0},{2,3},{3,2},{4,5},{5,4},{6,7},{7,6},{8,9},{9,8},{10,11... | collective-permute-start | bytes 737288 | tf_op jit(solution)/shard_map/ppermute | solution.py:38
  77.1 19.8 %collective-permute-start.5 = (bf16[192,640]{1,0:T(8,128)(2,1)S(1)}, bf16[192,640]{1,0:T(8,128)(2,1)S(1)}, u32[]{:S(2)}, u32[]{:S(2)}) collective-permute-start(bf16[192,640]{1,0:T(8,128)(2,1)S(1)} %get-tuple-element.25), channel_id=1, source_target_pairs={{0,1},{1,0},{2,3},{3,2},{4,5},{5,4},{6,7},{7,6},{8,9},{9,8},{10,11... | collective-permute-start | bytes 737288 | tf_op jit(solution)/shard_map/ppermute | solution.py:38
  93.6 2.2 %collective-permute-start.12 = (bf16[192,512]{1,0:T(8,128)(2,1)S(1)}, bf16[192,512]{1,0:T(8,128)(2,1)S(1)}, u32[]{:S(2)}, u32[]{:S(2)}) collective-permute-start(bf16[192,512]{1,0:T(8,128)(2,1)S(1)} %get-tuple-element.33), channel_id=1, source_target_pairs={{0,1},{1,0},{2,3},{3,2},{4,5},{5,4},{6,7},{7,6},{8,9},{9,8},{10,11... | collective-permute-start | bytes 589832 | tf_op jit(solution)/shard_map/ppermute | solution.py:38
  94.2 8.9 %collective-permute-start.7 = (bf16[192,640]{1,0:T(8,128)(2,1)S(1)}, bf16[192,640]{1,0:T(8,128)(2,1)S(1)}, u32[]{:S(2)}, u32[]{:S(2)}) collective-permute-start(bf16[192,640]{1,0:T(8,128)(2,1)S(1)} %add_convert_fusion.1), channel_id=1, source_target_pairs={{0,2},{1,3},{2,0},{3,1},{4,6},{5,7},{6,4},{7,5},{8,10},{9,11},{10,... | collective-permute-start | bytes 737288 | tf_op jit(solution)/shard_map/ppermute | solution.py:38
  95.8 12.9 %collective-permute-start.11 = (bf16[192,512]{1,0:T(8,128)(2,1)S(1)}, bf16[192,512]{1,0:T(8,128)(2,1)S(1)}, u32[]{:S(2)}, u32[]{:S(2)}) collective-permute-start(bf16[192,512]{1,0:T(8,128)(2,1)S(1)} %get-tuple-element.31), channel_id=1, source_target_pairs={{0,1},{1,0},{2,3},{3,2},{4,5},{5,4},{6,7},{7,6},{8,9},{9,8},{10,11... | collective-permute-start | bytes 589832 | tf_op jit(solution)/shard_map/ppermute | solution.py:38
  95.9 12.9 %collective-permute-start.13 = (bf16[192,512]{1,0:T(8,128)(2,1)S(1)}, bf16[192,512]{1,0:T(8,128)(2,1)S(1)}, u32[]{:S(2)}, u32[]{:S(2)}) collective-permute-start(bf16[192,512]{1,0:T(8,128)(2,1)S(1)} %add_convert_fusion.3), channel_id=1, source_target_pairs={{0,2},{1,3},{2,0},{3,1},{4,6},{5,7},{6,4},{7,5},{8,10},{9,11},{10,... | collective-permute-start | bytes 589832 | tf_op jit(solution)/shard_map/ppermute | solution.py:38
  103.9 11.5 %all-to-all-start.2 = ((bf16[4,48,640]{2,1,0:T(8,128)(2,1)}), bf16[4,48,640]{2,1,0:T(8,128)(2,1)S(1)}, u32[]{:S(2)}, u32[]{:S(2)}) async-start(bf16[4,48,640]{2,1,0:T(8,128)(2,1)} %bitcast.13), calls=%async_computation.2 | async-start | bytes 491520 | tf_op jit(solution)/shard_map/all_to_all | solution.py:43
  115.4 9.6 %all-to-all-start.4 = ((bf16[4,48,512]{2,1,0:T(8,128)(2,1)}), bf16[4,48,512]{2,1,0:T(8,128)(2,1)S(1)}, u32[]{:S(2)}, u32[]{:S(2)}) async-start(bf16[4,48,512]{2,1,0:T(8,128)(2,1)} %bitcast.17), calls=%async_computation.4 | async-start | bytes 393216 | tf_op jit(solution)/shard_map/all_to_all | solution.py:43

commit v5 on v4

--- a/solution.py
+++ b/solution.py
@@ -11,7 +11,7 @@
 VMEM = pl.BlockSpec(memory_space=pltpu.VMEM)
 SMEM = pl.BlockSpec(memory_space=pltpu.SMEM)
 ANY = pl.BlockSpec(memory_space=pl.ANY)
-UNIT_STEP = 256
+UNIT_STEP = 640
 
 
 class Grid:
@@ -19,6 +19,7 @@
         self.experts = experts
         self.pairs = devices // experts // 2
         index = lax.axis_index("dev")
+        self.expert = index // (self.pairs * 2)
         self.pair = (index // 2) % self.pairs
         self.core = index % 2
 
@@ -37,13 +38,6 @@
                     )
         return lax.ppermute(value, "dev", moves)
 
-    def exchange(self, value):
-        sharing = self.pairs * 2
-        groups = [[e * sharing + i for e in range(self.experts)] for i in range(sharing)]
-        return lax.all_to_all(
-            value, "dev", split_axis=0, concat_axis=0, axis_index_groups=groups, tiled=True
-        )
-
 
 class Packing:
     def __init__(self, cap, features):
@@ -71,14 +65,17 @@
 def place_kernel(packing, prompts, lengths_ref, across_ref, down_ref, slot_ref, spot_ref):
     experts, rows = slot_ref.shape
     dead = -65536.0
-    first_row = lax.axis_index("dev") * rows
+    index = lax.axis_index("dev")
+    first_row = index * rows
+    shift = experts - index // (lax.axis_size("dev") // experts)
+    across, down = lax.rem(across_ref[...] + shift, experts), lax.rem(down_ref[...] + shift, experts)
 
     def order(dim):
         ids = [lax.broadcasted_iota(jnp.int32, (rows, rows), d) for d in (dim, 1 - dim)]
         return (ids[0] < ids[1]).astype(jnp.float32)
 
     expert_at = lax.broadcasted_iota(jnp.int32, (experts, rows), 0)
-    routed = (across_ref[0:1, :] == expert_at) | (across_ref[1:2, :] == expert_at)
+    routed = (across[0:1, :] == expert_at) | (across[1:2, :] == expert_at)
     if prompts:
         row = lax.broadcasted_iota(jnp.int32, (experts, rows), 1)
         routed = routed & live(first_row + row, lengths_ref)
@@ -86,7 +83,7 @@
     slot_ref[...] = jnp.where(routed, slot, dead)
 
     expert_at = lax.broadcasted_iota(jnp.int32, (rows, experts), 1)
-    routed = (down_ref[:, 0:1] == expert_at) | (down_ref[:, 1:2] == expert_at)
+    routed = (down[:, 0:1] == expert_at) | (down[:, 1:2] == expert_at)
     if prompts:
         row = lax.broadcasted_iota(jnp.int32, (rows, experts), 0)
         routed = routed & live(first_row + row, lengths_ref)
@@ -94,7 +91,7 @@
     spot = expert_at.astype(jnp.float32) * float(packing.rows) + slot
     spot = jnp.where(routed, spot, dead)
     for t in range(2):
-        mine = down_ref[:, t : t + 1] == expert_at
+        mine = down[:, t : t + 1] == expert_at
         spot_ref[:, t : t + 1] = jnp.sum(jnp.where(mine, spot, 0.0), axis=1, keepdims=True)
 
 
@@ -113,12 +110,12 @@
     )(lengths, chosen.T, chosen)
 
 
-def modulate_kernel(packing, experts, slot_ref, scale_ref, shift_ref, value_ref, *refs):
-    normed_ref, packed_ref = refs[-2:]
+def modulate_kernel(packing, experts, count, slot_ref, scale_ref, shift_ref, *refs):
+    normed_ref, packed_refs = refs[-1 - experts], refs[-experts:]
     rows = normed_ref.shape[0]
-    values = value_ref[0].astype(jnp.float32)
-    for k in range(1, value_ref.shape[0]):
-        values = values + value_ref[k].astype(jnp.float32)
+    values = refs[0][...].astype(jnp.float32)
+    for ref in refs[1:count]:
+        values = values + ref[...].astype(jnp.float32)
     values = values.astype(jnp.bfloat16).astype(jnp.float32)
     center = values - jnp.mean(values, axis=1, keepdims=True)
     spread = jnp.mean(center * center, axis=1, keepdims=True)
@@ -142,20 +139,22 @@
             preferred_element_type=jnp.float32,
         )
         packed = term if packed is None else packed + term
-    packed_ref[...] = packed.astype(jnp.bfloat16)
+    for k in range(experts):
+        packed_refs[k][...] = packed[k * packing.rows : (k + 1) * packing.rows].astype(
+            jnp.bfloat16
+        )
 def modulate(terms, slot, mod_scale, mod_shift, packing, experts, after):
-    _, rows, features = terms.shape
-    return pl.pallas_call(
-        functools.partial(modulate_kernel, packing, experts),
-        out_shape=[
-            jax.ShapeDtypeStruct((rows, features), jnp.bfloat16),
-            jax.ShapeDtypeStruct((experts * packing.rows, packing.width), jnp.bfloat16),
-        ],
-        in_specs=[VMEM] * 4 + [ANY] * len(after),
-        out_specs=[VMEM] * 2,
+    rows, features = terms[0].shape
+    packed = jax.ShapeDtypeStruct((packing.rows, packing.width), jnp.bfloat16)
+    results = pl.pallas_call(
+        functools.partial(modulate_kernel, packing, experts, len(terms)),
+        out_shape=[jax.ShapeDtypeStruct((rows, features), jnp.bfloat16)] + [packed] * experts,
+        in_specs=[VMEM] * (3 + len(terms)) + [ANY] * len(after),
+        out_specs=[VMEM] * (1 + experts),
         compiler_params=pltpu.CompilerParams(vmem_limit_bytes=8 << 20),
         name="modulate",
-    )(slot, mod_scale.reshape(1, -1), mod_shift.reshape(1, -1), terms, *after)
+    )(slot, mod_scale.reshape(1, -1), mod_shift.reshape(1, -1), *terms, *after)
+    return (results[0], list(results[1:]))
 
 
 def route_kernel(chosen_ref, normed_ref, router_ref, weight_ref):
@@ -234,22 +233,34 @@
 
     def down(i, hidden):
         lo, hi = unit_cuts[i]
-        copies[3 * i + 2].wait()
         term = jnp.dot(hidden, down_ref[lo:hi, :], preferred_element_type=jnp.float32)
         if i == 0:
             total_ref[...] = term
         else:
             total_ref[...] += term
 
+    features = gate_hbm.shape[1]
+    middle = features // 256 * 128
+
+    def product(weight_ref, lo, hi):
+        return jnp.dot(
+            weight_ref[lo:hi, :middle], rows_ref[:middle, :], preferred_element_type=jnp.float32
+        ) + jnp.dot(
+            weight_ref[lo:hi, middle:], rows_ref[middle:, :], preferred_element_type=jnp.float32
+        )
+
     hidden = None
     for i, (lo, hi) in enumerate(unit_cuts):
+        if i > 0:
+            copies[3 * i - 1].wait()
         copies[3 * i].wait()
-        gate = jnp.dot(gate_ref[lo:hi, :], rows_ref[...], preferred_element_type=jnp.float32)
         copies[3 * i + 1].wait()
-        up = jnp.dot(up_ref[lo:hi, :], rows_ref[...], preferred_element_type=jnp.float32)
+        gate = product(gate_ref, lo, hi)
+        up = product(up_ref, lo, hi)
         if i > 0:
             down(i - 1, hidden)
         hidden = (gate * jax.nn.sigmoid(gate) * up).T[0:rows].astype(jnp.bfloat16)
+    copies[-1].wait()
     down(len(unit_cuts) - 1, hidden)
     total = total_ref[...].astype(jnp.bfloat16)
 
@@ -298,9 +309,10 @@
     )(*arrays, w_gate.T, w_up.T, w_down, *after)
 
 
-def combine_kernel(packing, spot_ref, weight_ref, block_ref, out_ref):
+def combine_kernel(packing, spot_ref, weight_ref, *refs):
+    block_refs, out_ref = refs[:-1], refs[-1]
     rows = out_ref.shape[0]
-    blocks = block_ref[...]
+    blocks = jnp.concatenate([ref[...] for ref in block_refs], axis=0)
     place = lax.broadcasted_iota(jnp.int32, (rows, blocks.shape[0]), 1).astype(jnp.float32)
     picks = [
         jnp.where(place - float(j * packing.cap) == spot_ref[:, t : t + 1], 1.0, 0.0)
@@ -326,15 +338,17 @@
     return pl.pallas_call(
         functools.partial(combine_kernel, packing),
         out_shape=jax.ShapeDtypeStruct((rows, features), jnp.bfloat16),
-        in_specs=[VMEM] * 3,
+        in_specs=[VMEM] * (2 + len(blocks)),
         out_specs=VMEM,
         compiler_params=pltpu.CompilerParams(vmem_limit_bytes=8 << 20),
         name="combine",
-    )(spot, weights, blocks)
+    )(spot, weights, *blocks)
 
 
 def dispatch(blocks, grid):
-    first = grid.exchange(blocks)
+    first = jnp.concatenate(
+        [blocks[0]] + [grid.send(blocks[k], 0, k) for k in range(1, grid.experts)], axis=0
+    )
     own = [first] + [grid.send(first, 1, k) for k in range(1, grid.pairs)]
     return own + [grid.send(value, 2, 1) for value in own]
 
@@ -347,26 +361,83 @@
     total = sums[-1]
     for k in range(1, grid.pairs):
         total = total + grid.send(sums[k - 1].astype(jnp.bfloat16), 1, -k).astype(jnp.float32)
-    return grid.exchange(total.astype(jnp.bfloat16))
+    total = total.astype(jnp.bfloat16)
+    rows = total.shape[0] // grid.experts
+    parts = [total[k * rows : (k + 1) * rows] for k in range(grid.experts)]
+    return [parts[0]] + [grid.send(parts[k], 0, -k) for k in range(1, grid.experts)]
+
+
+def project_kernel(experts, pairs, text_ref, weight_ref, *out_refs):
+    devices = experts * pairs * 2
+    rows = text_ref.shape[0] // devices
+    index = lax.axis_index("dev")
+    expert, pair, core = index // (pairs * 2), lax.rem(index // 2, pairs), lax.rem(index, 2)
+    place = 0
+    for c in (1, 0):
+        for p in list(range(1, pairs)) + [0]:
+            picked = []
+            for e in range(experts):
+                owner = lax.rem(expert + e, experts) * pairs + lax.rem(pair + p, pairs)
+                start = (owner * 2 + lax.rem(core + c, 2)) * rows
+                picked.append(text_ref[pl.ds(pl.multiple_of(start, rows), rows), :])
+            out = jnp.dot(
+                jnp.concatenate(picked, axis=0),
+                weight_ref[...],
+                preferred_element_type=jnp.float32,
+            )
+            out_refs[place][...] = out.astype(out_refs[place].dtype)
+            place += 1
+
+
+def partial_captions(text_hidden, caption_weight, grid):
+    groups = grid.pairs * 2
+    rows = text_hidden.shape[0] // (grid.experts * groups)
+    depth, features = caption_weight.shape
+    kinds = [jnp.bfloat16] * grid.pairs + [jnp.float32] * grid.pairs
+    if rows % 16 == 0:
+        return pl.pallas_call(
+            functools.partial(project_kernel, grid.experts, grid.pairs),
+            out_shape=[
+                jax.ShapeDtypeStruct((rows * grid.experts, features), kind) for kind in kinds
+            ],
+            in_specs=[VMEM] * 2,
+            out_specs=[VMEM] * len(kinds),
+            compiler_params=pltpu.CompilerParams(vmem_limit_bytes=16 << 20),
+            name="project",
+        )(text_hidden, caption_weight)
+    text = text_hidden.reshape(grid.experts, grid.pairs, 2, rows, depth)
+    text = jnp.roll(text, -grid.expert, axis=0)
+    text = jnp.roll(text, -1 - grid.pair, axis=1)
+    text = jnp.roll(text, -1 - grid.core, axis=2)
+    text = jnp.transpose(text, (2, 1, 0, 3, 4)).reshape(groups, -1, depth)
+    return [
+        jnp.dot(text[i], caption_weight, preferred_element_type=jnp.float32).astype(kind)
+        for i, kind in enumerate(kinds)
+    ]
 
 
 def project(text_hidden, caption_weight, grid):
     rows = text_hidden.shape[0] // (grid.experts * grid.pairs * 2)
-    text = text_hidden.reshape(grid.experts, grid.pairs, 2, rows, text_hidden.shape[1])
-    text = jnp.roll(text, -grid.pair, axis=1)
-    text = jnp.roll(text, -grid.core, axis=2)
-    text = jnp.transpose(text, (2, 1, 0, 3, 4)).reshape(2, -1, text_hidden.shape[1])
-    other = jnp.dot(text[1], caption_weight, preferred_element_type=jnp.float32)
-    own = jnp.dot(text[0], caption_weight, preferred_element_type=jnp.float32)
-    total = own + grid.send(other.astype(jnp.bfloat16), 2, 1).astype(jnp.float32)
-    rows_pair = rows * grid.experts
-    parts = [total[k * rows_pair : (k + 1) * rows_pair] for k in range(grid.pairs)]
-    total = parts[0]
-    crossing = [part.astype(jnp.bfloat16) for part in parts[1:]]
-    for k in range(1, grid.pairs):
-        total = total + grid.send(crossing[k - 1], 1, k).astype(jnp.float32)
-    terms = grid.exchange(total.astype(jnp.bfloat16))
-    return (terms.reshape(grid.experts, rows, -1), crossing)
+    partial = partial_captions(text_hidden, caption_weight, grid)
+    sums = [
+        partial[grid.pairs + i] + grid.send(partial[i], 2, 1).astype(jnp.float32)
+        for i in range(grid.pairs)
+    ]
+    half = grid.experts // 2
+    pieces = [list(range(grid.experts - half, grid.experts)), list(range(grid.experts - half))]
+    crossing, terms = [], [None] * grid.experts
+    for piece in pieces:
+        lo, hi = piece[0] * rows, (piece[-1] + 1) * rows
+        crossing.append([sums[k - 1][lo:hi].astype(jnp.bfloat16) for k in range(1, grid.pairs)])
+    for piece, sent in zip(pieces, crossing):
+        lo, hi = piece[0] * rows, (piece[-1] + 1) * rows
+        total = sums[-1][lo:hi]
+        for k in range(1, grid.pairs):
+            total = total + grid.send(sent[k - 1], 1, k).astype(jnp.float32)
+        for i, e in enumerate(piece):
+            part = total[i * rows : (i + 1) * rows]
+            terms[e] = part if e == 0 else grid.send(part.astype(jnp.bfloat16), 0, e)
+    return (terms, crossing[-1])
 
 
 def local(
@@ -398,21 +469,23 @@
         terms, caption_slot, mod_scale, mod_shift, caption_packing, experts, []
     )
     image_normed, image_blocks = modulate(
-        image_rows[None], image_slot, mod_scale, mod_shift, image_packing, experts, crossing[:1]
-    )
-
-    def finish(normed, blocks, chosen, spot, packing, after):
-        arrays = dispatch(blocks, grid)
+        [image_rows], image_slot, mod_scale, mod_shift, image_packing, experts, crossing[:1]
+    )
+
+    image_arrays = dispatch(image_blocks, grid)
+    caption_arrays = dispatch(caption_blocks, grid)
+
+    def finish(normed, arrays, chosen, spot, packing, after):
         weights = route(normed, chosen, router_weight)
         results = expert_rows(arrays, w_gate, w_up, w_down, packing, after + [weights])
         blocks = give_back(results, grid)
         return combine(spot, weights, blocks, packing, chosen.shape[0], features)
 
     image_out = finish(
-        image_normed, image_blocks, image_experts, image_spot, image_packing, [caption_blocks]
+        image_normed, image_arrays, image_experts, image_spot, image_packing, caption_arrays[:1]
     )
     caption_out = finish(
-        caption_normed, caption_blocks, caption_experts, caption_spot, caption_packing, []
+        caption_normed, caption_arrays, caption_experts, caption_spot, caption_packing, []
     )
     return (image_out, caption_out)
 

time: 127 us -> 98.7 us (0.78)
  waiting for transfers between devices: 48.8 us -> 25.4 us
  Pallas kernels: 40.4 us -> 31.5 us
  local copies, waits for them, and re-layouts: 0.42 us -> 8.22 us
  other arithmetic: 3.55 us -> 0.49 us
    all_to_all x5 -> x0, waiting for transfers between devices: 23.2 us -> none  [exchange(): lax.all_to_all(value, 'dev', split_axis=0, concat_axis=0, axis_index_grou...]
    ppermute x14 -> x31, starting transfers between devices: 10.7 us -> 31.8 us  [send(): return lax.ppermute(value, 'dev', moves)]
    all_to_all x5 -> x0, starting transfers between devices: 20.4 us -> none  [exchange(): lax.all_to_all(value, 'dev', split_axis=0, concat_axis=0, axis_index_grou...]
    pallas_call x2, Pallas kernels: 34 us -> 25.5 us  [expert_rows(): pl.pallas_call(functools.partial(expert_kernel, packing, len(arrays), len...]
    unnamed x18 -> x22, local copies, waits for them, and re-layouts: 0.34 us -> 6.68 us
    convert_element_type x3 -> x2, other arithmetic: 2.31 us -> 0.17 us  [give_back(): total = total.astype(jnp.bfloat16)]
    pallas_call x2 -> x3, Pallas kernels: 2.6 us -> 2.25 us  [the longest x2 1.22 us: modulate(): pl.pallas_call(functools.partial(modulate_kernel, packing, experts, len(t...]
    ppermute x14 -> x31, waiting for transfers between devices: 25.7 us -> 25.4 us  [send(): return lax.ppermute(value, 'dev', moves)]
  transfers between devices with their start and end apart: 19 -> 31, of which waited for: 9 -> 13; matrix products, arithmetic and copies ran while one was open for 1% -> 4% of each run, Pallas kernels for 31% -> 30%
where the time goes in v5:
time: 98.7 us; the launch traced here: 98.3 us
  starting transfers between devices  31.8 us (32%)
  Pallas kernels  31.5 us (32%)
  waiting for transfers between devices  25.4 us (26%)
  local copies, waits for them, and re-layouts  8.22 us (8%)
    ppermute x31, starting transfers between devices, send(): return lax.ppermute(value, 'dev', moves)  31.8 us
    pallas_call x2, Pallas kernels, expert_rows(): pl.pallas_call(functools.partial(expert_kernel, packing, len(arrays), len...  25.5 us
    ppermute x31, waiting for transfers between devices, send(): return lax.ppermute(value, 'dev', moves)  25.4 us
    unnamed x22, local copies, waits for them, and re-layouts  6.68 us
  transfers between devices with their start and end apart: 31, of which 13 were waited for; matrix products, arithmetic and copies ran while one was open for 4% of the time, Pallas kernels for 30%

profile of v5, /device:TPU:0, one launch (start us, length us, event | category | flops | bytes accessed | tf_op | source)
XLA Modules:
  0.0 98.3 jit_solution(5222065389619924640)
XLA Ops:
  0.6 1.3 %copy-done = bf16[256,2560]{1,0:T(8,128)(2,1)S(1)} copy-done((bf16[256,2560]{1,0:T(8,128)(2,1)S(1)}, bf16[256,2560]{1,0:T(8,128)(2,1)}, u32[]{:S(2)}) %copy-start) | copy-done | bytes 1310744
  1.9 0.9 copy-done.2
  2.9 1.0 %project.1 = (bf16[64,2560]{1,0:T(8,128)(2,1)S(1)}, bf16[64,2560]{1,0:T(8,128)(2,1)S(1)}, f32[64,2560]{1,0:T(8,128)S(1)}, f32[64,2560]{1,0:T(8,128)S(1)}) custom-call(bf16[256,256]{1,0:T(8,128)(2,1)S(1)} %copy-done.2, bf16[256,2560]{1,0:T(8,128)(2,1)S(1)} %copy-done), custom_call_target="tpu_custom_call" | custom-call | tf_op jit(solution)/shard_map/project/pallas_call | solution.py:398
  3.9 0.5 collective-permute-start
  4.4 0.1 collective-permute-start.7
  4.5 0.8 copy.16.down_ref.chosen_ref
  5.2 0.7 reshape.12.scale_ref
  5.9 0.7 reshape.13.shift_ref
  6.7 0.8 copy.14.down_ref.chosen_ref
  7.4 0.7 copy-done.4
  8.1 0.7 copy-done.6
  8.8 0.8 place.3
  9.6 0.7 copy-done.5
  10.3 0.8 place.2
  11.1 0.1 add_convert_fusion
  11.2 3.0 %collective-permute-start.8 = (bf16[32,2560]{1,0:T(8,128)(2,1)S(1)}, bf16[32,2560]{1,0:T(8,128)(2,1)S(1)}, u32[]{:S(2)}, u32[]{:S(2)}) collective-permute-start(bf16[32,2560]{1,0:T(8,128)(2,1)S(1)} %get-tuple-element.57.refs_1_), channel_id=1, source_target_pairs={{0,2},{1,3},{2,0},{3,1},{4,6},{5,7},{6,4},{7,5},{8,10},{9,11},{10,... | collective-permute-start | bytes 491528 | tf_op jit(solution)/shard_map/ppermute | solution.py:39
  14.2 0.1 collective-permute-start.10
  14.3 0.9 copy-done.3
  15.2 0.6 modulate.2
  15.8 2.1 %collective-permute-start.1 = (bf16[48,640]{1,0:T(8,128)(2,1)S(1)}, bf16[48,640]{1,0:T(8,128)(2,1)S(1)}, u32[]{:S(2)}, u32[]{:S(2)}) collective-permute-start(bf16[48,640]{1,0:T(8,128)(2,1)S(1)} %get-tuple-element.34), channel_id=1, source_target_pairs={{0,4},{1,5},{2,6},{3,7},{4,8},{5,9},{6,10},{7,11},{8,12},{9,13},{1... | collective-permute-start | bytes 184328 | tf_op jit(solution)/shard_map/ppermute | solution.py:39
  17.8 2.6 %collective-permute-start.2 = (bf16[48,640]{1,0:T(8,128)(2,1)S(1)}, bf16[48,640]{1,0:T(8,128)(2,1)S(1)}, u32[]{:S(2)}, u32[]{:S(2)}) collective-permute-start(bf16[48,640]{1,0:T(8,128)(2,1)S(1)} %get-tuple-element.35), channel_id=1, source_target_pairs={{0,8},{1,9},{2,10},{3,11},{4,12},{5,13},{6,14},{7,15},{8,0},{9,1},... | collective-permute-start | bytes 184328 | tf_op jit(solution)/shard_map/ppermute | solution.py:39
  20.4 1.3 %collective-permute-start.3 = (bf16[48,640]{1,0:T(8,128)(2,1)S(1)}, bf16[48,640]{1,0:T(8,128)(2,1)S(1)}, u32[]{:S(2)}, u32[]{:S(2)}) collective-permute-start(bf16[48,640]{1,0:T(8,128)(2,1)S(1)} %get-tuple-element.36), channel_id=1, source_target_pairs={{0,12},{1,13},{2,14},{3,15},{4,0},{5,1},{6,2},{7,3},{8,4},{9,5},{1... | collective-permute-start | bytes 184328 | tf_op jit(solution)/shard_map/ppermute | solution.py:39
  21.8 0.8 collective-permute-done.1
  22.6 2.3 %collective-permute-done.2 = bf16[48,640]{1,0:T(8,128)(2,1)S(1)} collective-permute-done((bf16[48,640]{1,0:T(8,128)(2,1)S(1)}, bf16[48,640]{1,0:T(8,128)(2,1)S(1)}, u32[]{:S(2)}, u32[]{:S(2)}) %collective-permute-start.2) | collective-permute-done | bytes 61472 | tf_op jit(solution)/shard_map/ppermute | solution.py:39
  25.0 0.1 fusion
  25.1 0.7 collective-permute-start.11
  25.7 1.6 %collective-permute-start.12 = (bf16[16,2560]{1,0:T(8,128)(2,1)S(1)}, bf16[16,2560]{1,0:T(8,128)(2,1)S(1)}, u32[]{:S(2)}, u32[]{:S(2)}) collective-permute-start(bf16[16,2560]{1,0:T(8,128)(2,1)S(1)} %get-tuple-element.66), channel_id=1, source_target_pairs={{0,12},{1,13},{2,14},{3,15},{4,0},{5,1},{6,2},{7,3},{8,4},{9,5},{1... | collective-permute-start | bytes 245768 | tf_op jit(solution)/shard_map/ppermute | solution.py:39
  27.3 0.5 collective-permute-start.9
  27.8 1.6 %collective-permute-start.4 = (bf16[192,640]{1,0:T(8,128)(2,1)S(1)}, bf16[192,640]{1,0:T(8,128)(2,1)S(1)}, u32[]{:S(2)}, u32[]{:S(2)}) collective-permute-start(bf16[192,640]{1,0:T(8,128)(2,1)S(1)} %constant_dynamic-update-slice_fusion.refs_0_), channel_id=1, source_target_pairs={{0,2},{1,3},{2,0},{3,1},{4,6},{5,7},{6,4},{7,5},{8,10},{9,11},{10,... | collective-permute-start | bytes 737288 | tf_op jit(solution)/shard_map/ppermute | solution.py:39
  29.4 2.2 %collective-permute-done.11.refs_2_ = bf16[16,2560]{1,0:T(8,128)(2,1)S(1)} collective-permute-done((bf16[16,2560]{1,0:T(8,128)(2,1)S(1)}, bf16[16,2560]{1,0:T(8,128)(2,1)S(1)}, u32[]{:S(2)}, u32[]{:S(2)}) %collective-permute-start.11) | collective-permute-done | bytes 81952 | tf_op jit(solution)/shard_map/ppermute | solution.py:39
  31.6 0.3 collective-permute-done.12.refs_3_
  31.9 1.7 %collective-permute-done.9.refs_1_ = bf16[16,2560]{1,0:T(8,128)(2,1)S(1)} collective-permute-done((bf16[16,2560]{1,0:T(8,128)(2,1)S(1)}, bf16[16,2560]{1,0:T(8,128)(2,1)S(1)}, u32[]{:S(2)}, u32[]{:S(2)}) %collective-permute-start.9) | collective-permute-done | bytes 81952 | tf_op jit(solution)/shard_map/ppermute | solution.py:39
  33.6 0.6 modulate.3
  34.2 0.1 collective-permute-start.13
  34.3 2.0 %collective-permute-start.14 = (bf16[48,512]{1,0:T(8,128)(2,1)S(1)}, bf16[48,512]{1,0:T(8,128)(2,1)S(1)}, u32[]{:S(2)}, u32[]{:S(2)}) collective-permute-start(bf16[48,512]{1,0:T(8,128)(2,1)S(1)} %get-tuple-element.42), channel_id=1, source_target_pairs={{0,8},{1,9},{2,10},{3,11},{4,12},{5,13},{6,14},{7,15},{8,0},{9,1},... | collective-permute-start | bytes 147464 | tf_op jit(solution)/shard_map/ppermute | solution.py:39
  36.4 2.2 %collective-permute-start.15 = (bf16[48,512]{1,0:T(8,128)(2,1)S(1)}, bf16[48,512]{1,0:T(8,128)(2,1)S(1)}, u32[]{:S(2)}, u32[]{:S(2)}) collective-permute-start(bf16[48,512]{1,0:T(8,128)(2,1)S(1)} %get-tuple-element.43), channel_id=1, source_target_pairs={{0,12},{1,13},{2,14},{3,15},{4,0},{5,1},{6,2},{7,3},{8,4},{9,5},{1... | collective-permute-start | bytes 147464 | tf_op jit(solution)/shard_map/ppermute | solution.py:39
  38.5 1.6 %collective-permute-done.13 = bf16[48,512]{1,0:T(8,128)(2,1)S(1)} collective-permute-done((bf16[48,512]{1,0:T(8,128)(2,1)S(1)}, bf16[48,512]{1,0:T(8,128)(2,1)S(1)}, u32[]{:S(2)}, u32[]{:S(2)}) %collective-permute-start.13) | collective-permute-done | bytes 49184 | tf_op jit(solution)/shard_map/ppermute | solution.py:39
  40.2 0.1 collective-permute-start.6
  40.3 0.5 collective-permute-done.15
  40.8 1.6 %collective-permute-start.22 = (bf16[192,512]{1,0:T(8,128)(2,1)S(1)}, bf16[192,512]{1,0:T(8,128)(2,1)S(1)}, u32[]{:S(2)}, u32[]{:S(2)}) collective-permute-start(bf16[192,512]{1,0:T(8,128)(2,1)S(1)} %constant_dynamic-update-slice_fusion.4.refs_7_.refs_0_), channel_id=1, source_target_pairs={{0,2},{1,3},{2,0},{3,1},{4,6},{5,7},{6,4},{7,5},{8,10},{9,11},{10,... | collective-permute-start | bytes 589832 | tf_op jit(solution)/shard_map/ppermute | solution.py:39
  42.3 0.2 route.2.refs_8_.weight_ref
  42.5 0.2 route.3.refs_7_.weight_ref
  42.8 4.9 %collective-permute-done.22.refs_1_ = bf16[192,512]{1,0:T(8,128)(2,1)S(1)} collective-permute-done((bf16[192,512]{1,0:T(8,128)(2,1)S(1)}, bf16[192,512]{1,0:T(8,128)(2,1)S(1)}, u32[]{:S(2)}, u32[]{:S(2)}) %collective-permute-start.22) | collective-permute-done | bytes 196640 | tf_op jit(solution)/shard_map/ppermute | solution.py:39
  47.7 13.2 %experts.2 = (bf16[192,640]{1,0:T(8,128)(2,1)S(1)}, bf16[192,640]{1,0:T(8,128)(2,1)S(1)}, bf16[192,640]{1,0:T(8,128)(2,1)S(1)}, bf16[192,640]{1,0:T(8,128)(2,1)S(1)}) custom-call(bf16[192,640]{1,0:T(8,128)(2,1)S(1)} %constant_dynamic-update-slice_fusion.refs_0_, bf16[192,640]{1,0:T(8,128)(2,1)S(1)} %collective-permute-done.4.refs_1_, ...), custom_call_target="tpu_custom_call" | custom-call | flops 5096079360 | bytes 26542080 | tf_op jit(solution)/shard_map/experts/pallas_call | solution.py:289
  60.9 0.6 collective-permute-start.17
  61.5 0.1 collective-permute-start.16
  61.6 12.2 %experts.3 = (bf16[192,512]{1,0:T(8,128)(2,1)S(1)}, bf16[192,512]{1,0:T(8,128)(2,1)S(1)}, bf16[192,512]{1,0:T(8,128)(2,1)S(1)}, bf16[192,512]{1,0:T(8,128)(2,1)S(1)}) custom-call(bf16[192,512]{1,0:T(8,128)(2,1)S(1)} %constant_dynamic-update-slice_fusion.4.refs_7_.refs_0_, bf16[192,512]{1,0:T(8,128)(2,1)S(1)} %collective-permute-done.22.refs_1_, ...), custom_call_target="tpu_custom_call" | custom-call | flops 3822059520 | bytes 26542080 | tf_op jit(solution)/shard_map/experts/pallas_call | solution.py:289
  73.8 0.5 collective-permute-start.26
  74.3 0.1 add_convert_fusion.2
  74.4 1.6 %collective-permute-start.18 = (bf16[192,640]{1,0:T(8,128)(2,1)S(1)}, bf16[192,640]{1,0:T(8,128)(2,1)S(1)}, u32[]{:S(2)}, u32[]{:S(2)}) collective-permute-start(bf16[192,640]{1,0:T(8,128)(2,1)S(1)} %add_convert_fusion.2), channel_id=1, source_target_pairs={{0,2},{1,3},{2,0},{3,1},{4,6},{5,7},{6,4},{7,5},{8,10},{9,11},{10,... | collective-permute-start | bytes 737288 | tf_op jit(solution)/shard_map/ppermute | solution.py:39
  76.1 1.0 %collective-permute-start.27 = (bf16[192,512]{1,0:T(8,128)(2,1)S(1)}, bf16[192,512]{1,0:T(8,128)(2,1)S(1)}, u32[]{:S(2)}, u32[]{:S(2)}) collective-permute-start(bf16[192,512]{1,0:T(8,128)(2,1)S(1)} %add_convert_fusion.4), channel_id=1, source_target_pairs={{0,2},{1,3},{2,0},{3,1},{4,6},{5,7},{6,4},{7,5},{8,10},{9,11},{10,... | collective-permute-start | bytes 589832 | tf_op jit(solution)/shard_map/ppermute | solution.py:39
  77.1 6.2 %collective-permute-done.18 = bf16[192,640]{1,0:T(8,128)(2,1)S(1)} collective-permute-done((bf16[192,640]{1,0:T(8,128)(2,1)S(1)}, bf16[192,640]{1,0:T(8,128)(2,1)S(1)}, u32[]{:S(2)}, u32[]{:S(2)}) %collective-permute-start.18) | collective-permute-done | bytes 245792 | tf_op jit(solution)/shard_map/ppermute | solution.py:39
  83.2 0.1 add_convert_fusion.1
  83.4 3.1 %collective-permute-start.19 = (bf16[48,640]{1,0:T(8,128)(2,1)S(1)}, bf16[48,640]{1,0:T(8,128)(2,1)S(1)}, u32[]{:S(2)}, u32[]{:S(2)}) collective-permute-start(bf16[48,640]{1,0:T(8,128)(2,1)S(1)} %get-tuple-element.60), channel_id=1, source_target_pairs={{0,12},{1,13},{2,14},{3,15},{4,0},{5,1},{6,2},{7,3},{8,4},{9,5},{1... | collective-permute-start | bytes 184328 | tf_op jit(solution)/shard_map/ppermute | solution.py:39
  86.5 0.6 collective-permute-start.21
  87.1 0.1 add_convert_fusion.3
  87.2 3.2 %collective-permute-start.28 = (bf16[48,512]{1,0:T(8,128)(2,1)S(1)}, bf16[48,512]{1,0:T(8,128)(2,1)S(1)}, u32[]{:S(2)}, u32[]{:S(2)}) collective-permute-start(bf16[48,512]{1,0:T(8,128)(2,1)S(1)} %get-tuple-element.64), channel_id=1, source_target_pairs={{0,12},{1,13},{2,14},{3,15},{4,0},{5,1},{6,2},{7,3},{8,4},{9,5},{1... | collective-permute-start | bytes 147464 | tf_op jit(solution)/shard_map/ppermute | solution.py:39
  90.5 1.1 %collective-permute-start.29 = (bf16[48,512]{1,0:T(8,128)(2,1)S(1)}, bf16[48,512]{1,0:T(8,128)(2,1)S(1)}, u32[]{:S(2)}, u32[]{:S(2)}) collective-permute-start(bf16[48,512]{1,0:T(8,128)(2,1)S(1)} %get-tuple-element.63), channel_id=1, source_target_pairs={{0,8},{1,9},{2,10},{3,11},{4,12},{5,13},{6,14},{7,15},{8,0},{9,1},... | collective-permute-start | bytes 147464 | tf_op jit(solution)/shard_map/ppermute | solution.py:39
  91.6 1.1 %collective-permute-done.20.refs_2_ = bf16[48,640]{1,0:T(8,128)(2,1)S(1)} collective-permute-done((bf16[48,640]{1,0:T(8,128)(2,1)S(1)}, bf16[48,640]{1,0:T(8,128)(2,1)S(1)}, u32[]{:S(2)}, u32[]{:S(2)}) %collective-permute-start.20) | collective-permute-done | bytes 61472 | tf_op jit(solution)/shard_map/ppermute | solution.py:39
  92.7 0.9 combine.2
  93.6 0.6 collective-permute-done.28.refs_1_
  94.2 1.2 %collective-permute-done.29.refs_2_ = bf16[48,512]{1,0:T(8,128)(2,1)S(1)} collective-permute-done((bf16[48,512]{1,0:T(8,128)(2,1)S(1)}, bf16[48,512]{1,0:T(8,128)(2,1)S(1)}, u32[]{:S(2)}, u32[]{:S(2)}) %collective-permute-start.29) | collective-permute-done | bytes 49184 | tf_op jit(solution)/shard_map/ppermute | solution.py:39
  95.4 2.0 %collective-permute-done.30.refs_3_ = bf16[48,512]{1,0:T(8,128)(2,1)S(1)} collective-permute-done((bf16[48,512]{1,0:T(8,128)(2,1)S(1)}, bf16[48,512]{1,0:T(8,128)(2,1)S(1)}, u32[]{:S(2)}, u32[]{:S(2)}) %collective-permute-start.30) | collective-permute-done | bytes 49184 | tf_op jit(solution)/shard_map/ppermute | solution.py:39
  97.5 0.9 combine.3
  (48 shorter events, 0.4 us)
Async XLA Ops:
  0.6 1.3 %copy-start = (bf16[256,2560]{1,0:T(8,128)(2,1)S(1)}, bf16[256,2560]{1,0:T(8,128)(2,1)}, u32[]{:S(2)}) copy-start(bf16[256,2560]{1,0:T(8,128)(2,1)} %weight_ref.1) | copy-start | bytes 3932164
  1.9 0.9 copy-start.2
  2.9 39.5 %copy-start.1 = (f32[2560,4]{0,1:T(4,128)S(1)}, f32[2560,4]{0,1:T(4,128)}, u32[]{:S(2)}) copy-start(f32[2560,4]{0,1:T(4,128)} %param.17) | copy-start | bytes 122884
  3.9 7.2 %collective-permute-start = (bf16[64,2560]{1,0:T(8,128)(2,1)S(1)}, bf16[64,2560]{1,0:T(8,128)(2,1)S(1)}, u32[]{:S(2)}, u32[]{:S(2)}) collective-permute-start(bf16[64,2560]{1,0:T(8,128)(2,1)S(1)} %get-tuple-element.31), channel_id=1, source_target_pairs={{0,1},{1,0},{2,3},{3,2},{4,5},{5,4},{6,7},{7,6},{8,9},{9,8},{10,11... | collective-permute-start | bytes 983048 | tf_op jit(solution)/shard_map/ppermute | solution.py:39
  4.4 16.0 %collective-permute-start.7 = (bf16[64,2560]{1,0:T(8,128)(2,1)S(1)}, bf16[64,2560]{1,0:T(8,128)(2,1)S(1)}, u32[]{:S(2)}, u32[]{:S(2)}) collective-permute-start(bf16[64,2560]{1,0:T(8,128)(2,1)S(1)} %get-tuple-element.39), channel_id=1, source_target_pairs={{0,1},{1,0},{2,3},{3,2},{4,5},{5,4},{6,7},{7,6},{8,9},{9,8},{10,11... | collective-permute-start | bytes 983048 | tf_op jit(solution)/shard_map/ppermute | solution.py:39
  7.4 0.7 copy-start.4
  8.1 0.7 copy-start.6
  9.6 0.7 copy-start.5
  11.2 13.8 %collective-permute-start.8 = (bf16[32,2560]{1,0:T(8,128)(2,1)S(1)}, bf16[32,2560]{1,0:T(8,128)(2,1)S(1)}, u32[]{:S(2)}, u32[]{:S(2)}) collective-permute-start(bf16[32,2560]{1,0:T(8,128)(2,1)S(1)} %get-tuple-element.57.refs_1_), channel_id=1, source_target_pairs={{0,2},{1,3},{2,0},{3,1},{4,6},{5,7},{6,4},{7,5},{8,10},{9,11},{10,... | collective-permute-start | bytes 491528 | tf_op jit(solution)/shard_map/ppermute | solution.py:39
  14.2 10.8 %collective-permute-start.10 = (bf16[32,2560]{1,0:T(8,128)(2,1)S(1)}, bf16[32,2560]{1,0:T(8,128)(2,1)S(1)}, u32[]{:S(2)}, u32[]{:S(2)}) collective-permute-start(bf16[32,2560]{1,0:T(8,128)(2,1)S(1)} %get-tuple-element.56), channel_id=1, source_target_pairs={{0,2},{1,3},{2,0},{3,1},{4,6},{5,7},{6,4},{7,5},{8,10},{9,11},{10,... | collective-permute-start | bytes 491528 | tf_op jit(solution)/shard_map/ppermute | solution.py:39
  14.3 0.9 copy-start.3
  15.8 6.9 %collective-permute-start.1 = (bf16[48,640]{1,0:T(8,128)(2,1)S(1)}, bf16[48,640]{1,0:T(8,128)(2,1)S(1)}, u32[]{:S(2)}, u32[]{:S(2)}) collective-permute-start(bf16[48,640]{1,0:T(8,128)(2,1)S(1)} %get-tuple-element.34), channel_id=1, source_target_pairs={{0,4},{1,5},{2,6},{3,7},{4,8},{5,9},{6,10},{7,11},{8,12},{9,13},{1... | collective-permute-start | bytes 184328 | tf_op jit(solution)/shard_map/ppermute | solution.py:39
  17.8 7.1 %collective-permute-start.2 = (bf16[48,640]{1,0:T(8,128)(2,1)S(1)}, bf16[48,640]{1,0:T(8,128)(2,1)S(1)}, u32[]{:S(2)}, u32[]{:S(2)}) collective-permute-start(bf16[48,640]{1,0:T(8,128)(2,1)S(1)} %get-tuple-element.35), channel_id=1, source_target_pairs={{0,8},{1,9},{2,10},{3,11},{4,12},{5,13},{6,14},{7,15},{8,0},{9,1},... | collective-permute-start | bytes 184328 | tf_op jit(solution)/shard_map/ppermute | solution.py:39
  20.4 7.4 %collective-permute-start.3 = (bf16[48,640]{1,0:T(8,128)(2,1)S(1)}, bf16[48,640]{1,0:T(8,128)(2,1)S(1)}, u32[]{:S(2)}, u32[]{:S(2)}) collective-permute-start(bf16[48,640]{1,0:T(8,128)(2,1)S(1)} %get-tuple-element.36), channel_id=1, source_target_pairs={{0,12},{1,13},{2,14},{3,15},{4,0},{5,1},{6,2},{7,3},{8,4},{9,5},{1... | collective-permute-start | bytes 184328 | tf_op jit(solution)/shard_map/ppermute | solution.py:39
  25.1 6.6 %collective-permute-start.11 = (bf16[16,2560]{1,0:T(8,128)(2,1)S(1)}, bf16[16,2560]{1,0:T(8,128)(2,1)S(1)}, u32[]{:S(2)}, u32[]{:S(2)}) collective-permute-start(bf16[16,2560]{1,0:T(8,128)(2,1)S(1)} %get-tuple-element.67), channel_id=1, source_target_pairs={{0,8},{1,9},{2,10},{3,11},{4,12},{5,13},{6,14},{7,15},{8,0},{9,1},... | collective-permute-start | bytes 245768 | tf_op jit(solution)/shard_map/ppermute | solution.py:39
  25.7 6.2 %collective-permute-start.12 = (bf16[16,2560]{1,0:T(8,128)(2,1)S(1)}, bf16[16,2560]{1,0:T(8,128)(2,1)S(1)}, u32[]{:S(2)}, u32[]{:S(2)}) collective-permute-start(bf16[16,2560]{1,0:T(8,128)(2,1)S(1)} %get-tuple-element.66), channel_id=1, source_target_pairs={{0,12},{1,13},{2,14},{3,15},{4,0},{5,1},{6,2},{7,3},{8,4},{9,5},{1... | collective-permute-start | bytes 245768 | tf_op jit(solution)/shard_map/ppermute | solution.py:39
  27.3 6.3 %collective-permute-start.9 = (bf16[16,2560]{1,0:T(8,128)(2,1)S(1)}, bf16[16,2560]{1,0:T(8,128)(2,1)S(1)}, u32[]{:S(2)}, u32[]{:S(2)}) collective-permute-start(bf16[16,2560]{1,0:T(8,128)(2,1)S(1)} %slice.90), channel_id=1, source_target_pairs={{0,4},{1,5},{2,6},{3,7},{4,8},{5,9},{6,10},{7,11},{8,12},{9,13},{1... | collective-permute-start | bytes 245768 | tf_op jit(solution)/shard_map/ppermute | solution.py:39
  27.8 12.4 %collective-permute-start.4 = (bf16[192,640]{1,0:T(8,128)(2,1)S(1)}, bf16[192,640]{1,0:T(8,128)(2,1)S(1)}, u32[]{:S(2)}, u32[]{:S(2)}) collective-permute-start(bf16[192,640]{1,0:T(8,128)(2,1)S(1)} %constant_dynamic-update-slice_fusion.refs_0_), channel_id=1, source_target_pairs={{0,2},{1,3},{2,0},{3,1},{4,6},{5,7},{6,4},{7,5},{8,10},{9,11},{10,... | collective-permute-start | bytes 737288 | tf_op jit(solution)/shard_map/ppermute | solution.py:39
  29.4 18.2 %collective-permute-start.5 = (bf16[192,640]{1,0:T(8,128)(2,1)S(1)}, bf16[192,640]{1,0:T(8,128)(2,1)S(1)}, u32[]{:S(2)}, u32[]{:S(2)}) collective-permute-start(bf16[192,640]{1,0:T(8,128)(2,1)S(1)} %constant_dynamic-update-slice_fusion.refs_0_), channel_id=1, source_target_pairs={{0,1},{1,0},{2,3},{3,2},{4,5},{5,4},{6,7},{7,6},{8,9},{9,8},{10,11... | collective-permute-start | bytes 737288 | tf_op jit(solution)/shard_map/ppermute | solution.py:39
  34.2 5.9 %collective-permute-start.13 = (bf16[48,512]{1,0:T(8,128)(2,1)S(1)}, bf16[48,512]{1,0:T(8,128)(2,1)S(1)}, u32[]{:S(2)}, u32[]{:S(2)}) collective-permute-start(bf16[48,512]{1,0:T(8,128)(2,1)S(1)} %get-tuple-element.41), channel_id=1, source_target_pairs={{0,4},{1,5},{2,6},{3,7},{4,8},{5,9},{6,10},{7,11},{8,12},{9,13},{1... | collective-permute-start | bytes 147464 | tf_op jit(solution)/shard_map/ppermute | solution.py:39
  34.3 5.9 %collective-permute-start.14 = (bf16[48,512]{1,0:T(8,128)(2,1)S(1)}, bf16[48,512]{1,0:T(8,128)(2,1)S(1)}, u32[]{:S(2)}, u32[]{:S(2)}) collective-permute-start(bf16[48,512]{1,0:T(8,128)(2,1)S(1)} %get-tuple-element.42), channel_id=1, source_target_pairs={{0,8},{1,9},{2,10},{3,11},{4,12},{5,13},{6,14},{7,15},{8,0},{9,1},... | collective-permute-start | bytes 147464 | tf_op jit(solution)/shard_map/ppermute | solution.py:39
  36.4 4.4 %collective-permute-start.15 = (bf16[48,512]{1,0:T(8,128)(2,1)S(1)}, bf16[48,512]{1,0:T(8,128)(2,1)S(1)}, u32[]{:S(2)}, u32[]{:S(2)}) collective-permute-start(bf16[48,512]{1,0:T(8,128)(2,1)S(1)} %get-tuple-element.43), channel_id=1, source_target_pairs={{0,12},{1,13},{2,14},{3,15},{4,0},{5,1},{6,2},{7,3},{8,4},{9,5},{1... | collective-permute-start | bytes 147464 | tf_op jit(solution)/shard_map/ppermute | solution.py:39
  40.2 7.5 %collective-permute-start.6 = (bf16[192,640]{1,0:T(8,128)(2,1)S(1)}, bf16[192,640]{1,0:T(8,128)(2,1)S(1)}, u32[]{:S(2)}, u32[]{:S(2)}) collective-permute-start(bf16[192,640]{1,0:T(8,128)(2,1)S(1)} %collective-permute-done.4.refs_1_), channel_id=1, source_target_pairs={{0,1},{1,0},{2,3},{3,2},{4,5},{5,4},{6,7},{7,6},{8,9},{9,8},{10,11... | collective-permute-start | bytes 737288 | tf_op jit(solution)/shard_map/ppermute | solution.py:39
  40.8 6.9 %collective-permute-start.22 = (bf16[192,512]{1,0:T(8,128)(2,1)S(1)}, bf16[192,512]{1,0:T(8,128)(2,1)S(1)}, u32[]{:S(2)}, u32[]{:S(2)}) collective-permute-start(bf16[192,512]{1,0:T(8,128)(2,1)S(1)} %constant_dynamic-update-slice_fusion.4.refs_7_.refs_0_), channel_id=1, source_target_pairs={{0,2},{1,3},{2,0},{3,1},{4,6},{5,7},{6,4},{7,5},{8,10},{9,11},{10,... | collective-permute-start | bytes 589832 | tf_op jit(solution)/shard_map/ppermute | solution.py:39
  42.7 18.9 %collective-permute-start.23 = (bf16[192,512]{1,0:T(8,128)(2,1)S(1)}, bf16[192,512]{1,0:T(8,128)(2,1)S(1)}, u32[]{:S(2)}, u32[]{:S(2)}) collective-permute-start(bf16[192,512]{1,0:T(8,128)(2,1)S(1)} %constant_dynamic-update-slice_fusion.4.refs_7_.refs_0_), channel_id=1, source_target_pairs={{0,1},{1,0},{2,3},{3,2},{4,5},{5,4},{6,7},{7,6},{8,9},{9,8},{10,11... | collective-permute-start | bytes 589832 | tf_op jit(solution)/shard_map/ppermute | solution.py:39
  47.7 13.9 %collective-permute-start.24 = (bf16[192,512]{1,0:T(8,128)(2,1)S(1)}, bf16[192,512]{1,0:T(8,128)(2,1)S(1)}, u32[]{:S(2)}, u32[]{:S(2)}) collective-permute-start(bf16[192,512]{1,0:T(8,128)(2,1)S(1)} %collective-permute-done.22.refs_1_), channel_id=1, source_target_pairs={{0,1},{1,0},{2,3},{3,2},{4,5},{5,4},{6,7},{7,6},{8,9},{9,8},{10,11... | collective-permute-start | bytes 589832 | tf_op jit(solution)/shard_map/ppermute | solution.py:39
  60.9 13.4 %collective-permute-start.17 = (bf16[192,640]{1,0:T(8,128)(2,1)S(1)}, bf16[192,640]{1,0:T(8,128)(2,1)S(1)}, u32[]{:S(2)}, u32[]{:S(2)}) collective-permute-start(bf16[192,640]{1,0:T(8,128)(2,1)S(1)} %get-tuple-element.47), channel_id=1, source_target_pairs={{0,1},{1,0},{2,3},{3,2},{4,5},{5,4},{6,7},{7,6},{8,9},{9,8},{10,11... | collective-permute-start | bytes 737288 | tf_op jit(solution)/shard_map/ppermute | solution.py:39
  61.5 15.6 %collective-permute-start.16 = (bf16[192,640]{1,0:T(8,128)(2,1)S(1)}, bf16[192,640]{1,0:T(8,128)(2,1)S(1)}, u32[]{:S(2)}, u32[]{:S(2)}) collective-permute-start(bf16[192,640]{1,0:T(8,128)(2,1)S(1)} %get-tuple-element.45), channel_id=1, source_target_pairs={{0,1},{1,0},{2,3},{3,2},{4,5},{5,4},{6,7},{7,6},{8,9},{9,8},{10,11... | collective-permute-start | bytes 737288 | tf_op jit(solution)/shard_map/ppermute | solution.py:39
  73.8 2.2 %collective-permute-start.26 = (bf16[192,512]{1,0:T(8,128)(2,1)S(1)}, bf16[192,512]{1,0:T(8,128)(2,1)S(1)}, u32[]{:S(2)}, u32[]{:S(2)}) collective-permute-start(bf16[192,512]{1,0:T(8,128)(2,1)S(1)} %get-tuple-element.53), channel_id=1, source_target_pairs={{0,1},{1,0},{2,3},{3,2},{4,5},{5,4},{6,7},{7,6},{8,9},{9,8},{10,11... | collective-permute-start | bytes 589832 | tf_op jit(solution)/shard_map/ppermute | solution.py:39
  74.4 8.9 %collective-permute-start.18 = (bf16[192,640]{1,0:T(8,128)(2,1)S(1)}, bf16[192,640]{1,0:T(8,128)(2,1)S(1)}, u32[]{:S(2)}, u32[]{:S(2)}) collective-permute-start(bf16[192,640]{1,0:T(8,128)(2,1)S(1)} %add_convert_fusion.2), channel_id=1, source_target_pairs={{0,2},{1,3},{2,0},{3,1},{4,6},{5,7},{6,4},{7,5},{8,10},{9,11},{10,... | collective-permute-start | bytes 737288 | tf_op jit(solution)/shard_map/ppermute | solution.py:39
  76.0 11.1 %collective-permute-start.25 = (bf16[192,512]{1,0:T(8,128)(2,1)S(1)}, bf16[192,512]{1,0:T(8,128)(2,1)S(1)}, u32[]{:S(2)}, u32[]{:S(2)}) collective-permute-start(bf16[192,512]{1,0:T(8,128)(2,1)S(1)} %get-tuple-element.51), channel_id=1, source_target_pairs={{0,1},{1,0},{2,3},{3,2},{4,5},{5,4},{6,7},{7,6},{8,9},{9,8},{10,11... | collective-permute-start | bytes 589832 | tf_op jit(solution)/shard_map/ppermute | solution.py:39
  76.1 11.1 %collective-permute-start.27 = (bf16[192,512]{1,0:T(8,128)(2,1)S(1)}, bf16[192,512]{1,0:T(8,128)(2,1)S(1)}, u32[]{:S(2)}, u32[]{:S(2)}) collective-permute-start(bf16[192,512]{1,0:T(8,128)(2,1)S(1)} %add_convert_fusion.4), channel_id=1, source_target_pairs={{0,2},{1,3},{2,0},{3,1},{4,6},{5,7},{6,4},{7,5},{8,10},{9,11},{10,... | collective-permute-start | bytes 589832 | tf_op jit(solution)/shard_map/ppermute | solution.py:39
  83.4 8.2 %collective-permute-start.19 = (bf16[48,640]{1,0:T(8,128)(2,1)S(1)}, bf16[48,640]{1,0:T(8,128)(2,1)S(1)}, u32[]{:S(2)}, u32[]{:S(2)}) collective-permute-start(bf16[48,640]{1,0:T(8,128)(2,1)S(1)} %get-tuple-element.60), channel_id=1, source_target_pairs={{0,12},{1,13},{2,14},{3,15},{4,0},{5,1},{6,2},{7,3},{8,4},{9,5},{1... | collective-permute-start | bytes 184328 | tf_op jit(solution)/shard_map/ppermute | solution.py:39
  86.5 6.3 %collective-permute-start.20 = (bf16[48,640]{1,0:T(8,128)(2,1)S(1)}, bf16[48,640]{1,0:T(8,128)(2,1)S(1)}, u32[]{:S(2)}, u32[]{:S(2)}) collective-permute-start(bf16[48,640]{1,0:T(8,128)(2,1)S(1)} %get-tuple-element.59), channel_id=1, source_target_pairs={{0,8},{1,9},{2,10},{3,11},{4,12},{5,13},{6,14},{7,15},{8,0},{9,1},... | collective-permute-start | bytes 184328 | tf_op jit(solution)/shard_map/ppermute | solution.py:39
  86.5 6.3 %collective-permute-start.21 = (bf16[48,640]{1,0:T(8,128)(2,1)S(1)}, bf16[48,640]{1,0:T(8,128)(2,1)S(1)}, u32[]{:S(2)}, u32[]{:S(2)}) collective-permute-start(bf16[48,640]{1,0:T(8,128)(2,1)S(1)} %get-tuple-element.58), channel_id=1, source_target_pairs={{0,4},{1,5},{2,6},{3,7},{4,8},{5,9},{6,10},{7,11},{8,12},{9,13},{1... | collective-permute-start | bytes 184328 | tf_op jit(solution)/shard_map/ppermute | solution.py:39
  87.2 7.0 %collective-permute-start.28 = (bf16[48,512]{1,0:T(8,128)(2,1)S(1)}, bf16[48,512]{1,0:T(8,128)(2,1)S(1)}, u32[]{:S(2)}, u32[]{:S(2)}) collective-permute-start(bf16[48,512]{1,0:T(8,128)(2,1)S(1)} %get-tuple-element.64), channel_id=1, source_target_pairs={{0,12},{1,13},{2,14},{3,15},{4,0},{5,1},{6,2},{7,3},{8,4},{9,5},{1... | collective-permute-start | bytes 147464 | tf_op jit(solution)/shard_map/ppermute | solution.py:39
  90.5 5.0 %collective-permute-start.29 = (bf16[48,512]{1,0:T(8,128)(2,1)S(1)}, bf16[48,512]{1,0:T(8,128)(2,1)S(1)}, u32[]{:S(2)}, u32[]{:S(2)}) collective-permute-start(bf16[48,512]{1,0:T(8,128)(2,1)S(1)} %get-tuple-element.63), channel_id=1, source_target_pairs={{0,8},{1,9},{2,10},{3,11},{4,12},{5,13},{6,14},{7,15},{8,0},{9,1},... | collective-permute-start | bytes 147464 | tf_op jit(solution)/shard_map/ppermute | solution.py:39
  91.6 5.9 %collective-permute-start.30 = (bf16[48,512]{1,0:T(8,128)(2,1)S(1)}, bf16[48,512]{1,0:T(8,128)(2,1)S(1)}, u32[]{:S(2)}, u32[]{:S(2)}) collective-permute-start(bf16[48,512]{1,0:T(8,128)(2,1)S(1)} %get-tuple-element.62), channel_id=1, source_target_pairs={{0,4},{1,5},{2,6},{3,7},{4,8},{5,9},{6,10},{7,11},{8,12},{9,13},{1... | collective-permute-start | bytes 147464 | tf_op jit(solution)/shard_map/ppermute | solution.py:39

commit v6 on v5

v6 whole, which is shorter than its diff:
```python
import functools

import jax
import jax.numpy as jnp
from jax import lax
from jax.experimental import pallas as pl
from jax.experimental.pallas import tpu as pltpu
from jax.sharding import PartitionSpec as P

PLEN = 128
VMEM = pl.BlockSpec(memory_space=pltpu.VMEM)
SMEM = pl.BlockSpec(memory_space=pltpu.SMEM)
ANY = pl.BlockSpec(memory_space=pl.ANY)


class Grid:
    def __init__(self, devices, experts):
        self.experts = experts
        self.pairs = devices // experts // 2
        index = lax.axis_index("dev")
        self.expert = index // (self.pairs * 2)
        self.pair = (index // 2) % self.pairs
        self.core = index % 2

    def send(self, value, axis, step):
        moves = []
        for expert in range(self.experts):
            for pair in range(self.pairs):
                for core in range(2):
                    to = [expert, pair, core]
                    to[axis] = (to[axis] + step) % (self.experts, self.pairs, 2)[axis]
                    moves.append(
                        (
                            (expert * self.pairs + pair) * 2 + core,
                            (to[0] * self.pairs + to[1]) * 2 + to[2],
                        )
                    )
        return lax.ppermute(value, "dev", moves)


class Packing:
    def __init__(self, cap, features):
        best = None
        for chunks in range(1, features // 128 + 1):
            if features % (128 * chunks):
                continue
            rows = -(-cap * chunks // 16) * 16
            cost = rows * (features // chunks)
            if best is None or cost < best[0]:
                best = (cost, chunks, rows)
        _, self.chunks, self.rows = best
        self.cap = cap
        self.width = features // self.chunks


def live(position, lengths_ref):
    prompt = position // PLEN
    length = jnp.zeros_like(position)
    for p in range(lengths_ref.shape[0]):
        length = jnp.where(prompt == p, lengths_ref[p], length)
    return position % PLEN < length


def place_kernel(packings, experts, after, lengths_ref, *refs):
    index = lax.axis_index("dev")
    shift = experts - index // (lax.axis_size("dev") // experts)
    for i, packing in enumerate(packings):
        chosen, out_ref = refs[i][...], refs[len(refs) - len(packings) + i]
        rows = chosen.shape[1]
        relative = lax.rem(chosen + shift, experts)
        expert_at = lax.broadcasted_iota(jnp.int32, (experts, rows), 0)
        routed = (relative[0:1, :] == expert_at) | (relative[1:2, :] == expert_at)
        if i == 1:
            position = index * rows + lax.broadcasted_iota(jnp.int32, (experts, rows), 1)
            routed = routed & live(position, lengths_ref)
        at = [lax.broadcasted_iota(jnp.int32, (rows, rows), d) for d in range(2)]
        before = (at[0] < at[1]).astype(jnp.float32)
        spot = jnp.dot(routed.astype(jnp.float32), before, preferred_element_type=jnp.float32)
        spot = spot + expert_at.astype(jnp.float32) * float(packing.rows)
        spot = jnp.where(routed, spot, -65536.0)
        for t in range(2):
            own = jnp.where(relative[t : t + 1, :] == expert_at, spot, 0.0)
            own = jnp.sum(own, axis=0, keepdims=True)
            for column, value in ((t, own), (2 + t, chosen[t : t + 1, :].astype(jnp.float32))):
                out_ref[:, column : column + 1] = jnp.sum(
                    jnp.where(at[0] == at[1], value, 0.0), axis=1, keepdims=True
                )


def place(chosen, lengths, experts, packings, after):
    return pl.pallas_call(
        functools.partial(place_kernel, packings, experts, len(after)),
        out_shape=[jax.ShapeDtypeStruct((ids.shape[0], 4), jnp.float32) for ids in chosen],
        in_specs=[SMEM] + [VMEM] * len(chosen) + [ANY] * len(after),
        out_specs=[VMEM] * len(chosen),
        compiler_params=pltpu.CompilerParams(vmem_limit_bytes=8 << 20),
        name="place",
    )(lengths, *[ids.T for ids in chosen], *after)


def tie(value, after):
    return pl.pallas_call(
        lambda *refs: None,
        out_shape=jax.ShapeDtypeStruct(value.shape, value.dtype),
        in_specs=[ANY] * (1 + len(after)),
        out_specs=ANY,
        input_output_aliases={0: 0},
        cost_estimate=pl.CostEstimate(flops=0, bytes_accessed=0, transcendentals=0),
        name="tie",
    )(value, *after)


def modulate_kernel(packing, experts, count, spot_ref, scale_ref, shift_ref, *refs):
    normed_ref, packed_refs = refs[-1 - experts], refs[-experts:]
    rows = normed_ref.shape[0]
    values = refs[0][...].astype(jnp.float32)
    for ref in refs[1:count]:
        values = values + ref[...].astype(jnp.float32)
    values = values.astype(jnp.bfloat16).astype(jnp.float32)
    center = values - jnp.mean(values, axis=1, keepdims=True)
    spread = jnp.mean(center * center, axis=1, keepdims=True)
    normed = center * lax.rsqrt(spread + 1e-06) * scale_ref[...][None, :] + shift_ref[...][None, :]
    normed = normed.astype(jnp.bfloat16)
    normed_ref[...] = normed

    place = lax.broadcasted_iota(jnp.int32, (rows, experts * packing.rows), 1).astype(jnp.float32)
    packed = None
    for j in range(packing.chunks):
        at = place - float(j * packing.cap)
        into = jnp.where((at == spot_ref[:, 0:1]) | (at == spot_ref[:, 1:2]), 1.0, 0.0)
        into = into.T.astype(jnp.bfloat16)
        term = jnp.dot(
            into,
            normed[:, j * packing.width : (j + 1) * packing.width],
            preferred_element_type=jnp.float32,
        )
        packed = term if packed is None else packed + term
    for k in range(experts):
        packed_refs[k][...] = packed[k * packing.rows : (k + 1) * packing.rows].astype(
            jnp.bfloat16
        )
def modulate(terms, spot, mod_scale, mod_shift, packing, experts, after):
    rows, features = terms[0].shape
    packed = jax.ShapeDtypeStruct((packing.rows, packing.width), jnp.bfloat16)
    results = pl.pallas_call(
        functools.partial(modulate_kernel, packing, experts, len(terms)),
        out_shape=[jax.ShapeDtypeStruct((rows, features), jnp.bfloat16)] + [packed] * experts,
        in_specs=[VMEM] * (3 + len(terms)) + [ANY] * len(after),
        out_specs=[VMEM] * (1 + experts),
        compiler_params=pltpu.CompilerParams(vmem_limit_bytes=8 << 20),
        name="modulate",
    )(spot, mod_scale, mod_shift, *terms, *after)
    return (results[0], list(results[1:]))


def route_kernel(spot_ref, normed_ref, router_ref, weight_ref):
    normed = normed_ref[...].astype(jnp.float32)
    logits = [
        jnp.sum(normed * router_ref[k : k + 1, :], axis=1, keepdims=True)
        for k in range(router_ref.shape[0])
    ]
    picked = []
    for t in range(2):
        logit = jnp.zeros_like(logits[0])
        for k, value in enumerate(logits):
            logit = jnp.where(spot_ref[:, 2 + t : 3 + t] == float(k), value, logit)
        picked.append(logit)
    weight_ref[:, 0:1] = jax.nn.sigmoid(picked[0] - picked[1])
    weight_ref[:, 1:2] = jax.nn.sigmoid(picked[1] - picked[0])


def route(normed, spot, router_weight):
    return pl.pallas_call(
        route_kernel,
        out_shape=jax.ShapeDtypeStruct((spot.shape[0], 2), jnp.float32),
        in_specs=[VMEM] * 3,
        out_specs=VMEM,
        compiler_params=pltpu.CompilerParams(vmem_limit_bytes=8 << 20),
        name="route",
    )(spot, normed, router_weight.T)


def cuts(units):
    edges = [0, units] if units <= 1024 else [0, 384, 1024, units]
    return list(zip(edges[:-1], edges[1:]))


def expert_kernel(packing, count, after, *refs):
    row_refs = refs[:count]
    gate_hbm, up_hbm, down_hbm = refs[count : count + 3]
    out_refs = refs[count + 3 + after : 2 * count + 3 + after]
    gate_ref, up_ref, down_ref, rows_ref, total_ref, packed_ref, sems = refs[2 * count + 3 + after :]
    rows = total_ref.shape[1]
    units = gate_hbm.shape[0]
    unit_cuts = cuts(units)
    copies = []
    for i, (lo, hi) in enumerate(unit_cuts):
        for t, (source, target) in enumerate(
            ((gate_hbm, gate_ref), (up_hbm, up_ref), (down_hbm, down_ref))
        ):
            copies.append(
                pltpu.make_async_copy(source.at[lo:hi], target.at[lo:hi], sems.at[3 * i + t])
            )
    for copy in copies:
        copy.start()

    cap, chunks, width, high = packing.cap, packing.chunks, packing.width, packing.rows
    per_ref = row_refs[0].shape[0] // high
    blocks = count * per_ref
    lanes = width // 128
    for i, ref in enumerate(row_refs):
        for c in range(lanes):
            packed_ref[c, i * per_ref * high : (i + 1) * per_ref * high, :] = ref[
                :, c * 128 : (c + 1) * 128
            ].astype(jnp.float32)
    spare = rows_ref.shape[1] - rows
    for j in range(chunks):
        for c in range(lanes):
            for slot in range(cap):
                total_ref[j * lanes + c, pl.ds(slot, blocks, stride=cap), :] = packed_ref[
                    c, pl.ds(j * cap + slot, blocks, stride=high), :
                ]
    for c in range(chunks * lanes):
        part = total_ref[c]
        if spare:
            part = jnp.concatenate([part, jnp.zeros((spare, 128), jnp.float32)], axis=0)
        rows_ref[c * 128 : (c + 1) * 128, :] = part.T.astype(jnp.bfloat16)

    def down(i, hidden):
        lo, hi = unit_cuts[i]
        term = jnp.dot(hidden, down_ref[lo:hi, :], preferred_element_type=jnp.float32)
        for c in range(chunks * lanes):
            if i == 0:
                total_ref[c] = term[:, c * 128 : (c + 1) * 128]
            else:
                total_ref[c] += term[:, c * 128 : (c + 1) * 128]

    features = gate_hbm.shape[1]
    middle = features // 256 * 128

    def product(weight_ref, lo, hi):
        return jnp.dot(
            weight_ref[lo:hi, :middle], rows_ref[:middle, :], preferred_element_type=jnp.float32
        ) + jnp.dot(
            weight_ref[lo:hi, middle:], rows_ref[middle:, :], preferred_element_type=jnp.float32
        )

    hidden = None
    for i, (lo, hi) in enumerate(unit_cuts):
        if i > 0:
            copies[3 * i - 1].wait()
        copies[3 * i].wait()
        copies[3 * i + 1].wait()
        gate = product(gate_ref, lo, hi)
        up = product(up_ref, lo, hi)
        if i > 0:
            down(i - 1, hidden)
        hidden = (gate * jax.nn.sigmoid(gate) * up).T[0:rows].astype(jnp.bfloat16)
    copies[-1].wait()
    down(len(unit_cuts) - 1, hidden)

    for c in range(lanes):
        for row in range(chunks * cap, high):
            packed_ref[c, pl.ds(row, blocks, stride=high), :] = jnp.zeros(
                (blocks, 128), jnp.float32
            )
        for j in range(chunks):
            for slot in range(cap):
                packed_ref[c, pl.ds(j * cap + slot, blocks, stride=high), :] = total_ref[
                    j * lanes + c, pl.ds(slot, blocks, stride=cap), :
                ]
    for i, ref in enumerate(out_refs):
        for c in range(lanes):
            ref[:, c * 128 : (c + 1) * 128] = packed_ref[
                c, i * per_ref * high : (i + 1) * per_ref * high, :
            ].astype(jnp.bfloat16)


def expert_rows(arrays, w_gate, w_up, w_down, packing, after):
    features, units = w_gate.shape
    rows = len(arrays) * (arrays[0].shape[0] // packing.rows) * packing.cap
    return pl.pallas_call(
        functools.partial(expert_kernel, packing, len(arrays), len(after)),
        out_shape=[jax.ShapeDtypeStruct(arrays[0].shape, jnp.bfloat16)] * len(arrays),
        in_specs=[VMEM] * len(arrays) + [ANY] * (3 + len(after)),
        out_specs=[VMEM] * len(arrays),
        scratch_shapes=[
            pltpu.VMEM((units, features), jnp.bfloat16),
            pltpu.VMEM((units, features), jnp.bfloat16),
            pltpu.VMEM((units, features), jnp.bfloat16),
            pltpu.VMEM((features, -(-rows // 128) * 128), jnp.bfloat16),
            pltpu.VMEM((features // 128, rows, 128), jnp.float32),
            pltpu.VMEM((packing.width // 128, len(arrays) * arrays[0].shape[0], 128), jnp.float32),
            pltpu.SemaphoreType.DMA((3 * len(cuts(units)),)),
        ],
        compiler_params=pltpu.CompilerParams(vmem_limit_bytes=48 << 20),
        cost_estimate=pl.CostEstimate(
            flops=6 * rows * features * units,
            bytes_accessed=6 * features * units,
            transcendentals=rows * units,
        ),
        name="experts",
    )(*arrays, w_gate.T, w_up.T, w_down, *after)


def combine_kernel(packing, spot_ref, weight_ref, *refs):
    block_refs, out_ref = refs[:-1], refs[-1]
    rows = out_ref.shape[0]
    blocks = jnp.concatenate([ref[...] for ref in block_refs], axis=0)
    place = lax.broadcasted_iota(jnp.int32, (rows, blocks.shape[0]), 1).astype(jnp.float32)
    picks = [
        jnp.where(place - float(j * packing.cap) == spot_ref[:, t : t + 1], 1.0, 0.0)
        for t in range(2)
        for j in range(packing.chunks)
    ]
    if rows % 16 == 0:
        table = jnp.concatenate(picks, axis=0).astype(jnp.bfloat16)
        picked = jnp.dot(table, blocks, preferred_element_type=jnp.float32)
        picked = [picked[i * rows : (i + 1) * rows] for i in range(len(picks))]
    else:
        picked = [
            jnp.dot(pick.astype(jnp.bfloat16), blocks, preferred_element_type=jnp.float32)
            for pick in picks
        ]
    for j in range(packing.chunks):
        out_ref[:, j * packing.width : (j + 1) * packing.width] = (
            weight_ref[:, 0:1] * picked[j] + weight_ref[:, 1:2] * picked[packing.chunks + j]
        ).astype(jnp.bfloat16)


def combine(spot, weights, blocks, packing, rows, features):
    return pl.pallas_call(
        functools.partial(combine_kernel, packing),
        out_shape=jax.ShapeDtypeStruct((rows, features), jnp.bfloat16),
        in_specs=[VMEM] * (2 + len(blocks)),
        out_specs=VMEM,
        compiler_params=pltpu.CompilerParams(vmem_limit_bytes=8 << 20),
        name="combine",
    )(spot, weights, *blocks)


def project_kernel(experts, pairs, text_hbm, weight_hbm, *refs):
    out_refs, (text_ref, weight_ref, sems) = refs[:-3], refs[-3:]
    copies = [
        pltpu.make_async_copy(text_hbm, text_ref, sems.at[0]),
        pltpu.make_async_copy(weight_hbm, weight_ref, sems.at[1]),
    ]
    for copy in copies:
        copy.start()
    rows = text_ref.shape[0] // (experts * pairs * 2)
    index = lax.axis_index("dev")
    expert, pair, core = index // (pairs * 2), lax.rem(index // 2, pairs), lax.rem(index, 2)
    copies[0].wait()
    picked = []
    for c in (1, 0):
        for p in list(range(1, pairs)) + [0]:
            for e in range(experts):
                owner = lax.rem(expert + e, experts) * pairs + lax.rem(pair + p, pairs)
                start = (owner * 2 + lax.rem(core + c, 2)) * rows
                picked.append(text_ref[pl.ds(pl.multiple_of(start, rows), rows), :])
    picked = jnp.concatenate(picked, axis=0)
    copies[1].wait()
    out = jnp.dot(picked, weight_ref[...], preferred_element_type=jnp.float32)
    high = rows * experts
    for i, ref in enumerate(out_refs):
        ref[...] = out[i * high : (i + 1) * high].astype(ref.dtype)


def partial_captions(text_hidden, caption_weight, grid):
    groups = grid.pairs * 2
    rows = text_hidden.shape[0] // (grid.experts * groups)
    depth, features = caption_weight.shape
    kinds = [jnp.bfloat16] * grid.pairs + [jnp.float32] * grid.pairs
    if rows % 16 == 0:
        return pl.pallas_call(
            functools.partial(project_kernel, grid.experts, grid.pairs),
            out_shape=[
                jax.ShapeDtypeStruct((rows * grid.experts, features), kind) for kind in kinds
            ],
            in_specs=[ANY] * 2,
            out_specs=[VMEM] * len(kinds),
            scratch_shapes=[
                pltpu.VMEM(text_hidden.shape, text_hidden.dtype),
                pltpu.VMEM(caption_weight.shape, caption_weight.dtype),
                pltpu.SemaphoreType.DMA((2,)),
            ],
            compiler_params=pltpu.CompilerParams(vmem_limit_bytes=16 << 20),
            name="project",
        )(text_hidden, caption_weight)
    text = text_hidden.reshape(grid.experts, grid.pairs, 2, rows, depth)
    text = jnp.roll(text, -grid.expert, axis=0)
    text = jnp.roll(text, -1 - grid.pair, axis=1)
    text = jnp.roll(text, -1 - grid.core, axis=2)
    text = jnp.transpose(text, (2, 1, 0, 3, 4)).reshape(groups, -1, depth)
    return [
        jnp.dot(text[i], caption_weight, preferred_element_type=jnp.float32).astype(kind)
        for i, kind in enumerate(kinds)
    ]


def local(
    image_rows,
    text_hidden,
    caption_weight,
    mod_scale,
    mod_shift,
    router_weight,
    image_experts,
    caption_experts,
    prompt_lengths,
    w_gate,
    w_up,
    w_down,
):
    devices = lax.axis_size("dev")
    features, experts = router_weight.shape
    grid = Grid(devices, experts)
    pairs = grid.pairs
    wide, narrow = jnp.float32, jnp.bfloat16
    image_packing = Packing(image_rows.shape[0] * 3 // 4, features)
    caption_packing = Packing(text_hidden.shape[0] // devices // 2 + 1, features)

    def split(value, count):
        rows = value.shape[0] // count
        return [value[k * rows : (k + 1) * rows] for k in range(count)]

    def to_experts(blocks):
        return [grid.send(blocks[k], 0, k) for k in range(1, experts)]

    def to_pairs(first):
        return [first] + [grid.send(first, 1, k) for k in range(1, pairs)]

    def over_cores(values):
        return [grid.send(value, 2, 1) for value in values]

    def join_cores(results):
        own, other = results[:pairs], results[pairs:]
        sums = [None] * pairs
        for k in list(range(1, pairs)) + [0]:
            sums[k] = own[k].astype(wide) + grid.send(other[k], 2, 1).astype(wide)
        return sums[0], [value.astype(narrow) for value in sums[1:]]

    def from_pairs(crossing):
        return [grid.send(value, 1, -k) for k, value in enumerate(crossing, 1)]

    def from_experts(kept, received):
        total = kept
        for value in received:
            total = total + value.astype(wide)
        parts = split(total.astype(narrow), experts)
        return [parts[0]] + [grid.send(parts[k], 0, -k) for k in range(1, experts)]

    partial = partial_captions(text_hidden, caption_weight, grid)
    sums = [
        partial[pairs + i] + grid.send(partial[i], 2, 1).astype(wide) for i in range(pairs)
    ]
    crossing = [value.astype(narrow) for value in sums[:-1]]
    total = sums[-1]
    for k in range(1, pairs):
        total = total + grid.send(crossing[k - 1], 1, k).astype(wide)

    image_spot, caption_spot = place(
        [image_experts, caption_experts],
        prompt_lengths,
        experts,
        [image_packing, caption_packing],
        crossing[:1],
    )
    image_normed, blocks = modulate(
        [image_rows], image_spot, mod_scale, mod_shift, image_packing, experts, crossing[:1]
    )
    image_first = [blocks[0]] + to_experts(blocks)

    parts = split(total, experts)
    sent = [part.astype(narrow) for part in parts]
    terms = [parts[0]] + to_experts(sent)

    image_first = jnp.concatenate([tie(image_first[0], sent[1:])] + image_first[1:], axis=0)
    image_own = to_pairs(image_first)
    image_arrays = image_own + over_cores(image_own)

    caption_normed, blocks = modulate(
        terms, caption_spot, mod_scale, mod_shift, caption_packing, experts, []
    )
    caption_first = jnp.concatenate([blocks[0]] + to_experts(blocks), axis=0)
    caption_own = to_pairs(caption_first)

    image_weights = route(image_normed, image_spot, router_weight)
    caption_weights = route(caption_normed, caption_spot, router_weight)
    image_results = expert_rows(
        image_arrays, w_gate, w_up, w_down, image_packing, [caption_first, image_weights]
    )
    caption_own = caption_own[:1] + [tie(value, image_results[:1]) for value in caption_own[1:]]
    image_results = list(image_results[:pairs]) + [
        tie(value, caption_own[1:2]) for value in image_results[pairs:]
    ]
    image_kept, image_crossing = join_cores(image_results)
    caption_results = expert_rows(
        caption_own + over_cores(caption_own),
        w_gate,
        w_up,
        w_down,
        caption_packing,
        image_crossing[:1] + [caption_weights],
    )
    image_received = [
        tie(value, caption_results[:1]) for value in from_pairs(image_crossing)
    ]
    caption_results = list(caption_results[:pairs]) + [
        tie(value, image_received[:1]) for value in caption_results[pairs:]
    ]
    caption_kept, caption_crossing = join_cores(caption_results)
    image_received = [tie(value, caption_crossing[:1]) for value in image_received]
    caption_received = from_pairs(caption_crossing)
    image_blocks = from_experts(image_kept, image_received)
    caption_blocks = from_experts(caption_kept, caption_received)

    rows = image_rows.shape[0]
    image_out = combine(image_spot, image_weights, image_blocks, image_packing, rows, features)
    rows = text_hidden.shape[0] // devices
    caption_out = combine(
        caption_spot, caption_weights, caption_blocks, caption_packing, rows, features
    )
    return (image_out, caption_out)


def solution(mesh):
    in_specs = (
        P(("groups", "dev"), None),
        P("groups", "dev"),
        P("dev", None),
        P(),
        P(),
        P(),
        P(("groups", "dev"), None),
        P(("groups", "dev"), None),
        P("groups"),
        P(None, "dev"),
        P(None, "dev"),
        P("dev", None),
    )
    out_specs = (P(("groups", "dev"), None), P(("groups", "dev"), None))
    return jax.shard_map(local, mesh=mesh, in_specs=in_specs, out_specs=out_specs, check_vma=False)
```

time: 98.7 us -> 101 us (1.023)
  local copies, waits for them, and re-layouts: 8.22 us -> 16.5 us
  waiting for transfers between devices: 25.4 us -> 20.2 us
  other arithmetic: 0.49 us -> 3.85 us
  starting transfers between devices: 31.8 us -> 28.7 us
  Pallas kernels: 31.5 us -> 30 us
    unnamed x22 -> x49, local copies, waits for them, and re-layouts: 6.68 us -> 15.7 us
    ppermute x31 -> x30, waiting for transfers between devices: 25.4 us -> 20.2 us  [send(): return lax.ppermute(value, 'dev', moves)]
    ppermute x31 -> x30, starting transfers between devices: 31.8 us -> 28.7 us  [send(): return lax.ppermute(value, 'dev', moves)]
    convert_element_type x4 -> x5, other arithmetic: 0.29 us -> 2.9 us  [the longest x2 2.05 us: from_experts(): parts = split(total.astype(narrow), experts)]
    reshape x2 -> x0, local copies, waits for them, and re-layouts: 1.43 us -> none  [the longest x1 0.71 us: modulate(): mod_scale.reshape(1, -1)]
    pallas_call x4 -> x11, Pallas kernels: 2.06 us -> 1.3 us  [the longest x1 0.76 us: place(): pl.pallas_call(functools.partial(place_kernel, packings, experts, len(aft...]
  transfers between devices with their start and end apart: 31 -> 30, of which waited for: 13 -> 15; matrix products, arithmetic and copies ran while one was open for 4% -> 4% of each run, Pallas kernels for 30% -> 28%
where the time goes in v6:
time: 101 us; the launch traced here: 100 us
  Pallas kernels  30 us (30%)
  starting transfers between devices  28.7 us (28%)
  waiting for transfers between devices  20.2 us (20%)
  local copies, waits for them, and re-layouts  16.5 us (16%)
  other arithmetic  3.85 us (4%)
    ppermute x30, starting transfers between devices, send(): return lax.ppermute(value, 'dev', moves)  28.7 us
    pallas_call x2, Pallas kernels, expert_rows(): pl.pallas_call(functools.partial(expert_kernel, packing, len(arrays), len...  24.9 us
    ppermute x30, waiting for transfers between devices, send(): return lax.ppermute(value, 'dev', moves)  20.2 us
    unnamed x49, local copies, waits for them, and re-layouts  15.7 us
    convert_element_type x2, other arithmetic, from_experts(): parts = split(total.astype(narrow), experts)  2.05 us
  transfers between devices with their start and end apart: 30, of which 15 were waited for; matrix products, arithmetic and copies ran while one was open for 4% of the time, Pallas kernels for 28%

profile of v6, /device:TPU:0, one launch (start us, length us, event | category | flops | bytes accessed | tf_op | source)
XLA Modules:
  0.0 100.0 jit_solution(16297477607931377050)
XLA Ops:
  0.6 1.3 %copy-done.2 = bf16[256,2560]{1,0:T(8,128)(2,1)S(1)} copy-done((bf16[256,2560]{1,0:T(8,128)(2,1)S(1)}, bf16[256,2560]{1,0:T(8,128)(2,1)}, u32[]{:S(2)}) %copy-start.2) | copy-done | bytes 1310744
  1.9 0.9 copy-done.13
  2.9 0.8 project.1
  3.7 0.5 collective-permute-start
  4.3 1.2 %collective-permute-done = bf16[64,2560]{1,0:T(8,128)(2,1)S(1)} collective-permute-done((bf16[64,2560]{1,0:T(8,128)(2,1)S(1)}, bf16[64,2560]{1,0:T(8,128)(2,1)S(1)}, u32[]{:S(2)}, u32[]{:S(2)}) %collective-permute-start) | collective-permute-done | bytes 327712 | tf_op jit(solution)/shard_map/ppermute | solution.py:38
  5.5 3.0 %collective-permute-start.2 = (bf16[64,2560]{1,0:T(8,128)(2,1)S(1)}, bf16[64,2560]{1,0:T(8,128)(2,1)S(1)}, u32[]{:S(2)}, u32[]{:S(2)}) collective-permute-start(bf16[64,2560]{1,0:T(8,128)(2,1)S(1)} %add_convert_fusion.refs_2_.refs_1_), channel_id=1, source_target_pairs={{0,2},{1,3},{2,0},{3,1},{4,6},{5,7},{6,4},{7,5},{8,10},{9,11},{10,... | collective-permute-start | bytes 983048 | tf_op jit(solution)/shard_map/ppermute | solution.py:38
  8.4 0.7 copy-done.19
  9.1 0.7 copy-done.20
  9.8 0.7 copy-done.21
  10.5 0.8 place.1
  11.2 0.9 copy-done.14
  12.1 0.7 copy-done.15
  12.8 0.7 copy-done.17
  13.5 0.6 modulate.2
  14.2 0.6 copy-done.6
  14.8 3.6 %collective-permute-start.5 = (bf16[48,640]{1,0:T(8,128)(2,1)S(1)}, bf16[48,640]{1,0:T(8,128)(2,1)S(1)}, u32[]{:S(2)}, u32[]{:S(2)}) collective-permute-start(bf16[48,640]{1,0:T(8,128)(2,1)S(1)} %get-tuple-element.35), channel_id=1, source_target_pairs={{0,12},{1,13},{2,14},{3,15},{4,0},{5,1},{6,2},{7,3},{8,4},{9,5},{1... | collective-permute-start | bytes 184328 | tf_op jit(solution)/shard_map/ppermute | solution.py:38
  18.4 1.0 %collective-permute-start.3 = (bf16[48,640]{1,0:T(8,128)(2,1)S(1)}, bf16[48,640]{1,0:T(8,128)(2,1)S(1)}, u32[]{:S(2)}, u32[]{:S(2)}) collective-permute-start(bf16[48,640]{1,0:T(8,128)(2,1)S(1)} %get-tuple-element.33), channel_id=1, source_target_pairs={{0,4},{1,5},{2,6},{3,7},{4,8},{5,9},{6,10},{7,11},{8,12},{9,13},{1... | collective-permute-start | bytes 184328 | tf_op jit(solution)/shard_map/ppermute | solution.py:38
  19.5 0.7 fusion.1
  20.2 0.6 collective-permute-done.5
  20.8 3.7 %collective-permute-done.4 = bf16[48,640]{1,0:T(8,128)(2,1)S(1)} collective-permute-done((bf16[48,640]{1,0:T(8,128)(2,1)S(1)}, bf16[48,640]{1,0:T(8,128)(2,1)S(1)}, u32[]{:S(2)}, u32[]{:S(2)}) %collective-permute-start.4) | collective-permute-done | bytes 61472 | tf_op jit(solution)/shard_map/ppermute | solution.py:38
  24.5 0.9 pad_maximum_fusion.refs_0_
  25.4 0.6 collective-permute-start.6
  26.2 2.3 %collective-permute-start.10 = (bf16[16,2560]{1,0:T(8,128)(2,1)}, bf16[16,2560]{1,0:T(8,128)(2,1)S(1)}, u32[]{:S(2)}, u32[]{:S(2)}) collective-permute-start(bf16[16,2560]{1,0:T(8,128)(2,1)} %get-tuple-element.53.refs_2_), channel_id=1, source_target_pairs={{0,8},{1,9},{2,10},{3,11},{4,12},{5,13},{6,14},{7,15},{8,0},{9,1},... | collective-permute-start | bytes 245768 | tf_op jit(solution)/shard_map/ppermute | solution.py:38
  28.5 2.2 %collective-permute-start.11 = (bf16[16,2560]{1,0:T(8,128)(2,1)}, bf16[16,2560]{1,0:T(8,128)(2,1)S(1)}, u32[]{:S(2)}, u32[]{:S(2)}) collective-permute-start(bf16[16,2560]{1,0:T(8,128)(2,1)} %get-tuple-element.52.refs_3_), channel_id=1, source_target_pairs={{0,12},{1,13},{2,14},{3,15},{4,0},{5,1},{6,2},{7,3},{8,4},{9,5},{1... | collective-permute-start | bytes 245768 | tf_op jit(solution)/shard_map/ppermute | solution.py:38
  30.7 0.8 copy-done.11
  31.8 1.3 %collective-permute-done.9.refs_1_ = bf16[16,2560]{1,0:T(8,128)(2,1)S(1)} collective-permute-done((bf16[16,2560]{1,0:T(8,128)(2,1)}, bf16[16,2560]{1,0:T(8,128)(2,1)S(1)}, u32[]{:S(2)}, u32[]{:S(2)}) %collective-permute-start.9) | collective-permute-done | bytes 81952 | tf_op jit(solution)/shard_map/ppermute | solution.py:38
  33.1 1.7 %collective-permute-done.10.refs_2_ = bf16[16,2560]{1,0:T(8,128)(2,1)S(1)} collective-permute-done((bf16[16,2560]{1,0:T(8,128)(2,1)}, bf16[16,2560]{1,0:T(8,128)(2,1)S(1)}, u32[]{:S(2)}, u32[]{:S(2)}) %collective-permute-start.10) | collective-permute-done | bytes 81952 | tf_op jit(solution)/shard_map/ppermute | solution.py:38
  34.8 0.7 copy-done.16
  35.5 0.7 copy-done.18
  36.2 0.6 modulate.3
  36.9 1.5 %collective-permute-start.12 = (bf16[48,512]{1,0:T(8,128)(2,1)S(1)}, bf16[48,512]{1,0:T(8,128)(2,1)S(1)}, u32[]{:S(2)}, u32[]{:S(2)}) collective-permute-start(bf16[48,512]{1,0:T(8,128)(2,1)S(1)} %get-tuple-element.38), channel_id=1, source_target_pairs={{0,4},{1,5},{2,6},{3,7},{4,8},{5,9},{6,10},{7,11},{8,12},{9,13},{1... | collective-permute-start | bytes 147464 | tf_op jit(solution)/shard_map/ppermute | solution.py:38
  38.4 2.1 %collective-permute-start.13 = (bf16[48,512]{1,0:T(8,128)(2,1)S(1)}, bf16[48,512]{1,0:T(8,128)(2,1)S(1)}, u32[]{:S(2)}, u32[]{:S(2)}) collective-permute-start(bf16[48,512]{1,0:T(8,128)(2,1)S(1)} %get-tuple-element.39), channel_id=1, source_target_pairs={{0,8},{1,9},{2,10},{3,11},{4,12},{5,13},{6,14},{7,15},{8,0},{9,1},... | collective-permute-start | bytes 147464 | tf_op jit(solution)/shard_map/ppermute | solution.py:38
  40.5 0.5 collective-permute-start.14
  41.0 1.8 %collective-permute-done.12 = bf16[48,512]{1,0:T(8,128)(2,1)S(1)} collective-permute-done((bf16[48,512]{1,0:T(8,128)(2,1)S(1)}, bf16[48,512]{1,0:T(8,128)(2,1)S(1)}, u32[]{:S(2)}, u32[]{:S(2)}) %collective-permute-start.12) | collective-permute-done | bytes 49184 | tf_op jit(solution)/shard_map/ppermute | solution.py:38
  42.8 1.0 %collective-permute-done.13 = bf16[48,512]{1,0:T(8,128)(2,1)S(1)} collective-permute-done((bf16[48,512]{1,0:T(8,128)(2,1)S(1)}, bf16[48,512]{1,0:T(8,128)(2,1)S(1)}, u32[]{:S(2)}, u32[]{:S(2)}) %collective-permute-start.13) | collective-permute-done | bytes 49184 | tf_op jit(solution)/shard_map/ppermute | solution.py:38
  43.9 0.7 collective-permute-done.14
  44.6 1.5 %collective-permute-start.15 = (bf16[192,512]{1,0:T(8,128)(2,1)S(1)}, bf16[192,512]{1,0:T(8,128)(2,1)S(1)}, u32[]{:S(2)}, u32[]{:S(2)}) collective-permute-start(bf16[192,512]{1,0:T(8,128)(2,1)S(1)} %constant_dynamic-update-slice_fusion.refs_7_.refs_0_), channel_id=1, source_target_pairs={{0,2},{1,3},{2,0},{3,1},{4,6},{5,7},{6,4},{7,5},{8,10},{9,11},{10,... | collective-permute-start | bytes 589832 | tf_op jit(solution)/shard_map/ppermute | solution.py:38
  46.1 12.8 %experts.2 = (bf16[192,640]{1,0:T(8,128)(2,1)S(1)}, bf16[192,640]{1,0:T(8,128)(2,1)S(1)}, bf16[192,640]{1,0:T(8,128)(2,1)S(1)}, bf16[192,640]{1,0:T(8,128)(2,1)S(1)}) custom-call(bf16[192,640]{1,0:T(8,128)(2,1)S(1)} %pad_maximum_fusion.refs_0_, bf16[192,640]{1,0:T(8,128)(2,1)S(1)} %collective-permute-done.6.refs_1_, ...), custom_call_target="tpu_custom_call" | custom-call | flops 5096079360 | bytes 26542080 | tf_op jit(solution)/shard_map/experts/pallas_call | solution.py:282
  58.9 0.7 copy-done.3
  59.6 0.7 copy-done.7
  60.3 0.7 copy-done.8
  61.0 0.7 copy-done
  62.0 0.5 collective-permute-start.19
  62.6 0.8 collective-permute-done.17
  63.5 0.6 collective-permute-start.18
  64.1 0.9 copy-done.1
  65.1 12.1 %experts.3 = (bf16[192,512]{1,0:T(8,128)(2,1)S(1)}, bf16[192,512]{1,0:T(8,128)(2,1)S(1)}, bf16[192,512]{1,0:T(8,128)(2,1)S(1)}, bf16[192,512]{1,0:T(8,128)(2,1)S(1)}) custom-call(bf16[192,512]{1,0:T(8,128)(2,1)S(1)} %constant_dynamic-update-slice_fusion.refs_7_.refs_0_, bf16[192,512]{1,0:T(8,128)(2,1)S(1)} %copy-done.1, ...), custom_call_target="tpu_custom_call" | custom-call | flops 3822059520 | bytes 26542080 | tf_op jit(solution)/shard_map/experts/pallas_call | solution.py:282
  77.2 0.7 copy-done.5
  77.8 0.7 copy-done.9
  78.5 0.7 copy-done.10
  79.2 0.7 copy-done.22
  80.7 0.9 collective-permute-done.21
  81.5 0.7 add_convert_fusion.4.refs_1_
  82.3 1.4 %collective-permute-start.26 = (bf16[192,512]{1,0:T(8,128)(2,1)}, bf16[192,512]{1,0:T(8,128)(2,1)S(1)}, u32[]{:S(2)}, u32[]{:S(2)}) collective-permute-start(bf16[192,512]{1,0:T(8,128)(2,1)} %add_convert_fusion.4.refs_1_), channel_id=1, source_target_pairs={{0,2},{1,3},{2,0},{3,1},{4,6},{5,7},{6,4},{7,5},{8,10},{9,11},{10,... | collective-permute-start | bytes 589832 | tf_op jit(solution)/shard_map/ppermute | solution.py:38
  83.7 1.1 %add_convert_fusion.1 = bf16[192,640]{1,0:T(8,128)(2,1)S(1)} fusion(bf16[192,640]{1,0:T(8,128)(2,1)} %tie.14, bf16[192,640]{1,0:T(8,128)(2,1)S(1)} %collective-permute-done.16, bf16[192,640]{1,0:T(8,128)(2,1)S(1)} %copy-done.4), kind=kLoop, calls=%fused_computation.2 | loop fusion | flops 737280 | bytes 983040 | tf_op jit(solution)/shard_map/convert_element_type | solution.py:450
  84.8 2.4 %collective-permute-start.22 = (bf16[48,640]{1,0:T(8,128)(2,1)S(1)}, bf16[48,640]{1,0:T(8,128)(2,1)S(1)}, u32[]{:S(2)}, u32[]{:S(2)}) collective-permute-start(bf16[48,640]{1,0:T(8,128)(2,1)S(1)} %get-tuple-element.57), channel_id=1, source_target_pairs={{0,12},{1,13},{2,14},{3,15},{4,0},{5,1},{6,2},{7,3},{8,4},{9,5},{1... | collective-permute-start | bytes 184328 | tf_op jit(solution)/shard_map/ppermute | solution.py:38
  87.2 0.7 collective-permute-start.24
  87.8 1.7 %collective-permute-done.26 = bf16[192,512]{1,0:T(8,128)(2,1)S(1)} collective-permute-done((bf16[192,512]{1,0:T(8,128)(2,1)}, bf16[192,512]{1,0:T(8,128)(2,1)S(1)}, u32[]{:S(2)}, u32[]{:S(2)}) %collective-permute-start.26) | collective-permute-done | bytes 196640 | tf_op jit(solution)/shard_map/ppermute | solution.py:38
  89.6 1.0 %add_convert_fusion.3 = bf16[192,512]{1,0:T(8,128)(2,1)S(1)} fusion(bf16[192,512]{1,0:T(8,128)(2,1)S(1)} %collective-permute-done.26, bf16[192,512]{1,0:T(8,128)(2,1)S(1)} %collective-permute-done.25, bf16[192,512]{1,0:T(8,128)(2,1)} %copy-done.5), kind=kLoop, calls=%fused_computation.4 | loop fusion | flops 589824 | bytes 786432 | tf_op jit(solution)/shard_map/convert_element_type | solution.py:450
  90.6 2.4 %collective-permute-start.27 = (bf16[48,512]{1,0:T(8,128)(2,1)S(1)}, bf16[48,512]{1,0:T(8,128)(2,1)S(1)}, u32[]{:S(2)}, u32[]{:S(2)}) collective-permute-start(bf16[48,512]{1,0:T(8,128)(2,1)S(1)} %get-tuple-element.61), channel_id=1, source_target_pairs={{0,12},{1,13},{2,14},{3,15},{4,0},{5,1},{6,2},{7,3},{8,4},{9,5},{1... | collective-permute-start | bytes 147464 | tf_op jit(solution)/shard_map/ppermute | solution.py:38
  93.9 0.9 combine.2
  94.8 3.4 %collective-permute-done.28.refs_2_ = bf16[48,512]{1,0:T(8,128)(2,1)S(1)} collective-permute-done((bf16[48,512]{1,0:T(8,128)(2,1)S(1)}, bf16[48,512]{1,0:T(8,128)(2,1)S(1)}, u32[]{:S(2)}, u32[]{:S(2)}) %collective-permute-start.28) | collective-permute-done | bytes 49184 | tf_op jit(solution)/shard_map/ppermute | solution.py:38
  98.1 1.0 collective-permute-done.29.refs_3_
  99.1 0.9 combine.3
  (75 shorter events, 3.1 us)
Async XLA Ops:
  0.6 1.3 %copy-start.2 = (bf16[256,2560]{1,0:T(8,128)(2,1)S(1)}, bf16[256,2560]{1,0:T(8,128)(2,1)}, u32[]{:S(2)}) copy-start(bf16[256,2560]{1,0:T(8,128)(2,1)} %weight_hbm.1) | copy-start | bytes 3932164
  1.9 0.9 copy-start.13
  3.7 1.8 %collective-permute-start = (bf16[64,2560]{1,0:T(8,128)(2,1)S(1)}, bf16[64,2560]{1,0:T(8,128)(2,1)S(1)}, u32[]{:S(2)}, u32[]{:S(2)}) collective-permute-start(bf16[64,2560]{1,0:T(8,128)(2,1)S(1)} %get-tuple-element.27), channel_id=1, source_target_pairs={{0,1},{1,0},{2,3},{3,2},{4,5},{5,4},{6,7},{7,6},{8,9},{9,8},{10,11... | collective-permute-start | bytes 983048 | tf_op jit(solution)/shard_map/ppermute | solution.py:38
  4.2 15.2 %collective-permute-start.1 = (bf16[64,2560]{1,0:T(8,128)(2,1)S(1)}, bf16[64,2560]{1,0:T(8,128)(2,1)S(1)}, u32[]{:S(2)}, u32[]{:S(2)}) collective-permute-start(bf16[64,2560]{1,0:T(8,128)(2,1)S(1)} %get-tuple-element.32), channel_id=1, source_target_pairs={{0,1},{1,0},{2,3},{3,2},{4,5},{5,4},{6,7},{7,6},{8,9},{9,8},{10,11... | collective-permute-start | bytes 983048 | tf_op jit(solution)/shard_map/ppermute | solution.py:38
  5.5 13.9 %collective-permute-start.2 = (bf16[64,2560]{1,0:T(8,128)(2,1)S(1)}, bf16[64,2560]{1,0:T(8,128)(2,1)S(1)}, u32[]{:S(2)}, u32[]{:S(2)}) collective-permute-start(bf16[64,2560]{1,0:T(8,128)(2,1)S(1)} %add_convert_fusion.refs_2_.refs_1_), channel_id=1, source_target_pairs={{0,2},{1,3},{2,0},{3,1},{4,6},{5,7},{6,4},{7,5},{8,10},{9,11},{10,... | collective-permute-start | bytes 983048 | tf_op jit(solution)/shard_map/ppermute | solution.py:38
  8.4 0.7 copy-start.19
  9.1 0.7 copy-start.20
  9.8 0.7 copy-start.21
  11.2 0.9 copy-start.14
  12.1 0.7 copy-start.15
  12.8 0.7 copy-start.17
  14.2 0.6 copy-start.6
  14.8 6.0 %collective-permute-start.5 = (bf16[48,640]{1,0:T(8,128)(2,1)S(1)}, bf16[48,640]{1,0:T(8,128)(2,1)S(1)}, u32[]{:S(2)}, u32[]{:S(2)}) collective-permute-start(bf16[48,640]{1,0:T(8,128)(2,1)S(1)} %get-tuple-element.35), channel_id=1, source_target_pairs={{0,12},{1,13},{2,14},{3,15},{4,0},{5,1},{6,2},{7,3},{8,4},{9,5},{1... | collective-permute-start | bytes 184328 | tf_op jit(solution)/shard_map/ppermute | solution.py:38
  18.4 6.1 %collective-permute-start.4 = (bf16[48,640]{1,0:T(8,128)(2,1)S(1)}, bf16[48,640]{1,0:T(8,128)(2,1)S(1)}, u32[]{:S(2)}, u32[]{:S(2)}) collective-permute-start(bf16[48,640]{1,0:T(8,128)(2,1)S(1)} %get-tuple-element.34), channel_id=1, source_target_pairs={{0,8},{1,9},{2,10},{3,11},{4,12},{5,13},{6,14},{7,15},{8,0},{9,1},... | collective-permute-start | bytes 184328 | tf_op jit(solution)/shard_map/ppermute | solution.py:38
  18.4 6.1 %collective-permute-start.3 = (bf16[48,640]{1,0:T(8,128)(2,1)S(1)}, bf16[48,640]{1,0:T(8,128)(2,1)S(1)}, u32[]{:S(2)}, u32[]{:S(2)}) collective-permute-start(bf16[48,640]{1,0:T(8,128)(2,1)S(1)} %get-tuple-element.33), channel_id=1, source_target_pairs={{0,4},{1,5},{2,6},{3,7},{4,8},{5,9},{6,10},{7,11},{8,12},{9,13},{1... | collective-permute-start | bytes 184328 | tf_op jit(solution)/shard_map/ppermute | solution.py:38
  25.4 15.6 %collective-permute-start.6 = (bf16[192,640]{1,0:T(8,128)(2,1)S(1)}, bf16[192,640]{1,0:T(8,128)(2,1)S(1)}, u32[]{:S(2)}, u32[]{:S(2)}) collective-permute-start(bf16[192,640]{1,0:T(8,128)(2,1)S(1)} %pad_maximum_fusion.refs_0_), channel_id=1, source_target_pairs={{0,2},{1,3},{2,0},{3,1},{4,6},{5,7},{6,4},{7,5},{8,10},{9,11},{10,... | collective-permute-start | bytes 737288 | tf_op jit(solution)/shard_map/ppermute | solution.py:38
  25.9 7.1 %collective-permute-start.9 = (bf16[16,2560]{1,0:T(8,128)(2,1)}, bf16[16,2560]{1,0:T(8,128)(2,1)S(1)}, u32[]{:S(2)}, u32[]{:S(2)}) collective-permute-start(bf16[16,2560]{1,0:T(8,128)(2,1)} %get-tuple-element.54.refs_1_), channel_id=1, source_target_pairs={{0,4},{1,5},{2,6},{3,7},{4,8},{5,9},{6,10},{7,11},{8,12},{9,13},{1... | collective-permute-start | bytes 245768 | tf_op jit(solution)/shard_map/ppermute | solution.py:38
  26.2 8.6 %collective-permute-start.10 = (bf16[16,2560]{1,0:T(8,128)(2,1)}, bf16[16,2560]{1,0:T(8,128)(2,1)S(1)}, u32[]{:S(2)}, u32[]{:S(2)}) collective-permute-start(bf16[16,2560]{1,0:T(8,128)(2,1)} %get-tuple-element.53.refs_2_), channel_id=1, source_target_pairs={{0,8},{1,9},{2,10},{3,11},{4,12},{5,13},{6,14},{7,15},{8,0},{9,1},... | collective-permute-start | bytes 245768 | tf_op jit(solution)/shard_map/ppermute | solution.py:38
  28.5 6.3 %collective-permute-start.11 = (bf16[16,2560]{1,0:T(8,128)(2,1)}, bf16[16,2560]{1,0:T(8,128)(2,1)S(1)}, u32[]{:S(2)}, u32[]{:S(2)}) collective-permute-start(bf16[16,2560]{1,0:T(8,128)(2,1)} %get-tuple-element.52.refs_3_), channel_id=1, source_target_pairs={{0,12},{1,13},{2,14},{3,15},{4,0},{5,1},{6,2},{7,3},{8,4},{9,5},{1... | collective-permute-start | bytes 245768 | tf_op jit(solution)/shard_map/ppermute | solution.py:38
  30.7 0.8 copy-start.11
  31.7 14.4 %collective-permute-start.7 = (bf16[192,640]{1,0:T(8,128)(2,1)S(1)}, bf16[192,640]{1,0:T(8,128)(2,1)S(1)}, u32[]{:S(2)}, u32[]{:S(2)}) collective-permute-start(bf16[192,640]{1,0:T(8,128)(2,1)S(1)} %pad_maximum_fusion.refs_0_), channel_id=1, source_target_pairs={{0,1},{1,0},{2,3},{3,2},{4,5},{5,4},{6,7},{7,6},{8,9},{9,8},{10,11... | collective-permute-start | bytes 737288 | tf_op jit(solution)/shard_map/ppermute | solution.py:38
  34.8 0.7 copy-start.16
  35.5 0.7 copy-start.18
  36.9 5.9 %collective-permute-start.12 = (bf16[48,512]{1,0:T(8,128)(2,1)S(1)}, bf16[48,512]{1,0:T(8,128)(2,1)S(1)}, u32[]{:S(2)}, u32[]{:S(2)}) collective-permute-start(bf16[48,512]{1,0:T(8,128)(2,1)S(1)} %get-tuple-element.38), channel_id=1, source_target_pairs={{0,4},{1,5},{2,6},{3,7},{4,8},{5,9},{6,10},{7,11},{8,12},{9,13},{1... | collective-permute-start | bytes 147464 | tf_op jit(solution)/shard_map/ppermute | solution.py:38
  38.4 5.5 %collective-permute-start.13 = (bf16[48,512]{1,0:T(8,128)(2,1)S(1)}, bf16[48,512]{1,0:T(8,128)(2,1)S(1)}, u32[]{:S(2)}, u32[]{:S(2)}) collective-permute-start(bf16[48,512]{1,0:T(8,128)(2,1)S(1)} %get-tuple-element.39), channel_id=1, source_target_pairs={{0,8},{1,9},{2,10},{3,11},{4,12},{5,13},{6,14},{7,15},{8,0},{9,1},... | collective-permute-start | bytes 147464 | tf_op jit(solution)/shard_map/ppermute | solution.py:38
  40.5 4.1 %collective-permute-start.14 = (bf16[48,512]{1,0:T(8,128)(2,1)S(1)}, bf16[48,512]{1,0:T(8,128)(2,1)S(1)}, u32[]{:S(2)}, u32[]{:S(2)}) collective-permute-start(bf16[48,512]{1,0:T(8,128)(2,1)S(1)} %get-tuple-element.40), channel_id=1, source_target_pairs={{0,12},{1,13},{2,14},{3,15},{4,0},{5,1},{6,2},{7,3},{8,4},{9,5},{1... | collective-permute-start | bytes 147464 | tf_op jit(solution)/shard_map/ppermute | solution.py:38
  41.0 5.1 %collective-permute-start.8 = (bf16[192,640]{1,0:T(8,128)(2,1)S(1)}, bf16[192,640]{1,0:T(8,128)(2,1)S(1)}, u32[]{:S(2)}, u32[]{:S(2)}) collective-permute-start(bf16[192,640]{1,0:T(8,128)(2,1)S(1)} %collective-permute-done.6.refs_1_), channel_id=1, source_target_pairs={{0,1},{1,0},{2,3},{3,2},{4,5},{5,4},{6,7},{7,6},{8,9},{9,8},{10,11... | collective-permute-start | bytes 737288 | tf_op jit(solution)/shard_map/ppermute | solution.py:38
  44.6 16.4 %collective-permute-start.15 = (bf16[192,512]{1,0:T(8,128)(2,1)S(1)}, bf16[192,512]{1,0:T(8,128)(2,1)S(1)}, u32[]{:S(2)}, u32[]{:S(2)}) collective-permute-start(bf16[192,512]{1,0:T(8,128)(2,1)S(1)} %constant_dynamic-update-slice_fusion.refs_7_.refs_0_), channel_id=1, source_target_pairs={{0,2},{1,3},{2,0},{3,1},{4,6},{5,7},{6,4},{7,5},{8,10},{9,11},{10,... | collective-permute-start | bytes 589832 | tf_op jit(solution)/shard_map/ppermute | solution.py:38
  46.1 15.6 %copy-start.12 = (f32[2560,4]{0,1:T(4,128)S(1)}, f32[2560,4]{0,1:T(4,128)}, u32[]{:S(2)}) copy-start(f32[2560,4]{0,1:T(4,128)} %param.17) | copy-start | bytes 122884
  58.9 0.7 copy-start.3
  59.6 0.7 copy-start.7
  60.3 0.7 copy-start.8
  61.0 0.7 copy-start
  61.7 1.7 %collective-permute-start.17 = (bf16[192,640]{1,0:T(8,128)(2,1)}, bf16[192,640]{1,0:T(8,128)(2,1)S(1)}, u32[]{:S(2)}, u32[]{:S(2)}) collective-permute-start(bf16[192,640]{1,0:T(8,128)(2,1)} %tie.11), channel_id=1, source_target_pairs={{0,1},{1,0},{2,3},{3,2},{4,5},{5,4},{6,7},{7,6},{8,9},{9,8},{10,11... | collective-permute-start | bytes 737288 | tf_op jit(solution)/shard_map/ppermute | solution.py:38
  62.0 2.1 %collective-permute-start.19 = (bf16[192,512]{1,0:T(8,128)(2,1)S(1)}, bf16[192,512]{1,0:T(8,128)(2,1)S(1)}, u32[]{:S(2)}, u32[]{:S(2)}) collective-permute-start(bf16[192,512]{1,0:T(8,128)(2,1)S(1)} %constant_dynamic-update-slice_fusion.refs_7_.refs_0_), channel_id=1, source_target_pairs={{0,1},{1,0},{2,3},{3,2},{4,5},{5,4},{6,7},{7,6},{8,9},{9,8},{10,11... | collective-permute-start | bytes 589832 | tf_op jit(solution)/shard_map/ppermute | solution.py:38
  62.5 1.7 %collective-permute-start.20 = (bf16[192,512]{1,0:T(8,128)(2,1)}, bf16[192,512]{1,0:T(8,128)(2,1)S(1)}, u32[]{:S(2)}, u32[]{:S(2)}) collective-permute-start(bf16[192,512]{1,0:T(8,128)(2,1)} %tie.9.refs_1_), channel_id=1, source_target_pairs={{0,1},{1,0},{2,3},{3,2},{4,5},{5,4},{6,7},{7,6},{8,9},{9,8},{10,11... | collective-permute-start | bytes 589832 | tf_op jit(solution)/shard_map/ppermute | solution.py:38
  63.4 20.3 %copy-start.4 = (bf16[192,640]{1,0:T(8,128)(2,1)S(1)}, bf16[192,640]{1,0:T(8,128)(2,1)}, u32[]{:S(2)}) copy-start(bf16[192,640]{1,0:T(8,128)(2,1)} %copy-done.3) | copy-start | bytes 737284
  63.5 15.7 %collective-permute-start.18 = (bf16[192,640]{1,0:T(8,128)(2,1)S(1)}, bf16[192,640]{1,0:T(8,128)(2,1)S(1)}, u32[]{:S(2)}, u32[]{:S(2)}) collective-permute-start(bf16[192,640]{1,0:T(8,128)(2,1)S(1)} %add_convert_fusion.2.refs_7_), channel_id=1, source_target_pairs={{0,2},{1,3},{2,0},{3,1},{4,6},{5,7},{6,4},{7,5},{8,10},{9,11},{10,... | collective-permute-start | bytes 737288 | tf_op jit(solution)/shard_map/ppermute | solution.py:38
  64.1 0.9 copy-start.1
  77.2 0.7 copy-start.5
  77.8 0.7 copy-start.9
  78.5 0.7 copy-start.10
  79.2 0.7 copy-start.22
  79.9 1.7 %collective-permute-start.21 = (bf16[192,512]{1,0:T(8,128)(2,1)}, bf16[192,512]{1,0:T(8,128)(2,1)S(1)}, u32[]{:S(2)}, u32[]{:S(2)}) collective-permute-start(bf16[192,512]{1,0:T(8,128)(2,1)} %tie.13), channel_id=1, source_target_pairs={{0,1},{1,0},{2,3},{3,2},{4,5},{5,4},{6,7},{7,6},{8,9},{9,8},{10,11... | collective-permute-start | bytes 589832 | tf_op jit(solution)/shard_map/ppermute | solution.py:38
  80.1 3.5 %collective-permute-start.16 = (bf16[192,640]{1,0:T(8,128)(2,1)}, bf16[192,640]{1,0:T(8,128)(2,1)S(1)}, u32[]{:S(2)}, u32[]{:S(2)}) collective-permute-start(bf16[192,640]{1,0:T(8,128)(2,1)} %tie.10), channel_id=1, source_target_pairs={{0,1},{1,0},{2,3},{3,2},{4,5},{5,4},{6,7},{7,6},{8,9},{9,8},{10,11... | collective-permute-start | bytes 737288 | tf_op jit(solution)/shard_map/ppermute | solution.py:38
  80.4 7.5 %collective-permute-start.25 = (bf16[192,512]{1,0:T(8,128)(2,1)}, bf16[192,512]{1,0:T(8,128)(2,1)S(1)}, u32[]{:S(2)}, u32[]{:S(2)}) collective-permute-start(bf16[192,512]{1,0:T(8,128)(2,1)} %tie.15), channel_id=1, source_target_pairs={{0,1},{1,0},{2,3},{3,2},{4,5},{5,4},{6,7},{7,6},{8,9},{9,8},{10,11... | collective-permute-start | bytes 589832 | tf_op jit(solution)/shard_map/ppermute | solution.py:38
  82.3 7.3 %collective-permute-start.26 = (bf16[192,512]{1,0:T(8,128)(2,1)}, bf16[192,512]{1,0:T(8,128)(2,1)S(1)}, u32[]{:S(2)}, u32[]{:S(2)}) collective-permute-start(bf16[192,512]{1,0:T(8,128)(2,1)} %add_convert_fusion.4.refs_1_), channel_id=1, source_target_pairs={{0,2},{1,3},{2,0},{3,1},{4,6},{5,7},{6,4},{7,5},{8,10},{9,11},{10,... | collective-permute-start | bytes 589832 | tf_op jit(solution)/shard_map/ppermute | solution.py:38
  84.8 8.4 %collective-permute-start.22 = (bf16[48,640]{1,0:T(8,128)(2,1)S(1)}, bf16[48,640]{1,0:T(8,128)(2,1)S(1)}, u32[]{:S(2)}, u32[]{:S(2)}) collective-permute-start(bf16[48,640]{1,0:T(8,128)(2,1)S(1)} %get-tuple-element.57), channel_id=1, source_target_pairs={{0,12},{1,13},{2,14},{3,15},{4,0},{5,1},{6,2},{7,3},{8,4},{9,5},{1... | collective-permute-start | bytes 184328 | tf_op jit(solution)/shard_map/ppermute | solution.py:38
  87.2 6.7 %collective-permute-start.23 = (bf16[48,640]{1,0:T(8,128)(2,1)S(1)}, bf16[48,640]{1,0:T(8,128)(2,1)S(1)}, u32[]{:S(2)}, u32[]{:S(2)}) collective-permute-start(bf16[48,640]{1,0:T(8,128)(2,1)S(1)} %get-tuple-element.56), channel_id=1, source_target_pairs={{0,8},{1,9},{2,10},{3,11},{4,12},{5,13},{6,14},{7,15},{8,0},{9,1},... | collective-permute-start | bytes 184328 | tf_op jit(solution)/shard_map/ppermute | solution.py:38
  87.2 6.7 %collective-permute-start.24 = (bf16[48,640]{1,0:T(8,128)(2,1)S(1)}, bf16[48,640]{1,0:T(8,128)(2,1)S(1)}, u32[]{:S(2)}, u32[]{:S(2)}) collective-permute-start(bf16[48,640]{1,0:T(8,128)(2,1)S(1)} %get-tuple-element.55), channel_id=1, source_target_pairs={{0,4},{1,5},{2,6},{3,7},{4,8},{5,9},{6,10},{7,11},{8,12},{9,13},{1... | collective-permute-start | bytes 184328 | tf_op jit(solution)/shard_map/ppermute | solution.py:38
  90.6 4.2 %collective-permute-start.27 = (bf16[48,512]{1,0:T(8,128)(2,1)S(1)}, bf16[48,512]{1,0:T(8,128)(2,1)S(1)}, u32[]{:S(2)}, u32[]{:S(2)}) collective-permute-start(bf16[48,512]{1,0:T(8,128)(2,1)S(1)} %get-tuple-element.61), channel_id=1, source_target_pairs={{0,12},{1,13},{2,14},{3,15},{4,0},{5,1},{6,2},{7,3},{8,4},{9,5},{1... | collective-permute-start | bytes 147464 | tf_op jit(solution)/shard_map/ppermute | solution.py:38
  93.0 5.2 %collective-permute-start.28 = (bf16[48,512]{1,0:T(8,128)(2,1)S(1)}, bf16[48,512]{1,0:T(8,128)(2,1)S(1)}, u32[]{:S(2)}, u32[]{:S(2)}) collective-permute-start(bf16[48,512]{1,0:T(8,128)(2,1)S(1)} %get-tuple-element.60), channel_id=1, source_target_pairs={{0,8},{1,9},{2,10},{3,11},{4,12},{5,13},{6,14},{7,15},{8,0},{9,1},... | collective-permute-start | bytes 147464 | tf_op jit(solution)/shard_map/ppermute | solution.py:38
  93.2 5.9 %collective-permute-start.29 = (bf16[48,512]{1,0:T(8,128)(2,1)S(1)}, bf16[48,512]{1,0:T(8,128)(2,1)S(1)}, u32[]{:S(2)}, u32[]{:S(2)}) collective-permute-start(bf16[48,512]{1,0:T(8,128)(2,1)S(1)} %get-tuple-element.59), channel_id=1, source_target_pairs={{0,4},{1,5},{2,6},{3,7},{4,8},{5,9},{6,10},{7,11},{8,12},{9,13},{1... | collective-permute-start | bytes 147464 | tf_op jit(solution)/shard_map/ppermute | solution.py:38

commit v7 on v6

--- a/solution.py
+++ b/solution.py
@@ -11,6 +11,7 @@
 VMEM = pl.BlockSpec(memory_space=pltpu.VMEM)
 SMEM = pl.BlockSpec(memory_space=pltpu.SMEM)
 ANY = pl.BlockSpec(memory_space=pl.ANY)
+HBM = pl.BlockSpec(memory_space=pltpu.HBM)
 
 
 class Grid:
@@ -18,6 +19,7 @@
         self.experts = experts
         self.pairs = devices // experts // 2
         index = lax.axis_index("dev")
+        self.index = index
         self.expert = index // (self.pairs * 2)
         self.pair = (index // 2) % self.pairs
         self.core = index % 2
@@ -53,84 +55,41 @@
         self.width = features // self.chunks
 
 
-def live(position, lengths_ref):
-    prompt = position // PLEN
-    length = jnp.zeros_like(position)
-    for p in range(lengths_ref.shape[0]):
-        length = jnp.where(prompt == p, lengths_ref[p], length)
-    return position % PLEN < length
-
-
-def place_kernel(packings, experts, after, lengths_ref, *refs):
+def place(chosen, packing, experts, out_ref):
     index = lax.axis_index("dev")
-    shift = experts - index // (lax.axis_size("dev") // experts)
-    for i, packing in enumerate(packings):
-        chosen, out_ref = refs[i][...], refs[len(refs) - len(packings) + i]
-        rows = chosen.shape[1]
-        relative = lax.rem(chosen + shift, experts)
-        expert_at = lax.broadcasted_iota(jnp.int32, (experts, rows), 0)
-        routed = (relative[0:1, :] == expert_at) | (relative[1:2, :] == expert_at)
-        if i == 1:
-            position = index * rows + lax.broadcasted_iota(jnp.int32, (experts, rows), 1)
-            routed = routed & live(position, lengths_ref)
-        at = [lax.broadcasted_iota(jnp.int32, (rows, rows), d) for d in range(2)]
-        before = (at[0] < at[1]).astype(jnp.float32)
-        spot = jnp.dot(routed.astype(jnp.float32), before, preferred_element_type=jnp.float32)
-        spot = spot + expert_at.astype(jnp.float32) * float(packing.rows)
-        spot = jnp.where(routed, spot, -65536.0)
-        for t in range(2):
-            own = jnp.where(relative[t : t + 1, :] == expert_at, spot, 0.0)
-            own = jnp.sum(own, axis=0, keepdims=True)
-            for column, value in ((t, own), (2 + t, chosen[t : t + 1, :].astype(jnp.float32))):
-                out_ref[:, column : column + 1] = jnp.sum(
-                    jnp.where(at[0] == at[1], value, 0.0), axis=1, keepdims=True
-                )
-
-
-def place(chosen, lengths, experts, packings, after):
-    return pl.pallas_call(
-        functools.partial(place_kernel, packings, experts, len(after)),
-        out_shape=[jax.ShapeDtypeStruct((ids.shape[0], 4), jnp.float32) for ids in chosen],
-        in_specs=[SMEM] + [VMEM] * len(chosen) + [ANY] * len(after),
-        out_specs=[VMEM] * len(chosen),
-        compiler_params=pltpu.CompilerParams(vmem_limit_bytes=8 << 20),
-        name="place",
-    )(lengths, *[ids.T for ids in chosen], *after)
-
-
-def tie(value, after):
-    return pl.pallas_call(
-        lambda *refs: None,
-        out_shape=jax.ShapeDtypeStruct(value.shape, value.dtype),
-        in_specs=[ANY] * (1 + len(after)),
-        out_specs=ANY,
-        input_output_aliases={0: 0},
-        cost_estimate=pl.CostEstimate(flops=0, bytes_accessed=0, transcendentals=0),
-        name="tie",
-    )(value, *after)
-
-
-def modulate_kernel(packing, experts, count, spot_ref, scale_ref, shift_ref, *refs):
-    normed_ref, packed_refs = refs[-1 - experts], refs[-experts:]
-    rows = normed_ref.shape[0]
-    values = refs[0][...].astype(jnp.float32)
-    for ref in refs[1:count]:
-        values = values + ref[...].astype(jnp.float32)
-    values = values.astype(jnp.bfloat16).astype(jnp.float32)
+    rows = chosen.shape[1]
+    relative = lax.rem(chosen + (experts - index // (lax.axis_size("dev") // experts)), experts)
+    expert_at = lax.broadcasted_iota(jnp.int32, (experts, rows), 0)
+    routed = (relative[0:1, :] == expert_at) | (relative[1:2, :] == expert_at)
+    routed = routed & (chosen[0:1, :] >= 0)
+    at = [lax.broadcasted_iota(jnp.int32, (rows, rows), d) for d in range(2)]
+    before = (at[0] < at[1]).astype(jnp.float32)
+    spot = jnp.dot(routed.astype(jnp.float32), before, preferred_element_type=jnp.float32)
+    spot = spot + expert_at.astype(jnp.float32) * float(packing.rows)
+    spot = jnp.where(routed, spot, -65536.0)
+    for t in range(2):
+        own = jnp.where(relative[t : t + 1, :] == expert_at, spot, 0.0)
+        own = jnp.sum(own, axis=0, keepdims=True)
+        for column, value in ((t, own), (2 + t, chosen[t : t + 1, :].astype(jnp.float32))):
+            out_ref[:, column : column + 1] = jnp.sum(
+                jnp.where(at[0] == at[1], value, 0.0), axis=1, keepdims=True
+            )
+
+
+def norm_and_pack(values, small_ref, spot_ref, packing, experts, normed_ref, packed_refs):
+    rows = values.shape[0]
     center = values - jnp.mean(values, axis=1, keepdims=True)
     spread = jnp.mean(center * center, axis=1, keepdims=True)
-    normed = center * lax.rsqrt(spread + 1e-06) * scale_ref[...][None, :] + shift_ref[...][None, :]
+    normed = center * lax.rsqrt(spread + 1e-06) * small_ref[0:1, :] + small_ref[1:2, :]
     normed = normed.astype(jnp.bfloat16)
     normed_ref[...] = normed
-
     place = lax.broadcasted_iota(jnp.int32, (rows, experts * packing.rows), 1).astype(jnp.float32)
     packed = None
     for j in range(packing.chunks):
         at = place - float(j * packing.cap)
         into = jnp.where((at == spot_ref[:, 0:1]) | (at == spot_ref[:, 1:2]), 1.0, 0.0)
-        into = into.T.astype(jnp.bfloat16)
         term = jnp.dot(
-            into,
+            into.T.astype(jnp.bfloat16),
             normed[:, j * packing.width : (j + 1) * packing.width],
             preferred_element_type=jnp.float32,
         )
@@ -139,25 +98,87 @@
         packed_refs[k][...] = packed[k * packing.rows : (k + 1) * packing.rows].astype(
             jnp.bfloat16
         )
-def modulate(terms, spot, mod_scale, mod_shift, packing, experts, after):
+
+
+def prepare_kernel(packings, experts, after, ids_ref, small_ref, image_ref, *refs):
+    image_spot, caption_spot, normed_ref = refs[after : after + 3]
+    image_rows, caption_rows = image_spot.shape[0], caption_spot.shape[0]
+    place(ids_ref[0:2, 0:image_rows], packings[0], experts, image_spot)
+    place(ids_ref[2:4, 0:caption_rows], packings[1], experts, caption_spot)
+    norm_and_pack(
+        image_ref[...].astype(jnp.float32),
+        small_ref,
+        image_spot,
+        packings[0],
+        experts,
+        normed_ref,
+        refs[after + 3 :],
+    )
+
+
+def prepare(ids, small, image_rows, caption_rows, packings, experts, after):
+    rows, features = image_rows.shape
+    packed = jax.ShapeDtypeStruct((packings[0].rows, packings[0].width), jnp.bfloat16)
+    results = pl.pallas_call(
+        functools.partial(prepare_kernel, packings, experts, len(after)),
+        out_shape=[
+            jax.ShapeDtypeStruct((rows, 4), jnp.float32),
+            jax.ShapeDtypeStruct((caption_rows, 4), jnp.float32),
+            jax.ShapeDtypeStruct((rows, features), jnp.bfloat16),
+        ]
+        + [packed] * experts,
+        in_specs=[VMEM] * 3 + [ANY] * len(after),
+        out_specs=[VMEM] * (3 + experts),
+        compiler_params=pltpu.CompilerParams(vmem_limit_bytes=8 << 20),
+        name="prepare",
+    )(ids, small, image_rows, *after)
+    return results[:3], list(results[3:])
+
+
+def tie_kernel(value_ref, *refs):
+    refs[-1][...] = value_ref[...]
+
+
+def tie(value, after):
+    return pl.pallas_call(
+        tie_kernel,
+        out_shape=jax.ShapeDtypeStruct(value.shape, value.dtype),
+        in_specs=[VMEM] + [ANY] * len(after),
+        out_specs=VMEM,
+        compiler_params=pltpu.CompilerParams(vmem_limit_bytes=8 << 20),
+        name="tie",
+    )(value, *after)
+
+
+def modulate_kernel(packing, experts, count, spot_ref, small_ref, *refs):
+    values = refs[0][...].astype(jnp.float32)
+    for ref in refs[1:count]:
+        values = values + ref[...].astype(jnp.float32)
+    values = values.astype(jnp.bfloat16).astype(jnp.float32)
+    norm_and_pack(
+        values, small_ref, spot_ref, packing, experts, refs[count], refs[count + 1 :]
+    )
+
+
+def modulate(terms, spot, small, packing, experts):
     rows, features = terms[0].shape
     packed = jax.ShapeDtypeStruct((packing.rows, packing.width), jnp.bfloat16)
     results = pl.pallas_call(
         functools.partial(modulate_kernel, packing, experts, len(terms)),
         out_shape=[jax.ShapeDtypeStruct((rows, features), jnp.bfloat16)] + [packed] * experts,
-        in_specs=[VMEM] * (3 + len(terms)) + [ANY] * len(after),
+        in_specs=[VMEM] * (2 + len(terms)),
         out_specs=[VMEM] * (1 + experts),
         compiler_params=pltpu.CompilerParams(vmem_limit_bytes=8 << 20),
         name="modulate",
-    )(spot, mod_scale, mod_shift, *terms, *after)
+    )(spot, small, *terms)
     return (results[0], list(results[1:]))
 
 
-def route_kernel(spot_ref, normed_ref, router_ref, weight_ref):
+def route_kernel(spot_ref, normed_ref, small_ref, weight_ref):
     normed = normed_ref[...].astype(jnp.float32)
     logits = [
-        jnp.sum(normed * router_ref[k : k + 1, :], axis=1, keepdims=True)
-        for k in range(router_ref.shape[0])
+        jnp.sum(normed * small_ref[2 + k : 3 + k, :], axis=1, keepdims=True)
+        for k in range(small_ref.shape[0] - 2)
     ]
     picked = []
     for t in range(2):
@@ -169,7 +190,7 @@
     weight_ref[:, 1:2] = jax.nn.sigmoid(picked[1] - picked[0])
 
 
-def route(normed, spot, router_weight):
+def route(normed, spot, small):
     return pl.pallas_call(
         route_kernel,
         out_shape=jax.ShapeDtypeStruct((spot.shape[0], 2), jnp.float32),
@@ -177,11 +198,11 @@
         out_specs=VMEM,
         compiler_params=pltpu.CompilerParams(vmem_limit_bytes=8 << 20),
         name="route",
-    )(spot, normed, router_weight.T)
+    )(spot, normed, small)
 
 
 def cuts(units):
-    edges = [0, units] if units <= 1024 else [0, 384, 1024, units]
+    edges = [0, units] if units <= 1024 else [0, 256, 768, 1280, units]
     return list(zip(edges[:-1], edges[1:]))
 
 
@@ -201,7 +222,7 @@
             copies.append(
                 pltpu.make_async_copy(source.at[lo:hi], target.at[lo:hi], sems.at[3 * i + t])
             )
-    for copy in copies:
+    for copy in copies[:6]:
         copy.start()
 
     cap, chunks, width, high = packing.cap, packing.chunks, packing.width, packing.rows
@@ -251,6 +272,8 @@
             copies[3 * i - 1].wait()
         copies[3 * i].wait()
         copies[3 * i + 1].wait()
+        for copy in copies[3 * (i + 2) : 3 * (i + 3)]:
+            copy.start()
         gate = product(gate_ref, lo, hi)
         up = product(up_ref, lo, hi)
         if i > 0:
@@ -282,7 +305,7 @@
     return pl.pallas_call(
         functools.partial(expert_kernel, packing, len(arrays), len(after)),
         out_shape=[jax.ShapeDtypeStruct(arrays[0].shape, jnp.bfloat16)] * len(arrays),
-        in_specs=[VMEM] * len(arrays) + [ANY] * (3 + len(after)),
+        in_specs=[VMEM] * len(arrays) + [HBM] * 3 + [ANY] * len(after),
         out_specs=[VMEM] * len(arrays),
         scratch_shapes=[
             pltpu.VMEM((units, features), jnp.bfloat16),
@@ -339,62 +362,22 @@
     )(spot, weights, *blocks)
 
 
-def project_kernel(experts, pairs, text_hbm, weight_hbm, *refs):
-    out_refs, (text_ref, weight_ref, sems) = refs[:-3], refs[-3:]
-    copies = [
-        pltpu.make_async_copy(text_hbm, text_ref, sems.at[0]),
-        pltpu.make_async_copy(weight_hbm, weight_ref, sems.at[1]),
-    ]
-    for copy in copies:
-        copy.start()
-    rows = text_ref.shape[0] // (experts * pairs * 2)
-    index = lax.axis_index("dev")
-    expert, pair, core = index // (pairs * 2), lax.rem(index // 2, pairs), lax.rem(index, 2)
-    copies[0].wait()
-    picked = []
-    for c in (1, 0):
-        for p in list(range(1, pairs)) + [0]:
-            for e in range(experts):
-                owner = lax.rem(expert + e, experts) * pairs + lax.rem(pair + p, pairs)
-                start = (owner * 2 + lax.rem(core + c, 2)) * rows
-                picked.append(text_ref[pl.ds(pl.multiple_of(start, rows), rows), :])
-    picked = jnp.concatenate(picked, axis=0)
-    copies[1].wait()
-    out = jnp.dot(picked, weight_ref[...], preferred_element_type=jnp.float32)
-    high = rows * experts
-    for i, ref in enumerate(out_refs):
-        ref[...] = out[i * high : (i + 1) * high].astype(ref.dtype)
-
-
 def partial_captions(text_hidden, caption_weight, grid):
     groups = grid.pairs * 2
     rows = text_hidden.shape[0] // (grid.experts * groups)
-    depth, features = caption_weight.shape
-    kinds = [jnp.bfloat16] * grid.pairs + [jnp.float32] * grid.pairs
-    if rows % 16 == 0:
-        return pl.pallas_call(
-            functools.partial(project_kernel, grid.experts, grid.pairs),
-            out_shape=[
-                jax.ShapeDtypeStruct((rows * grid.experts, features), kind) for kind in kinds
-            ],
-            in_specs=[ANY] * 2,
-            out_specs=[VMEM] * len(kinds),
-            scratch_shapes=[
-                pltpu.VMEM(text_hidden.shape, text_hidden.dtype),
-                pltpu.VMEM(caption_weight.shape, caption_weight.dtype),
-                pltpu.SemaphoreType.DMA((2,)),
-            ],
-            compiler_params=pltpu.CompilerParams(vmem_limit_bytes=16 << 20),
-            name="project",
-        )(text_hidden, caption_weight)
+    depth = caption_weight.shape[0]
     text = text_hidden.reshape(grid.experts, grid.pairs, 2, rows, depth)
     text = jnp.roll(text, -grid.expert, axis=0)
     text = jnp.roll(text, -1 - grid.pair, axis=1)
     text = jnp.roll(text, -1 - grid.core, axis=2)
-    text = jnp.transpose(text, (2, 1, 0, 3, 4)).reshape(groups, -1, depth)
+    text = jnp.transpose(text, (2, 1, 0, 3, 4)).reshape(2, -1, depth)
+    other, own = [
+        jnp.dot(text[c], caption_weight, preferred_element_type=jnp.float32).astype(kind)
+        for c, kind in enumerate((jnp.bfloat16, jnp.float32))
+    ]
+    high = rows * grid.experts
     return [
-        jnp.dot(text[i], caption_weight, preferred_element_type=jnp.float32).astype(kind)
-        for i, kind in enumerate(kinds)
+        value[k * high : (k + 1) * high] for value in (other, own) for k in range(grid.pairs)
     ]
 
 
@@ -455,38 +438,38 @@
         partial[pairs + i] + grid.send(partial[i], 2, 1).astype(wide) for i in range(pairs)
     ]
     crossing = [value.astype(narrow) for value in sums[:-1]]
+    received = [grid.send(value, 1, k) for k, value in enumerate(crossing, 1)]
+
+    rows = text_hidden.shape[0] // devices
+    position = grid.index * rows + jnp.arange(rows, dtype=jnp.int32)
+    prompts = jnp.arange(prompt_lengths.shape[0], dtype=jnp.int32)
+    lengths = jnp.where(position[:, None] // PLEN == prompts, prompt_lengths, 0).sum(axis=1)
+    ids = jnp.where((position % PLEN < lengths)[None, :], caption_experts.T, -1)
+    ids = jnp.pad(ids, ((0, 0), (0, image_rows.shape[0] - rows)))
+    ids = jnp.concatenate([image_experts.T, ids], axis=0)
+    small = jnp.concatenate([mod_scale[None], mod_shift[None], router_weight.T], axis=0)
+    (image_spot, caption_spot, image_normed), blocks = prepare(
+        ids, small, image_rows, rows, [image_packing, caption_packing], experts, crossing[:1]
+    )
+    image_first = [blocks[0]] + to_experts(blocks)
+
+    received[0] = tie(received[0], blocks[1:2])
     total = sums[-1]
-    for k in range(1, pairs):
-        total = total + grid.send(crossing[k - 1], 1, k).astype(wide)
-
-    image_spot, caption_spot = place(
-        [image_experts, caption_experts],
-        prompt_lengths,
-        experts,
-        [image_packing, caption_packing],
-        crossing[:1],
-    )
-    image_normed, blocks = modulate(
-        [image_rows], image_spot, mod_scale, mod_shift, image_packing, experts, crossing[:1]
-    )
-    image_first = [blocks[0]] + to_experts(blocks)
-
+    for value in received:
+        total = total + value.astype(wide)
     parts = split(total, experts)
-    sent = [part.astype(narrow) for part in parts]
-    terms = [parts[0]] + to_experts(sent)
-
-    image_first = jnp.concatenate([tie(image_first[0], sent[1:])] + image_first[1:], axis=0)
-    image_own = to_pairs(image_first)
-    image_arrays = image_own + over_cores(image_own)
-
-    caption_normed, blocks = modulate(
-        terms, caption_spot, mod_scale, mod_shift, caption_packing, experts, []
-    )
+    terms = [parts[0]] + to_experts([part.astype(narrow) for part in parts])
+    caption_normed, blocks = modulate(terms, caption_spot, small, caption_packing, experts)
     caption_first = jnp.concatenate([blocks[0]] + to_experts(blocks), axis=0)
     caption_own = to_pairs(caption_first)
 
-    image_weights = route(image_normed, image_spot, router_weight)
-    caption_weights = route(caption_normed, caption_spot, router_weight)
+    image_first = jnp.concatenate([tie(image_first[0], blocks[1:2])] + image_first[1:], axis=0)
+    image_own = to_pairs(image_first)
+    image_own = image_own[:1] + [tie(value, [caption_first]) for value in image_own[1:]]
+    image_arrays = image_own + over_cores(image_own)
+
+    image_weights = route(image_normed, image_spot, small)
+    caption_weights = route(caption_normed, caption_spot, small)
     image_results = expert_rows(
         image_arrays, w_gate, w_up, w_down, image_packing, [caption_first, image_weights]
     )

time: 101 us -> 86.1 us (0.85)
  local copies, waits for them, and re-layouts: 16.5 us -> 0.25 us
  starting transfers between devices: 28.7 us -> 32.9 us
  Pallas kernels: 30 us -> 27.6 us
  other arithmetic: 3.85 us -> 1.82 us
  waiting for transfers between devices: 20.2 us -> 21.5 us
    unnamed x49 -> x19, local copies, waits for them, and re-layouts: 15.7 us -> 0.09 us
    ppermute x30, starting transfers between devices: 28.7 us -> 32.9 us  [send(): return lax.ppermute(value, 'dev', moves)]
    convert_element_type x2, other arithmetic: 2.05 us -> 0.18 us  [from_experts(): parts = split(total.astype(narrow), experts)]
    ppermute x30, waiting for transfers between devices: 20.2 us -> 21.5 us  [send(): return lax.ppermute(value, 'dev', moves)]
    pallas_call x2, Pallas kernels: 24.9 us -> 23.7 us  [expert_rows(): pl.pallas_call(functools.partial(expert_kernel, packing, len(arrays), len...]
  transfers between devices with their start and end apart: 30 -> 30, of which waited for: 15 -> 13; matrix products, arithmetic and copies ran while one was open for 4% -> 1% of each run, Pallas kernels for 28% -> 31%
where the time goes in v7:
time: 86.1 us; the launch traced here: 85.9 us
  starting transfers between devices  32.9 us (38%)
  Pallas kernels  27.6 us (32%)
  waiting for transfers between devices  21.5 us (25%)
  other arithmetic  1.82 us (2%)
  between operations  1.16 us (1%)
    ppermute x30, starting transfers between devices, send(): return lax.ppermute(value, 'dev', moves)  32.9 us
    pallas_call x2, Pallas kernels, expert_rows(): pl.pallas_call(functools.partial(expert_kernel, packing, len(arrays), len...  23.7 us
    ppermute x30, waiting for transfers between devices, send(): return lax.ppermute(value, 'dev', moves)  21.5 us
    pallas_call x2, Pallas kernels, combine(): pl.pallas_call(functools.partial(combine_kernel, packing), out_shape=jax....  1.77 us
  transfers between devices with their start and end apart: 30, of which 13 were waited for; matrix products, arithmetic and copies ran while one was open for 1% of the time, Pallas kernels for 31%

profile of v7, /device:TPU:0, one launch (start us, length us, event | category | flops | bytes accessed | tf_op | source)
XLA Modules:
  0.0 85.9 jit_solution(9210797979954596002)
XLA Ops:
  0.6 0.0 copy-start
  0.7 1.0 %fusion.5 = bf16[4,2,2,16,256]{4,3,2,1,0:T(8,128)(2,1)S(1)} fusion(s32[]{:T(128)S(6)} %select_n.88, bf16[4,2,2,16,256]{4,3,2,1,0:T(8,128)(2,1)} %bitcast.21), kind=kLoop, calls=%fused_computation.19 | loop fusion | flops 65536 | bytes 262148 | tf_op jit(solution)/shard_map/jit(_roll_dynamic)/concatenate | solution.py:370
  1.8 0.1 fusion.4
  1.9 0.1 fusion.3
  2.0 0.0 copy-done
  2.0 0.0 copy-start.3
  2.0 0.3 convolution_convert_fusion
  2.4 0.5 collective-permute-start
  3.0 0.1 collective-permute-start.1
  3.1 0.1 fusion.6
  3.3 0.3 fusion.15
  3.6 0.0 copy-start.2
  3.7 0.6 collective-permute-done
  4.2 0.1 fusion.1.refs_0_
  4.3 3.0 %collective-permute-start.2 = (bf16[64,2560]{1,0:T(8,128)(2,1)S(1)}, bf16[64,2560]{1,0:T(8,128)(2,1)S(1)}, u32[]{:S(2)}, u32[]{:S(2)}) collective-permute-start(bf16[64,2560]{1,0:T(8,128)(2,1)S(1)} %fusion.1.refs_0_), channel_id=1, source_target_pairs={{0,2},{1,3},{2,0},{3,1},{4,6},{5,7},{6,4},{7,5},{8,10},{9,11},{10,... | collective-permute-start | bytes 983048 | tf_op jit(solution)/shard_map/ppermute | solution.py:40
  7.3 0.8 prepare.1
  8.1 7.1 %collective-permute-done.2.value_ref = bf16[64,2560]{1,0:T(8,128)(2,1)S(1)} collective-permute-done((bf16[64,2560]{1,0:T(8,128)(2,1)S(1)}, bf16[64,2560]{1,0:T(8,128)(2,1)S(1)}, u32[]{:S(2)}, u32[]{:S(2)}) %collective-permute-start.2) | collective-permute-done | bytes 327712 | tf_op jit(solution)/shard_map/ppermute | solution.py:40
  15.3 0.1 fusion.8
  15.4 1.8 %collective-permute-start.3 = (bf16[16,2560]{1,0:T(8,128)(2,1)S(1)}, bf16[16,2560]{1,0:T(8,128)(2,1)S(1)}, u32[]{:S(2)}, u32[]{:S(2)}) collective-permute-start(bf16[16,2560]{1,0:T(8,128)(2,1)S(1)} %get-tuple-element.48), channel_id=1, source_target_pairs={{0,4},{1,5},{2,6},{3,7},{4,8},{5,9},{6,10},{7,11},{8,12},{9,13},{1... | collective-permute-start | bytes 245768 | tf_op jit(solution)/shard_map/ppermute | solution.py:40
  17.3 2.6 %collective-permute-start.4 = (bf16[16,2560]{1,0:T(8,128)(2,1)S(1)}, bf16[16,2560]{1,0:T(8,128)(2,1)S(1)}, u32[]{:S(2)}, u32[]{:S(2)}) collective-permute-start(bf16[16,2560]{1,0:T(8,128)(2,1)S(1)} %get-tuple-element.47), channel_id=1, source_target_pairs={{0,8},{1,9},{2,10},{3,11},{4,12},{5,13},{6,14},{7,15},{8,0},{9,1},... | collective-permute-start | bytes 245768 | tf_op jit(solution)/shard_map/ppermute | solution.py:40
  19.9 1.3 %collective-permute-start.5 = (bf16[16,2560]{1,0:T(8,128)(2,1)S(1)}, bf16[16,2560]{1,0:T(8,128)(2,1)S(1)}, u32[]{:S(2)}, u32[]{:S(2)}) collective-permute-start(bf16[16,2560]{1,0:T(8,128)(2,1)S(1)} %get-tuple-element.46), channel_id=1, source_target_pairs={{0,12},{1,13},{2,14},{3,15},{4,0},{5,1},{6,2},{7,3},{8,4},{9,5},{1... | collective-permute-start | bytes 245768 | tf_op jit(solution)/shard_map/ppermute | solution.py:40
  21.2 0.5 collective-permute-start.8
  21.7 1.7 %collective-permute-start.7 = (bf16[48,640]{1,0:T(8,128)(2,1)S(1)}, bf16[48,640]{1,0:T(8,128)(2,1)S(1)}, u32[]{:S(2)}, u32[]{:S(2)}) collective-permute-start(bf16[48,640]{1,0:T(8,128)(2,1)S(1)} %get-tuple-element.28), channel_id=1, source_target_pairs={{0,8},{1,9},{2,10},{3,11},{4,12},{5,13},{6,14},{7,15},{8,0},{9,1},... | collective-permute-start | bytes 184328 | tf_op jit(solution)/shard_map/ppermute | solution.py:40
  23.4 2.7 %collective-permute-start.6 = (bf16[48,640]{1,0:T(8,128)(2,1)S(1)}, bf16[48,640]{1,0:T(8,128)(2,1)S(1)}, u32[]{:S(2)}, u32[]{:S(2)}) collective-permute-start(bf16[48,640]{1,0:T(8,128)(2,1)S(1)} %get-tuple-element.26.refs_0_), channel_id=1, source_target_pairs={{0,4},{1,5},{2,6},{3,7},{4,8},{5,9},{6,10},{7,11},{8,12},{9,13},{1... | collective-permute-start | bytes 184328 | tf_op jit(solution)/shard_map/ppermute | solution.py:40
  26.1 0.6 modulate.1
  26.8 4.7 %collective-permute-start.10 = (bf16[48,512]{1,0:T(8,128)(2,1)S(1)}, bf16[48,512]{1,0:T(8,128)(2,1)S(1)}, u32[]{:S(2)}, u32[]{:S(2)}) collective-permute-start(bf16[48,512]{1,0:T(8,128)(2,1)S(1)} %get-tuple-element.27.refs_0_), channel_id=1, source_target_pairs={{0,4},{1,5},{2,6},{3,7},{4,8},{5,9},{6,10},{7,11},{8,12},{9,13},{1... | collective-permute-start | bytes 147464 | tf_op jit(solution)/shard_map/ppermute | solution.py:40
  31.5 0.9 %collective-permute-done.7 = bf16[48,640]{1,0:T(8,128)(2,1)S(1)} collective-permute-done((bf16[48,640]{1,0:T(8,128)(2,1)S(1)}, bf16[48,640]{1,0:T(8,128)(2,1)S(1)}, u32[]{:S(2)}, u32[]{:S(2)}) %collective-permute-start.7) | collective-permute-done | bytes 61472 | tf_op jit(solution)/shard_map/ppermute | solution.py:40
  32.3 1.6 %collective-permute-start.9 = (bf16[192,640]{1,0:T(8,128)(2,1)S(1)}, bf16[192,640]{1,0:T(8,128)(2,1)S(1)}, u32[]{:S(2)}, u32[]{:S(2)}) collective-permute-start(bf16[192,640]{1,0:T(8,128)(2,1)S(1)} %pad_maximum_fusion.refs_0_), channel_id=1, source_target_pairs={{0,2},{1,3},{2,0},{3,1},{4,6},{5,7},{6,4},{7,5},{8,10},{9,11},{10,... | collective-permute-start | bytes 737288 | tf_op jit(solution)/shard_map/ppermute | solution.py:40
  33.9 1.5 %collective-permute-start.11 = (bf16[48,512]{1,0:T(8,128)(2,1)S(1)}, bf16[48,512]{1,0:T(8,128)(2,1)S(1)}, u32[]{:S(2)}, u32[]{:S(2)}) collective-permute-start(bf16[48,512]{1,0:T(8,128)(2,1)S(1)} %get-tuple-element.31), channel_id=1, source_target_pairs={{0,8},{1,9},{2,10},{3,11},{4,12},{5,13},{6,14},{7,15},{8,0},{9,1},... | collective-permute-start | bytes 147464 | tf_op jit(solution)/shard_map/ppermute | solution.py:40
  35.4 0.7 collective-permute-start.12
  36.1 3.4 %collective-permute-done.11 = bf16[48,512]{1,0:T(8,128)(2,1)S(1)} collective-permute-done((bf16[48,512]{1,0:T(8,128)(2,1)S(1)}, bf16[48,512]{1,0:T(8,128)(2,1)S(1)}, u32[]{:S(2)}, u32[]{:S(2)}) %collective-permute-start.11) | collective-permute-done | bytes 49184 | tf_op jit(solution)/shard_map/ppermute | solution.py:40
  39.5 0.8 collective-permute-done.12
  40.3 0.1 collective-permute-start.14
  40.4 0.3 route.2.refs_8_.weight_ref
  40.6 1.1 %collective-permute-start.15 = (bf16[192,512]{1,0:T(8,128)(2,1)S(1)}, bf16[192,512]{1,0:T(8,128)(2,1)S(1)}, u32[]{:S(2)}, u32[]{:S(2)}) collective-permute-start(bf16[192,512]{1,0:T(8,128)(2,1)S(1)} %constant_dynamic-update-slice_fusion.refs_0_.refs_7_), channel_id=1, source_target_pairs={{0,2},{1,3},{2,0},{3,1},{4,6},{5,7},{6,4},{7,5},{8,10},{9,11},{10,... | collective-permute-start | bytes 589832 | tf_op jit(solution)/shard_map/ppermute | solution.py:40
  41.8 0.1 collective-permute-done.14.refs_3_
  41.9 12.1 %experts.2 = (bf16[192,640]{1,0:T(8,128)(2,1)S(1)}, bf16[192,640]{1,0:T(8,128)(2,1)S(1)}, bf16[192,640]{1,0:T(8,128)(2,1)S(1)}, bf16[192,640]{1,0:T(8,128)(2,1)S(1)}) custom-call(bf16[192,640]{1,0:T(8,128)(2,1)S(1)} %pad_maximum_fusion.refs_0_, bf16[192,640]{1,0:T(8,128)(2,1)S(1)} %tie.12.refs_1_, bf16[192,640]{1,0:T(8,128)(2,1)S(1)} %collective-permute-done.13.refs_2_, ...), custom_call_target="tpu_custom_call" | custom-call | flops 5096079360 | bytes 26542080 | tf_op jit(solution)/shard_map/experts/pallas_call | solution.py:305
  54.0 0.2 collective-permute-start.17
  54.3 0.3 route.3.refs_8_.weight_ref
  54.5 0.4 collective-permute-start.19
  54.9 0.1 collective-permute-start.20
  55.1 0.6 collective-permute-done.17
  55.6 0.1 add_convert_fusion.1.refs_7_
  55.7 1.2 %collective-permute-start.18 = (bf16[192,640]{1,0:T(8,128)(2,1)S(1)}, bf16[192,640]{1,0:T(8,128)(2,1)S(1)}, u32[]{:S(2)}, u32[]{:S(2)}) collective-permute-start(bf16[192,640]{1,0:T(8,128)(2,1)S(1)} %add_convert_fusion.1.refs_7_), channel_id=1, source_target_pairs={{0,2},{1,3},{2,0},{3,1},{4,6},{5,7},{6,4},{7,5},{8,10},{9,11},{10,... | collective-permute-start | bytes 737288 | tf_op jit(solution)/shard_map/ppermute | solution.py:40
  56.9 11.6 %experts.3 = (bf16[192,512]{1,0:T(8,128)(2,1)S(1)}, bf16[192,512]{1,0:T(8,128)(2,1)S(1)}, bf16[192,512]{1,0:T(8,128)(2,1)S(1)}, bf16[192,512]{1,0:T(8,128)(2,1)S(1)}) custom-call(bf16[192,512]{1,0:T(8,128)(2,1)S(1)} %constant_dynamic-update-slice_fusion.refs_0_.refs_7_, bf16[192,512]{1,0:T(8,128)(2,1)S(1)} %tie.13.refs_0_.refs_1_, ...), custom_call_target="tpu_custom_call" | custom-call | flops 3822059520 | bytes 26542080 | tf_op jit(solution)/shard_map/experts/pallas_call | solution.py:305
  68.5 0.1 collective-permute-start.21
  68.6 0.6 collective-permute-start.16
  69.2 0.1 collective-permute-start.25
  69.2 0.7 collective-permute-done.21
  70.0 0.1 add_convert_fusion.3.refs_0_
  70.1 1.0 %collective-permute-start.26 = (bf16[192,512]{1,0:T(8,128)(2,1)S(1)}, bf16[192,512]{1,0:T(8,128)(2,1)S(1)}, u32[]{:S(2)}, u32[]{:S(2)}) collective-permute-start(bf16[192,512]{1,0:T(8,128)(2,1)S(1)} %add_convert_fusion.3.refs_0_), channel_id=1, source_target_pairs={{0,2},{1,3},{2,0},{3,1},{4,6},{5,7},{6,4},{7,5},{8,10},{9,11},{10,... | collective-permute-start | bytes 589832 | tf_op jit(solution)/shard_map/ppermute | solution.py:40
  71.1 0.1 add_convert_fusion
  71.2 2.2 %collective-permute-start.22 = (bf16[48,640]{1,0:T(8,128)(2,1)S(1)}, bf16[48,640]{1,0:T(8,128)(2,1)S(1)}, u32[]{:S(2)}, u32[]{:S(2)}) collective-permute-start(bf16[48,640]{1,0:T(8,128)(2,1)S(1)} %get-tuple-element.51), channel_id=1, source_target_pairs={{0,12},{1,13},{2,14},{3,15},{4,0},{5,1},{6,2},{7,3},{8,4},{9,5},{1... | collective-permute-start | bytes 184328 | tf_op jit(solution)/shard_map/ppermute | solution.py:40
  73.4 0.6 collective-permute-start.24
  74.1 3.0 %collective-permute-done.26 = bf16[192,512]{1,0:T(8,128)(2,1)S(1)} collective-permute-done((bf16[192,512]{1,0:T(8,128)(2,1)S(1)}, bf16[192,512]{1,0:T(8,128)(2,1)S(1)}, u32[]{:S(2)}, u32[]{:S(2)}) %collective-permute-start.26) | collective-permute-done | bytes 196640 | tf_op jit(solution)/shard_map/ppermute | solution.py:40
  77.1 0.1 add_convert_fusion.2
  77.2 2.0 %collective-permute-start.27 = (bf16[48,512]{1,0:T(8,128)(2,1)S(1)}, bf16[48,512]{1,0:T(8,128)(2,1)S(1)}, u32[]{:S(2)}, u32[]{:S(2)}) collective-permute-start(bf16[48,512]{1,0:T(8,128)(2,1)S(1)} %get-tuple-element.55), channel_id=1, source_target_pairs={{0,12},{1,13},{2,14},{3,15},{4,0},{5,1},{6,2},{7,3},{8,4},{9,5},{1... | collective-permute-start | bytes 147464 | tf_op jit(solution)/shard_map/ppermute | solution.py:40
  79.2 0.6 collective-permute-start.29
  79.8 0.4 collective-permute-done.23.refs_2_
  80.2 0.9 %combine.2 = bf16[16,2560]{1,0:T(8,128)(2,1)} custom-call(f32[16,4]{1,0:T(8,128)S(1)} %get-tuple-element.22.spot_ref, f32[16,2]{1,0:T(8,128)S(1)} %route.2.refs_8_.weight_ref, bf16[48,640]{1,0:T(8,128)(2,1)S(1)} %get-tuple-element.52.refs_0_, bf16[48,640]{1,0:T(8,128)(2,1)S(1)} %collective-permute-done.22.refs_1_, ...), custom_call_target="tpu_custom_call" | custom-call | tf_op jit(solution)/shard_map/combine/pallas_call | solution.py:355
  81.1 0.2 collective-permute-done.27.refs_1_
  81.3 2.9 %collective-permute-done.28.refs_2_ = bf16[48,512]{1,0:T(8,128)(2,1)S(1)} collective-permute-done((bf16[48,512]{1,0:T(8,128)(2,1)S(1)}, bf16[48,512]{1,0:T(8,128)(2,1)S(1)}, u32[]{:S(2)}, u32[]{:S(2)}) %collective-permute-start.28) | collective-permute-done | bytes 49184 | tf_op jit(solution)/shard_map/ppermute | solution.py:40
  84.2 0.8 collective-permute-done.29.refs_3_
  85.1 0.9 %combine.3 = bf16[16,2560]{1,0:T(8,128)(2,1)} custom-call(f32[16,4]{1,0:T(8,128)S(1)} %get-tuple-element.25.spot_ref, f32[16,2]{1,0:T(8,128)S(1)} %route.3.refs_8_.weight_ref, bf16[48,512]{1,0:T(8,128)(2,1)S(1)} %get-tuple-element.56.refs_0_, bf16[48,512]{1,0:T(8,128)(2,1)S(1)} %collective-permute-done.27.refs_1_, ...), custom_call_target="tpu_custom_call" | custom-call | tf_op jit(solution)/shard_map/combine/pallas_call | solution.py:355
  (62 shorter events, 0.5 us)
Async XLA Ops:
  0.6 1.4 %copy-start = (bf16[256,2560]{1,0:T(8,128)(2,1)S(1)}, bf16[256,2560]{1,0:T(8,128)(2,1)}, u32[]{:S(2)}) copy-start(bf16[256,2560]{1,0:T(8,128)(2,1)} %param.14) | copy-start | bytes 3932164
  2.0 1.0 %copy-start.7 = (s32[2]{0:T(128)S(1)}, s32[2]{0:T(128)}, u32[]{:S(2)}) copy-start(s32[2]{0:T(128)} %param.20) | copy-start | bytes 28
  2.0 1.2 %copy-start.5 = (s32[16,2]{0,1:T(2,128)S(1)}, s32[16,2]{0,1:T(2,128)}, u32[]{:S(2)}) copy-start(s32[16,2]{0,1:T(2,128)} %param.19) | copy-start | bytes 388
  2.0 1.2 %copy-start.6 = (s32[16,2]{0,1:T(2,128)S(1)}, s32[16,2]{0,1:T(2,128)}, u32[]{:S(2)}) copy-start(s32[16,2]{0,1:T(2,128)} %param.18) | copy-start | bytes 388
  2.0 1.2 %copy-start.3 = (f32[2560]{0:T(1024)S(1)}, f32[2560]{0:T(1024)}, u32[]{:S(2)}) copy-start(f32[2560]{0:T(1024)} %param.16) | copy-start | bytes 30724
  2.0 1.2 %copy-start.4 = (f32[2560]{0:T(1024)S(1)}, f32[2560]{0:T(1024)}, u32[]{:S(2)}) copy-start(f32[2560]{0:T(1024)} %param.15) | copy-start | bytes 30724
  2.4 1.8 %collective-permute-start = (bf16[64,2560]{1,0:T(8,128)(2,1)S(1)}, bf16[64,2560]{1,0:T(8,128)(2,1)S(1)}, u32[]{:S(2)}, u32[]{:S(2)}) collective-permute-start(bf16[64,2560]{1,0:T(8,128)(2,1)S(1)} %get-tuple-element.45), channel_id=1, source_target_pairs={{0,1},{1,0},{2,3},{3,2},{4,5},{5,4},{6,7},{7,6},{8,9},{9,8},{10,11... | collective-permute-start | bytes 983048 | tf_op jit(solution)/shard_map/ppermute | solution.py:40
  3.0 12.3 %collective-permute-start.1 = (bf16[64,2560]{1,0:T(8,128)(2,1)S(1)}, bf16[64,2560]{1,0:T(8,128)(2,1)S(1)}, u32[]{:S(2)}, u32[]{:S(2)}) collective-permute-start(bf16[64,2560]{1,0:T(8,128)(2,1)S(1)} %get-tuple-element.44), channel_id=1, source_target_pairs={{0,1},{1,0},{2,3},{3,2},{4,5},{5,4},{6,7},{7,6},{8,9},{9,8},{10,11... | collective-permute-start | bytes 983048 | tf_op jit(solution)/shard_map/ppermute | solution.py:40
  3.6 3.6 %copy-start.2 = (f32[2560,4]{0,1:T(4,128)S(1)}, f32[2560,4]{0,1:T(4,128)}, u32[]{:S(2)}) copy-start(f32[2560,4]{0,1:T(4,128)} %param.17) | copy-start | bytes 122884
  3.6 3.6 %copy-start.1 = (bf16[16,2560]{1,0:T(8,128)(2,1)S(1)}, bf16[16,2560]{1,0:T(8,128)(2,1)}, u32[]{:S(2)}) copy-start(bf16[16,2560]{1,0:T(8,128)(2,1)} %image_ref.1) | copy-start | bytes 245764
  4.3 11.0 %collective-permute-start.2 = (bf16[64,2560]{1,0:T(8,128)(2,1)S(1)}, bf16[64,2560]{1,0:T(8,128)(2,1)S(1)}, u32[]{:S(2)}, u32[]{:S(2)}) collective-permute-start(bf16[64,2560]{1,0:T(8,128)(2,1)S(1)} %fusion.1.refs_0_), channel_id=1, source_target_pairs={{0,2},{1,3},{2,0},{3,1},{4,6},{5,7},{6,4},{7,5},{8,10},{9,11},{10,... | collective-permute-start | bytes 983048 | tf_op jit(solution)/shard_map/ppermute | solution.py:40
  15.4 7.9 %collective-permute-start.3 = (bf16[16,2560]{1,0:T(8,128)(2,1)S(1)}, bf16[16,2560]{1,0:T(8,128)(2,1)S(1)}, u32[]{:S(2)}, u32[]{:S(2)}) collective-permute-start(bf16[16,2560]{1,0:T(8,128)(2,1)S(1)} %get-tuple-element.48), channel_id=1, source_target_pairs={{0,4},{1,5},{2,6},{3,7},{4,8},{5,9},{6,10},{7,11},{8,12},{9,13},{1... | collective-permute-start | bytes 245768 | tf_op jit(solution)/shard_map/ppermute | solution.py:40
  17.3 8.8 %collective-permute-start.4 = (bf16[16,2560]{1,0:T(8,128)(2,1)S(1)}, bf16[16,2560]{1,0:T(8,128)(2,1)S(1)}, u32[]{:S(2)}, u32[]{:S(2)}) collective-permute-start(bf16[16,2560]{1,0:T(8,128)(2,1)S(1)} %get-tuple-element.47), channel_id=1, source_target_pairs={{0,8},{1,9},{2,10},{3,11},{4,12},{5,13},{6,14},{7,15},{8,0},{9,1},... | collective-permute-start | bytes 245768 | tf_op jit(solution)/shard_map/ppermute | solution.py:40
  19.9 6.2 %collective-permute-start.5 = (bf16[16,2560]{1,0:T(8,128)(2,1)S(1)}, bf16[16,2560]{1,0:T(8,128)(2,1)S(1)}, u32[]{:S(2)}, u32[]{:S(2)}) collective-permute-start(bf16[16,2560]{1,0:T(8,128)(2,1)S(1)} %get-tuple-element.46), channel_id=1, source_target_pairs={{0,12},{1,13},{2,14},{3,15},{4,0},{5,1},{6,2},{7,3},{8,4},{9,5},{1... | collective-permute-start | bytes 245768 | tf_op jit(solution)/shard_map/ppermute | solution.py:40
  21.2 10.2 %collective-permute-start.8 = (bf16[48,640]{1,0:T(8,128)(2,1)S(1)}, bf16[48,640]{1,0:T(8,128)(2,1)S(1)}, u32[]{:S(2)}, u32[]{:S(2)}) collective-permute-start(bf16[48,640]{1,0:T(8,128)(2,1)S(1)} %get-tuple-element.29), channel_id=1, source_target_pairs={{0,12},{1,13},{2,14},{3,15},{4,0},{5,1},{6,2},{7,3},{8,4},{9,5},{1... | collective-permute-start | bytes 184328 | tf_op jit(solution)/shard_map/ppermute | solution.py:40
  21.7 10.7 %collective-permute-start.7 = (bf16[48,640]{1,0:T(8,128)(2,1)S(1)}, bf16[48,640]{1,0:T(8,128)(2,1)S(1)}, u32[]{:S(2)}, u32[]{:S(2)}) collective-permute-start(bf16[48,640]{1,0:T(8,128)(2,1)S(1)} %get-tuple-element.28), channel_id=1, source_target_pairs={{0,8},{1,9},{2,10},{3,11},{4,12},{5,13},{6,14},{7,15},{8,0},{9,1},... | collective-permute-start | bytes 184328 | tf_op jit(solution)/shard_map/ppermute | solution.py:40
  23.4 8.9 %collective-permute-start.6 = (bf16[48,640]{1,0:T(8,128)(2,1)S(1)}, bf16[48,640]{1,0:T(8,128)(2,1)S(1)}, u32[]{:S(2)}, u32[]{:S(2)}) collective-permute-start(bf16[48,640]{1,0:T(8,128)(2,1)S(1)} %get-tuple-element.26.refs_0_), channel_id=1, source_target_pairs={{0,4},{1,5},{2,6},{3,7},{4,8},{5,9},{6,10},{7,11},{8,12},{9,13},{1... | collective-permute-start | bytes 184328 | tf_op jit(solution)/shard_map/ppermute | solution.py:40
  26.8 9.4 %collective-permute-start.10 = (bf16[48,512]{1,0:T(8,128)(2,1)S(1)}, bf16[48,512]{1,0:T(8,128)(2,1)S(1)}, u32[]{:S(2)}, u32[]{:S(2)}) collective-permute-start(bf16[48,512]{1,0:T(8,128)(2,1)S(1)} %get-tuple-element.27.refs_0_), channel_id=1, source_target_pairs={{0,4},{1,5},{2,6},{3,7},{4,8},{5,9},{6,10},{7,11},{8,12},{9,13},{1... | collective-permute-start | bytes 147464 | tf_op jit(solution)/shard_map/ppermute | solution.py:40
  32.3 7.9 %collective-permute-start.9 = (bf16[192,640]{1,0:T(8,128)(2,1)S(1)}, bf16[192,640]{1,0:T(8,128)(2,1)S(1)}, u32[]{:S(2)}, u32[]{:S(2)}) collective-permute-start(bf16[192,640]{1,0:T(8,128)(2,1)S(1)} %pad_maximum_fusion.refs_0_), channel_id=1, source_target_pairs={{0,2},{1,3},{2,0},{3,1},{4,6},{5,7},{6,4},{7,5},{8,10},{9,11},{10,... | collective-permute-start | bytes 737288 | tf_op jit(solution)/shard_map/ppermute | solution.py:40
  33.9 7.8 %collective-permute-start.13 = (bf16[192,640]{1,0:T(8,128)(2,1)S(1)}, bf16[192,640]{1,0:T(8,128)(2,1)S(1)}, u32[]{:S(2)}, u32[]{:S(2)}) collective-permute-start(bf16[192,640]{1,0:T(8,128)(2,1)S(1)} %pad_maximum_fusion.refs_0_), channel_id=1, source_target_pairs={{0,1},{1,0},{2,3},{3,2},{4,5},{5,4},{6,7},{7,6},{8,9},{9,8},{10,11... | collective-permute-start | bytes 737288 | tf_op jit(solution)/shard_map/ppermute | solution.py:40
  33.9 5.6 %collective-permute-start.11 = (bf16[48,512]{1,0:T(8,128)(2,1)S(1)}, bf16[48,512]{1,0:T(8,128)(2,1)S(1)}, u32[]{:S(2)}, u32[]{:S(2)}) collective-permute-start(bf16[48,512]{1,0:T(8,128)(2,1)S(1)} %get-tuple-element.31), channel_id=1, source_target_pairs={{0,8},{1,9},{2,10},{3,11},{4,12},{5,13},{6,14},{7,15},{8,0},{9,1},... | collective-permute-start | bytes 147464 | tf_op jit(solution)/shard_map/ppermute | solution.py:40
  35.4 4.8 %collective-permute-start.12 = (bf16[48,512]{1,0:T(8,128)(2,1)S(1)}, bf16[48,512]{1,0:T(8,128)(2,1)S(1)}, u32[]{:S(2)}, u32[]{:S(2)}) collective-permute-start(bf16[48,512]{1,0:T(8,128)(2,1)S(1)} %get-tuple-element.32), channel_id=1, source_target_pairs={{0,12},{1,13},{2,14},{3,15},{4,0},{5,1},{6,2},{7,3},{8,4},{9,5},{1... | collective-permute-start | bytes 147464 | tf_op jit(solution)/shard_map/ppermute | solution.py:40
  40.3 1.6 %collective-permute-start.14 = (bf16[192,640]{1,0:T(8,128)(2,1)S(1)}, bf16[192,640]{1,0:T(8,128)(2,1)S(1)}, u32[]{:S(2)}, u32[]{:S(2)}) collective-permute-start(bf16[192,640]{1,0:T(8,128)(2,1)S(1)} %tie.12.refs_1_), channel_id=1, source_target_pairs={{0,1},{1,0},{2,3},{3,2},{4,5},{5,4},{6,7},{7,6},{8,9},{9,8},{10,11... | collective-permute-start | bytes 737288 | tf_op jit(solution)/shard_map/ppermute | solution.py:40
  40.6 13.3 %collective-permute-start.15 = (bf16[192,512]{1,0:T(8,128)(2,1)S(1)}, bf16[192,512]{1,0:T(8,128)(2,1)S(1)}, u32[]{:S(2)}, u32[]{:S(2)}) collective-permute-start(bf16[192,512]{1,0:T(8,128)(2,1)S(1)} %constant_dynamic-update-slice_fusion.refs_0_.refs_7_), channel_id=1, source_target_pairs={{0,2},{1,3},{2,0},{3,1},{4,6},{5,7},{6,4},{7,5},{8,10},{9,11},{10,... | collective-permute-start | bytes 589832 | tf_op jit(solution)/shard_map/ppermute | solution.py:40
  54.0 1.6 %collective-permute-start.17 = (bf16[192,640]{1,0:T(8,128)(2,1)S(1)}, bf16[192,640]{1,0:T(8,128)(2,1)S(1)}, u32[]{:S(2)}, u32[]{:S(2)}) collective-permute-start(bf16[192,640]{1,0:T(8,128)(2,1)S(1)} %tie.15), channel_id=1, source_target_pairs={{0,1},{1,0},{2,3},{3,2},{4,5},{5,4},{6,7},{7,6},{8,9},{9,8},{10,11... | collective-permute-start | bytes 737288 | tf_op jit(solution)/shard_map/ppermute | solution.py:40
  54.5 2.3 %collective-permute-start.19 = (bf16[192,512]{1,0:T(8,128)(2,1)S(1)}, bf16[192,512]{1,0:T(8,128)(2,1)S(1)}, u32[]{:S(2)}, u32[]{:S(2)}) collective-permute-start(bf16[192,512]{1,0:T(8,128)(2,1)S(1)} %constant_dynamic-update-slice_fusion.refs_0_.refs_7_), channel_id=1, source_target_pairs={{0,1},{1,0},{2,3},{3,2},{4,5},{5,4},{6,7},{7,6},{8,9},{9,8},{10,11... | collective-permute-start | bytes 589832 | tf_op jit(solution)/shard_map/ppermute | solution.py:40
  54.9 1.9 %collective-permute-start.20 = (bf16[192,512]{1,0:T(8,128)(2,1)S(1)}, bf16[192,512]{1,0:T(8,128)(2,1)S(1)}, u32[]{:S(2)}, u32[]{:S(2)}) collective-permute-start(bf16[192,512]{1,0:T(8,128)(2,1)S(1)} %tie.13.refs_0_.refs_1_), channel_id=1, source_target_pairs={{0,1},{1,0},{2,3},{3,2},{4,5},{5,4},{6,7},{7,6},{8,9},{9,8},{10,11... | collective-permute-start | bytes 589832 | tf_op jit(solution)/shard_map/ppermute | solution.py:40
  55.7 12.7 %collective-permute-start.18 = (bf16[192,640]{1,0:T(8,128)(2,1)S(1)}, bf16[192,640]{1,0:T(8,128)(2,1)S(1)}, u32[]{:S(2)}, u32[]{:S(2)}) collective-permute-start(bf16[192,640]{1,0:T(8,128)(2,1)S(1)} %add_convert_fusion.1.refs_7_), channel_id=1, source_target_pairs={{0,2},{1,3},{2,0},{3,1},{4,6},{5,7},{6,4},{7,5},{8,10},{9,11},{10,... | collective-permute-start | bytes 737288 | tf_op jit(solution)/shard_map/ppermute | solution.py:40
  68.5 1.5 %collective-permute-start.21 = (bf16[192,512]{1,0:T(8,128)(2,1)S(1)}, bf16[192,512]{1,0:T(8,128)(2,1)S(1)}, u32[]{:S(2)}, u32[]{:S(2)}) collective-permute-start(bf16[192,512]{1,0:T(8,128)(2,1)S(1)} %tie.17), channel_id=1, source_target_pairs={{0,1},{1,0},{2,3},{3,2},{4,5},{5,4},{6,7},{7,6},{8,9},{9,8},{10,11... | collective-permute-start | bytes 589832 | tf_op jit(solution)/shard_map/ppermute | solution.py:40
  68.6 2.5 %collective-permute-start.16 = (bf16[192,640]{1,0:T(8,128)(2,1)S(1)}, bf16[192,640]{1,0:T(8,128)(2,1)S(1)}, u32[]{:S(2)}, u32[]{:S(2)}) collective-permute-start(bf16[192,640]{1,0:T(8,128)(2,1)S(1)} %tie.14), channel_id=1, source_target_pairs={{0,1},{1,0},{2,3},{3,2},{4,5},{5,4},{6,7},{7,6},{8,9},{9,8},{10,11... | collective-permute-start | bytes 737288 | tf_op jit(solution)/shard_map/ppermute | solution.py:40
  69.2 4.9 %collective-permute-start.25 = (bf16[192,512]{1,0:T(8,128)(2,1)S(1)}, bf16[192,512]{1,0:T(8,128)(2,1)S(1)}, u32[]{:S(2)}, u32[]{:S(2)}) collective-permute-start(bf16[192,512]{1,0:T(8,128)(2,1)S(1)} %tie.19), channel_id=1, source_target_pairs={{0,1},{1,0},{2,3},{3,2},{4,5},{5,4},{6,7},{7,6},{8,9},{9,8},{10,11... | collective-permute-start | bytes 589832 | tf_op jit(solution)/shard_map/ppermute | solution.py:40
  70.1 7.0 %collective-permute-start.26 = (bf16[192,512]{1,0:T(8,128)(2,1)S(1)}, bf16[192,512]{1,0:T(8,128)(2,1)S(1)}, u32[]{:S(2)}, u32[]{:S(2)}) collective-permute-start(bf16[192,512]{1,0:T(8,128)(2,1)S(1)} %add_convert_fusion.3.refs_0_), channel_id=1, source_target_pairs={{0,2},{1,3},{2,0},{3,1},{4,6},{5,7},{6,4},{7,5},{8,10},{9,11},{10,... | collective-permute-start | bytes 589832 | tf_op jit(solution)/shard_map/ppermute | solution.py:40
  71.2 8.0 %collective-permute-start.22 = (bf16[48,640]{1,0:T(8,128)(2,1)S(1)}, bf16[48,640]{1,0:T(8,128)(2,1)S(1)}, u32[]{:S(2)}, u32[]{:S(2)}) collective-permute-start(bf16[48,640]{1,0:T(8,128)(2,1)S(1)} %get-tuple-element.51), channel_id=1, source_target_pairs={{0,12},{1,13},{2,14},{3,15},{4,0},{5,1},{6,2},{7,3},{8,4},{9,5},{1... | collective-permute-start | bytes 184328 | tf_op jit(solution)/shard_map/ppermute | solution.py:40
  73.4 6.8 %collective-permute-start.23 = (bf16[48,640]{1,0:T(8,128)(2,1)S(1)}, bf16[48,640]{1,0:T(8,128)(2,1)S(1)}, u32[]{:S(2)}, u32[]{:S(2)}) collective-permute-start(bf16[48,640]{1,0:T(8,128)(2,1)S(1)} %get-tuple-element.50), channel_id=1, source_target_pairs={{0,8},{1,9},{2,10},{3,11},{4,12},{5,13},{6,14},{7,15},{8,0},{9,1},... | collective-permute-start | bytes 184328 | tf_op jit(solution)/shard_map/ppermute | solution.py:40
  73.4 6.8 %collective-permute-start.24 = (bf16[48,640]{1,0:T(8,128)(2,1)S(1)}, bf16[48,640]{1,0:T(8,128)(2,1)S(1)}, u32[]{:S(2)}, u32[]{:S(2)}) collective-permute-start(bf16[48,640]{1,0:T(8,128)(2,1)S(1)} %get-tuple-element.49), channel_id=1, source_target_pairs={{0,4},{1,5},{2,6},{3,7},{4,8},{5,9},{6,10},{7,11},{8,12},{9,13},{1... | collective-permute-start | bytes 184328 | tf_op jit(solution)/shard_map/ppermute | solution.py:40
  77.2 4.1 %collective-permute-start.27 = (bf16[48,512]{1,0:T(8,128)(2,1)S(1)}, bf16[48,512]{1,0:T(8,128)(2,1)S(1)}, u32[]{:S(2)}, u32[]{:S(2)}) collective-permute-start(bf16[48,512]{1,0:T(8,128)(2,1)S(1)} %get-tuple-element.55), channel_id=1, source_target_pairs={{0,12},{1,13},{2,14},{3,15},{4,0},{5,1},{6,2},{7,3},{8,4},{9,5},{1... | collective-permute-start | bytes 147464 | tf_op jit(solution)/shard_map/ppermute | solution.py:40
  79.2 5.1 %collective-permute-start.28 = (bf16[48,512]{1,0:T(8,128)(2,1)S(1)}, bf16[48,512]{1,0:T(8,128)(2,1)S(1)}, u32[]{:S(2)}, u32[]{:S(2)}) collective-permute-start(bf16[48,512]{1,0:T(8,128)(2,1)S(1)} %get-tuple-element.54), channel_id=1, source_target_pairs={{0,8},{1,9},{2,10},{3,11},{4,12},{5,13},{6,14},{7,15},{8,0},{9,1},... | collective-permute-start | bytes 147464 | tf_op jit(solution)/shard_map/ppermute | solution.py:40
  79.2 5.9 %collective-permute-start.29 = (bf16[48,512]{1,0:T(8,128)(2,1)S(1)}, bf16[48,512]{1,0:T(8,128)(2,1)S(1)}, u32[]{:S(2)}, u32[]{:S(2)}) collective-permute-start(bf16[48,512]{1,0:T(8,128)(2,1)S(1)} %get-tuple-element.53), channel_id=1, source_target_pairs={{0,4},{1,5},{2,6},{3,7},{4,8},{5,9},{6,10},{7,11},{8,12},{9,13},{1... | collective-permute-start | bytes 147464 | tf_op jit(solution)/shard_map/ppermute | solution.py:40

commit v8 on v7

--- a/solution.py
+++ b/solution.py
@@ -24,13 +24,13 @@
         self.pair = (index // 2) % self.pairs
         self.core = index % 2
 
-    def send(self, value, axis, step):
+    def swap(self, value, axis, step):
         moves = []
         for expert in range(self.experts):
             for pair in range(self.pairs):
                 for core in range(2):
                     to = [expert, pair, core]
-                    to[axis] = (to[axis] + step) % (self.experts, self.pairs, 2)[axis]
+                    to[axis] ^= step
                     moves.append(
                         (
                             (expert * self.pairs + pair) * 2 + core,
@@ -58,7 +58,7 @@
 def place(chosen, packing, experts, out_ref):
     index = lax.axis_index("dev")
     rows = chosen.shape[1]
-    relative = lax.rem(chosen + (experts - index // (lax.axis_size("dev") // experts)), experts)
+    relative = chosen ^ (index // (lax.axis_size("dev") // experts))
     expert_at = lax.broadcasted_iota(jnp.int32, (experts, rows), 0)
     routed = (relative[0:1, :] == expert_at) | (relative[1:2, :] == expert_at)
     routed = routed & (chosen[0:1, :] >= 0)
@@ -66,10 +66,10 @@
     before = (at[0] < at[1]).astype(jnp.float32)
     spot = jnp.dot(routed.astype(jnp.float32), before, preferred_element_type=jnp.float32)
     spot = spot + expert_at.astype(jnp.float32) * float(packing.rows)
-    spot = jnp.where(routed, spot, -65536.0)
     for t in range(2):
         own = jnp.where(relative[t : t + 1, :] == expert_at, spot, 0.0)
         own = jnp.sum(own, axis=0, keepdims=True)
+        own = jnp.where(chosen[t : t + 1, :] >= 0, own, -65536.0)
         for column, value in ((t, own), (2 + t, chosen[t : t + 1, :].astype(jnp.float32))):
             out_ref[:, column : column + 1] = jnp.sum(
                 jnp.where(at[0] == at[1], value, 0.0), axis=1, keepdims=True
@@ -202,7 +202,7 @@
 
 
 def cuts(units):
-    edges = [0, units] if units <= 1024 else [0, 256, 768, 1280, units]
+    edges = [0, units] if units <= 1024 else [0, 384, 1152, units]
     return list(zip(edges[:-1], edges[1:]))
 
 
@@ -210,18 +210,20 @@
     row_refs = refs[:count]
     gate_hbm, up_hbm, down_hbm = refs[count : count + 3]
     out_refs = refs[count + 3 + after : 2 * count + 3 + after]
-    gate_ref, up_ref, down_ref, rows_ref, total_ref, packed_ref, sems = refs[2 * count + 3 + after :]
+    inner_ref, down_ref, rows_ref, total_ref, packed_ref, sems = refs[2 * count + 3 + after :]
     rows = total_ref.shape[1]
     units = gate_hbm.shape[0]
     unit_cuts = cuts(units)
     copies = []
     for i, (lo, hi) in enumerate(unit_cuts):
         for t, (source, target) in enumerate(
-            ((gate_hbm, gate_ref), (up_hbm, up_ref), (down_hbm, down_ref))
+            (
+                (gate_hbm, inner_ref.at[2 * lo : lo + hi]),
+                (up_hbm, inner_ref.at[lo + hi : 2 * hi]),
+                (down_hbm, down_ref.at[lo:hi]),
+            )
         ):
-            copies.append(
-                pltpu.make_async_copy(source.at[lo:hi], target.at[lo:hi], sems.at[3 * i + t])
-            )
+            copies.append(pltpu.make_async_copy(source.at[lo:hi], target, sems.at[3 * i + t]))
     for copy in copies[:6]:
         copy.start()
 
@@ -259,11 +261,11 @@
     features = gate_hbm.shape[1]
     middle = features // 256 * 128
 
-    def product(weight_ref, lo, hi):
+    def product(lo, hi):
         return jnp.dot(
-            weight_ref[lo:hi, :middle], rows_ref[:middle, :], preferred_element_type=jnp.float32
+            inner_ref[lo:hi, :middle], rows_ref[:middle, :], preferred_element_type=jnp.float32
         ) + jnp.dot(
-            weight_ref[lo:hi, middle:], rows_ref[middle:, :], preferred_element_type=jnp.float32
+            inner_ref[lo:hi, middle:], rows_ref[middle:, :], preferred_element_type=jnp.float32
         )
 
     hidden = None
@@ -274,8 +276,8 @@
         copies[3 * i + 1].wait()
         for copy in copies[3 * (i + 2) : 3 * (i + 3)]:
             copy.start()
-        gate = product(gate_ref, lo, hi)
-        up = product(up_ref, lo, hi)
+        inner = product(2 * lo, 2 * hi)
+        gate, up = inner[: hi - lo], inner[hi - lo :]
         if i > 0:
             down(i - 1, hidden)
         hidden = (gate * jax.nn.sigmoid(gate) * up).T[0:rows].astype(jnp.bfloat16)
@@ -308,8 +310,7 @@
         in_specs=[VMEM] * len(arrays) + [HBM] * 3 + [ANY] * len(after),
         out_specs=[VMEM] * len(arrays),
         scratch_shapes=[
-            pltpu.VMEM((units, features), jnp.bfloat16),
-            pltpu.VMEM((units, features), jnp.bfloat16),
+            pltpu.VMEM((2 * units, features), jnp.bfloat16),
             pltpu.VMEM((units, features), jnp.bfloat16),
             pltpu.VMEM((features, -(-rows // 128) * 128), jnp.bfloat16),
             pltpu.VMEM((features // 128, rows, 128), jnp.float32),
@@ -365,12 +366,19 @@
 def partial_captions(text_hidden, caption_weight, grid):
     groups = grid.pairs * 2
     rows = text_hidden.shape[0] // (grid.experts * groups)
-    depth = caption_weight.shape[0]
-    text = text_hidden.reshape(grid.experts, grid.pairs, 2, rows, depth)
-    text = jnp.roll(text, -grid.expert, axis=0)
-    text = jnp.roll(text, -1 - grid.pair, axis=1)
-    text = jnp.roll(text, -1 - grid.core, axis=2)
-    text = jnp.transpose(text, (2, 1, 0, 3, 4)).reshape(2, -1, depth)
+    text = [
+        [
+            lax.dynamic_slice_in_dim(
+                text_hidden,
+                (((grid.expert ^ e) * grid.pairs + (grid.pair ^ p)) * 2 + (grid.core ^ c)) * rows,
+                rows,
+            )
+            for p in list(range(1, grid.pairs)) + [0]
+            for e in range(grid.experts)
+        ]
+        for c in (1, 0)
+    ]
+    text = [jnp.concatenate(part, axis=0) for part in text]
     other, own = [
         jnp.dot(text[c], caption_weight, preferred_element_type=jnp.float32).astype(kind)
         for c, kind in enumerate((jnp.bfloat16, jnp.float32))
@@ -408,37 +416,37 @@
         return [value[k * rows : (k + 1) * rows] for k in range(count)]
 
     def to_experts(blocks):
-        return [grid.send(blocks[k], 0, k) for k in range(1, experts)]
+        return [grid.swap(blocks[k], 0, k) for k in range(1, experts)]
 
     def to_pairs(first):
-        return [first] + [grid.send(first, 1, k) for k in range(1, pairs)]
+        return [first] + [grid.swap(first, 1, k) for k in range(1, pairs)]
 
     def over_cores(values):
-        return [grid.send(value, 2, 1) for value in values]
+        return [grid.swap(value, 2, 1) for value in values]
 
     def join_cores(results):
         own, other = results[:pairs], results[pairs:]
         sums = [None] * pairs
         for k in list(range(1, pairs)) + [0]:
-            sums[k] = own[k].astype(wide) + grid.send(other[k], 2, 1).astype(wide)
+            sums[k] = own[k].astype(wide) + grid.swap(other[k], 2, 1).astype(wide)
         return sums[0], [value.astype(narrow) for value in sums[1:]]
 
     def from_pairs(crossing):
-        return [grid.send(value, 1, -k) for k, value in enumerate(crossing, 1)]
-
-    def from_experts(kept, received):
+        return [grid.swap(value, 1, k) for k, value in enumerate(crossing, 1)]
+
+    def from_experts(kept, received, high, first=0):
         total = kept
         for value in received:
             total = total + value.astype(wide)
-        parts = split(total.astype(narrow), experts)
-        return [parts[0]] + [grid.send(parts[k], 0, -k) for k in range(1, experts)]
+        parts = split(total.astype(narrow), kept.shape[0] // high)
+        return [grid.swap(part, 0, k) if k else part for k, part in enumerate(parts, first)]
 
     partial = partial_captions(text_hidden, caption_weight, grid)
     sums = [
-        partial[pairs + i] + grid.send(partial[i], 2, 1).astype(wide) for i in range(pairs)
+        partial[pairs + i] + grid.swap(partial[i], 2, 1).astype(wide) for i in range(pairs)
     ]
     crossing = [value.astype(narrow) for value in sums[:-1]]
-    received = [grid.send(value, 1, k) for k, value in enumerate(crossing, 1)]
+    received = [grid.swap(value, 1, k) for k, value in enumerate(crossing, 1)]
 
     rows = text_hidden.shape[0] // devices
     position = grid.index * rows + jnp.arange(rows, dtype=jnp.int32)
@@ -453,19 +461,19 @@
     )
     image_first = [blocks[0]] + to_experts(blocks)
 
-    received[0] = tie(received[0], blocks[1:2])
+    received[0] = tie(received[0], image_first[1:])
     total = sums[-1]
     for value in received:
         total = total + value.astype(wide)
     parts = split(total, experts)
-    terms = [parts[0]] + to_experts([part.astype(narrow) for part in parts])
+    sent = [part.astype(narrow) for part in parts]
+    terms = [parts[0]] + to_experts(sent)
+    image_first = jnp.concatenate([tie(image_first[0], sent[1:])] + image_first[1:], axis=0)
+    image_own = to_pairs(image_first)
     caption_normed, blocks = modulate(terms, caption_spot, small, caption_packing, experts)
     caption_first = jnp.concatenate([blocks[0]] + to_experts(blocks), axis=0)
     caption_own = to_pairs(caption_first)
-
-    image_first = jnp.concatenate([tie(image_first[0], blocks[1:2])] + image_first[1:], axis=0)
-    image_own = to_pairs(image_first)
-    image_own = image_own[:1] + [tie(value, [caption_first]) for value in image_own[1:]]
+    image_own = image_own[:1] + [tie(value, blocks[1:2]) for value in image_own[1:]]
     image_arrays = image_own + over_cores(image_own)
 
     image_weights = route(image_normed, image_spot, small)
@@ -494,9 +502,14 @@
     ]
     caption_kept, caption_crossing = join_cores(caption_results)
     image_received = [tie(value, caption_crossing[:1]) for value in image_received]
-    caption_received = from_pairs(caption_crossing)
-    image_blocks = from_experts(image_kept, image_received)
-    caption_blocks = from_experts(caption_kept, caption_received)
+    image_blocks = from_experts(image_kept, image_received, image_packing.rows)
+    caption_blocks = [None] * experts
+    high = caption_packing.rows
+    for lo, hi in ((experts // 2, experts), (0, experts // 2)):
+        strip = slice(lo * high, hi * high)
+        caption_blocks[lo:hi] = from_experts(
+            caption_kept[strip], from_pairs([value[strip] for value in caption_crossing]), high, lo
+        )
 
     rows = image_rows.shape[0]
     image_out = combine(image_spot, image_weights, image_blocks, image_packing, rows, features)

time: 86.1 us -> 92.1 us (1.070)
  local copies, waits for them, and re-layouts: 0.25 us -> 6.04 us
  Pallas kernels: 27.6 us -> 33 us
  waiting for transfers between devices: 21.5 us -> 18 us
  starting transfers between devices: 32.9 us -> 31.4 us
  other arithmetic: 1.82 us -> 0.7 us
    pallas_call x2, Pallas kernels: 23.7 us -> 29 us  [expert_rows(): pl.pallas_call(functools.partial(expert_kernel, packing, len(arrays), len...]
    unnamed x19 -> x26, local copies, waits for them, and re-layouts: 0.09 us -> 5.17 us
    ppermute x30 -> x31, waiting for transfers between devices: 21.5 us -> 18 us  [swap(): return lax.ppermute(value, 'dev', moves)]
    ppermute x30 -> x31, starting transfers between devices: 32.9 us -> 31.4 us  [swap(): return lax.ppermute(value, 'dev', moves)]
    concatenate x3 -> x1, other arithmetic: 1.14 us -> 0.02 us  [local(): jnp.concatenate([tie(image_first[0], sent[1:])] + image_first[1:], axis=0)]
  transfers between devices with their start and end apart: 30 -> 31, of which waited for: 13 -> 11; matrix products, arithmetic and copies ran while one was open for 1% -> 1% of each run, Pallas kernels for 31% -> 35%
where the time goes in v8:
time: 92.1 us; the launch traced here: 91.1 us
  Pallas kernels  33 us (36%)
  starting transfers between devices  31.4 us (34%)
  waiting for transfers between devices  18 us (20%)
  local copies, waits for them, and re-layouts  6.04 us (7%)
  between operations  1.24 us (1%)
    ppermute x31, starting transfers between devices, swap(): return lax.ppermute(value, 'dev', moves)  31.4 us
    pallas_call x2, Pallas kernels, expert_rows(): pl.pallas_call(functools.partial(expert_kernel, packing, len(arrays), len...  29 us
    ppermute x31, waiting for transfers between devices, swap(): return lax.ppermute(value, 'dev', moves)  18 us
    unnamed x26, local copies, waits for them, and re-layouts  5.17 us
  transfers between devices with their start and end apart: 31, of which 11 were waited for; matrix products, arithmetic and copies ran while one was open for 1% of the time, Pallas kernels for 35%

profile of v8, /device:TPU:0, one launch (start us, length us, event | category | flops | bytes accessed | tf_op | source)
XLA Modules:
  0.0 91.1 jit_solution(609869849468733913)
XLA Ops:
  0.8 0.8 constant_dynamic-update-slice_fusion.15
  1.6 0.7 constant_dynamic-update-slice_fusion.14
  2.3 0.7 constant_dynamic-update-slice_fusion.13
  3.0 0.7 constant_dynamic-update-slice_fusion.12
  3.8 0.7 constant_dynamic-update-slice_fusion.11
  4.5 0.7 constant_dynamic-update-slice_fusion.10
  5.2 0.7 constant_dynamic-update-slice_fusion.9
  5.9 0.7 constant_dynamic-update-slice_fusion.8
  6.7 0.3 convolution_convert_fusion
  7.1 0.5 collective-permute-start.1
  7.6 0.1 collective-permute-start
  7.7 0.1 fusion.4
  7.9 0.3 fusion.14
  8.3 1.1 %collective-permute-done = bf16[64,2560]{1,0:T(8,128)(2,1)S(1)} collective-permute-done((bf16[64,2560]{1,0:T(8,128)(2,1)S(1)}, bf16[64,2560]{1,0:T(8,128)(2,1)S(1)}, u32[]{:S(2)}, u32[]{:S(2)}) %collective-permute-start) | collective-permute-done | bytes 327712 | tf_op jit(solution)/shard_map/ppermute | solution.py:40
  9.3 0.1 fusion.1.refs_0_
  9.4 2.9 %collective-permute-start.2 = (bf16[64,2560]{1,0:T(8,128)(2,1)S(1)}, bf16[64,2560]{1,0:T(8,128)(2,1)S(1)}, u32[]{:S(2)}, u32[]{:S(2)}) collective-permute-start(bf16[64,2560]{1,0:T(8,128)(2,1)S(1)} %fusion.1.refs_0_), channel_id=1, source_target_pairs={{0,2},{1,3},{2,0},{3,1},{4,6},{5,7},{6,4},{7,5},{8,10},{9,11},{10,... | collective-permute-start | bytes 983048 | tf_op jit(solution)/shard_map/ppermute | solution.py:40
  12.4 0.8 prepare.1
  13.2 1.6 %collective-permute-start.3 = (bf16[48,640]{1,0:T(8,128)(2,1)S(1)}, bf16[48,640]{1,0:T(8,128)(2,1)S(1)}, u32[]{:S(2)}, u32[]{:S(2)}) collective-permute-start(bf16[48,640]{1,0:T(8,128)(2,1)S(1)} %get-tuple-element.25), channel_id=1, source_target_pairs={{0,4},{1,5},{2,6},{3,7},{4,0},{5,1},{6,2},{7,3},{8,12},{9,13},{10,... | collective-permute-start | bytes 184328 | tf_op jit(solution)/shard_map/ppermute | solution.py:40
  14.9 2.6 %collective-permute-start.4 = (bf16[48,640]{1,0:T(8,128)(2,1)S(1)}, bf16[48,640]{1,0:T(8,128)(2,1)S(1)}, u32[]{:S(2)}, u32[]{:S(2)}) collective-permute-start(bf16[48,640]{1,0:T(8,128)(2,1)S(1)} %get-tuple-element.26), channel_id=1, source_target_pairs={{0,8},{1,9},{2,10},{3,11},{4,12},{5,13},{6,14},{7,15},{8,0},{9,1},... | collective-permute-start | bytes 184328 | tf_op jit(solution)/shard_map/ppermute | solution.py:40
  17.5 0.2 collective-permute-start.5
  17.7 3.6 %collective-permute-done.4.refs_1_ = bf16[48,640]{1,0:T(8,128)(2,1)S(1)} collective-permute-done((bf16[48,640]{1,0:T(8,128)(2,1)S(1)}, bf16[48,640]{1,0:T(8,128)(2,1)S(1)}, u32[]{:S(2)}, u32[]{:S(2)}) %collective-permute-start.4) | collective-permute-done | bytes 61472 | tf_op jit(solution)/shard_map/ppermute | solution.py:40
  21.2 2.2 %collective-permute-done.5.refs_2_ = bf16[48,640]{1,0:T(8,128)(2,1)S(1)} collective-permute-done((bf16[48,640]{1,0:T(8,128)(2,1)S(1)}, bf16[48,640]{1,0:T(8,128)(2,1)S(1)}, u32[]{:S(2)}, u32[]{:S(2)}) %collective-permute-start.5) | collective-permute-done | bytes 61472 | tf_op jit(solution)/shard_map/ppermute | solution.py:40
  23.5 0.1 fusion.6
  23.7 0.6 collective-permute-start.6
  24.3 1.7 %collective-permute-start.9 = (bf16[16,2560]{1,0:T(8,128)(2,1)S(1)}, bf16[16,2560]{1,0:T(8,128)(2,1)S(1)}, u32[]{:S(2)}, u32[]{:S(2)}) collective-permute-start(bf16[16,2560]{1,0:T(8,128)(2,1)S(1)} %get-tuple-element.48.refs_2_), channel_id=1, source_target_pairs={{0,12},{1,13},{2,14},{3,15},{4,8},{5,9},{6,10},{7,11},{8,4},{9,5},... | collective-permute-start | bytes 245768 | tf_op jit(solution)/shard_map/ppermute | solution.py:40
  26.0 2.7 %collective-permute-start.7 = (bf16[16,2560]{1,0:T(8,128)(2,1)S(1)}, bf16[16,2560]{1,0:T(8,128)(2,1)S(1)}, u32[]{:S(2)}, u32[]{:S(2)}) collective-permute-start(bf16[16,2560]{1,0:T(8,128)(2,1)S(1)} %get-tuple-element.50.refs_0_), channel_id=1, source_target_pairs={{0,4},{1,5},{2,6},{3,7},{4,0},{5,1},{6,2},{7,3},{8,12},{9,13},{10,... | collective-permute-start | bytes 245768 | tf_op jit(solution)/shard_map/ppermute | solution.py:40
  28.7 0.3 route.2.refs_8_.weight_ref
  29.0 2.3 %collective-permute-done.9.refs_3_ = bf16[16,2560]{1,0:T(8,128)(2,1)S(1)} collective-permute-done((bf16[16,2560]{1,0:T(8,128)(2,1)S(1)}, bf16[16,2560]{1,0:T(8,128)(2,1)S(1)}, u32[]{:S(2)}, u32[]{:S(2)}) %collective-permute-start.9) | collective-permute-done | bytes 81952 | tf_op jit(solution)/shard_map/ppermute | solution.py:40
  31.4 1.4 %collective-permute-done.8.refs_2_ = bf16[16,2560]{1,0:T(8,128)(2,1)S(1)} collective-permute-done((bf16[16,2560]{1,0:T(8,128)(2,1)S(1)}, bf16[16,2560]{1,0:T(8,128)(2,1)S(1)}, u32[]{:S(2)}, u32[]{:S(2)}) %collective-permute-start.8) | collective-permute-done | bytes 81952 | tf_op jit(solution)/shard_map/ppermute | solution.py:40
  32.8 0.6 modulate.1
  33.5 0.9 %collective-permute-start.13 = (bf16[48,512]{1,0:T(8,128)(2,1)S(1)}, bf16[48,512]{1,0:T(8,128)(2,1)S(1)}, u32[]{:S(2)}, u32[]{:S(2)}) collective-permute-start(bf16[48,512]{1,0:T(8,128)(2,1)S(1)} %get-tuple-element.31), channel_id=1, source_target_pairs={{0,8},{1,9},{2,10},{3,11},{4,12},{5,13},{6,14},{7,15},{8,0},{9,1},... | collective-permute-start | bytes 147464 | tf_op jit(solution)/shard_map/ppermute | solution.py:40
  34.4 1.9 %collective-permute-start.14 = (bf16[48,512]{1,0:T(8,128)(2,1)S(1)}, bf16[48,512]{1,0:T(8,128)(2,1)S(1)}, u32[]{:S(2)}, u32[]{:S(2)}) collective-permute-start(bf16[48,512]{1,0:T(8,128)(2,1)S(1)} %get-tuple-element.32), channel_id=1, source_target_pairs={{0,12},{1,13},{2,14},{3,15},{4,8},{5,9},{6,10},{7,11},{8,4},{9,5},... | collective-permute-start | bytes 147464 | tf_op jit(solution)/shard_map/ppermute | solution.py:40
  36.3 0.8 collective-permute-start.12
  37.0 0.1 collective-permute-start.11
  37.1 3.7 %collective-permute-done.12 = bf16[48,512]{1,0:T(8,128)(2,1)S(1)} collective-permute-done((bf16[48,512]{1,0:T(8,128)(2,1)S(1)}, bf16[48,512]{1,0:T(8,128)(2,1)S(1)}, u32[]{:S(2)}, u32[]{:S(2)}) %collective-permute-start.12) | collective-permute-done | bytes 49184 | tf_op jit(solution)/shard_map/ppermute | solution.py:40
  40.9 1.2 %collective-permute-start.15 = (bf16[192,512]{1,0:T(8,128)(2,1)S(1)}, bf16[192,512]{1,0:T(8,128)(2,1)S(1)}, u32[]{:S(2)}, u32[]{:S(2)}) collective-permute-start(bf16[192,512]{1,0:T(8,128)(2,1)S(1)} %constant_dynamic-update-slice_fusion.16.refs_7_.refs_0_), channel_id=1, source_target_pairs={{0,2},{1,3},{2,0},{3,1},{4,6},{5,7},{6,4},{7,5},{8,10},{9,11},{10,... | collective-permute-start | bytes 589832 | tf_op jit(solution)/shard_map/ppermute | solution.py:40
  42.1 14.9 %experts.2 = (bf16[192,640]{1,0:T(8,128)(2,1)S(1)}, bf16[192,640]{1,0:T(8,128)(2,1)S(1)}, bf16[192,640]{1,0:T(8,128)(2,1)S(1)}, bf16[192,640]{1,0:T(8,128)(2,1)S(1)}) custom-call(bf16[192,640]{1,0:T(8,128)(2,1)S(1)} %pad_maximum_fusion.refs_0_, bf16[192,640]{1,0:T(8,128)(2,1)S(1)} %tie.12.refs_1_, bf16[192,640]{1,0:T(8,128)(2,1)S(1)} %collective-permute-done.10.refs_2_, ...), custom_call_target="tpu_custom_call" | custom-call | flops 5096079360 | bytes 26542080 | tf_op jit(solution)/shard_map/experts/pallas_call | solution.py:307
  57.1 0.3 collective-permute-start.17
  57.3 0.3 route.3.refs_8_.weight_ref
  57.6 0.5 collective-permute-start.19
  58.1 0.1 collective-permute-start.20
  58.2 0.6 collective-permute-done.17
  58.8 0.1 add_convert_fusion.1.refs_7_
  58.9 1.0 %collective-permute-start.18 = (bf16[192,640]{1,0:T(8,128)(2,1)S(1)}, bf16[192,640]{1,0:T(8,128)(2,1)S(1)}, u32[]{:S(2)}, u32[]{:S(2)}) collective-permute-start(bf16[192,640]{1,0:T(8,128)(2,1)S(1)} %add_convert_fusion.1.refs_7_), channel_id=1, source_target_pairs={{0,2},{1,3},{2,0},{3,1},{4,6},{5,7},{6,4},{7,5},{8,10},{9,11},{10,... | collective-permute-start | bytes 737288 | tf_op jit(solution)/shard_map/ppermute | solution.py:40
  59.9 14.1 %experts.3 = (bf16[192,512]{1,0:T(8,128)(2,1)S(1)}, bf16[192,512]{1,0:T(8,128)(2,1)S(1)}, bf16[192,512]{1,0:T(8,128)(2,1)S(1)}, bf16[192,512]{1,0:T(8,128)(2,1)S(1)}) custom-call(bf16[192,512]{1,0:T(8,128)(2,1)S(1)} %constant_dynamic-update-slice_fusion.16.refs_7_.refs_0_, bf16[192,512]{1,0:T(8,128)(2,1)S(1)} %tie.13.refs_0_.refs_1_, ...), custom_call_target="tpu_custom_call" | custom-call | flops 3822059520 | bytes 26542080 | tf_op jit(solution)/shard_map/experts/pallas_call | solution.py:307
  74.1 0.1 collective-permute-start.21
  74.2 0.6 collective-permute-start.16
  74.7 0.1 collective-permute-start.25
  74.8 0.7 collective-permute-done.21
  75.6 0.1 add_convert_fusion.2.refs_0_
  75.7 1.2 %collective-permute-start.28 = (bf16[96,512]{1,0:T(8,128)(2,1)S(1)}, bf16[96,512]{1,0:T(8,128)(2,1)S(1)}, u32[]{:S(2)}, u32[]{:S(2)}) collective-permute-start(bf16[96,512]{1,0:T(8,128)(2,1)S(1)} %get-tuple-element.55), channel_id=1, source_target_pairs={{0,2},{1,3},{2,0},{3,1},{4,6},{5,7},{6,4},{7,5},{8,10},{9,11},{10,... | collective-permute-start | bytes 294920 | tf_op jit(solution)/shard_map/ppermute | solution.py:40
  76.8 0.9 %collective-permute-start.26 = (bf16[96,512]{1,0:T(8,128)(2,1)S(1)}, bf16[96,512]{1,0:T(8,128)(2,1)S(1)}, u32[]{:S(2)}, u32[]{:S(2)}) collective-permute-start(bf16[96,512]{1,0:T(8,128)(2,1)S(1)} %get-tuple-element.56), channel_id=1, source_target_pairs={{0,2},{1,3},{2,0},{3,1},{4,6},{5,7},{6,4},{7,5},{8,10},{9,11},{10,... | collective-permute-start | bytes 294920 | tf_op jit(solution)/shard_map/ppermute | solution.py:40
  77.8 0.1 add_convert_fusion
  77.9 2.0 %collective-permute-start.24 = (bf16[48,640]{1,0:T(8,128)(2,1)S(1)}, bf16[48,640]{1,0:T(8,128)(2,1)S(1)}, u32[]{:S(2)}, u32[]{:S(2)}) collective-permute-start(bf16[48,640]{1,0:T(8,128)(2,1)S(1)} %get-tuple-element.51), channel_id=1, source_target_pairs={{0,12},{1,13},{2,14},{3,15},{4,8},{5,9},{6,10},{7,11},{8,4},{9,5},... | collective-permute-start | bytes 184328 | tf_op jit(solution)/shard_map/ppermute | solution.py:40
  79.9 2.5 %collective-permute-start.22 = (bf16[48,640]{1,0:T(8,128)(2,1)S(1)}, bf16[48,640]{1,0:T(8,128)(2,1)S(1)}, u32[]{:S(2)}, u32[]{:S(2)}) collective-permute-start(bf16[48,640]{1,0:T(8,128)(2,1)S(1)} %get-tuple-element.53), channel_id=1, source_target_pairs={{0,4},{1,5},{2,6},{3,7},{4,0},{5,1},{6,2},{7,3},{8,12},{9,13},{10,... | collective-permute-start | bytes 184328 | tf_op jit(solution)/shard_map/ppermute | solution.py:40
  82.4 0.3 collective-permute-done.26
  82.7 0.1 fusion.2
  82.8 2.0 %collective-permute-start.30 = (bf16[48,512]{1,0:T(8,128)(2,1)S(1)}, bf16[48,512]{1,0:T(8,128)(2,1)S(1)}, u32[]{:S(2)}, u32[]{:S(2)}) collective-permute-start(bf16[48,512]{1,0:T(8,128)(2,1)S(1)} %get-tuple-element.73), channel_id=1, source_target_pairs={{0,12},{1,13},{2,14},{3,15},{4,8},{5,9},{6,10},{7,11},{8,4},{9,5},... | collective-permute-start | bytes 147464 | tf_op jit(solution)/shard_map/ppermute | solution.py:40
  84.7 0.0 collective-permute-start.29
  84.8 2.5 %collective-permute-start.27 = (bf16[48,512]{1,0:T(8,128)(2,1)S(1)}, bf16[48,512]{1,0:T(8,128)(2,1)S(1)}, u32[]{:S(2)}, u32[]{:S(2)}) collective-permute-start(bf16[48,512]{1,0:T(8,128)(2,1)S(1)} %get-tuple-element.75), channel_id=1, source_target_pairs={{0,4},{1,5},{2,6},{3,7},{4,0},{5,1},{6,2},{7,3},{8,12},{9,13},{10,... | collective-permute-start | bytes 147464 | tf_op jit(solution)/shard_map/ppermute | solution.py:40
  87.3 0.9 combine.2
  88.2 0.8 collective-permute-done.30.refs_3_
  89.0 1.2 %collective-permute-done.29.refs_2_ = bf16[48,512]{1,0:T(8,128)(2,1)S(1)} collective-permute-done((bf16[48,512]{1,0:T(8,128)(2,1)S(1)}, bf16[48,512]{1,0:T(8,128)(2,1)S(1)}, u32[]{:S(2)}, u32[]{:S(2)}) %collective-permute-start.29) | collective-permute-done | bytes 49184 | tf_op jit(solution)/shard_map/ppermute | solution.py:40
  90.2 0.9 combine.3
  (69 shorter events, 0.6 us)
Async XLA Ops:
  0.6 6.0 %copy-start = (bf16[256,2560]{1,0:T(8,128)(2,1)S(1)}, bf16[256,2560]{1,0:T(8,128)(2,1)}, u32[]{:S(2)}) copy-start(bf16[256,2560]{1,0:T(8,128)(2,1)} %param.14) | copy-start | bytes 3932164
  6.6 1.1 %copy-start.7 = (s32[2]{0:T(128)S(1)}, s32[2]{0:T(128)}, u32[]{:S(2)}) copy-start(s32[2]{0:T(128)} %param.20) | copy-start | bytes 28
  6.6 1.2 %copy-start.5 = (s32[16,2]{0,1:T(2,128)S(1)}, s32[16,2]{0,1:T(2,128)}, u32[]{:S(2)}) copy-start(s32[16,2]{0,1:T(2,128)} %param.19) | copy-start | bytes 388
  6.6 1.2 %copy-start.6 = (s32[16,2]{0,1:T(2,128)S(1)}, s32[16,2]{0,1:T(2,128)}, u32[]{:S(2)}) copy-start(s32[16,2]{0,1:T(2,128)} %param.18) | copy-start | bytes 388
  6.6 1.2 %copy-start.3 = (f32[2560]{0:T(1024)S(1)}, f32[2560]{0:T(1024)}, u32[]{:S(2)}) copy-start(f32[2560]{0:T(1024)} %param.15) | copy-start | bytes 30724
  6.7 1.2 %copy-start.4 = (f32[2560]{0:T(1024)S(1)}, f32[2560]{0:T(1024)}, u32[]{:S(2)}) copy-start(f32[2560]{0:T(1024)} %param.16) | copy-start | bytes 30724
  7.1 16.4 %collective-permute-start.1 = (bf16[64,2560]{1,0:T(8,128)(2,1)S(1)}, bf16[64,2560]{1,0:T(8,128)(2,1)S(1)}, u32[]{:S(2)}, u32[]{:S(2)}) collective-permute-start(bf16[64,2560]{1,0:T(8,128)(2,1)S(1)} %get-tuple-element.44), channel_id=1, source_target_pairs={{0,1},{1,0},{2,3},{3,2},{4,5},{5,4},{6,7},{7,6},{8,9},{9,8},{10,11... | collective-permute-start | bytes 983048 | tf_op jit(solution)/shard_map/ppermute | solution.py:40
  7.6 1.7 %collective-permute-start = (bf16[64,2560]{1,0:T(8,128)(2,1)S(1)}, bf16[64,2560]{1,0:T(8,128)(2,1)S(1)}, u32[]{:S(2)}, u32[]{:S(2)}) collective-permute-start(bf16[64,2560]{1,0:T(8,128)(2,1)S(1)} %get-tuple-element.45), channel_id=1, source_target_pairs={{0,1},{1,0},{2,3},{3,2},{4,5},{5,4},{6,7},{7,6},{8,9},{9,8},{10,11... | collective-permute-start | bytes 983048 | tf_op jit(solution)/shard_map/ppermute | solution.py:40
  8.2 4.1 %copy-start.2 = (f32[2560,4]{0,1:T(4,128)S(1)}, f32[2560,4]{0,1:T(4,128)}, u32[]{:S(2)}) copy-start(f32[2560,4]{0,1:T(4,128)} %param.17) | copy-start | bytes 122884
  8.3 4.1 %copy-start.1 = (bf16[16,2560]{1,0:T(8,128)(2,1)S(1)}, bf16[16,2560]{1,0:T(8,128)(2,1)}, u32[]{:S(2)}) copy-start(bf16[16,2560]{1,0:T(8,128)(2,1)} %image_ref.1) | copy-start | bytes 245764
  9.4 14.1 %collective-permute-start.2 = (bf16[64,2560]{1,0:T(8,128)(2,1)S(1)}, bf16[64,2560]{1,0:T(8,128)(2,1)S(1)}, u32[]{:S(2)}, u32[]{:S(2)}) collective-permute-start(bf16[64,2560]{1,0:T(8,128)(2,1)S(1)} %fusion.1.refs_0_), channel_id=1, source_target_pairs={{0,2},{1,3},{2,0},{3,1},{4,6},{5,7},{6,4},{7,5},{8,10},{9,11},{10,... | collective-permute-start | bytes 983048 | tf_op jit(solution)/shard_map/ppermute | solution.py:40
  13.2 4.5 %collective-permute-start.3 = (bf16[48,640]{1,0:T(8,128)(2,1)S(1)}, bf16[48,640]{1,0:T(8,128)(2,1)S(1)}, u32[]{:S(2)}, u32[]{:S(2)}) collective-permute-start(bf16[48,640]{1,0:T(8,128)(2,1)S(1)} %get-tuple-element.25), channel_id=1, source_target_pairs={{0,4},{1,5},{2,6},{3,7},{4,0},{5,1},{6,2},{7,3},{8,12},{9,13},{10,... | collective-permute-start | bytes 184328 | tf_op jit(solution)/shard_map/ppermute | solution.py:40
  14.9 6.4 %collective-permute-start.4 = (bf16[48,640]{1,0:T(8,128)(2,1)S(1)}, bf16[48,640]{1,0:T(8,128)(2,1)S(1)}, u32[]{:S(2)}, u32[]{:S(2)}) collective-permute-start(bf16[48,640]{1,0:T(8,128)(2,1)S(1)} %get-tuple-element.26), channel_id=1, source_target_pairs={{0,8},{1,9},{2,10},{3,11},{4,12},{5,13},{6,14},{7,15},{8,0},{9,1},... | collective-permute-start | bytes 184328 | tf_op jit(solution)/shard_map/ppermute | solution.py:40
  17.5 6.0 %collective-permute-start.5 = (bf16[48,640]{1,0:T(8,128)(2,1)S(1)}, bf16[48,640]{1,0:T(8,128)(2,1)S(1)}, u32[]{:S(2)}, u32[]{:S(2)}) collective-permute-start(bf16[48,640]{1,0:T(8,128)(2,1)S(1)} %get-tuple-element.27), channel_id=1, source_target_pairs={{0,12},{1,13},{2,14},{3,15},{4,8},{5,9},{6,10},{7,11},{8,4},{9,5},... | collective-permute-start | bytes 184328 | tf_op jit(solution)/shard_map/ppermute | solution.py:40
  23.7 13.3 %collective-permute-start.6 = (bf16[192,640]{1,0:T(8,128)(2,1)S(1)}, bf16[192,640]{1,0:T(8,128)(2,1)S(1)}, u32[]{:S(2)}, u32[]{:S(2)}) collective-permute-start(bf16[192,640]{1,0:T(8,128)(2,1)S(1)} %pad_maximum_fusion.refs_0_), channel_id=1, source_target_pairs={{0,2},{1,3},{2,0},{3,1},{4,6},{5,7},{6,4},{7,5},{8,10},{9,11},{10,... | collective-permute-start | bytes 737288 | tf_op jit(solution)/shard_map/ppermute | solution.py:40
  24.3 7.1 %collective-permute-start.9 = (bf16[16,2560]{1,0:T(8,128)(2,1)S(1)}, bf16[16,2560]{1,0:T(8,128)(2,1)S(1)}, u32[]{:S(2)}, u32[]{:S(2)}) collective-permute-start(bf16[16,2560]{1,0:T(8,128)(2,1)S(1)} %get-tuple-element.48.refs_2_), channel_id=1, source_target_pairs={{0,12},{1,13},{2,14},{3,15},{4,8},{5,9},{6,10},{7,11},{8,4},{9,5},... | collective-permute-start | bytes 245768 | tf_op jit(solution)/shard_map/ppermute | solution.py:40
  26.0 6.8 %collective-permute-start.8 = (bf16[16,2560]{1,0:T(8,128)(2,1)S(1)}, bf16[16,2560]{1,0:T(8,128)(2,1)S(1)}, u32[]{:S(2)}, u32[]{:S(2)}) collective-permute-start(bf16[16,2560]{1,0:T(8,128)(2,1)S(1)} %get-tuple-element.49.refs_1_), channel_id=1, source_target_pairs={{0,8},{1,9},{2,10},{3,11},{4,12},{5,13},{6,14},{7,15},{8,0},{9,1},... | collective-permute-start | bytes 245768 | tf_op jit(solution)/shard_map/ppermute | solution.py:40
  26.0 6.8 %collective-permute-start.7 = (bf16[16,2560]{1,0:T(8,128)(2,1)S(1)}, bf16[16,2560]{1,0:T(8,128)(2,1)S(1)}, u32[]{:S(2)}, u32[]{:S(2)}) collective-permute-start(bf16[16,2560]{1,0:T(8,128)(2,1)S(1)} %get-tuple-element.50.refs_0_), channel_id=1, source_target_pairs={{0,4},{1,5},{2,6},{3,7},{4,0},{5,1},{6,2},{7,3},{8,12},{9,13},{10,... | collective-permute-start | bytes 245768 | tf_op jit(solution)/shard_map/ppermute | solution.py:40
  29.0 13.1 %collective-permute-start.10 = (bf16[192,640]{1,0:T(8,128)(2,1)S(1)}, bf16[192,640]{1,0:T(8,128)(2,1)S(1)}, u32[]{:S(2)}, u32[]{:S(2)}) collective-permute-start(bf16[192,640]{1,0:T(8,128)(2,1)S(1)} %pad_maximum_fusion.refs_0_), channel_id=1, source_target_pairs={{0,1},{1,0},{2,3},{3,2},{4,5},{5,4},{6,7},{7,6},{8,9},{9,8},{10,11... | collective-permute-start | bytes 737288 | tf_op jit(solution)/shard_map/ppermute | solution.py:40
  33.5 7.4 %collective-permute-start.13 = (bf16[48,512]{1,0:T(8,128)(2,1)S(1)}, bf16[48,512]{1,0:T(8,128)(2,1)S(1)}, u32[]{:S(2)}, u32[]{:S(2)}) collective-permute-start(bf16[48,512]{1,0:T(8,128)(2,1)S(1)} %get-tuple-element.31), channel_id=1, source_target_pairs={{0,8},{1,9},{2,10},{3,11},{4,12},{5,13},{6,14},{7,15},{8,0},{9,1},... | collective-permute-start | bytes 147464 | tf_op jit(solution)/shard_map/ppermute | solution.py:40
  34.4 6.5 %collective-permute-start.14 = (bf16[48,512]{1,0:T(8,128)(2,1)S(1)}, bf16[48,512]{1,0:T(8,128)(2,1)S(1)}, u32[]{:S(2)}, u32[]{:S(2)}) collective-permute-start(bf16[48,512]{1,0:T(8,128)(2,1)S(1)} %get-tuple-element.32), channel_id=1, source_target_pairs={{0,12},{1,13},{2,14},{3,15},{4,8},{5,9},{6,10},{7,11},{8,4},{9,5},... | collective-permute-start | bytes 147464 | tf_op jit(solution)/shard_map/ppermute | solution.py:40
  36.3 4.6 %collective-permute-start.12 = (bf16[48,512]{1,0:T(8,128)(2,1)S(1)}, bf16[48,512]{1,0:T(8,128)(2,1)S(1)}, u32[]{:S(2)}, u32[]{:S(2)}) collective-permute-start(bf16[48,512]{1,0:T(8,128)(2,1)S(1)} %get-tuple-element.29.refs_0_), channel_id=1, source_target_pairs={{0,4},{1,5},{2,6},{3,7},{4,0},{5,1},{6,2},{7,3},{8,12},{9,13},{10,... | collective-permute-start | bytes 147464 | tf_op jit(solution)/shard_map/ppermute | solution.py:40
  37.0 5.0 %collective-permute-start.11 = (bf16[192,640]{1,0:T(8,128)(2,1)S(1)}, bf16[192,640]{1,0:T(8,128)(2,1)S(1)}, u32[]{:S(2)}, u32[]{:S(2)}) collective-permute-start(bf16[192,640]{1,0:T(8,128)(2,1)S(1)} %tie.12.refs_1_), channel_id=1, source_target_pairs={{0,1},{1,0},{2,3},{3,2},{4,5},{5,4},{6,7},{7,6},{8,9},{9,8},{10,11... | collective-permute-start | bytes 737288 | tf_op jit(solution)/shard_map/ppermute | solution.py:40
  40.9 16.1 %collective-permute-start.15 = (bf16[192,512]{1,0:T(8,128)(2,1)S(1)}, bf16[192,512]{1,0:T(8,128)(2,1)S(1)}, u32[]{:S(2)}, u32[]{:S(2)}) collective-permute-start(bf16[192,512]{1,0:T(8,128)(2,1)S(1)} %constant_dynamic-update-slice_fusion.16.refs_7_.refs_0_), channel_id=1, source_target_pairs={{0,2},{1,3},{2,0},{3,1},{4,6},{5,7},{6,4},{7,5},{8,10},{9,11},{10,... | collective-permute-start | bytes 589832 | tf_op jit(solution)/shard_map/ppermute | solution.py:40
  57.1 1.8 %collective-permute-start.17 = (bf16[192,640]{1,0:T(8,128)(2,1)S(1)}, bf16[192,640]{1,0:T(8,128)(2,1)S(1)}, u32[]{:S(2)}, u32[]{:S(2)}) collective-permute-start(bf16[192,640]{1,0:T(8,128)(2,1)S(1)} %tie.15), channel_id=1, source_target_pairs={{0,1},{1,0},{2,3},{3,2},{4,5},{5,4},{6,7},{7,6},{8,9},{9,8},{10,11... | collective-permute-start | bytes 737288 | tf_op jit(solution)/shard_map/ppermute | solution.py:40
  57.6 2.3 %collective-permute-start.19 = (bf16[192,512]{1,0:T(8,128)(2,1)S(1)}, bf16[192,512]{1,0:T(8,128)(2,1)S(1)}, u32[]{:S(2)}, u32[]{:S(2)}) collective-permute-start(bf16[192,512]{1,0:T(8,128)(2,1)S(1)} %constant_dynamic-update-slice_fusion.16.refs_7_.refs_0_), channel_id=1, source_target_pairs={{0,1},{1,0},{2,3},{3,2},{4,5},{5,4},{6,7},{7,6},{8,9},{9,8},{10,11... | collective-permute-start | bytes 589832 | tf_op jit(solution)/shard_map/ppermute | solution.py:40
  58.1 1.8 %collective-permute-start.20 = (bf16[192,512]{1,0:T(8,128)(2,1)S(1)}, bf16[192,512]{1,0:T(8,128)(2,1)S(1)}, u32[]{:S(2)}, u32[]{:S(2)}) collective-permute-start(bf16[192,512]{1,0:T(8,128)(2,1)S(1)} %tie.13.refs_0_.refs_1_), channel_id=1, source_target_pairs={{0,1},{1,0},{2,3},{3,2},{4,5},{5,4},{6,7},{7,6},{8,9},{9,8},{10,11... | collective-permute-start | bytes 589832 | tf_op jit(solution)/shard_map/ppermute | solution.py:40
  58.9 15.1 %collective-permute-start.18 = (bf16[192,640]{1,0:T(8,128)(2,1)S(1)}, bf16[192,640]{1,0:T(8,128)(2,1)S(1)}, u32[]{:S(2)}, u32[]{:S(2)}) collective-permute-start(bf16[192,640]{1,0:T(8,128)(2,1)S(1)} %add_convert_fusion.1.refs_7_), channel_id=1, source_target_pairs={{0,2},{1,3},{2,0},{3,1},{4,6},{5,7},{6,4},{7,5},{8,10},{9,11},{10,... | collective-permute-start | bytes 737288 | tf_op jit(solution)/shard_map/ppermute | solution.py:40
  74.1 1.5 %collective-permute-start.21 = (bf16[192,512]{1,0:T(8,128)(2,1)S(1)}, bf16[192,512]{1,0:T(8,128)(2,1)S(1)}, u32[]{:S(2)}, u32[]{:S(2)}) collective-permute-start(bf16[192,512]{1,0:T(8,128)(2,1)S(1)} %tie.17), channel_id=1, source_target_pairs={{0,1},{1,0},{2,3},{3,2},{4,5},{5,4},{6,7},{7,6},{8,9},{9,8},{10,11... | collective-permute-start | bytes 589832 | tf_op jit(solution)/shard_map/ppermute | solution.py:40
  74.2 3.6 %collective-permute-start.16 = (bf16[192,640]{1,0:T(8,128)(2,1)S(1)}, bf16[192,640]{1,0:T(8,128)(2,1)S(1)}, u32[]{:S(2)}, u32[]{:S(2)}) collective-permute-start(bf16[192,640]{1,0:T(8,128)(2,1)S(1)} %tie.14), channel_id=1, source_target_pairs={{0,1},{1,0},{2,3},{3,2},{4,5},{5,4},{6,7},{7,6},{8,9},{9,8},{10,11... | collective-permute-start | bytes 737288 | tf_op jit(solution)/shard_map/ppermute | solution.py:40
  74.7 5.1 %collective-permute-start.25 = (bf16[192,512]{1,0:T(8,128)(2,1)S(1)}, bf16[192,512]{1,0:T(8,128)(2,1)S(1)}, u32[]{:S(2)}, u32[]{:S(2)}) collective-permute-start(bf16[192,512]{1,0:T(8,128)(2,1)S(1)} %tie.19), channel_id=1, source_target_pairs={{0,1},{1,0},{2,3},{3,2},{4,5},{5,4},{6,7},{7,6},{8,9},{9,8},{10,11... | collective-permute-start | bytes 589832 | tf_op jit(solution)/shard_map/ppermute | solution.py:40
  75.7 6.7 %collective-permute-start.28 = (bf16[96,512]{1,0:T(8,128)(2,1)S(1)}, bf16[96,512]{1,0:T(8,128)(2,1)S(1)}, u32[]{:S(2)}, u32[]{:S(2)}) collective-permute-start(bf16[96,512]{1,0:T(8,128)(2,1)S(1)} %get-tuple-element.55), channel_id=1, source_target_pairs={{0,2},{1,3},{2,0},{3,1},{4,6},{5,7},{6,4},{7,5},{8,10},{9,11},{10,... | collective-permute-start | bytes 294920 | tf_op jit(solution)/shard_map/ppermute | solution.py:40
  76.8 5.8 %collective-permute-start.26 = (bf16[96,512]{1,0:T(8,128)(2,1)S(1)}, bf16[96,512]{1,0:T(8,128)(2,1)S(1)}, u32[]{:S(2)}, u32[]{:S(2)}) collective-permute-start(bf16[96,512]{1,0:T(8,128)(2,1)S(1)} %get-tuple-element.56), channel_id=1, source_target_pairs={{0,2},{1,3},{2,0},{3,1},{4,6},{5,7},{6,4},{7,5},{8,10},{9,11},{10,... | collective-permute-start | bytes 294920 | tf_op jit(solution)/shard_map/ppermute | solution.py:40
  77.9 6.9 %collective-permute-start.24 = (bf16[48,640]{1,0:T(8,128)(2,1)S(1)}, bf16[48,640]{1,0:T(8,128)(2,1)S(1)}, u32[]{:S(2)}, u32[]{:S(2)}) collective-permute-start(bf16[48,640]{1,0:T(8,128)(2,1)S(1)} %get-tuple-element.51), channel_id=1, source_target_pairs={{0,12},{1,13},{2,14},{3,15},{4,8},{5,9},{6,10},{7,11},{8,4},{9,5},... | collective-permute-start | bytes 184328 | tf_op jit(solution)/shard_map/ppermute | solution.py:40
  79.9 7.4 %collective-permute-start.23 = (bf16[48,640]{1,0:T(8,128)(2,1)S(1)}, bf16[48,640]{1,0:T(8,128)(2,1)S(1)}, u32[]{:S(2)}, u32[]{:S(2)}) collective-permute-start(bf16[48,640]{1,0:T(8,128)(2,1)S(1)} %get-tuple-element.52), channel_id=1, source_target_pairs={{0,8},{1,9},{2,10},{3,11},{4,12},{5,13},{6,14},{7,15},{8,0},{9,1},... | collective-permute-start | bytes 184328 | tf_op jit(solution)/shard_map/ppermute | solution.py:40
  79.9 7.4 %collective-permute-start.22 = (bf16[48,640]{1,0:T(8,128)(2,1)S(1)}, bf16[48,640]{1,0:T(8,128)(2,1)S(1)}, u32[]{:S(2)}, u32[]{:S(2)}) collective-permute-start(bf16[48,640]{1,0:T(8,128)(2,1)S(1)} %get-tuple-element.53), channel_id=1, source_target_pairs={{0,4},{1,5},{2,6},{3,7},{4,0},{5,1},{6,2},{7,3},{8,12},{9,13},{10,... | collective-permute-start | bytes 184328 | tf_op jit(solution)/shard_map/ppermute | solution.py:40
  82.8 6.2 %collective-permute-start.30 = (bf16[48,512]{1,0:T(8,128)(2,1)S(1)}, bf16[48,512]{1,0:T(8,128)(2,1)S(1)}, u32[]{:S(2)}, u32[]{:S(2)}) collective-permute-start(bf16[48,512]{1,0:T(8,128)(2,1)S(1)} %get-tuple-element.73), channel_id=1, source_target_pairs={{0,12},{1,13},{2,14},{3,15},{4,8},{5,9},{6,10},{7,11},{8,4},{9,5},... | collective-permute-start | bytes 147464 | tf_op jit(solution)/shard_map/ppermute | solution.py:40
  84.7 5.4 %collective-permute-start.29 = (bf16[48,512]{1,0:T(8,128)(2,1)S(1)}, bf16[48,512]{1,0:T(8,128)(2,1)S(1)}, u32[]{:S(2)}, u32[]{:S(2)}) collective-permute-start(bf16[48,512]{1,0:T(8,128)(2,1)S(1)} %get-tuple-element.74), channel_id=1, source_target_pairs={{0,8},{1,9},{2,10},{3,11},{4,12},{5,13},{6,14},{7,15},{8,0},{9,1},... | collective-permute-start | bytes 147464 | tf_op jit(solution)/shard_map/ppermute | solution.py:40
  84.8 5.4 %collective-permute-start.27 = (bf16[48,512]{1,0:T(8,128)(2,1)S(1)}, bf16[48,512]{1,0:T(8,128)(2,1)S(1)}, u32[]{:S(2)}, u32[]{:S(2)}) collective-permute-start(bf16[48,512]{1,0:T(8,128)(2,1)S(1)} %get-tuple-element.75), channel_id=1, source_target_pairs={{0,4},{1,5},{2,6},{3,7},{4,0},{5,1},{6,2},{7,3},{8,12},{9,13},{10,... | collective-permute-start | bytes 147464 | tf_op jit(solution)/shard_map/ppermute | solution.py:40

commit v9 on v8

--- a/solution.py
+++ b/solution.py
@@ -201,29 +201,31 @@
     )(spot, normed, small)
 
 
-def cuts(units):
-    edges = [0, units] if units <= 1024 else [0, 384, 1152, units]
+def cuts(units, part, parts):
+    first, last = [units * p // parts // 16 * 16 for p in (part, part + 1)]
+    edges = [first] + list(range(first + 256, last - 255, 512 if parts == 1 else 320)) + [last]
     return list(zip(edges[:-1], edges[1:]))
 
 
-def expert_kernel(packing, count, after, *refs):
-    row_refs = refs[:count]
-    gate_hbm, up_hbm, down_hbm = refs[count : count + 3]
-    out_refs = refs[count + 3 + after : 2 * count + 3 + after]
-    inner_ref, down_ref, rows_ref, total_ref, packed_ref, sems = refs[2 * count + 3 + after :]
+def expert_kernel(packing, unit_cuts, count, before, after, *refs):
+    row_refs, before_refs = refs[:count], refs[count : count + before]
+    gate_hbm, up_hbm, down_hbm = refs[count + before : count + before + 3]
+    place = count + before + 3 + after
+    out_refs = refs[place : place + count]
+    gate_ref, up_ref, down_ref, rows_ref, total_ref, packed_ref, sems = refs[place + count :]
     rows = total_ref.shape[1]
-    units = gate_hbm.shape[0]
-    unit_cuts = cuts(units)
+    origin = unit_cuts[0][0]
     copies = []
     for i, (lo, hi) in enumerate(unit_cuts):
         for t, (source, target) in enumerate(
-            (
-                (gate_hbm, inner_ref.at[2 * lo : lo + hi]),
-                (up_hbm, inner_ref.at[lo + hi : 2 * hi]),
-                (down_hbm, down_ref.at[lo:hi]),
+            ((gate_hbm, gate_ref), (up_hbm, up_ref), (down_hbm, down_ref))
+        ):
+            copies.append(
+                pltpu.make_async_copy(
+                    source.at[lo:hi], target.at[lo - origin : hi - origin], sems.at[3 * i + t]
+                )
             )
-        ):
-            copies.append(pltpu.make_async_copy(source.at[lo:hi], target, sems.at[3 * i + t]))
+    unit_cuts = [(lo - origin, hi - origin) for lo, hi in unit_cuts]
     for copy in copies[:6]:
         copy.start()
 
@@ -261,11 +263,11 @@
     features = gate_hbm.shape[1]
     middle = features // 256 * 128
 
-    def product(lo, hi):
+    def product(weight_ref, lo, hi):
         return jnp.dot(
-            inner_ref[lo:hi, :middle], rows_ref[:middle, :], preferred_element_type=jnp.float32
+            weight_ref[lo:hi, :middle], rows_ref[:middle, :], preferred_element_type=jnp.float32
         ) + jnp.dot(
-            inner_ref[lo:hi, middle:], rows_ref[middle:, :], preferred_element_type=jnp.float32
+            weight_ref[lo:hi, middle:], rows_ref[middle:, :], preferred_element_type=jnp.float32
         )
 
     hidden = None
@@ -276,8 +278,8 @@
         copies[3 * i + 1].wait()
         for copy in copies[3 * (i + 2) : 3 * (i + 3)]:
             copy.start()
-        inner = product(2 * lo, 2 * hi)
-        gate, up = inner[: hi - lo], inner[hi - lo :]
+        gate = product(gate_ref, lo, hi)
+        up = product(up_ref, lo, hi)
         if i > 0:
             down(i - 1, hidden)
         hidden = (gate * jax.nn.sigmoid(gate) * up).T[0:rows].astype(jnp.bfloat16)
@@ -296,35 +298,42 @@
                 ]
     for i, ref in enumerate(out_refs):
         for c in range(lanes):
-            ref[:, c * 128 : (c + 1) * 128] = packed_ref[
-                c, i * per_ref * high : (i + 1) * per_ref * high, :
-            ].astype(jnp.bfloat16)
-
-
-def expert_rows(arrays, w_gate, w_up, w_down, packing, after):
+            columns = slice(c * 128, (c + 1) * 128)
+            part = packed_ref[c, i * per_ref * high : (i + 1) * per_ref * high, :]
+            if before:
+                part = part + before_refs[i][:, columns].astype(jnp.float32)
+            ref[:, columns] = part.astype(jnp.bfloat16)
+
+
+def expert_rows(arrays, w_gate, w_up, w_down, packing, after, part=0, parts=1, before=()):
     features, units = w_gate.shape
     rows = len(arrays) * (arrays[0].shape[0] // packing.rows) * packing.cap
+    unit_cuts = cuts(units, part, parts)
+    own = unit_cuts[-1][1] - unit_cuts[0][0]
     return pl.pallas_call(
-        functools.partial(expert_kernel, packing, len(arrays), len(after)),
+        functools.partial(
+            expert_kernel, packing, unit_cuts, len(arrays), len(before), len(after)
+        ),
         out_shape=[jax.ShapeDtypeStruct(arrays[0].shape, jnp.bfloat16)] * len(arrays),
-        in_specs=[VMEM] * len(arrays) + [HBM] * 3 + [ANY] * len(after),
+        in_specs=[VMEM] * (len(arrays) + len(before)) + [HBM] * 3 + [ANY] * len(after),
         out_specs=[VMEM] * len(arrays),
         scratch_shapes=[
-            pltpu.VMEM((2 * units, features), jnp.bfloat16),
-            pltpu.VMEM((units, features), jnp.bfloat16),
+            pltpu.VMEM((own, features), jnp.bfloat16),
+            pltpu.VMEM((own, features), jnp.bfloat16),
+            pltpu.VMEM((own, features), jnp.bfloat16),
             pltpu.VMEM((features, -(-rows // 128) * 128), jnp.bfloat16),
             pltpu.VMEM((features // 128, rows, 128), jnp.float32),
             pltpu.VMEM((packing.width // 128, len(arrays) * arrays[0].shape[0], 128), jnp.float32),
-            pltpu.SemaphoreType.DMA((3 * len(cuts(units)),)),
+            pltpu.SemaphoreType.DMA((3 * len(unit_cuts),)),
         ],
         compiler_params=pltpu.CompilerParams(vmem_limit_bytes=48 << 20),
         cost_estimate=pl.CostEstimate(
-            flops=6 * rows * features * units,
-            bytes_accessed=6 * features * units,
-            transcendentals=rows * units,
+            flops=6 * rows * features * own,
+            bytes_accessed=6 * features * own,
+            transcendentals=rows * own,
         ),
         name="experts",
-    )(*arrays, w_gate.T, w_up.T, w_down, *after)
+    )(*arrays, *before, w_gate.T, w_up.T, w_down, *after)
 
 
 def combine_kernel(packing, spot_ref, weight_ref, *refs):
@@ -366,19 +375,16 @@
 def partial_captions(text_hidden, caption_weight, grid):
     groups = grid.pairs * 2
     rows = text_hidden.shape[0] // (grid.experts * groups)
+    bits = (grid.experts * groups).bit_length() - 1
+    text = text_hidden.reshape((2,) * bits + (rows, -1))
+    for bit in range(bits):
+        text = jnp.roll(text, (grid.index >> (bits - 1 - bit)) & 1, axis=bit)
+    text = text.reshape(grid.experts, grid.pairs, 2, rows, -1)
+    text = jnp.concatenate([text[:, 1:], text[:, :1]], axis=1)
     text = [
-        [
-            lax.dynamic_slice_in_dim(
-                text_hidden,
-                (((grid.expert ^ e) * grid.pairs + (grid.pair ^ p)) * 2 + (grid.core ^ c)) * rows,
-                rows,
-            )
-            for p in list(range(1, grid.pairs)) + [0]
-            for e in range(grid.experts)
-        ]
+        jnp.transpose(text[:, :, c], (1, 0, 2, 3)).reshape(-1, text_hidden.shape[1])
         for c in (1, 0)
     ]
-    text = [jnp.concatenate(part, axis=0) for part in text]
     other, own = [
         jnp.dot(text[c], caption_weight, preferred_element_type=jnp.float32).astype(kind)
         for c, kind in enumerate((jnp.bfloat16, jnp.float32))
@@ -434,12 +440,12 @@
     def from_pairs(crossing):
         return [grid.swap(value, 1, k) for k, value in enumerate(crossing, 1)]
 
-    def from_experts(kept, received, high, first=0):
+    def from_experts(kept, received):
         total = kept
         for value in received:
             total = total + value.astype(wide)
-        parts = split(total.astype(narrow), kept.shape[0] // high)
-        return [grid.swap(part, 0, k) if k else part for k, part in enumerate(parts, first)]
+        parts = split(total.astype(narrow), experts)
+        return [parts[0]] + [grid.swap(parts[k], 0, k) for k in range(1, experts)]
 
     partial = partial_captions(text_hidden, caption_weight, grid)
     sums = [
@@ -470,16 +476,20 @@
     terms = [parts[0]] + to_experts(sent)
     image_first = jnp.concatenate([tie(image_first[0], sent[1:])] + image_first[1:], axis=0)
     image_own = to_pairs(image_first)
+    image_own = image_own[:1] + [tie(value, terms[1:]) for value in image_own[1:]]
+    image_arrays = image_own + over_cores(image_own)
+    weights = (w_gate, w_up, w_down)
+
     caption_normed, blocks = modulate(terms, caption_spot, small, caption_packing, experts)
-    caption_first = jnp.concatenate([blocks[0]] + to_experts(blocks), axis=0)
+    image_half = expert_rows(image_arrays, *weights, image_packing, blocks[1:2], 0, 2)
+    received = to_experts(blocks)
+    caption_first = jnp.concatenate([tie(blocks[0], image_half[:1])] + received, axis=0)
     caption_own = to_pairs(caption_first)
-    image_own = image_own[:1] + [tie(value, blocks[1:2]) for value in image_own[1:]]
-    image_arrays = image_own + over_cores(image_own)
 
     image_weights = route(image_normed, image_spot, small)
     caption_weights = route(caption_normed, caption_spot, small)
     image_results = expert_rows(
-        image_arrays, w_gate, w_up, w_down, image_packing, [caption_first, image_weights]
+        image_arrays, *weights, image_packing, [caption_first, image_weights], 1, 2, image_half
     )
     caption_own = caption_own[:1] + [tie(value, image_results[:1]) for value in caption_own[1:]]
     image_results = list(image_results[:pairs]) + [
@@ -488,9 +498,7 @@
     image_kept, image_crossing = join_cores(image_results)
     caption_results = expert_rows(
         caption_own + over_cores(caption_own),
-        w_gate,
-        w_up,
-        w_down,
+        *weights,
         caption_packing,
         image_crossing[:1] + [caption_weights],
     )
@@ -502,14 +510,9 @@
     ]
     caption_kept, caption_crossing = join_cores(caption_results)
     image_received = [tie(value, caption_crossing[:1]) for value in image_received]
-    image_blocks = from_experts(image_kept, image_received, image_packing.rows)
-    caption_blocks = [None] * experts
-    high = caption_packing.rows
-    for lo, hi in ((experts // 2, experts), (0, experts // 2)):
-        strip = slice(lo * high, hi * high)
-        caption_blocks[lo:hi] = from_experts(
-            caption_kept[strip], from_pairs([value[strip] for value in caption_crossing]), high, lo
-        )
+    image_blocks = from_experts(image_kept, image_received)
+    caption_received = from_pairs(caption_crossing)
+    caption_blocks = from_experts(caption_kept, caption_received)
 
     rows = image_rows.shape[0]
     image_out = combine(image_spot, image_weights, image_blocks, image_packing, rows, features)

time: 92.1 us -> 82.3 us (0.89)
  local copies, waits for them, and re-layouts: 6.04 us -> 0.21 us
  waiting for transfers between devices: 18 us -> 15.7 us
  Pallas kernels: 33 us -> 31.7 us
  other arithmetic: 0.7 us -> 1.93 us
    unnamed x26 -> x16, local copies, waits for them, and re-layouts: 5.17 us -> 0.05 us
    ppermute x31 -> x30, waiting for transfers between devices: 18 us -> 15.7 us  [swap(): return lax.ppermute(value, 'dev', moves)]
    pallas_call x2 -> x3, Pallas kernels: 29 us -> 27.7 us  [expert_rows(): pl.pallas_call(functools.partial(expert_kernel, packing, unit_cuts, len(a...]
    concatenate x0 -> x5, other arithmetic: none -> 1.3 us  [the longest x3 1.27 us: partial_captions(): text = jnp.roll(text, grid.index >> bits - 1 - bit & 1, axis=bit)]
    ppermute x31 -> x30, starting transfers between devices: 31.4 us -> 30.7 us  [swap(): return lax.ppermute(value, 'dev', moves)]
  transfers between devices with their start and end apart: 31 -> 30, of which waited for: 11 -> 11; matrix products, arithmetic and copies ran while one was open for 1% -> 1% of each run, Pallas kernels for 35% -> 37%
where the time goes in v9:
time: 82.3 us; the launch traced here: 82.1 us
  Pallas kernels  31.7 us (39%)
  starting transfers between devices  30.7 us (37%)
  waiting for transfers between devices  15.7 us (19%)
  other arithmetic  1.93 us (2%)
  between operations  1.3 us (2%)
    ppermute x30, starting transfers between devices, swap(): return lax.ppermute(value, 'dev', moves)  30.7 us
    pallas_call x3, Pallas kernels, expert_rows(): pl.pallas_call(functools.partial(expert_kernel, packing, unit_cuts, len(a...  27.7 us
    ppermute x30, waiting for transfers between devices, swap(): return lax.ppermute(value, 'dev', moves)  15.7 us
    pallas_call x2, Pallas kernels, combine(): pl.pallas_call(functools.partial(combine_kernel, packing), out_shape=jax....  1.78 us
  transfers between devices with their start and end apart: 30, of which 11 were waited for; matrix products, arithmetic and copies ran while one was open for 1% of the time, Pallas kernels for 37%

profile of v9, /device:TPU:0, one launch (start us, length us, event | category | flops | bytes accessed | tf_op | source)
XLA Modules:
  0.0 82.1 jit_solution(10903112591130371002)
XLA Ops:
  0.6 0.0 copy-start
  0.7 1.1 %fusion.5 = bf16[2,2,2,2,16,256]{5,4,3,2,1,0:T(8,128)(2,1)S(1)} fusion(s32[]{:T(128)S(6)} %select_n.80, bf16[2,2,2,2,16,256]{5,4,3,2,1,0:T(8,128)(2,1)} %bitcast.31), kind=kLoop, calls=%fused_computation.22 | loop fusion | flops 65536 | bytes 262148 | tf_op jit(solution)/shard_map/jit(_roll_dynamic)/concatenate | solution.py:381
  1.8 0.1 fusion.3
  1.9 0.1 fusion.2
  2.0 0.0 copy-start.7
  2.1 0.0 copy-start.5
  2.1 0.0 copy-start.3
  2.1 0.3 convolution_convert_fusion
  2.5 0.5 collective-permute-start.1
  3.0 0.1 collective-permute-start
  3.1 0.1 fusion.7
  3.3 0.3 fusion.16
  3.7 1.1 %collective-permute-done = bf16[64,2560]{1,0:T(8,128)(2,1)S(1)} collective-permute-done((bf16[64,2560]{1,0:T(8,128)(2,1)S(1)}, bf16[64,2560]{1,0:T(8,128)(2,1)S(1)}, u32[]{:S(2)}, u32[]{:S(2)}) %collective-permute-start) | collective-permute-done | bytes 327712 | tf_op jit(solution)/shard_map/ppermute | solution.py:40
  4.7 0.1 fusion.1.refs_0_
  4.8 2.9 %collective-permute-start.2 = (bf16[64,2560]{1,0:T(8,128)(2,1)S(1)}, bf16[64,2560]{1,0:T(8,128)(2,1)S(1)}, u32[]{:S(2)}, u32[]{:S(2)}) collective-permute-start(bf16[64,2560]{1,0:T(8,128)(2,1)S(1)} %fusion.1.refs_0_), channel_id=1, source_target_pairs={{0,2},{1,3},{2,0},{3,1},{4,6},{5,7},{6,4},{7,5},{8,10},{9,11},{10,... | collective-permute-start | bytes 983048 | tf_op jit(solution)/shard_map/ppermute | solution.py:40
  7.8 0.8 %prepare.1 = (f32[16,4]{1,0:T(8,128)S(1)}, f32[16,4]{1,0:T(8,128)S(1)}, bf16[16,2560]{1,0:T(8,128)(2,1)S(1)}, bf16[48,640]{1,0:T(8,128)(2,1)S(1)}, bf16[48,640]{...) custom-call(s32[4,16]{1,0:T(4,128)S(1)} %pad_add_fusion.ids_ref, ...), custom_call_target="tpu_custom_call" | custom-call | tf_op jit(solution)/shard_map/prepare/pallas_call | solution.py:122
  8.6 1.6 %collective-permute-start.3 = (bf16[48,640]{1,0:T(8,128)(2,1)S(1)}, bf16[48,640]{1,0:T(8,128)(2,1)S(1)}, u32[]{:S(2)}, u32[]{:S(2)}) collective-permute-start(bf16[48,640]{1,0:T(8,128)(2,1)S(1)} %get-tuple-element.29), channel_id=1, source_target_pairs={{0,4},{1,5},{2,6},{3,7},{4,0},{5,1},{6,2},{7,3},{8,12},{9,13},{10,... | collective-permute-start | bytes 184328 | tf_op jit(solution)/shard_map/ppermute | solution.py:40
  10.3 2.6 %collective-permute-start.4 = (bf16[48,640]{1,0:T(8,128)(2,1)S(1)}, bf16[48,640]{1,0:T(8,128)(2,1)S(1)}, u32[]{:S(2)}, u32[]{:S(2)}) collective-permute-start(bf16[48,640]{1,0:T(8,128)(2,1)S(1)} %get-tuple-element.30), channel_id=1, source_target_pairs={{0,8},{1,9},{2,10},{3,11},{4,12},{5,13},{6,14},{7,15},{8,0},{9,1},... | collective-permute-start | bytes 184328 | tf_op jit(solution)/shard_map/ppermute | solution.py:40
  12.8 0.3 collective-permute-start.5
  13.1 4.2 %collective-permute-done.4.refs_1_ = bf16[48,640]{1,0:T(8,128)(2,1)S(1)} collective-permute-done((bf16[48,640]{1,0:T(8,128)(2,1)S(1)}, bf16[48,640]{1,0:T(8,128)(2,1)S(1)}, u32[]{:S(2)}, u32[]{:S(2)}) %collective-permute-start.4) | collective-permute-done | bytes 61472 | tf_op jit(solution)/shard_map/ppermute | solution.py:40
  17.3 1.6 %collective-permute-done.5.refs_2_ = bf16[48,640]{1,0:T(8,128)(2,1)S(1)} collective-permute-done((bf16[48,640]{1,0:T(8,128)(2,1)S(1)}, bf16[48,640]{1,0:T(8,128)(2,1)S(1)}, u32[]{:S(2)}, u32[]{:S(2)}) %collective-permute-start.5) | collective-permute-done | bytes 61472 | tf_op jit(solution)/shard_map/ppermute | solution.py:40
  18.9 0.1 fusion.9
  19.1 0.6 collective-permute-start.6
  19.6 1.7 %collective-permute-start.9 = (bf16[16,2560]{1,0:T(8,128)(2,1)S(1)}, bf16[16,2560]{1,0:T(8,128)(2,1)S(1)}, u32[]{:S(2)}, u32[]{:S(2)}) collective-permute-start(bf16[16,2560]{1,0:T(8,128)(2,1)S(1)} %get-tuple-element.54.refs_2_), channel_id=1, source_target_pairs={{0,12},{1,13},{2,14},{3,15},{4,8},{5,9},{6,10},{7,11},{8,4},{9,5},... | collective-permute-start | bytes 245768 | tf_op jit(solution)/shard_map/ppermute | solution.py:40
  21.4 2.7 %collective-permute-start.7 = (bf16[16,2560]{1,0:T(8,128)(2,1)S(1)}, bf16[16,2560]{1,0:T(8,128)(2,1)S(1)}, u32[]{:S(2)}, u32[]{:S(2)}) collective-permute-start(bf16[16,2560]{1,0:T(8,128)(2,1)S(1)} %get-tuple-element.56.refs_0_), channel_id=1, source_target_pairs={{0,4},{1,5},{2,6},{3,7},{4,0},{5,1},{6,2},{7,3},{8,12},{9,13},{10,... | collective-permute-start | bytes 245768 | tf_op jit(solution)/shard_map/ppermute | solution.py:40
  24.0 2.7 %collective-permute-done.9.refs_2_.refs_3_ = bf16[16,2560]{1,0:T(8,128)(2,1)S(1)} collective-permute-done((bf16[16,2560]{1,0:T(8,128)(2,1)S(1)}, bf16[16,2560]{1,0:T(8,128)(2,1)S(1)}, u32[]{:S(2)}, u32[]{:S(2)}) %collective-permute-start.9) | collective-permute-done | bytes 81952 | tf_op jit(solution)/shard_map/ppermute | solution.py:40
  26.7 1.4 %collective-permute-done.8.refs_1_.refs_2_ = bf16[16,2560]{1,0:T(8,128)(2,1)S(1)} collective-permute-done((bf16[16,2560]{1,0:T(8,128)(2,1)S(1)}, bf16[16,2560]{1,0:T(8,128)(2,1)S(1)}, u32[]{:S(2)}, u32[]{:S(2)}) %collective-permute-start.8) | collective-permute-done | bytes 81952 | tf_op jit(solution)/shard_map/ppermute | solution.py:40
  28.2 0.1 collective-permute-start.11
  28.2 0.3 route.2.refs_12_.weight_ref
  28.6 0.6 modulate.1
  29.2 0.9 %collective-permute-start.13 = (bf16[48,512]{1,0:T(8,128)(2,1)S(1)}, bf16[48,512]{1,0:T(8,128)(2,1)S(1)}, u32[]{:S(2)}, u32[]{:S(2)}) collective-permute-start(bf16[48,512]{1,0:T(8,128)(2,1)S(1)} %get-tuple-element.39), channel_id=1, source_target_pairs={{0,8},{1,9},{2,10},{3,11},{4,12},{5,13},{6,14},{7,15},{8,0},{9,1},... | collective-permute-start | bytes 147464 | tf_op jit(solution)/shard_map/ppermute | solution.py:40
  30.2 1.8 %collective-permute-start.14 = (bf16[48,512]{1,0:T(8,128)(2,1)S(1)}, bf16[48,512]{1,0:T(8,128)(2,1)S(1)}, u32[]{:S(2)}, u32[]{:S(2)}) collective-permute-start(bf16[48,512]{1,0:T(8,128)(2,1)S(1)} %get-tuple-element.40), channel_id=1, source_target_pairs={{0,12},{1,13},{2,14},{3,15},{4,8},{5,9},{6,10},{7,11},{8,4},{9,5},... | collective-permute-start | bytes 147464 | tf_op jit(solution)/shard_map/ppermute | solution.py:40
  32.0 0.8 collective-permute-start.12
  32.8 8.1 %experts.3 = (bf16[192,640]{1,0:T(8,128)(2,1)S(1)}, bf16[192,640]{1,0:T(8,128)(2,1)S(1)}, bf16[192,640]{1,0:T(8,128)(2,1)S(1)}, bf16[192,640]{1,0:T(8,128)(2,1)S(1)}) custom-call(bf16[192,640]{1,0:T(8,128)(2,1)S(1)} %pad_maximum_fusion.refs_0_, bf16[192,640]{1,0:T(8,128)(2,1)S(1)} %tie.13.refs_1_, bf16[192,640]{1,0:T(8,128)(2,1)S(1)} %collective-permute-done.10.refs_2_, ...), custom_call_target="tpu_custom_call" | custom-call | flops 2548039680 | bytes 13271040 | tf_op jit(solution)/shard_map/experts/pallas_call | solution.py:313
  40.9 1.6 %collective-permute-start.15 = (bf16[192,512]{1,0:T(8,128)(2,1)S(1)}, bf16[192,512]{1,0:T(8,128)(2,1)S(1)}, u32[]{:S(2)}, u32[]{:S(2)}) collective-permute-start(bf16[192,512]{1,0:T(8,128)(2,1)S(1)} %pad_maximum_fusion.1.refs_11_.refs_0_), channel_id=1, source_target_pairs={{0,2},{1,3},{2,0},{3,1},{4,6},{5,7},{6,4},{7,5},{8,10},{9,11},{10,... | collective-permute-start | bytes 589832 | tf_op jit(solution)/shard_map/ppermute | solution.py:40
  42.5 8.1 %experts.4 = (bf16[192,640]{1,0:T(8,128)(2,1)S(1)}, bf16[192,640]{1,0:T(8,128)(2,1)S(1)}, bf16[192,640]{1,0:T(8,128)(2,1)S(1)}, bf16[192,640]{1,0:T(8,128)(2,1)S(1)}) custom-call(bf16[192,640]{1,0:T(8,128)(2,1)S(1)} %pad_maximum_fusion.refs_0_, bf16[192,640]{1,0:T(8,128)(2,1)S(1)} %tie.13.refs_1_, bf16[192,640]{1,0:T(8,128)(2,1)S(1)} %collective-permute-done.10.refs_2_, ...), custom_call_target="tpu_custom_call" | custom-call | flops 2548039680 | bytes 13271040 | tf_op jit(solution)/shard_map/experts/pallas_call | solution.py:313
  50.7 0.1 collective-permute-start.17
  50.7 0.3 route.3.refs_8_.weight_ref
  51.2 0.6 collective-permute-start.19
  51.7 0.1 collective-permute-start.20
  51.8 0.4 collective-permute-done.17
  52.2 0.1 add_convert_fusion.1.refs_7_
  52.3 0.5 collective-permute-start.18
  52.9 0.3 collective-permute-done.20.refs_3_
  53.2 11.5 %experts.5 = (bf16[192,512]{1,0:T(8,128)(2,1)S(1)}, bf16[192,512]{1,0:T(8,128)(2,1)S(1)}, bf16[192,512]{1,0:T(8,128)(2,1)S(1)}, bf16[192,512]{1,0:T(8,128)(2,1)S(1)}) custom-call(bf16[192,512]{1,0:T(8,128)(2,1)S(1)} %pad_maximum_fusion.1.refs_11_.refs_0_, bf16[192,512]{1,0:T(8,128)(2,1)S(1)} %tie.15.refs_0_.refs_1_, ...), custom_call_target="tpu_custom_call" | custom-call | flops 3822059520 | bytes 26542080 | tf_op jit(solution)/shard_map/experts/pallas_call | solution.py:313
  64.8 0.3 collective-permute-start.21
  65.1 0.3 collective-permute-start.16
  65.5 0.3 collective-permute-start.25
  65.8 0.5 collective-permute-done.21
  66.3 0.1 add_convert_fusion.3.refs_0_
  66.4 1.3 %collective-permute-start.26 = (bf16[192,512]{1,0:T(8,128)(2,1)S(1)}, bf16[192,512]{1,0:T(8,128)(2,1)S(1)}, u32[]{:S(2)}, u32[]{:S(2)}) collective-permute-start(bf16[192,512]{1,0:T(8,128)(2,1)S(1)} %add_convert_fusion.3.refs_0_), channel_id=1, source_target_pairs={{0,2},{1,3},{2,0},{3,1},{4,6},{5,7},{6,4},{7,5},{8,10},{9,11},{10,... | collective-permute-start | bytes 589832 | tf_op jit(solution)/shard_map/ppermute | solution.py:40
  67.7 0.1 add_convert_fusion
  67.8 1.9 %collective-permute-start.24 = (bf16[48,640]{1,0:T(8,128)(2,1)S(1)}, bf16[48,640]{1,0:T(8,128)(2,1)S(1)}, u32[]{:S(2)}, u32[]{:S(2)}) collective-permute-start(bf16[48,640]{1,0:T(8,128)(2,1)S(1)} %get-tuple-element.57), channel_id=1, source_target_pairs={{0,12},{1,13},{2,14},{3,15},{4,8},{5,9},{6,10},{7,11},{8,4},{9,5},... | collective-permute-start | bytes 184328 | tf_op jit(solution)/shard_map/ppermute | solution.py:40
  69.8 0.8 collective-permute-start.23
  70.6 1.7 %collective-permute-start.22 = (bf16[48,640]{1,0:T(8,128)(2,1)S(1)}, bf16[48,640]{1,0:T(8,128)(2,1)S(1)}, u32[]{:S(2)}, u32[]{:S(2)}) collective-permute-start(bf16[48,640]{1,0:T(8,128)(2,1)S(1)} %get-tuple-element.59), channel_id=1, source_target_pairs={{0,4},{1,5},{2,6},{3,7},{4,0},{5,1},{6,2},{7,3},{8,12},{9,13},{10,... | collective-permute-start | bytes 184328 | tf_op jit(solution)/shard_map/ppermute | solution.py:40
  72.3 1.2 %collective-permute-done.26 = bf16[192,512]{1,0:T(8,128)(2,1)S(1)} collective-permute-done((bf16[192,512]{1,0:T(8,128)(2,1)S(1)}, bf16[192,512]{1,0:T(8,128)(2,1)S(1)}, u32[]{:S(2)}, u32[]{:S(2)}) %collective-permute-start.26) | collective-permute-done | bytes 196640 | tf_op jit(solution)/shard_map/ppermute | solution.py:40
  73.5 0.1 add_convert_fusion.2
  73.6 2.3 %collective-permute-start.29 = (bf16[48,512]{1,0:T(8,128)(2,1)S(1)}, bf16[48,512]{1,0:T(8,128)(2,1)S(1)}, u32[]{:S(2)}, u32[]{:S(2)}) collective-permute-start(bf16[48,512]{1,0:T(8,128)(2,1)S(1)} %get-tuple-element.61), channel_id=1, source_target_pairs={{0,12},{1,13},{2,14},{3,15},{4,8},{5,9},{6,10},{7,11},{8,4},{9,5},... | collective-permute-start | bytes 147464 | tf_op jit(solution)/shard_map/ppermute | solution.py:40
  75.9 0.5 collective-permute-start.28
  76.4 1.7 %collective-permute-start.27 = (bf16[48,512]{1,0:T(8,128)(2,1)S(1)}, bf16[48,512]{1,0:T(8,128)(2,1)S(1)}, u32[]{:S(2)}, u32[]{:S(2)}) collective-permute-start(bf16[48,512]{1,0:T(8,128)(2,1)S(1)} %get-tuple-element.63), channel_id=1, source_target_pairs={{0,4},{1,5},{2,6},{3,7},{4,0},{5,1},{6,2},{7,3},{8,12},{9,13},{10,... | collective-permute-start | bytes 147464 | tf_op jit(solution)/shard_map/ppermute | solution.py:40
  78.1 0.9 %combine.2 = bf16[16,2560]{1,0:T(8,128)(2,1)} custom-call(f32[16,4]{1,0:T(8,128)S(1)} %get-tuple-element.26.spot_ref, f32[16,2]{1,0:T(8,128)S(1)} %route.2.refs_12_.weight_ref, bf16[48,640]{1,0:T(8,128)(2,1)S(1)} %get-tuple-element.60.refs_0_, bf16[48,640]{1,0:T(8,128)(2,1)S(1)} %collective-permute-done.22.refs_1_, ...), custom_call_target="tpu_custom_call" | custom-call | tf_op jit(solution)/shard_map/combine/pallas_call | solution.py:365
  79.0 0.6 collective-permute-done.29.refs_3_
  79.6 1.7 %collective-permute-done.28.refs_2_ = bf16[48,512]{1,0:T(8,128)(2,1)S(1)} collective-permute-done((bf16[48,512]{1,0:T(8,128)(2,1)S(1)}, bf16[48,512]{1,0:T(8,128)(2,1)S(1)}, u32[]{:S(2)}, u32[]{:S(2)}) %collective-permute-start.28) | collective-permute-done | bytes 49184 | tf_op jit(solution)/shard_map/ppermute | solution.py:40
  81.2 0.9 %combine.3 = bf16[16,2560]{1,0:T(8,128)(2,1)} custom-call(f32[16,4]{1,0:T(8,128)S(1)} %get-tuple-element.32.spot_ref, f32[16,2]{1,0:T(8,128)S(1)} %route.3.refs_8_.weight_ref, bf16[48,512]{1,0:T(8,128)(2,1)S(1)} %get-tuple-element.64.refs_0_, bf16[48,512]{1,0:T(8,128)(2,1)S(1)} %collective-permute-done.27.refs_1_, ...), custom_call_target="tpu_custom_call" | custom-call | tf_op jit(solution)/shard_map/combine/pallas_call | solution.py:365
  (60 shorter events, 0.6 us)
Async XLA Ops:
  0.6 1.4 %copy-start = (bf16[256,2560]{1,0:T(8,128)(2,1)S(1)}, bf16[256,2560]{1,0:T(8,128)(2,1)}, u32[]{:S(2)}) copy-start(bf16[256,2560]{1,0:T(8,128)(2,1)} %param.14) | copy-start | bytes 3932164
  2.0 1.1 %copy-start.7 = (s32[2]{0:T(128)S(1)}, s32[2]{0:T(128)}, u32[]{:S(2)}) copy-start(s32[2]{0:T(128)} %param.20) | copy-start | bytes 28
  2.1 1.2 %copy-start.5 = (s32[16,2]{0,1:T(2,128)S(1)}, s32[16,2]{0,1:T(2,128)}, u32[]{:S(2)}) copy-start(s32[16,2]{0,1:T(2,128)} %param.19) | copy-start | bytes 388
  2.1 1.2 %copy-start.6 = (s32[16,2]{0,1:T(2,128)S(1)}, s32[16,2]{0,1:T(2,128)}, u32[]{:S(2)}) copy-start(s32[16,2]{0,1:T(2,128)} %param.18) | copy-start | bytes 388
  2.1 1.2 %copy-start.3 = (f32[2560]{0:T(1024)S(1)}, f32[2560]{0:T(1024)}, u32[]{:S(2)}) copy-start(f32[2560]{0:T(1024)} %param.15) | copy-start | bytes 30724
  2.1 1.2 %copy-start.4 = (f32[2560]{0:T(1024)S(1)}, f32[2560]{0:T(1024)}, u32[]{:S(2)}) copy-start(f32[2560]{0:T(1024)} %param.16) | copy-start | bytes 30724
  2.5 16.4 %collective-permute-start.1 = (bf16[64,2560]{1,0:T(8,128)(2,1)S(1)}, bf16[64,2560]{1,0:T(8,128)(2,1)S(1)}, u32[]{:S(2)}, u32[]{:S(2)}) collective-permute-start(bf16[64,2560]{1,0:T(8,128)(2,1)S(1)} %get-tuple-element.52), channel_id=1, source_target_pairs={{0,1},{1,0},{2,3},{3,2},{4,5},{5,4},{6,7},{7,6},{8,9},{9,8},{10,11... | collective-permute-start | bytes 983048 | tf_op jit(solution)/shard_map/ppermute | solution.py:40
  3.0 1.7 %collective-permute-start = (bf16[64,2560]{1,0:T(8,128)(2,1)S(1)}, bf16[64,2560]{1,0:T(8,128)(2,1)S(1)}, u32[]{:S(2)}, u32[]{:S(2)}) collective-permute-start(bf16[64,2560]{1,0:T(8,128)(2,1)S(1)} %get-tuple-element.53), channel_id=1, source_target_pairs={{0,1},{1,0},{2,3},{3,2},{4,5},{5,4},{6,7},{7,6},{8,9},{9,8},{10,11... | collective-permute-start | bytes 983048 | tf_op jit(solution)/shard_map/ppermute | solution.py:40
  3.7 4.1 %copy-start.2 = (f32[2560,4]{0,1:T(4,128)S(1)}, f32[2560,4]{0,1:T(4,128)}, u32[]{:S(2)}) copy-start(f32[2560,4]{0,1:T(4,128)} %param.17) | copy-start | bytes 122884
  3.7 4.1 %copy-start.1 = (bf16[16,2560]{1,0:T(8,128)(2,1)S(1)}, bf16[16,2560]{1,0:T(8,128)(2,1)}, u32[]{:S(2)}) copy-start(bf16[16,2560]{1,0:T(8,128)(2,1)} %image_ref.1) | copy-start | bytes 245764
  4.8 14.0 %collective-permute-start.2 = (bf16[64,2560]{1,0:T(8,128)(2,1)S(1)}, bf16[64,2560]{1,0:T(8,128)(2,1)S(1)}, u32[]{:S(2)}, u32[]{:S(2)}) collective-permute-start(bf16[64,2560]{1,0:T(8,128)(2,1)S(1)} %fusion.1.refs_0_), channel_id=1, source_target_pairs={{0,2},{1,3},{2,0},{3,1},{4,6},{5,7},{6,4},{7,5},{8,10},{9,11},{10,... | collective-permute-start | bytes 983048 | tf_op jit(solution)/shard_map/ppermute | solution.py:40
  8.6 4.5 %collective-permute-start.3 = (bf16[48,640]{1,0:T(8,128)(2,1)S(1)}, bf16[48,640]{1,0:T(8,128)(2,1)S(1)}, u32[]{:S(2)}, u32[]{:S(2)}) collective-permute-start(bf16[48,640]{1,0:T(8,128)(2,1)S(1)} %get-tuple-element.29), channel_id=1, source_target_pairs={{0,4},{1,5},{2,6},{3,7},{4,0},{5,1},{6,2},{7,3},{8,12},{9,13},{10,... | collective-permute-start | bytes 184328 | tf_op jit(solution)/shard_map/ppermute | solution.py:40
  10.3 7.0 %collective-permute-start.4 = (bf16[48,640]{1,0:T(8,128)(2,1)S(1)}, bf16[48,640]{1,0:T(8,128)(2,1)S(1)}, u32[]{:S(2)}, u32[]{:S(2)}) collective-permute-start(bf16[48,640]{1,0:T(8,128)(2,1)S(1)} %get-tuple-element.30), channel_id=1, source_target_pairs={{0,8},{1,9},{2,10},{3,11},{4,12},{5,13},{6,14},{7,15},{8,0},{9,1},... | collective-permute-start | bytes 184328 | tf_op jit(solution)/shard_map/ppermute | solution.py:40
  12.8 6.0 %collective-permute-start.5 = (bf16[48,640]{1,0:T(8,128)(2,1)S(1)}, bf16[48,640]{1,0:T(8,128)(2,1)S(1)}, u32[]{:S(2)}, u32[]{:S(2)}) collective-permute-start(bf16[48,640]{1,0:T(8,128)(2,1)S(1)} %get-tuple-element.31), channel_id=1, source_target_pairs={{0,12},{1,13},{2,14},{3,15},{4,8},{5,9},{6,10},{7,11},{8,4},{9,5},... | collective-permute-start | bytes 184328 | tf_op jit(solution)/shard_map/ppermute | solution.py:40
  19.1 9.1 %collective-permute-start.6 = (bf16[192,640]{1,0:T(8,128)(2,1)S(1)}, bf16[192,640]{1,0:T(8,128)(2,1)S(1)}, u32[]{:S(2)}, u32[]{:S(2)}) collective-permute-start(bf16[192,640]{1,0:T(8,128)(2,1)S(1)} %pad_maximum_fusion.refs_0_), channel_id=1, source_target_pairs={{0,2},{1,3},{2,0},{3,1},{4,6},{5,7},{6,4},{7,5},{8,10},{9,11},{10,... | collective-permute-start | bytes 737288 | tf_op jit(solution)/shard_map/ppermute | solution.py:40
  19.6 7.1 %collective-permute-start.9 = (bf16[16,2560]{1,0:T(8,128)(2,1)S(1)}, bf16[16,2560]{1,0:T(8,128)(2,1)S(1)}, u32[]{:S(2)}, u32[]{:S(2)}) collective-permute-start(bf16[16,2560]{1,0:T(8,128)(2,1)S(1)} %get-tuple-element.54.refs_2_), channel_id=1, source_target_pairs={{0,12},{1,13},{2,14},{3,15},{4,8},{5,9},{6,10},{7,11},{8,4},{9,5},... | collective-permute-start | bytes 245768 | tf_op jit(solution)/shard_map/ppermute | solution.py:40
  21.4 6.8 %collective-permute-start.8 = (bf16[16,2560]{1,0:T(8,128)(2,1)S(1)}, bf16[16,2560]{1,0:T(8,128)(2,1)S(1)}, u32[]{:S(2)}, u32[]{:S(2)}) collective-permute-start(bf16[16,2560]{1,0:T(8,128)(2,1)S(1)} %get-tuple-element.55.refs_1_), channel_id=1, source_target_pairs={{0,8},{1,9},{2,10},{3,11},{4,12},{5,13},{6,14},{7,15},{8,0},{9,1},... | collective-permute-start | bytes 245768 | tf_op jit(solution)/shard_map/ppermute | solution.py:40
  21.4 6.8 %collective-permute-start.7 = (bf16[16,2560]{1,0:T(8,128)(2,1)S(1)}, bf16[16,2560]{1,0:T(8,128)(2,1)S(1)}, u32[]{:S(2)}, u32[]{:S(2)}) collective-permute-start(bf16[16,2560]{1,0:T(8,128)(2,1)S(1)} %get-tuple-element.56.refs_0_), channel_id=1, source_target_pairs={{0,4},{1,5},{2,6},{3,7},{4,0},{5,1},{6,2},{7,3},{8,12},{9,13},{10,... | collective-permute-start | bytes 245768 | tf_op jit(solution)/shard_map/ppermute | solution.py:40
  24.0 8.7 %collective-permute-start.10 = (bf16[192,640]{1,0:T(8,128)(2,1)S(1)}, bf16[192,640]{1,0:T(8,128)(2,1)S(1)}, u32[]{:S(2)}, u32[]{:S(2)}) collective-permute-start(bf16[192,640]{1,0:T(8,128)(2,1)S(1)} %pad_maximum_fusion.refs_0_), channel_id=1, source_target_pairs={{0,1},{1,0},{2,3},{3,2},{4,5},{5,4},{6,7},{7,6},{8,9},{9,8},{10,11... | collective-permute-start | bytes 737288 | tf_op jit(solution)/shard_map/ppermute | solution.py:40
  28.2 4.6 %collective-permute-start.11 = (bf16[192,640]{1,0:T(8,128)(2,1)S(1)}, bf16[192,640]{1,0:T(8,128)(2,1)S(1)}, u32[]{:S(2)}, u32[]{:S(2)}) collective-permute-start(bf16[192,640]{1,0:T(8,128)(2,1)S(1)} %tie.13.refs_1_), channel_id=1, source_target_pairs={{0,1},{1,0},{2,3},{3,2},{4,5},{5,4},{6,7},{7,6},{8,9},{9,8},{10,11... | collective-permute-start | bytes 737288 | tf_op jit(solution)/shard_map/ppermute | solution.py:40
  29.2 11.6 %collective-permute-start.13 = (bf16[48,512]{1,0:T(8,128)(2,1)S(1)}, bf16[48,512]{1,0:T(8,128)(2,1)S(1)}, u32[]{:S(2)}, u32[]{:S(2)}) collective-permute-start(bf16[48,512]{1,0:T(8,128)(2,1)S(1)} %get-tuple-element.39), channel_id=1, source_target_pairs={{0,8},{1,9},{2,10},{3,11},{4,12},{5,13},{6,14},{7,15},{8,0},{9,1},... | collective-permute-start | bytes 147464 | tf_op jit(solution)/shard_map/ppermute | solution.py:40
  30.2 10.7 %collective-permute-start.14 = (bf16[48,512]{1,0:T(8,128)(2,1)S(1)}, bf16[48,512]{1,0:T(8,128)(2,1)S(1)}, u32[]{:S(2)}, u32[]{:S(2)}) collective-permute-start(bf16[48,512]{1,0:T(8,128)(2,1)S(1)} %get-tuple-element.40), channel_id=1, source_target_pairs={{0,12},{1,13},{2,14},{3,15},{4,8},{5,9},{6,10},{7,11},{8,4},{9,5},... | collective-permute-start | bytes 147464 | tf_op jit(solution)/shard_map/ppermute | solution.py:40
  32.0 8.9 %collective-permute-start.12 = (bf16[48,512]{1,0:T(8,128)(2,1)S(1)}, bf16[48,512]{1,0:T(8,128)(2,1)S(1)}, u32[]{:S(2)}, u32[]{:S(2)}) collective-permute-start(bf16[48,512]{1,0:T(8,128)(2,1)S(1)} %get-tuple-element.33.refs_7_), channel_id=1, source_target_pairs={{0,4},{1,5},{2,6},{3,7},{4,0},{5,1},{6,2},{7,3},{8,12},{9,13},{10,... | collective-permute-start | bytes 147464 | tf_op jit(solution)/shard_map/ppermute | solution.py:40
  40.9 9.7 %collective-permute-start.15 = (bf16[192,512]{1,0:T(8,128)(2,1)S(1)}, bf16[192,512]{1,0:T(8,128)(2,1)S(1)}, u32[]{:S(2)}, u32[]{:S(2)}) collective-permute-start(bf16[192,512]{1,0:T(8,128)(2,1)S(1)} %pad_maximum_fusion.1.refs_11_.refs_0_), channel_id=1, source_target_pairs={{0,2},{1,3},{2,0},{3,1},{4,6},{5,7},{6,4},{7,5},{8,10},{9,11},{10,... | collective-permute-start | bytes 589832 | tf_op jit(solution)/shard_map/ppermute | solution.py:40
  50.7 1.6 %collective-permute-start.17 = (bf16[192,640]{1,0:T(8,128)(2,1)S(1)}, bf16[192,640]{1,0:T(8,128)(2,1)S(1)}, u32[]{:S(2)}, u32[]{:S(2)}) collective-permute-start(bf16[192,640]{1,0:T(8,128)(2,1)S(1)} %tie.17), channel_id=1, source_target_pairs={{0,1},{1,0},{2,3},{3,2},{4,5},{5,4},{6,7},{7,6},{8,9},{9,8},{10,11... | collective-permute-start | bytes 737288 | tf_op jit(solution)/shard_map/ppermute | solution.py:40
  51.2 1.7 %collective-permute-start.19 = (bf16[192,512]{1,0:T(8,128)(2,1)S(1)}, bf16[192,512]{1,0:T(8,128)(2,1)S(1)}, u32[]{:S(2)}, u32[]{:S(2)}) collective-permute-start(bf16[192,512]{1,0:T(8,128)(2,1)S(1)} %pad_maximum_fusion.1.refs_11_.refs_0_), channel_id=1, source_target_pairs={{0,1},{1,0},{2,3},{3,2},{4,5},{5,4},{6,7},{7,6},{8,9},{9,8},{10,11... | collective-permute-start | bytes 589832 | tf_op jit(solution)/shard_map/ppermute | solution.py:40
  51.7 1.4 %collective-permute-start.20 = (bf16[192,512]{1,0:T(8,128)(2,1)S(1)}, bf16[192,512]{1,0:T(8,128)(2,1)S(1)}, u32[]{:S(2)}, u32[]{:S(2)}) collective-permute-start(bf16[192,512]{1,0:T(8,128)(2,1)S(1)} %tie.15.refs_0_.refs_1_), channel_id=1, source_target_pairs={{0,1},{1,0},{2,3},{3,2},{4,5},{5,4},{6,7},{7,6},{8,9},{9,8},{10,11... | collective-permute-start | bytes 589832 | tf_op jit(solution)/shard_map/ppermute | solution.py:40
  52.3 12.4 %collective-permute-start.18 = (bf16[192,640]{1,0:T(8,128)(2,1)S(1)}, bf16[192,640]{1,0:T(8,128)(2,1)S(1)}, u32[]{:S(2)}, u32[]{:S(2)}) collective-permute-start(bf16[192,640]{1,0:T(8,128)(2,1)S(1)} %add_convert_fusion.1.refs_7_), channel_id=1, source_target_pairs={{0,2},{1,3},{2,0},{3,1},{4,6},{5,7},{6,4},{7,5},{8,10},{9,11},{10,... | collective-permute-start | bytes 737288 | tf_op jit(solution)/shard_map/ppermute | solution.py:40
  64.8 1.5 %collective-permute-start.21 = (bf16[192,512]{1,0:T(8,128)(2,1)S(1)}, bf16[192,512]{1,0:T(8,128)(2,1)S(1)}, u32[]{:S(2)}, u32[]{:S(2)}) collective-permute-start(bf16[192,512]{1,0:T(8,128)(2,1)S(1)} %tie.19), channel_id=1, source_target_pairs={{0,1},{1,0},{2,3},{3,2},{4,5},{5,4},{6,7},{7,6},{8,9},{9,8},{10,11... | collective-permute-start | bytes 589832 | tf_op jit(solution)/shard_map/ppermute | solution.py:40
  65.1 2.5 %collective-permute-start.16 = (bf16[192,640]{1,0:T(8,128)(2,1)S(1)}, bf16[192,640]{1,0:T(8,128)(2,1)S(1)}, u32[]{:S(2)}, u32[]{:S(2)}) collective-permute-start(bf16[192,640]{1,0:T(8,128)(2,1)S(1)} %tie.16), channel_id=1, source_target_pairs={{0,1},{1,0},{2,3},{3,2},{4,5},{5,4},{6,7},{7,6},{8,9},{9,8},{10,11... | collective-permute-start | bytes 737288 | tf_op jit(solution)/shard_map/ppermute | solution.py:40
  65.5 6.8 %collective-permute-start.25 = (bf16[192,512]{1,0:T(8,128)(2,1)S(1)}, bf16[192,512]{1,0:T(8,128)(2,1)S(1)}, u32[]{:S(2)}, u32[]{:S(2)}) collective-permute-start(bf16[192,512]{1,0:T(8,128)(2,1)S(1)} %tie.21), channel_id=1, source_target_pairs={{0,1},{1,0},{2,3},{3,2},{4,5},{5,4},{6,7},{7,6},{8,9},{9,8},{10,11... | collective-permute-start | bytes 589832 | tf_op jit(solution)/shard_map/ppermute | solution.py:40
  66.4 7.2 %collective-permute-start.26 = (bf16[192,512]{1,0:T(8,128)(2,1)S(1)}, bf16[192,512]{1,0:T(8,128)(2,1)S(1)}, u32[]{:S(2)}, u32[]{:S(2)}) collective-permute-start(bf16[192,512]{1,0:T(8,128)(2,1)S(1)} %add_convert_fusion.3.refs_0_), channel_id=1, source_target_pairs={{0,2},{1,3},{2,0},{3,1},{4,6},{5,7},{6,4},{7,5},{8,10},{9,11},{10,... | collective-permute-start | bytes 589832 | tf_op jit(solution)/shard_map/ppermute | solution.py:40
  67.8 8.5 %collective-permute-start.24 = (bf16[48,640]{1,0:T(8,128)(2,1)S(1)}, bf16[48,640]{1,0:T(8,128)(2,1)S(1)}, u32[]{:S(2)}, u32[]{:S(2)}) collective-permute-start(bf16[48,640]{1,0:T(8,128)(2,1)S(1)} %get-tuple-element.57), channel_id=1, source_target_pairs={{0,12},{1,13},{2,14},{3,15},{4,8},{5,9},{6,10},{7,11},{8,4},{9,5},... | collective-permute-start | bytes 184328 | tf_op jit(solution)/shard_map/ppermute | solution.py:40
  69.8 8.3 %collective-permute-start.23 = (bf16[48,640]{1,0:T(8,128)(2,1)S(1)}, bf16[48,640]{1,0:T(8,128)(2,1)S(1)}, u32[]{:S(2)}, u32[]{:S(2)}) collective-permute-start(bf16[48,640]{1,0:T(8,128)(2,1)S(1)} %get-tuple-element.58), channel_id=1, source_target_pairs={{0,8},{1,9},{2,10},{3,11},{4,12},{5,13},{6,14},{7,15},{8,0},{9,1},... | collective-permute-start | bytes 184328 | tf_op jit(solution)/shard_map/ppermute | solution.py:40
  70.6 7.5 %collective-permute-start.22 = (bf16[48,640]{1,0:T(8,128)(2,1)S(1)}, bf16[48,640]{1,0:T(8,128)(2,1)S(1)}, u32[]{:S(2)}, u32[]{:S(2)}) collective-permute-start(bf16[48,640]{1,0:T(8,128)(2,1)S(1)} %get-tuple-element.59), channel_id=1, source_target_pairs={{0,4},{1,5},{2,6},{3,7},{4,0},{5,1},{6,2},{7,3},{8,12},{9,13},{10,... | collective-permute-start | bytes 184328 | tf_op jit(solution)/shard_map/ppermute | solution.py:40
  73.6 6.0 %collective-permute-start.29 = (bf16[48,512]{1,0:T(8,128)(2,1)S(1)}, bf16[48,512]{1,0:T(8,128)(2,1)S(1)}, u32[]{:S(2)}, u32[]{:S(2)}) collective-permute-start(bf16[48,512]{1,0:T(8,128)(2,1)S(1)} %get-tuple-element.61), channel_id=1, source_target_pairs={{0,12},{1,13},{2,14},{3,15},{4,8},{5,9},{6,10},{7,11},{8,4},{9,5},... | collective-permute-start | bytes 147464 | tf_op jit(solution)/shard_map/ppermute | solution.py:40
  75.9 5.3 %collective-permute-start.28 = (bf16[48,512]{1,0:T(8,128)(2,1)S(1)}, bf16[48,512]{1,0:T(8,128)(2,1)S(1)}, u32[]{:S(2)}, u32[]{:S(2)}) collective-permute-start(bf16[48,512]{1,0:T(8,128)(2,1)S(1)} %get-tuple-element.62), channel_id=1, source_target_pairs={{0,8},{1,9},{2,10},{3,11},{4,12},{5,13},{6,14},{7,15},{8,0},{9,1},... | collective-permute-start | bytes 147464 | tf_op jit(solution)/shard_map/ppermute | solution.py:40
  76.4 4.9 %collective-permute-start.27 = (bf16[48,512]{1,0:T(8,128)(2,1)S(1)}, bf16[48,512]{1,0:T(8,128)(2,1)S(1)}, u32[]{:S(2)}, u32[]{:S(2)}) collective-permute-start(bf16[48,512]{1,0:T(8,128)(2,1)S(1)} %get-tuple-element.63), channel_id=1, source_target_pairs={{0,4},{1,5},{2,6},{3,7},{4,0},{5,1},{6,2},{7,3},{8,12},{9,13},{10,... | collective-permute-start | bytes 147464 | tf_op jit(solution)/shard_map/ppermute | solution.py:40

commit v10 on v9

--- a/solution.py
+++ b/solution.py
@@ -8,6 +8,7 @@
 from jax.sharding import PartitionSpec as P
 
 PLEN = 128
+HINT = 1 << 33
 VMEM = pl.BlockSpec(memory_space=pltpu.VMEM)
 SMEM = pl.BlockSpec(memory_space=pltpu.SMEM)
 ANY = pl.BlockSpec(memory_space=pl.ANY)
@@ -135,19 +136,24 @@
     return results[:3], list(results[3:])
 
 
-def tie_kernel(value_ref, *refs):
-    refs[-1][...] = value_ref[...]
-
-
-def tie(value, after):
+def tie_kernel(count, *refs):
+    value = refs[0][...]
+    for ref in refs[1:count]:
+        value = value.astype(jnp.float32) + ref[...].astype(jnp.float32)
+    refs[-1][...] = value
+
+
+def tie(values, after, cost=0):
+    kind = values[0].dtype if len(values) == 1 else jnp.float32
     return pl.pallas_call(
-        tie_kernel,
-        out_shape=jax.ShapeDtypeStruct(value.shape, value.dtype),
-        in_specs=[VMEM] + [ANY] * len(after),
+        functools.partial(tie_kernel, len(values)),
+        out_shape=jax.ShapeDtypeStruct(values[0].shape, kind),
+        in_specs=[VMEM] * len(values) + [ANY] * len(after),
         out_specs=VMEM,
         compiler_params=pltpu.CompilerParams(vmem_limit_bytes=8 << 20),
+        cost_estimate=pl.CostEstimate(flops=cost, bytes_accessed=0, transcendentals=0),
         name="tie",
-    )(value, *after)
+    )(*values, *after)
 
 
 def modulate_kernel(packing, experts, count, spot_ref, small_ref, *refs):
@@ -169,6 +175,7 @@
         in_specs=[VMEM] * (2 + len(terms)),
         out_specs=[VMEM] * (1 + experts),
         compiler_params=pltpu.CompilerParams(vmem_limit_bytes=8 << 20),
+        cost_estimate=pl.CostEstimate(flops=HINT, bytes_accessed=0, transcendentals=0),
         name="modulate",
     )(spot, small, *terms)
     return (results[0], list(results[1:]))
@@ -203,7 +210,7 @@
 
 def cuts(units, part, parts):
     first, last = [units * p // parts // 16 * 16 for p in (part, part + 1)]
-    edges = [first] + list(range(first + 256, last - 255, 512 if parts == 1 else 320)) + [last]
+    edges = [first] + list(range(first + (256 if parts == 1 else 384), last - 255, 512)) + [last]
     return list(zip(edges[:-1], edges[1:]))
 
 
@@ -467,33 +474,32 @@
     )
     image_first = [blocks[0]] + to_experts(blocks)
 
-    received[0] = tie(received[0], image_first[1:])
+    received[0] = tie([received[0]], blocks[1:2], HINT)
     total = sums[-1]
     for value in received:
         total = total + value.astype(wide)
     parts = split(total, experts)
-    sent = [part.astype(narrow) for part in parts]
-    terms = [parts[0]] + to_experts(sent)
-    image_first = jnp.concatenate([tie(image_first[0], sent[1:])] + image_first[1:], axis=0)
+    sent = [part.astype(narrow) for part in parts[1:]]
+    terms = parts[:1] + [grid.swap(part, 0, k) for k, part in enumerate(sent, 1)]
+    image_first = jnp.concatenate([tie([image_first[0]], sent)] + image_first[1:], axis=0)
     image_own = to_pairs(image_first)
-    image_own = image_own[:1] + [tie(value, terms[1:]) for value in image_own[1:]]
+    weights = (w_gate, w_up, w_down)
+
+    caption_normed, blocks = modulate(terms, caption_spot, small, caption_packing, experts)
+    received = to_experts(blocks)
+    image_own = image_own[:1] + [tie([value], blocks[1:2]) for value in image_own[1:]]
     image_arrays = image_own + over_cores(image_own)
-    weights = (w_gate, w_up, w_down)
-
-    caption_normed, blocks = modulate(terms, caption_spot, small, caption_packing, experts)
-    image_half = expert_rows(image_arrays, *weights, image_packing, blocks[1:2], 0, 2)
-    received = to_experts(blocks)
-    caption_first = jnp.concatenate([tie(blocks[0], image_half[:1])] + received, axis=0)
+    caption_first = jnp.concatenate([blocks[0]] + received, axis=0)
     caption_own = to_pairs(caption_first)
 
     image_weights = route(image_normed, image_spot, small)
     caption_weights = route(caption_normed, caption_spot, small)
     image_results = expert_rows(
-        image_arrays, *weights, image_packing, [caption_first, image_weights], 1, 2, image_half
-    )
-    caption_own = caption_own[:1] + [tie(value, image_results[:1]) for value in caption_own[1:]]
+        image_arrays, *weights, image_packing, [caption_first, image_weights]
+    )
+    caption_own = caption_own[:1] + [tie([value], image_results[:1]) for value in caption_own[1:]]
     image_results = list(image_results[:pairs]) + [
-        tie(value, caption_own[1:2]) for value in image_results[pairs:]
+        tie([value], caption_own[1:2]) for value in image_results[pairs:]
     ]
     image_kept, image_crossing = join_cores(image_results)
     caption_results = expert_rows(
@@ -503,13 +509,13 @@
         image_crossing[:1] + [caption_weights],
     )
     image_received = [
-        tie(value, caption_results[:1]) for value in from_pairs(image_crossing)
+        tie([value], caption_results[:1]) for value in from_pairs(image_crossing)
     ]
     caption_results = list(caption_results[:pairs]) + [
-        tie(value, image_received[:1]) for value in caption_results[pairs:]
+        tie([value], image_received[:1]) for value in caption_results[pairs:]
     ]
     caption_kept, caption_crossing = join_cores(caption_results)
-    image_received = [tie(value, caption_crossing[:1]) for value in image_received]
+    image_received = [tie([value], caption_crossing[:1]) for value in image_received]
     image_blocks = from_experts(image_kept, image_received)
     caption_received = from_pairs(caption_crossing)
     caption_blocks = from_experts(caption_kept, caption_received)

time: 82.3 us -> 81.4 us (0.989)
  Pallas kernels: 31.7 us -> 27.6 us
  starting transfers between devices: 30.7 us -> 33 us
  waiting for transfers between devices: 15.7 us -> 16.7 us
    pallas_call x3 -> x2, Pallas kernels: 27.7 us -> 23.7 us  [expert_rows(): pl.pallas_call(functools.partial(expert_kernel, packing, unit_cuts, len(a...]
    ppermute x30, starting transfers between devices: 30.7 us -> 33 us  [swap(): return lax.ppermute(value, 'dev', moves)]
    ppermute x30, waiting for transfers between devices: 15.7 us -> 16.7 us  [swap(): return lax.ppermute(value, 'dev', moves)]
  transfers between devices with their start and end apart: 30 -> 30, of which waited for: 11 -> 11; matrix products, arithmetic and copies ran while one was open for 1% -> 1% of each run, Pallas kernels for 37% -> 33%
where the time goes in v10:
time: 81.4 us; the launch traced here: 81.2 us
  starting transfers between devices  33 us (41%)
  Pallas kernels  27.6 us (34%)
  waiting for transfers between devices  16.7 us (21%)
  other arithmetic  1.93 us (2%)
  between operations  1.14 us (1%)
    ppermute x30, starting transfers between devices, swap(): return lax.ppermute(value, 'dev', moves)  33 us
    pallas_call x2, Pallas kernels, expert_rows(): pl.pallas_call(functools.partial(expert_kernel, packing, unit_cuts, len(a...  23.7 us
    ppermute x30, waiting for transfers between devices, swap(): return lax.ppermute(value, 'dev', moves)  16.7 us
    pallas_call x2, Pallas kernels, combine(): pl.pallas_call(functools.partial(combine_kernel, packing), out_shape=jax....  1.77 us
  transfers between devices with their start and end apart: 30, of which 11 were waited for; matrix products, arithmetic and copies ran while one was open for 1% of the time, Pallas kernels for 33%

profile of v10, /device:TPU:0, one launch (start us, length us, event | category | flops | bytes accessed | tf_op | source)
XLA Modules:
  0.0 81.2 jit_solution(8545683307654684808)
XLA Ops:
  0.6 0.0 copy-start
  0.7 1.1 %fusion.5 = bf16[2,2,2,2,16,256]{5,4,3,2,1,0:T(8,128)(2,1)S(1)} fusion(s32[]{:T(128)S(6)} %select_n.80, bf16[2,2,2,2,16,256]{5,4,3,2,1,0:T(8,128)(2,1)} %bitcast.29), kind=kLoop, calls=%fused_computation.21 | loop fusion | flops 65536 | bytes 262148 | tf_op jit(solution)/shard_map/jit(_roll_dynamic)/concatenate | solution.py:388
  1.8 0.1 fusion.3
  1.9 0.1 fusion.2
  2.0 0.0 copy-start.7
  2.0 0.0 copy-start.5
  2.1 0.0 copy-start.6
  2.1 0.3 convolution_convert_fusion
  2.5 0.5 collective-permute-start
  3.0 0.1 collective-permute-start.1
  3.1 0.1 fusion.7
  3.3 0.3 fusion.16
  3.7 0.0 copy-start.2
  3.7 0.6 collective-permute-done
  4.3 0.1 fusion.1.refs_0_
  4.3 3.0 %collective-permute-start.2 = (bf16[64,2560]{1,0:T(8,128)(2,1)S(1)}, bf16[64,2560]{1,0:T(8,128)(2,1)S(1)}, u32[]{:S(2)}, u32[]{:S(2)}) collective-permute-start(bf16[64,2560]{1,0:T(8,128)(2,1)S(1)} %fusion.1.refs_0_), channel_id=1, source_target_pairs={{0,2},{1,3},{2,0},{3,1},{4,6},{5,7},{6,4},{7,5},{8,10},{9,11},{10,... | collective-permute-start | bytes 983048 | tf_op jit(solution)/shard_map/ppermute | solution.py:41
  7.3 0.8 %prepare.1 = (f32[16,4]{1,0:T(8,128)S(1)}, f32[16,4]{1,0:T(8,128)S(1)}, bf16[16,2560]{1,0:T(8,128)(2,1)S(1)}, bf16[48,640]{1,0:T(8,128)(2,1)S(1)}, bf16[48,640]{...) custom-call(s32[4,16]{1,0:T(4,128)S(1)} %pad_add_fusion.ids_ref, ...), custom_call_target="tpu_custom_call" | custom-call | tf_op jit(solution)/shard_map/prepare/pallas_call | solution.py:123
  8.2 3.6 %collective-permute-start.5 = (bf16[48,640]{1,0:T(8,128)(2,1)S(1)}, bf16[48,640]{1,0:T(8,128)(2,1)S(1)}, u32[]{:S(2)}, u32[]{:S(2)}) collective-permute-start(bf16[48,640]{1,0:T(8,128)(2,1)S(1)} %get-tuple-element.27), channel_id=1, source_target_pairs={{0,12},{1,13},{2,14},{3,15},{4,8},{5,9},{6,10},{7,11},{8,4},{9,5},... | collective-permute-start | bytes 184328 | tf_op jit(solution)/shard_map/ppermute | solution.py:41
  11.8 0.8 %collective-permute-start.3 = (bf16[48,640]{1,0:T(8,128)(2,1)S(1)}, bf16[48,640]{1,0:T(8,128)(2,1)S(1)}, u32[]{:S(2)}, u32[]{:S(2)}) collective-permute-start(bf16[48,640]{1,0:T(8,128)(2,1)S(1)} %get-tuple-element.25.refs_1_), channel_id=1, source_target_pairs={{0,4},{1,5},{2,6},{3,7},{4,0},{5,1},{6,2},{7,3},{8,12},{9,13},{10,... | collective-permute-start | bytes 184328 | tf_op jit(solution)/shard_map/ppermute | solution.py:41
  12.6 0.3 route.2.refs_8_.weight_ref
  12.9 2.4 %collective-permute-done.2.refs_0_ = bf16[64,2560]{1,0:T(8,128)(2,1)S(1)} collective-permute-done((bf16[64,2560]{1,0:T(8,128)(2,1)S(1)}, bf16[64,2560]{1,0:T(8,128)(2,1)S(1)}, u32[]{:S(2)}, u32[]{:S(2)}) %collective-permute-start.2) | collective-permute-done | bytes 327712 | tf_op jit(solution)/shard_map/ppermute | solution.py:41
  15.3 0.1 fusion.9
  15.5 1.9 %collective-permute-start.7 = (bf16[16,2560]{1,0:T(8,128)(2,1)S(1)}, bf16[16,2560]{1,0:T(8,128)(2,1)S(1)}, u32[]{:S(2)}, u32[]{:S(2)}) collective-permute-start(bf16[16,2560]{1,0:T(8,128)(2,1)S(1)} %get-tuple-element.48.refs_1_), channel_id=1, source_target_pairs={{0,4},{1,5},{2,6},{3,7},{4,0},{5,1},{6,2},{7,3},{8,12},{9,13},{10,... | collective-permute-start | bytes 245768 | tf_op jit(solution)/shard_map/ppermute | solution.py:41
  17.4 2.5 %collective-permute-start.8 = (bf16[16,2560]{1,0:T(8,128)(2,1)S(1)}, bf16[16,2560]{1,0:T(8,128)(2,1)S(1)}, u32[]{:S(2)}, u32[]{:S(2)}) collective-permute-start(bf16[16,2560]{1,0:T(8,128)(2,1)S(1)} %get-tuple-element.47.refs_2_), channel_id=1, source_target_pairs={{0,8},{1,9},{2,10},{3,11},{4,12},{5,13},{6,14},{7,15},{8,0},{9,1},... | collective-permute-start | bytes 245768 | tf_op jit(solution)/shard_map/ppermute | solution.py:41
  19.9 0.1 collective-permute-start.9
  20.1 1.8 %collective-permute-start.6 = (bf16[192,640]{1,0:T(8,128)(2,1)S(1)}, bf16[192,640]{1,0:T(8,128)(2,1)S(1)}, u32[]{:S(2)}, u32[]{:S(2)}) collective-permute-start(bf16[192,640]{1,0:T(8,128)(2,1)S(1)} %pad_maximum_fusion.refs_0_), channel_id=1, source_target_pairs={{0,2},{1,3},{2,0},{3,1},{4,6},{5,7},{6,4},{7,5},{8,10},{9,11},{10,... | collective-permute-start | bytes 737288 | tf_op jit(solution)/shard_map/ppermute | solution.py:41
  21.9 3.3 %collective-permute-done.8.refs_2_ = bf16[16,2560]{1,0:T(8,128)(2,1)S(1)} collective-permute-done((bf16[16,2560]{1,0:T(8,128)(2,1)S(1)}, bf16[16,2560]{1,0:T(8,128)(2,1)S(1)}, u32[]{:S(2)}, u32[]{:S(2)}) %collective-permute-start.8) | collective-permute-done | bytes 81952 | tf_op jit(solution)/shard_map/ppermute | solution.py:41
  25.1 1.2 %collective-permute-done.9.refs_3_ = bf16[16,2560]{1,0:T(8,128)(2,1)S(1)} collective-permute-done((bf16[16,2560]{1,0:T(8,128)(2,1)S(1)}, bf16[16,2560]{1,0:T(8,128)(2,1)S(1)}, u32[]{:S(2)}, u32[]{:S(2)}) %collective-permute-start.9) | collective-permute-done | bytes 81952 | tf_op jit(solution)/shard_map/ppermute | solution.py:41
  26.3 0.6 modulate.1
  27.0 1.2 %collective-permute-start.12 = (bf16[48,512]{1,0:T(8,128)(2,1)S(1)}, bf16[48,512]{1,0:T(8,128)(2,1)S(1)}, u32[]{:S(2)}, u32[]{:S(2)}) collective-permute-start(bf16[48,512]{1,0:T(8,128)(2,1)S(1)} %get-tuple-element.29.refs_1_), channel_id=1, source_target_pairs={{0,4},{1,5},{2,6},{3,7},{4,0},{5,1},{6,2},{7,3},{8,12},{9,13},{10,... | collective-permute-start | bytes 147464 | tf_op jit(solution)/shard_map/ppermute | solution.py:41
  28.2 1.6 %collective-permute-start.13 = (bf16[48,512]{1,0:T(8,128)(2,1)S(1)}, bf16[48,512]{1,0:T(8,128)(2,1)S(1)}, u32[]{:S(2)}, u32[]{:S(2)}) collective-permute-start(bf16[48,512]{1,0:T(8,128)(2,1)S(1)} %get-tuple-element.31), channel_id=1, source_target_pairs={{0,8},{1,9},{2,10},{3,11},{4,12},{5,13},{6,14},{7,15},{8,0},{9,1},... | collective-permute-start | bytes 147464 | tf_op jit(solution)/shard_map/ppermute | solution.py:41
  29.7 1.7 %collective-permute-start.14 = (bf16[48,512]{1,0:T(8,128)(2,1)S(1)}, bf16[48,512]{1,0:T(8,128)(2,1)S(1)}, u32[]{:S(2)}, u32[]{:S(2)}) collective-permute-start(bf16[48,512]{1,0:T(8,128)(2,1)S(1)} %get-tuple-element.32), channel_id=1, source_target_pairs={{0,12},{1,13},{2,14},{3,15},{4,8},{5,9},{6,10},{7,11},{8,4},{9,5},... | collective-permute-start | bytes 147464 | tf_op jit(solution)/shard_map/ppermute | solution.py:41
  31.5 0.1 collective-permute-start.11
  31.6 2.4 %collective-permute-done.13 = bf16[48,512]{1,0:T(8,128)(2,1)S(1)} collective-permute-done((bf16[48,512]{1,0:T(8,128)(2,1)S(1)}, bf16[48,512]{1,0:T(8,128)(2,1)S(1)}, u32[]{:S(2)}, u32[]{:S(2)}) %collective-permute-start.13) | collective-permute-done | bytes 49184 | tf_op jit(solution)/shard_map/ppermute | solution.py:41
  33.9 1.7 %collective-permute-done.14 = bf16[48,512]{1,0:T(8,128)(2,1)S(1)} collective-permute-done((bf16[48,512]{1,0:T(8,128)(2,1)S(1)}, bf16[48,512]{1,0:T(8,128)(2,1)S(1)}, u32[]{:S(2)}, u32[]{:S(2)}) %collective-permute-start.14) | collective-permute-done | bytes 49184 | tf_op jit(solution)/shard_map/ppermute | solution.py:41
  35.6 1.5 %collective-permute-start.15 = (bf16[192,512]{1,0:T(8,128)(2,1)S(1)}, bf16[192,512]{1,0:T(8,128)(2,1)S(1)}, u32[]{:S(2)}, u32[]{:S(2)}) collective-permute-start(bf16[192,512]{1,0:T(8,128)(2,1)S(1)} %constant_dynamic-update-slice_fusion.refs_7_.refs_0_), channel_id=1, source_target_pairs={{0,2},{1,3},{2,0},{3,1},{4,6},{5,7},{6,4},{7,5},{8,10},{9,11},{10,... | collective-permute-start | bytes 589832 | tf_op jit(solution)/shard_map/ppermute | solution.py:41
  37.2 12.1 %experts.2 = (bf16[192,640]{1,0:T(8,128)(2,1)S(1)}, bf16[192,640]{1,0:T(8,128)(2,1)S(1)}, bf16[192,640]{1,0:T(8,128)(2,1)S(1)}, bf16[192,640]{1,0:T(8,128)(2,1)S(1)}) custom-call(bf16[192,640]{1,0:T(8,128)(2,1)S(1)} %pad_maximum_fusion.refs_0_, bf16[192,640]{1,0:T(8,128)(2,1)S(1)} %tie.12.refs_1_, bf16[192,640]{1,0:T(8,128)(2,1)S(1)} %collective-permute-done.10.refs_2_, ...), custom_call_target="tpu_custom_call" | custom-call | flops 5096079360 | bytes 26542080 | tf_op jit(solution)/shard_map/experts/pallas_call | solution.py:320
  49.3 0.1 collective-permute-start.17
  49.4 0.3 route.3.refs_8_.weight_ref
  49.7 0.5 collective-permute-start.19
  50.2 0.1 collective-permute-start.20
  50.3 0.6 collective-permute-done.17
  50.9 0.1 add_convert_fusion.1.refs_7_
  51.0 0.6 collective-permute-start.18
  51.6 0.1 collective-permute-done.20.refs_3_
  51.6 11.6 %experts.3 = (bf16[192,512]{1,0:T(8,128)(2,1)S(1)}, bf16[192,512]{1,0:T(8,128)(2,1)S(1)}, bf16[192,512]{1,0:T(8,128)(2,1)S(1)}, bf16[192,512]{1,0:T(8,128)(2,1)S(1)}) custom-call(bf16[192,512]{1,0:T(8,128)(2,1)S(1)} %constant_dynamic-update-slice_fusion.refs_7_.refs_0_, bf16[192,512]{1,0:T(8,128)(2,1)S(1)} %tie.13.refs_1_, ...), custom_call_target="tpu_custom_call" | custom-call | flops 3822059520 | bytes 26542080 | tf_op jit(solution)/shard_map/experts/pallas_call | solution.py:320
  63.3 0.3 collective-permute-start.21
  63.6 0.3 collective-permute-start.16
  64.0 0.3 collective-permute-start.25
  64.3 0.5 collective-permute-done.21
  64.8 0.1 add_convert_fusion.3.refs_1_
  64.9 1.5 %collective-permute-start.26 = (bf16[192,512]{1,0:T(8,128)(2,1)S(1)}, bf16[192,512]{1,0:T(8,128)(2,1)S(1)}, u32[]{:S(2)}, u32[]{:S(2)}) collective-permute-start(bf16[192,512]{1,0:T(8,128)(2,1)S(1)} %add_convert_fusion.3.refs_1_), channel_id=1, source_target_pairs={{0,2},{1,3},{2,0},{3,1},{4,6},{5,7},{6,4},{7,5},{8,10},{9,11},{10,... | collective-permute-start | bytes 589832 | tf_op jit(solution)/shard_map/ppermute | solution.py:41
  66.4 0.1 add_convert_fusion
  66.5 0.1 collective-permute-start.22
  66.6 2.3 %collective-permute-start.23 = (bf16[48,640]{1,0:T(8,128)(2,1)S(1)}, bf16[48,640]{1,0:T(8,128)(2,1)S(1)}, u32[]{:S(2)}, u32[]{:S(2)}) collective-permute-start(bf16[48,640]{1,0:T(8,128)(2,1)S(1)} %get-tuple-element.50), channel_id=1, source_target_pairs={{0,8},{1,9},{2,10},{3,11},{4,12},{5,13},{6,14},{7,15},{8,0},{9,1},... | collective-permute-start | bytes 184328 | tf_op jit(solution)/shard_map/ppermute | solution.py:41
  68.8 2.1 %collective-permute-start.24 = (bf16[48,640]{1,0:T(8,128)(2,1)S(1)}, bf16[48,640]{1,0:T(8,128)(2,1)S(1)}, u32[]{:S(2)}, u32[]{:S(2)}) collective-permute-start(bf16[48,640]{1,0:T(8,128)(2,1)S(1)} %get-tuple-element.49), channel_id=1, source_target_pairs={{0,12},{1,13},{2,14},{3,15},{4,8},{5,9},{6,10},{7,11},{8,4},{9,5},... | collective-permute-start | bytes 184328 | tf_op jit(solution)/shard_map/ppermute | solution.py:41
  71.0 1.1 %collective-permute-done.26 = bf16[192,512]{1,0:T(8,128)(2,1)S(1)} collective-permute-done((bf16[192,512]{1,0:T(8,128)(2,1)S(1)}, bf16[192,512]{1,0:T(8,128)(2,1)S(1)}, u32[]{:S(2)}, u32[]{:S(2)}) %collective-permute-start.26) | collective-permute-done | bytes 196640 | tf_op jit(solution)/shard_map/ppermute | solution.py:41
  72.0 0.1 add_convert_fusion.2
  72.1 0.1 collective-permute-start.27
  72.2 2.3 %collective-permute-start.28 = (bf16[48,512]{1,0:T(8,128)(2,1)S(1)}, bf16[48,512]{1,0:T(8,128)(2,1)S(1)}, u32[]{:S(2)}, u32[]{:S(2)}) collective-permute-start(bf16[48,512]{1,0:T(8,128)(2,1)S(1)} %get-tuple-element.54), channel_id=1, source_target_pairs={{0,8},{1,9},{2,10},{3,11},{4,12},{5,13},{6,14},{7,15},{8,0},{9,1},... | collective-permute-start | bytes 147464 | tf_op jit(solution)/shard_map/ppermute | solution.py:41
  74.5 2.1 %collective-permute-start.29 = (bf16[48,512]{1,0:T(8,128)(2,1)S(1)}, bf16[48,512]{1,0:T(8,128)(2,1)S(1)}, u32[]{:S(2)}, u32[]{:S(2)}) collective-permute-start(bf16[48,512]{1,0:T(8,128)(2,1)S(1)} %get-tuple-element.53), channel_id=1, source_target_pairs={{0,12},{1,13},{2,14},{3,15},{4,8},{5,9},{6,10},{7,11},{8,4},{9,5},... | collective-permute-start | bytes 147464 | tf_op jit(solution)/shard_map/ppermute | solution.py:41
  76.6 0.9 %combine.2 = bf16[16,2560]{1,0:T(8,128)(2,1)} custom-call(f32[16,4]{1,0:T(8,128)S(1)} %get-tuple-element.22.spot_ref, f32[16,2]{1,0:T(8,128)S(1)} %route.2.refs_8_.weight_ref, bf16[48,640]{1,0:T(8,128)(2,1)S(1)} %get-tuple-element.52.refs_0_, bf16[48,640]{1,0:T(8,128)(2,1)S(1)} %collective-permute-done.22.refs_1_, ...), custom_call_target="tpu_custom_call" | custom-call | tf_op jit(solution)/shard_map/combine/pallas_call | solution.py:372
  77.5 2.9 %collective-permute-done.29.refs_3_ = bf16[48,512]{1,0:T(8,128)(2,1)S(1)} collective-permute-done((bf16[48,512]{1,0:T(8,128)(2,1)S(1)}, bf16[48,512]{1,0:T(8,128)(2,1)S(1)}, u32[]{:S(2)}, u32[]{:S(2)}) %collective-permute-start.29) | collective-permute-done | bytes 49184 | tf_op jit(solution)/shard_map/ppermute | solution.py:41
  80.3 0.9 %combine.3 = bf16[16,2560]{1,0:T(8,128)(2,1)} custom-call(f32[16,4]{1,0:T(8,128)S(1)} %get-tuple-element.28.spot_ref, f32[16,2]{1,0:T(8,128)S(1)} %route.3.refs_8_.weight_ref, bf16[48,512]{1,0:T(8,128)(2,1)S(1)} %get-tuple-element.56.refs_0_, bf16[48,512]{1,0:T(8,128)(2,1)S(1)} %collective-permute-done.27.refs_1_, ...), custom_call_target="tpu_custom_call" | custom-call | tf_op jit(solution)/shard_map/combine/pallas_call | solution.py:372
  (61 shorter events, 0.5 us)
Async XLA Ops:
  0.6 1.4 %copy-start = (bf16[256,2560]{1,0:T(8,128)(2,1)S(1)}, bf16[256,2560]{1,0:T(8,128)(2,1)}, u32[]{:S(2)}) copy-start(bf16[256,2560]{1,0:T(8,128)(2,1)} %param.14) | copy-start | bytes 3932164
  2.0 1.1 %copy-start.7 = (s32[2]{0:T(128)S(1)}, s32[2]{0:T(128)}, u32[]{:S(2)}) copy-start(s32[2]{0:T(128)} %param.20) | copy-start | bytes 28
  2.0 1.2 %copy-start.5 = (s32[16,2]{0,1:T(2,128)S(1)}, s32[16,2]{0,1:T(2,128)}, u32[]{:S(2)}) copy-start(s32[16,2]{0,1:T(2,128)} %param.19) | copy-start | bytes 388
  2.1 1.2 %copy-start.6 = (s32[16,2]{0,1:T(2,128)S(1)}, s32[16,2]{0,1:T(2,128)}, u32[]{:S(2)}) copy-start(s32[16,2]{0,1:T(2,128)} %param.18) | copy-start | bytes 388
  2.1 1.2 %copy-start.3 = (f32[2560]{0:T(1024)S(1)}, f32[2560]{0:T(1024)}, u32[]{:S(2)}) copy-start(f32[2560]{0:T(1024)} %param.16) | copy-start | bytes 30724
  2.1 1.2 %copy-start.4 = (f32[2560]{0:T(1024)S(1)}, f32[2560]{0:T(1024)}, u32[]{:S(2)}) copy-start(f32[2560]{0:T(1024)} %param.15) | copy-start | bytes 30724
  2.5 1.8 %collective-permute-start = (bf16[64,2560]{1,0:T(8,128)(2,1)S(1)}, bf16[64,2560]{1,0:T(8,128)(2,1)S(1)}, u32[]{:S(2)}, u32[]{:S(2)}) collective-permute-start(bf16[64,2560]{1,0:T(8,128)(2,1)S(1)} %get-tuple-element.45), channel_id=1, source_target_pairs={{0,1},{1,0},{2,3},{3,2},{4,5},{5,4},{6,7},{7,6},{8,9},{9,8},{10,11... | collective-permute-start | bytes 983048 | tf_op jit(solution)/shard_map/ppermute | solution.py:41
  3.0 12.3 %collective-permute-start.1 = (bf16[64,2560]{1,0:T(8,128)(2,1)S(1)}, bf16[64,2560]{1,0:T(8,128)(2,1)S(1)}, u32[]{:S(2)}, u32[]{:S(2)}) collective-permute-start(bf16[64,2560]{1,0:T(8,128)(2,1)S(1)} %get-tuple-element.44), channel_id=1, source_target_pairs={{0,1},{1,0},{2,3},{3,2},{4,5},{5,4},{6,7},{7,6},{8,9},{9,8},{10,11... | collective-permute-start | bytes 983048 | tf_op jit(solution)/shard_map/ppermute | solution.py:41
  3.7 3.6 %copy-start.2 = (f32[2560,4]{0,1:T(4,128)S(1)}, f32[2560,4]{0,1:T(4,128)}, u32[]{:S(2)}) copy-start(f32[2560,4]{0,1:T(4,128)} %param.17) | copy-start | bytes 122884
  3.7 3.7 %copy-start.1 = (bf16[16,2560]{1,0:T(8,128)(2,1)S(1)}, bf16[16,2560]{1,0:T(8,128)(2,1)}, u32[]{:S(2)}) copy-start(bf16[16,2560]{1,0:T(8,128)(2,1)} %image_ref.1) | copy-start | bytes 245764
  4.3 11.0 %collective-permute-start.2 = (bf16[64,2560]{1,0:T(8,128)(2,1)S(1)}, bf16[64,2560]{1,0:T(8,128)(2,1)S(1)}, u32[]{:S(2)}, u32[]{:S(2)}) collective-permute-start(bf16[64,2560]{1,0:T(8,128)(2,1)S(1)} %fusion.1.refs_0_), channel_id=1, source_target_pairs={{0,2},{1,3},{2,0},{3,1},{4,6},{5,7},{6,4},{7,5},{8,10},{9,11},{10,... | collective-permute-start | bytes 983048 | tf_op jit(solution)/shard_map/ppermute | solution.py:41
  8.2 11.7 %collective-permute-start.5 = (bf16[48,640]{1,0:T(8,128)(2,1)S(1)}, bf16[48,640]{1,0:T(8,128)(2,1)S(1)}, u32[]{:S(2)}, u32[]{:S(2)}) collective-permute-start(bf16[48,640]{1,0:T(8,128)(2,1)S(1)} %get-tuple-element.27), channel_id=1, source_target_pairs={{0,12},{1,13},{2,14},{3,15},{4,8},{5,9},{6,10},{7,11},{8,4},{9,5},... | collective-permute-start | bytes 184328 | tf_op jit(solution)/shard_map/ppermute | solution.py:41
  11.8 8.2 %collective-permute-start.4 = (bf16[48,640]{1,0:T(8,128)(2,1)S(1)}, bf16[48,640]{1,0:T(8,128)(2,1)S(1)}, u32[]{:S(2)}, u32[]{:S(2)}) collective-permute-start(bf16[48,640]{1,0:T(8,128)(2,1)S(1)} %get-tuple-element.26), channel_id=1, source_target_pairs={{0,8},{1,9},{2,10},{3,11},{4,12},{5,13},{6,14},{7,15},{8,0},{9,1},... | collective-permute-start | bytes 184328 | tf_op jit(solution)/shard_map/ppermute | solution.py:41
  11.8 8.2 %collective-permute-start.3 = (bf16[48,640]{1,0:T(8,128)(2,1)S(1)}, bf16[48,640]{1,0:T(8,128)(2,1)S(1)}, u32[]{:S(2)}, u32[]{:S(2)}) collective-permute-start(bf16[48,640]{1,0:T(8,128)(2,1)S(1)} %get-tuple-element.25.refs_1_), channel_id=1, source_target_pairs={{0,4},{1,5},{2,6},{3,7},{4,0},{5,1},{6,2},{7,3},{8,12},{9,13},{10,... | collective-permute-start | bytes 184328 | tf_op jit(solution)/shard_map/ppermute | solution.py:41
  15.5 6.4 %collective-permute-start.7 = (bf16[16,2560]{1,0:T(8,128)(2,1)S(1)}, bf16[16,2560]{1,0:T(8,128)(2,1)S(1)}, u32[]{:S(2)}, u32[]{:S(2)}) collective-permute-start(bf16[16,2560]{1,0:T(8,128)(2,1)S(1)} %get-tuple-element.48.refs_1_), channel_id=1, source_target_pairs={{0,4},{1,5},{2,6},{3,7},{4,0},{5,1},{6,2},{7,3},{8,12},{9,13},{10,... | collective-permute-start | bytes 245768 | tf_op jit(solution)/shard_map/ppermute | solution.py:41
  17.4 7.8 %collective-permute-start.8 = (bf16[16,2560]{1,0:T(8,128)(2,1)S(1)}, bf16[16,2560]{1,0:T(8,128)(2,1)S(1)}, u32[]{:S(2)}, u32[]{:S(2)}) collective-permute-start(bf16[16,2560]{1,0:T(8,128)(2,1)S(1)} %get-tuple-element.47.refs_2_), channel_id=1, source_target_pairs={{0,8},{1,9},{2,10},{3,11},{4,12},{5,13},{6,14},{7,15},{8,0},{9,1},... | collective-permute-start | bytes 245768 | tf_op jit(solution)/shard_map/ppermute | solution.py:41
  19.9 6.4 %collective-permute-start.9 = (bf16[16,2560]{1,0:T(8,128)(2,1)S(1)}, bf16[16,2560]{1,0:T(8,128)(2,1)S(1)}, u32[]{:S(2)}, u32[]{:S(2)}) collective-permute-start(bf16[16,2560]{1,0:T(8,128)(2,1)S(1)} %get-tuple-element.46.refs_3_), channel_id=1, source_target_pairs={{0,12},{1,13},{2,14},{3,15},{4,8},{5,9},{6,10},{7,11},{8,4},{9,5},... | collective-permute-start | bytes 245768 | tf_op jit(solution)/shard_map/ppermute | solution.py:41
  20.1 11.4 %collective-permute-start.6 = (bf16[192,640]{1,0:T(8,128)(2,1)S(1)}, bf16[192,640]{1,0:T(8,128)(2,1)S(1)}, u32[]{:S(2)}, u32[]{:S(2)}) collective-permute-start(bf16[192,640]{1,0:T(8,128)(2,1)S(1)} %pad_maximum_fusion.refs_0_), channel_id=1, source_target_pairs={{0,2},{1,3},{2,0},{3,1},{4,6},{5,7},{6,4},{7,5},{8,10},{9,11},{10,... | collective-permute-start | bytes 737288 | tf_op jit(solution)/shard_map/ppermute | solution.py:41
  21.9 15.3 %collective-permute-start.10 = (bf16[192,640]{1,0:T(8,128)(2,1)S(1)}, bf16[192,640]{1,0:T(8,128)(2,1)S(1)}, u32[]{:S(2)}, u32[]{:S(2)}) collective-permute-start(bf16[192,640]{1,0:T(8,128)(2,1)S(1)} %pad_maximum_fusion.refs_0_), channel_id=1, source_target_pairs={{0,1},{1,0},{2,3},{3,2},{4,5},{5,4},{6,7},{7,6},{8,9},{9,8},{10,11... | collective-permute-start | bytes 737288 | tf_op jit(solution)/shard_map/ppermute | solution.py:41
  27.0 4.6 %collective-permute-start.12 = (bf16[48,512]{1,0:T(8,128)(2,1)S(1)}, bf16[48,512]{1,0:T(8,128)(2,1)S(1)}, u32[]{:S(2)}, u32[]{:S(2)}) collective-permute-start(bf16[48,512]{1,0:T(8,128)(2,1)S(1)} %get-tuple-element.29.refs_1_), channel_id=1, source_target_pairs={{0,4},{1,5},{2,6},{3,7},{4,0},{5,1},{6,2},{7,3},{8,12},{9,13},{10,... | collective-permute-start | bytes 147464 | tf_op jit(solution)/shard_map/ppermute | solution.py:41
  28.2 5.7 %collective-permute-start.13 = (bf16[48,512]{1,0:T(8,128)(2,1)S(1)}, bf16[48,512]{1,0:T(8,128)(2,1)S(1)}, u32[]{:S(2)}, u32[]{:S(2)}) collective-permute-start(bf16[48,512]{1,0:T(8,128)(2,1)S(1)} %get-tuple-element.31), channel_id=1, source_target_pairs={{0,8},{1,9},{2,10},{3,11},{4,12},{5,13},{6,14},{7,15},{8,0},{9,1},... | collective-permute-start | bytes 147464 | tf_op jit(solution)/shard_map/ppermute | solution.py:41
  29.7 5.9 %collective-permute-start.14 = (bf16[48,512]{1,0:T(8,128)(2,1)S(1)}, bf16[48,512]{1,0:T(8,128)(2,1)S(1)}, u32[]{:S(2)}, u32[]{:S(2)}) collective-permute-start(bf16[48,512]{1,0:T(8,128)(2,1)S(1)} %get-tuple-element.32), channel_id=1, source_target_pairs={{0,12},{1,13},{2,14},{3,15},{4,8},{5,9},{6,10},{7,11},{8,4},{9,5},... | collective-permute-start | bytes 147464 | tf_op jit(solution)/shard_map/ppermute | solution.py:41
  31.5 5.7 %collective-permute-start.11 = (bf16[192,640]{1,0:T(8,128)(2,1)S(1)}, bf16[192,640]{1,0:T(8,128)(2,1)S(1)}, u32[]{:S(2)}, u32[]{:S(2)}) collective-permute-start(bf16[192,640]{1,0:T(8,128)(2,1)S(1)} %tie.12.refs_1_), channel_id=1, source_target_pairs={{0,1},{1,0},{2,3},{3,2},{4,5},{5,4},{6,7},{7,6},{8,9},{9,8},{10,11... | collective-permute-start | bytes 737288 | tf_op jit(solution)/shard_map/ppermute | solution.py:41
  35.6 13.6 %collective-permute-start.15 = (bf16[192,512]{1,0:T(8,128)(2,1)S(1)}, bf16[192,512]{1,0:T(8,128)(2,1)S(1)}, u32[]{:S(2)}, u32[]{:S(2)}) collective-permute-start(bf16[192,512]{1,0:T(8,128)(2,1)S(1)} %constant_dynamic-update-slice_fusion.refs_7_.refs_0_), channel_id=1, source_target_pairs={{0,2},{1,3},{2,0},{3,1},{4,6},{5,7},{6,4},{7,5},{8,10},{9,11},{10,... | collective-permute-start | bytes 589832 | tf_op jit(solution)/shard_map/ppermute | solution.py:41
  49.3 1.6 %collective-permute-start.17 = (bf16[192,640]{1,0:T(8,128)(2,1)S(1)}, bf16[192,640]{1,0:T(8,128)(2,1)S(1)}, u32[]{:S(2)}, u32[]{:S(2)}) collective-permute-start(bf16[192,640]{1,0:T(8,128)(2,1)S(1)} %tie.15), channel_id=1, source_target_pairs={{0,1},{1,0},{2,3},{3,2},{4,5},{5,4},{6,7},{7,6},{8,9},{9,8},{10,11... | collective-permute-start | bytes 737288 | tf_op jit(solution)/shard_map/ppermute | solution.py:41
  49.7 1.9 %collective-permute-start.19 = (bf16[192,512]{1,0:T(8,128)(2,1)S(1)}, bf16[192,512]{1,0:T(8,128)(2,1)S(1)}, u32[]{:S(2)}, u32[]{:S(2)}) collective-permute-start(bf16[192,512]{1,0:T(8,128)(2,1)S(1)} %constant_dynamic-update-slice_fusion.refs_7_.refs_0_), channel_id=1, source_target_pairs={{0,1},{1,0},{2,3},{3,2},{4,5},{5,4},{6,7},{7,6},{8,9},{9,8},{10,11... | collective-permute-start | bytes 589832 | tf_op jit(solution)/shard_map/ppermute | solution.py:41
  50.2 1.4 %collective-permute-start.20 = (bf16[192,512]{1,0:T(8,128)(2,1)S(1)}, bf16[192,512]{1,0:T(8,128)(2,1)S(1)}, u32[]{:S(2)}, u32[]{:S(2)}) collective-permute-start(bf16[192,512]{1,0:T(8,128)(2,1)S(1)} %tie.13.refs_1_), channel_id=1, source_target_pairs={{0,1},{1,0},{2,3},{3,2},{4,5},{5,4},{6,7},{7,6},{8,9},{9,8},{10,11... | collective-permute-start | bytes 589832 | tf_op jit(solution)/shard_map/ppermute | solution.py:41
  51.0 12.2 %collective-permute-start.18 = (bf16[192,640]{1,0:T(8,128)(2,1)S(1)}, bf16[192,640]{1,0:T(8,128)(2,1)S(1)}, u32[]{:S(2)}, u32[]{:S(2)}) collective-permute-start(bf16[192,640]{1,0:T(8,128)(2,1)S(1)} %add_convert_fusion.1.refs_7_), channel_id=1, source_target_pairs={{0,2},{1,3},{2,0},{3,1},{4,6},{5,7},{6,4},{7,5},{8,10},{9,11},{10,... | collective-permute-start | bytes 737288 | tf_op jit(solution)/shard_map/ppermute | solution.py:41
  63.3 1.5 %collective-permute-start.21 = (bf16[192,512]{1,0:T(8,128)(2,1)S(1)}, bf16[192,512]{1,0:T(8,128)(2,1)S(1)}, u32[]{:S(2)}, u32[]{:S(2)}) collective-permute-start(bf16[192,512]{1,0:T(8,128)(2,1)S(1)} %tie.17), channel_id=1, source_target_pairs={{0,1},{1,0},{2,3},{3,2},{4,5},{5,4},{6,7},{7,6},{8,9},{9,8},{10,11... | collective-permute-start | bytes 589832 | tf_op jit(solution)/shard_map/ppermute | solution.py:41
  63.6 2.7 %collective-permute-start.16 = (bf16[192,640]{1,0:T(8,128)(2,1)S(1)}, bf16[192,640]{1,0:T(8,128)(2,1)S(1)}, u32[]{:S(2)}, u32[]{:S(2)}) collective-permute-start(bf16[192,640]{1,0:T(8,128)(2,1)S(1)} %tie.14), channel_id=1, source_target_pairs={{0,1},{1,0},{2,3},{3,2},{4,5},{5,4},{6,7},{7,6},{8,9},{9,8},{10,11... | collective-permute-start | bytes 737288 | tf_op jit(solution)/shard_map/ppermute | solution.py:41
  64.0 7.0 %collective-permute-start.25 = (bf16[192,512]{1,0:T(8,128)(2,1)S(1)}, bf16[192,512]{1,0:T(8,128)(2,1)S(1)}, u32[]{:S(2)}, u32[]{:S(2)}) collective-permute-start(bf16[192,512]{1,0:T(8,128)(2,1)S(1)} %tie.19), channel_id=1, source_target_pairs={{0,1},{1,0},{2,3},{3,2},{4,5},{5,4},{6,7},{7,6},{8,9},{9,8},{10,11... | collective-permute-start | bytes 589832 | tf_op jit(solution)/shard_map/ppermute | solution.py:41
  64.9 7.1 %collective-permute-start.26 = (bf16[192,512]{1,0:T(8,128)(2,1)S(1)}, bf16[192,512]{1,0:T(8,128)(2,1)S(1)}, u32[]{:S(2)}, u32[]{:S(2)}) collective-permute-start(bf16[192,512]{1,0:T(8,128)(2,1)S(1)} %add_convert_fusion.3.refs_1_), channel_id=1, source_target_pairs={{0,2},{1,3},{2,0},{3,1},{4,6},{5,7},{6,4},{7,5},{8,10},{9,11},{10,... | collective-permute-start | bytes 589832 | tf_op jit(solution)/shard_map/ppermute | solution.py:41
  66.5 8.0 %collective-permute-start.22 = (bf16[48,640]{1,0:T(8,128)(2,1)S(1)}, bf16[48,640]{1,0:T(8,128)(2,1)S(1)}, u32[]{:S(2)}, u32[]{:S(2)}) collective-permute-start(bf16[48,640]{1,0:T(8,128)(2,1)S(1)} %get-tuple-element.51), channel_id=1, source_target_pairs={{0,4},{1,5},{2,6},{3,7},{4,0},{5,1},{6,2},{7,3},{8,12},{9,13},{10,... | collective-permute-start | bytes 184328 | tf_op jit(solution)/shard_map/ppermute | solution.py:41
  66.6 10.0 %collective-permute-start.23 = (bf16[48,640]{1,0:T(8,128)(2,1)S(1)}, bf16[48,640]{1,0:T(8,128)(2,1)S(1)}, u32[]{:S(2)}, u32[]{:S(2)}) collective-permute-start(bf16[48,640]{1,0:T(8,128)(2,1)S(1)} %get-tuple-element.50), channel_id=1, source_target_pairs={{0,8},{1,9},{2,10},{3,11},{4,12},{5,13},{6,14},{7,15},{8,0},{9,1},... | collective-permute-start | bytes 184328 | tf_op jit(solution)/shard_map/ppermute | solution.py:41
  68.8 7.7 %collective-permute-start.24 = (bf16[48,640]{1,0:T(8,128)(2,1)S(1)}, bf16[48,640]{1,0:T(8,128)(2,1)S(1)}, u32[]{:S(2)}, u32[]{:S(2)}) collective-permute-start(bf16[48,640]{1,0:T(8,128)(2,1)S(1)} %get-tuple-element.49), channel_id=1, source_target_pairs={{0,12},{1,13},{2,14},{3,15},{4,8},{5,9},{6,10},{7,11},{8,4},{9,5},... | collective-permute-start | bytes 184328 | tf_op jit(solution)/shard_map/ppermute | solution.py:41
  72.1 5.4 %collective-permute-start.27 = (bf16[48,512]{1,0:T(8,128)(2,1)S(1)}, bf16[48,512]{1,0:T(8,128)(2,1)S(1)}, u32[]{:S(2)}, u32[]{:S(2)}) collective-permute-start(bf16[48,512]{1,0:T(8,128)(2,1)S(1)} %get-tuple-element.55), channel_id=1, source_target_pairs={{0,4},{1,5},{2,6},{3,7},{4,0},{5,1},{6,2},{7,3},{8,12},{9,13},{10,... | collective-permute-start | bytes 147464 | tf_op jit(solution)/shard_map/ppermute | solution.py:41
  72.2 5.3 %collective-permute-start.28 = (bf16[48,512]{1,0:T(8,128)(2,1)S(1)}, bf16[48,512]{1,0:T(8,128)(2,1)S(1)}, u32[]{:S(2)}, u32[]{:S(2)}) collective-permute-start(bf16[48,512]{1,0:T(8,128)(2,1)S(1)} %get-tuple-element.54), channel_id=1, source_target_pairs={{0,8},{1,9},{2,10},{3,11},{4,12},{5,13},{6,14},{7,15},{8,0},{9,1},... | collective-permute-start | bytes 147464 | tf_op jit(solution)/shard_map/ppermute | solution.py:41
  74.5 5.9 %collective-permute-start.29 = (bf16[48,512]{1,0:T(8,128)(2,1)S(1)}, bf16[48,512]{1,0:T(8,128)(2,1)S(1)}, u32[]{:S(2)}, u32[]{:S(2)}) collective-permute-start(bf16[48,512]{1,0:T(8,128)(2,1)S(1)} %get-tuple-element.53), channel_id=1, source_target_pairs={{0,12},{1,13},{2,14},{3,15},{4,8},{5,9},{6,10},{7,11},{8,4},{9,5},... | collective-permute-start | bytes 147464 | tf_op jit(solution)/shard_map/ppermute | solution.py:41

commit v11 on v10

--- a/solution.py
+++ b/solution.py
@@ -208,20 +208,17 @@
     )(spot, normed, small)
 
 
-def cuts(units, part, parts):
-    first, last = [units * p // parts // 16 * 16 for p in (part, part + 1)]
-    edges = [first] + list(range(first + (256 if parts == 1 else 384), last - 255, 512)) + [last]
+def cuts(units):
+    edges = [0] + list(range(256, units - 255, 512)) + [units]
     return list(zip(edges[:-1], edges[1:]))
 
 
-def expert_kernel(packing, unit_cuts, count, before, after, *refs):
-    row_refs, before_refs = refs[:count], refs[count : count + before]
-    gate_hbm, up_hbm, down_hbm = refs[count + before : count + before + 3]
-    place = count + before + 3 + after
+def expert_kernel(packing, unit_cuts, count, after, *refs):
+    row_refs = refs[:count]
+    gate_hbm, up_hbm, down_hbm = refs[count : count + 3]
+    place = count + 3 + after
     out_refs = refs[place : place + count]
     gate_ref, up_ref, down_ref, rows_ref, total_ref, packed_ref, sems = refs[place + count :]
-    rows = total_ref.shape[1]
-    origin = unit_cuts[0][0]
     copies = []
     for i, (lo, hi) in enumerate(unit_cuts):
         for t, (source, target) in enumerate(
@@ -229,16 +226,16 @@
         ):
             copies.append(
                 pltpu.make_async_copy(
-                    source.at[lo:hi], target.at[lo - origin : hi - origin], sems.at[3 * i + t]
+                    source.at[lo:hi], target.at[lo:hi], sems.at[3 * i + t]
                 )
             )
-    unit_cuts = [(lo - origin, hi - origin) for lo, hi in unit_cuts]
     for copy in copies[:6]:
         copy.start()
 
     cap, chunks, width, high = packing.cap, packing.chunks, packing.width, packing.rows
     per_ref = row_refs[0].shape[0] // high
     blocks = count * per_ref
+    rows = blocks * cap
     lanes = width // 128
     for i, ref in enumerate(row_refs):
         for c in range(lanes):
@@ -253,19 +250,19 @@
                     c, pl.ds(j * cap + slot, blocks, stride=high), :
                 ]
     for c in range(chunks * lanes):
-        part = total_ref[c]
+        part = total_ref[c, 0:rows, :]
         if spare:
             part = jnp.concatenate([part, jnp.zeros((spare, 128), jnp.float32)], axis=0)
-        rows_ref[c * 128 : (c + 1) * 128, :] = part.T.astype(jnp.bfloat16)
+        rows_ref[c * 128 : (c + 1) * 128, :] = part.astype(jnp.bfloat16).T
 
     def down(i, hidden):
         lo, hi = unit_cuts[i]
         term = jnp.dot(hidden, down_ref[lo:hi, :], preferred_element_type=jnp.float32)
         for c in range(chunks * lanes):
             if i == 0:
-                total_ref[c] = term[:, c * 128 : (c + 1) * 128]
+                total_ref[c, 0:rows, :] = term[:, c * 128 : (c + 1) * 128]
             else:
-                total_ref[c] += term[:, c * 128 : (c + 1) * 128]
+                total_ref[c, 0:rows, :] += term[:, c * 128 : (c + 1) * 128]
 
     features = gate_hbm.shape[1]
     middle = features // 256 * 128
@@ -277,7 +274,10 @@
             weight_ref[lo:hi, middle:], rows_ref[middle:, :], preferred_element_type=jnp.float32
         )
 
-    hidden = None
+    def gated(gate, up):
+        return (gate * jax.nn.sigmoid(gate) * up).astype(jnp.bfloat16).T[0:rows]
+
+    inner = None
     for i, (lo, hi) in enumerate(unit_cuts):
         if i > 0:
             copies[3 * i - 1].wait()
@@ -285,13 +285,12 @@
         copies[3 * i + 1].wait()
         for copy in copies[3 * (i + 2) : 3 * (i + 3)]:
             copy.start()
-        gate = product(gate_ref, lo, hi)
-        up = product(up_ref, lo, hi)
+        following = product(gate_ref, lo, hi), product(up_ref, lo, hi)
         if i > 0:
-            down(i - 1, hidden)
-        hidden = (gate * jax.nn.sigmoid(gate) * up).T[0:rows].astype(jnp.bfloat16)
+            down(i - 1, gated(*inner))
+        inner = following
     copies[-1].wait()
-    down(len(unit_cuts) - 1, hidden)
+    down(len(unit_cuts) - 1, gated(*inner))
 
     for c in range(lanes):
         for row in range(chunks * cap, high):
@@ -307,40 +306,38 @@
         for c in range(lanes):
             columns = slice(c * 128, (c + 1) * 128)
             part = packed_ref[c, i * per_ref * high : (i + 1) * per_ref * high, :]
-            if before:
-                part = part + before_refs[i][:, columns].astype(jnp.float32)
             ref[:, columns] = part.astype(jnp.bfloat16)
 
 
-def expert_rows(arrays, w_gate, w_up, w_down, packing, after, part=0, parts=1, before=()):
+def expert_rows(arrays, w_gate, w_up, w_down, packing, after):
     features, units = w_gate.shape
     rows = len(arrays) * (arrays[0].shape[0] // packing.rows) * packing.cap
-    unit_cuts = cuts(units, part, parts)
-    own = unit_cuts[-1][1] - unit_cuts[0][0]
+    unit_cuts = cuts(units)
     return pl.pallas_call(
-        functools.partial(
-            expert_kernel, packing, unit_cuts, len(arrays), len(before), len(after)
-        ),
+        functools.partial(expert_kernel, packing, unit_cuts, len(arrays), len(after)),
         out_shape=[jax.ShapeDtypeStruct(arrays[0].shape, jnp.bfloat16)] * len(arrays),
-        in_specs=[VMEM] * (len(arrays) + len(before)) + [HBM] * 3 + [ANY] * len(after),
+        in_specs=[VMEM] * len(arrays) + [HBM] * 3 + [ANY] * len(after),
         out_specs=[VMEM] * len(arrays),
         scratch_shapes=[
-            pltpu.VMEM((own, features), jnp.bfloat16),
-            pltpu.VMEM((own, features), jnp.bfloat16),
-            pltpu.VMEM((own, features), jnp.bfloat16),
+            pltpu.VMEM((units, features), jnp.bfloat16),
+            pltpu.VMEM((units, features), jnp.bfloat16),
+            pltpu.VMEM((units, features), jnp.bfloat16),
             pltpu.VMEM((features, -(-rows // 128) * 128), jnp.bfloat16),
-            pltpu.VMEM((features // 128, rows, 128), jnp.float32),
-            pltpu.VMEM((packing.width // 128, len(arrays) * arrays[0].shape[0], 128), jnp.float32),
+            pltpu.VMEM((features // 128, rows + 16, 128), jnp.float32),
+            pltpu.VMEM(
+                (packing.width // 128, len(arrays) * arrays[0].shape[0] + packing.rows, 128),
+                jnp.float32,
+            ),
             pltpu.SemaphoreType.DMA((3 * len(unit_cuts),)),
         ],
         compiler_params=pltpu.CompilerParams(vmem_limit_bytes=48 << 20),
         cost_estimate=pl.CostEstimate(
-            flops=6 * rows * features * own,
-            bytes_accessed=6 * features * own,
-            transcendentals=rows * own,
+            flops=6 * rows * features * units,
+            bytes_accessed=6 * features * units,
+            transcendentals=rows * units,
         ),
         name="experts",
-    )(*arrays, *before, w_gate.T, w_up.T, w_down, *after)
+    )(*arrays, w_gate.T, w_up.T, w_down, *after)
 
 
 def combine_kernel(packing, spot_ref, weight_ref, *refs):

time: 81.4 us -> 81.6 us (level)
  no operation moved by 1% of the time
where the time goes in v11:
time: 81.6 us; the launch traced here: 81.4 us
  starting transfers between devices  33 us (40%)
  Pallas kernels  27.8 us (34%)
  waiting for transfers between devices  16.6 us (20%)
  other arithmetic  1.93 us (2%)
  between operations  1.14 us (1%)
    ppermute x30, starting transfers between devices, swap(): return lax.ppermute(value, 'dev', moves)  33 us
    pallas_call x2, Pallas kernels, expert_rows(): pl.pallas_call(functools.partial(expert_kernel, packing, unit_cuts, len(a...  23.9 us
    ppermute x30, waiting for transfers between devices, swap(): return lax.ppermute(value, 'dev', moves)  16.6 us
    pallas_call x2, Pallas kernels, combine(): pl.pallas_call(functools.partial(combine_kernel, packing), out_shape=jax....  1.77 us
  transfers between devices with their start and end apart: 30, of which 11 were waited for; matrix products, arithmetic and copies ran while one was open for 1% of the time, Pallas kernels for 33%

profile of v11, /device:TPU:0, one launch (start us, length us, event | category | flops | bytes accessed | tf_op | source)
XLA Modules:
  0.0 81.4 jit_solution(5220200501359425572)
XLA Ops:
  0.6 0.0 copy-start
  0.7 1.1 %fusion.5 = bf16[2,2,2,2,16,256]{5,4,3,2,1,0:T(8,128)(2,1)S(1)} fusion(s32[]{:T(128)S(6)} %select_n.80, bf16[2,2,2,2,16,256]{5,4,3,2,1,0:T(8,128)(2,1)} %bitcast.29), kind=kLoop, calls=%fused_computation.21 | loop fusion | flops 65536 | bytes 262148 | tf_op jit(solution)/shard_map/jit(_roll_dynamic)/concatenate | solution.py:385
  1.8 0.1 fusion.3
  1.9 0.1 fusion.2
  2.0 0.0 copy-start.7
  2.0 0.0 copy-start.5
  2.1 0.0 copy-start.6
  2.1 0.0 copy-start.4
  2.1 0.3 convolution_convert_fusion
  2.5 0.5 collective-permute-start
  3.0 0.1 collective-permute-start.1
  3.1 0.1 fusion.7
  3.3 0.3 fusion.16
  3.7 0.6 collective-permute-done
  4.3 0.1 fusion.1.refs_0_
  4.3 3.0 %collective-permute-start.2 = (bf16[64,2560]{1,0:T(8,128)(2,1)S(1)}, bf16[64,2560]{1,0:T(8,128)(2,1)S(1)}, u32[]{:S(2)}, u32[]{:S(2)}) collective-permute-start(bf16[64,2560]{1,0:T(8,128)(2,1)S(1)} %fusion.1.refs_0_), channel_id=1, source_target_pairs={{0,2},{1,3},{2,0},{3,1},{4,6},{5,7},{6,4},{7,5},{8,10},{9,11},{10,... | collective-permute-start | bytes 983048 | tf_op jit(solution)/shard_map/ppermute | solution.py:41
  7.3 0.8 %prepare.1 = (f32[16,4]{1,0:T(8,128)S(1)}, f32[16,4]{1,0:T(8,128)S(1)}, bf16[16,2560]{1,0:T(8,128)(2,1)S(1)}, bf16[48,640]{1,0:T(8,128)(2,1)S(1)}, bf16[48,640]{...) custom-call(s32[4,16]{1,0:T(4,128)S(1)} %pad_add_fusion.ids_ref, ...), custom_call_target="tpu_custom_call" | custom-call | tf_op jit(solution)/shard_map/prepare/pallas_call | solution.py:123
  8.2 3.6 %collective-permute-start.5 = (bf16[48,640]{1,0:T(8,128)(2,1)S(1)}, bf16[48,640]{1,0:T(8,128)(2,1)S(1)}, u32[]{:S(2)}, u32[]{:S(2)}) collective-permute-start(bf16[48,640]{1,0:T(8,128)(2,1)S(1)} %get-tuple-element.27), channel_id=1, source_target_pairs={{0,12},{1,13},{2,14},{3,15},{4,8},{5,9},{6,10},{7,11},{8,4},{9,5},... | collective-permute-start | bytes 184328 | tf_op jit(solution)/shard_map/ppermute | solution.py:41
  11.8 0.8 collective-permute-start.3
  12.6 0.3 route.2.refs_8_.weight_ref
  12.9 2.4 %collective-permute-done.2.refs_0_ = bf16[64,2560]{1,0:T(8,128)(2,1)S(1)} collective-permute-done((bf16[64,2560]{1,0:T(8,128)(2,1)S(1)}, bf16[64,2560]{1,0:T(8,128)(2,1)S(1)}, u32[]{:S(2)}, u32[]{:S(2)}) %collective-permute-start.2) | collective-permute-done | bytes 327712 | tf_op jit(solution)/shard_map/ppermute | solution.py:41
  15.3 0.1 fusion.9
  15.5 1.9 %collective-permute-start.7 = (bf16[16,2560]{1,0:T(8,128)(2,1)S(1)}, bf16[16,2560]{1,0:T(8,128)(2,1)S(1)}, u32[]{:S(2)}, u32[]{:S(2)}) collective-permute-start(bf16[16,2560]{1,0:T(8,128)(2,1)S(1)} %get-tuple-element.48.refs_1_), channel_id=1, source_target_pairs={{0,4},{1,5},{2,6},{3,7},{4,0},{5,1},{6,2},{7,3},{8,12},{9,13},{10,... | collective-permute-start | bytes 245768 | tf_op jit(solution)/shard_map/ppermute | solution.py:41
  17.4 2.5 %collective-permute-start.8 = (bf16[16,2560]{1,0:T(8,128)(2,1)S(1)}, bf16[16,2560]{1,0:T(8,128)(2,1)S(1)}, u32[]{:S(2)}, u32[]{:S(2)}) collective-permute-start(bf16[16,2560]{1,0:T(8,128)(2,1)S(1)} %get-tuple-element.47.refs_2_), channel_id=1, source_target_pairs={{0,8},{1,9},{2,10},{3,11},{4,12},{5,13},{6,14},{7,15},{8,0},{9,1},... | collective-permute-start | bytes 245768 | tf_op jit(solution)/shard_map/ppermute | solution.py:41
  19.9 0.1 collective-permute-start.9
  20.1 1.8 %collective-permute-start.6 = (bf16[192,640]{1,0:T(8,128)(2,1)S(1)}, bf16[192,640]{1,0:T(8,128)(2,1)S(1)}, u32[]{:S(2)}, u32[]{:S(2)}) collective-permute-start(bf16[192,640]{1,0:T(8,128)(2,1)S(1)} %pad_maximum_fusion.refs_0_), channel_id=1, source_target_pairs={{0,2},{1,3},{2,0},{3,1},{4,6},{5,7},{6,4},{7,5},{8,10},{9,11},{10,... | collective-permute-start | bytes 737288 | tf_op jit(solution)/shard_map/ppermute | solution.py:41
  21.9 3.3 %collective-permute-done.8.refs_2_ = bf16[16,2560]{1,0:T(8,128)(2,1)S(1)} collective-permute-done((bf16[16,2560]{1,0:T(8,128)(2,1)S(1)}, bf16[16,2560]{1,0:T(8,128)(2,1)S(1)}, u32[]{:S(2)}, u32[]{:S(2)}) %collective-permute-start.8) | collective-permute-done | bytes 81952 | tf_op jit(solution)/shard_map/ppermute | solution.py:41
  25.1 1.2 %collective-permute-done.9.refs_3_ = bf16[16,2560]{1,0:T(8,128)(2,1)S(1)} collective-permute-done((bf16[16,2560]{1,0:T(8,128)(2,1)S(1)}, bf16[16,2560]{1,0:T(8,128)(2,1)S(1)}, u32[]{:S(2)}, u32[]{:S(2)}) %collective-permute-start.9) | collective-permute-done | bytes 81952 | tf_op jit(solution)/shard_map/ppermute | solution.py:41
  26.3 0.6 modulate.1
  27.0 1.2 %collective-permute-start.12 = (bf16[48,512]{1,0:T(8,128)(2,1)S(1)}, bf16[48,512]{1,0:T(8,128)(2,1)S(1)}, u32[]{:S(2)}, u32[]{:S(2)}) collective-permute-start(bf16[48,512]{1,0:T(8,128)(2,1)S(1)} %get-tuple-element.29.refs_1_), channel_id=1, source_target_pairs={{0,4},{1,5},{2,6},{3,7},{4,0},{5,1},{6,2},{7,3},{8,12},{9,13},{10,... | collective-permute-start | bytes 147464 | tf_op jit(solution)/shard_map/ppermute | solution.py:41
  28.2 1.6 %collective-permute-start.13 = (bf16[48,512]{1,0:T(8,128)(2,1)S(1)}, bf16[48,512]{1,0:T(8,128)(2,1)S(1)}, u32[]{:S(2)}, u32[]{:S(2)}) collective-permute-start(bf16[48,512]{1,0:T(8,128)(2,1)S(1)} %get-tuple-element.31), channel_id=1, source_target_pairs={{0,8},{1,9},{2,10},{3,11},{4,12},{5,13},{6,14},{7,15},{8,0},{9,1},... | collective-permute-start | bytes 147464 | tf_op jit(solution)/shard_map/ppermute | solution.py:41
  29.7 1.7 %collective-permute-start.14 = (bf16[48,512]{1,0:T(8,128)(2,1)S(1)}, bf16[48,512]{1,0:T(8,128)(2,1)S(1)}, u32[]{:S(2)}, u32[]{:S(2)}) collective-permute-start(bf16[48,512]{1,0:T(8,128)(2,1)S(1)} %get-tuple-element.32), channel_id=1, source_target_pairs={{0,12},{1,13},{2,14},{3,15},{4,8},{5,9},{6,10},{7,11},{8,4},{9,5},... | collective-permute-start | bytes 147464 | tf_op jit(solution)/shard_map/ppermute | solution.py:41
  31.5 0.1 collective-permute-start.11
  31.6 2.4 %collective-permute-done.13 = bf16[48,512]{1,0:T(8,128)(2,1)S(1)} collective-permute-done((bf16[48,512]{1,0:T(8,128)(2,1)S(1)}, bf16[48,512]{1,0:T(8,128)(2,1)S(1)}, u32[]{:S(2)}, u32[]{:S(2)}) %collective-permute-start.13) | collective-permute-done | bytes 49184 | tf_op jit(solution)/shard_map/ppermute | solution.py:41
  33.9 1.7 %collective-permute-done.14 = bf16[48,512]{1,0:T(8,128)(2,1)S(1)} collective-permute-done((bf16[48,512]{1,0:T(8,128)(2,1)S(1)}, bf16[48,512]{1,0:T(8,128)(2,1)S(1)}, u32[]{:S(2)}, u32[]{:S(2)}) %collective-permute-start.14) | collective-permute-done | bytes 49184 | tf_op jit(solution)/shard_map/ppermute | solution.py:41
  35.6 1.5 %collective-permute-start.15 = (bf16[192,512]{1,0:T(8,128)(2,1)S(1)}, bf16[192,512]{1,0:T(8,128)(2,1)S(1)}, u32[]{:S(2)}, u32[]{:S(2)}) collective-permute-start(bf16[192,512]{1,0:T(8,128)(2,1)S(1)} %constant_dynamic-update-slice_fusion.refs_7_.refs_0_), channel_id=1, source_target_pairs={{0,2},{1,3},{2,0},{3,1},{4,6},{5,7},{6,4},{7,5},{8,10},{9,11},{10,... | collective-permute-start | bytes 589832 | tf_op jit(solution)/shard_map/ppermute | solution.py:41
  37.2 12.1 %experts.2 = (bf16[192,640]{1,0:T(8,128)(2,1)S(1)}, bf16[192,640]{1,0:T(8,128)(2,1)S(1)}, bf16[192,640]{1,0:T(8,128)(2,1)S(1)}, bf16[192,640]{1,0:T(8,128)(2,1)S(1)}) custom-call(bf16[192,640]{1,0:T(8,128)(2,1)S(1)} %pad_maximum_fusion.refs_0_, bf16[192,640]{1,0:T(8,128)(2,1)S(1)} %tie.12.refs_1_, bf16[192,640]{1,0:T(8,128)(2,1)S(1)} %collective-permute-done.10.refs_2_, ...), custom_call_target="tpu_custom_call" | custom-call | flops 5096079360 | bytes 26542080 | tf_op jit(solution)/shard_map/experts/pallas_call | solution.py:316
  49.4 0.1 collective-permute-start.17
  49.4 0.3 route.3.refs_8_.weight_ref
  49.7 0.5 collective-permute-start.19
  50.2 0.1 collective-permute-start.20
  50.3 0.6 collective-permute-done.17
  50.9 0.1 add_convert_fusion.1.refs_7_
  51.0 0.6 collective-permute-start.18
  51.6 0.1 collective-permute-done.20.refs_3_
  51.7 11.7 %experts.3 = (bf16[192,512]{1,0:T(8,128)(2,1)S(1)}, bf16[192,512]{1,0:T(8,128)(2,1)S(1)}, bf16[192,512]{1,0:T(8,128)(2,1)S(1)}, bf16[192,512]{1,0:T(8,128)(2,1)S(1)}) custom-call(bf16[192,512]{1,0:T(8,128)(2,1)S(1)} %constant_dynamic-update-slice_fusion.refs_7_.refs_0_, bf16[192,512]{1,0:T(8,128)(2,1)S(1)} %tie.13.refs_1_, ...), custom_call_target="tpu_custom_call" | custom-call | flops 3822059520 | bytes 26542080 | tf_op jit(solution)/shard_map/experts/pallas_call | solution.py:316
  63.5 0.3 collective-permute-start.21
  63.9 0.3 collective-permute-start.16
  64.2 0.3 collective-permute-start.25
  64.5 0.5 collective-permute-done.21
  65.0 0.1 add_convert_fusion.3.refs_1_
  65.1 1.5 %collective-permute-start.26 = (bf16[192,512]{1,0:T(8,128)(2,1)S(1)}, bf16[192,512]{1,0:T(8,128)(2,1)S(1)}, u32[]{:S(2)}, u32[]{:S(2)}) collective-permute-start(bf16[192,512]{1,0:T(8,128)(2,1)S(1)} %add_convert_fusion.3.refs_1_), channel_id=1, source_target_pairs={{0,2},{1,3},{2,0},{3,1},{4,6},{5,7},{6,4},{7,5},{8,10},{9,11},{10,... | collective-permute-start | bytes 589832 | tf_op jit(solution)/shard_map/ppermute | solution.py:41
  66.6 0.1 add_convert_fusion
  66.7 0.1 collective-permute-start.22
  66.8 2.2 %collective-permute-start.23 = (bf16[48,640]{1,0:T(8,128)(2,1)S(1)}, bf16[48,640]{1,0:T(8,128)(2,1)S(1)}, u32[]{:S(2)}, u32[]{:S(2)}) collective-permute-start(bf16[48,640]{1,0:T(8,128)(2,1)S(1)} %get-tuple-element.50), channel_id=1, source_target_pairs={{0,8},{1,9},{2,10},{3,11},{4,12},{5,13},{6,14},{7,15},{8,0},{9,1},... | collective-permute-start | bytes 184328 | tf_op jit(solution)/shard_map/ppermute | solution.py:41
  69.0 2.1 %collective-permute-start.24 = (bf16[48,640]{1,0:T(8,128)(2,1)S(1)}, bf16[48,640]{1,0:T(8,128)(2,1)S(1)}, u32[]{:S(2)}, u32[]{:S(2)}) collective-permute-start(bf16[48,640]{1,0:T(8,128)(2,1)S(1)} %get-tuple-element.49), channel_id=1, source_target_pairs={{0,12},{1,13},{2,14},{3,15},{4,8},{5,9},{6,10},{7,11},{8,4},{9,5},... | collective-permute-start | bytes 184328 | tf_op jit(solution)/shard_map/ppermute | solution.py:41
  71.2 1.1 %collective-permute-done.26 = bf16[192,512]{1,0:T(8,128)(2,1)S(1)} collective-permute-done((bf16[192,512]{1,0:T(8,128)(2,1)S(1)}, bf16[192,512]{1,0:T(8,128)(2,1)S(1)}, u32[]{:S(2)}, u32[]{:S(2)}) %collective-permute-start.26) | collective-permute-done | bytes 196640 | tf_op jit(solution)/shard_map/ppermute | solution.py:41
  72.2 0.1 add_convert_fusion.2
  72.3 0.1 collective-permute-start.27
  72.4 2.2 %collective-permute-start.28 = (bf16[48,512]{1,0:T(8,128)(2,1)S(1)}, bf16[48,512]{1,0:T(8,128)(2,1)S(1)}, u32[]{:S(2)}, u32[]{:S(2)}) collective-permute-start(bf16[48,512]{1,0:T(8,128)(2,1)S(1)} %get-tuple-element.54), channel_id=1, source_target_pairs={{0,8},{1,9},{2,10},{3,11},{4,12},{5,13},{6,14},{7,15},{8,0},{9,1},... | collective-permute-start | bytes 147464 | tf_op jit(solution)/shard_map/ppermute | solution.py:41
  74.7 2.1 %collective-permute-start.29 = (bf16[48,512]{1,0:T(8,128)(2,1)S(1)}, bf16[48,512]{1,0:T(8,128)(2,1)S(1)}, u32[]{:S(2)}, u32[]{:S(2)}) collective-permute-start(bf16[48,512]{1,0:T(8,128)(2,1)S(1)} %get-tuple-element.53), channel_id=1, source_target_pairs={{0,12},{1,13},{2,14},{3,15},{4,8},{5,9},{6,10},{7,11},{8,4},{9,5},... | collective-permute-start | bytes 147464 | tf_op jit(solution)/shard_map/ppermute | solution.py:41
  76.8 0.9 %combine.2 = bf16[16,2560]{1,0:T(8,128)(2,1)} custom-call(f32[16,4]{1,0:T(8,128)S(1)} %get-tuple-element.22.spot_ref, f32[16,2]{1,0:T(8,128)S(1)} %route.2.refs_8_.weight_ref, bf16[48,640]{1,0:T(8,128)(2,1)S(1)} %get-tuple-element.52.refs_0_, bf16[48,640]{1,0:T(8,128)(2,1)S(1)} %collective-permute-done.22.refs_1_, ...), custom_call_target="tpu_custom_call" | custom-call | tf_op jit(solution)/shard_map/combine/pallas_call | solution.py:369
  77.7 2.8 %collective-permute-done.29.refs_3_ = bf16[48,512]{1,0:T(8,128)(2,1)S(1)} collective-permute-done((bf16[48,512]{1,0:T(8,128)(2,1)S(1)}, bf16[48,512]{1,0:T(8,128)(2,1)S(1)}, u32[]{:S(2)}, u32[]{:S(2)}) %collective-permute-start.29) | collective-permute-done | bytes 49184 | tf_op jit(solution)/shard_map/ppermute | solution.py:41
  80.5 0.9 %combine.3 = bf16[16,2560]{1,0:T(8,128)(2,1)} custom-call(f32[16,4]{1,0:T(8,128)S(1)} %get-tuple-element.28.spot_ref, f32[16,2]{1,0:T(8,128)S(1)} %route.3.refs_8_.weight_ref, bf16[48,512]{1,0:T(8,128)(2,1)S(1)} %get-tuple-element.56.refs_0_, bf16[48,512]{1,0:T(8,128)(2,1)S(1)} %collective-permute-done.27.refs_1_, ...), custom_call_target="tpu_custom_call" | custom-call | tf_op jit(solution)/shard_map/combine/pallas_call | solution.py:369
  (61 shorter events, 0.5 us)
Async XLA Ops:
  0.6 1.4 %copy-start = (bf16[256,2560]{1,0:T(8,128)(2,1)S(1)}, bf16[256,2560]{1,0:T(8,128)(2,1)}, u32[]{:S(2)}) copy-start(bf16[256,2560]{1,0:T(8,128)(2,1)} %param.14) | copy-start | bytes 3932164
  2.0 1.1 %copy-start.7 = (s32[2]{0:T(128)S(1)}, s32[2]{0:T(128)}, u32[]{:S(2)}) copy-start(s32[2]{0:T(128)} %param.20) | copy-start | bytes 28
  2.0 1.2 %copy-start.5 = (s32[16,2]{0,1:T(2,128)S(1)}, s32[16,2]{0,1:T(2,128)}, u32[]{:S(2)}) copy-start(s32[16,2]{0,1:T(2,128)} %param.19) | copy-start | bytes 388
  2.1 1.2 %copy-start.6 = (s32[16,2]{0,1:T(2,128)S(1)}, s32[16,2]{0,1:T(2,128)}, u32[]{:S(2)}) copy-start(s32[16,2]{0,1:T(2,128)} %param.18) | copy-start | bytes 388
  2.1 1.2 %copy-start.3 = (f32[2560]{0:T(1024)S(1)}, f32[2560]{0:T(1024)}, u32[]{:S(2)}) copy-start(f32[2560]{0:T(1024)} %param.16) | copy-start | bytes 30724
  2.1 1.2 %copy-start.4 = (f32[2560]{0:T(1024)S(1)}, f32[2560]{0:T(1024)}, u32[]{:S(2)}) copy-start(f32[2560]{0:T(1024)} %param.15) | copy-start | bytes 30724
  2.5 1.8 %collective-permute-start = (bf16[64,2560]{1,0:T(8,128)(2,1)S(1)}, bf16[64,2560]{1,0:T(8,128)(2,1)S(1)}, u32[]{:S(2)}, u32[]{:S(2)}) collective-permute-start(bf16[64,2560]{1,0:T(8,128)(2,1)S(1)} %get-tuple-element.45), channel_id=1, source_target_pairs={{0,1},{1,0},{2,3},{3,2},{4,5},{5,4},{6,7},{7,6},{8,9},{9,8},{10,11... | collective-permute-start | bytes 983048 | tf_op jit(solution)/shard_map/ppermute | solution.py:41
  3.0 12.3 %collective-permute-start.1 = (bf16[64,2560]{1,0:T(8,128)(2,1)S(1)}, bf16[64,2560]{1,0:T(8,128)(2,1)S(1)}, u32[]{:S(2)}, u32[]{:S(2)}) collective-permute-start(bf16[64,2560]{1,0:T(8,128)(2,1)S(1)} %get-tuple-element.44), channel_id=1, source_target_pairs={{0,1},{1,0},{2,3},{3,2},{4,5},{5,4},{6,7},{7,6},{8,9},{9,8},{10,11... | collective-permute-start | bytes 983048 | tf_op jit(solution)/shard_map/ppermute | solution.py:41
  3.7 3.6 %copy-start.2 = (f32[2560,4]{0,1:T(4,128)S(1)}, f32[2560,4]{0,1:T(4,128)}, u32[]{:S(2)}) copy-start(f32[2560,4]{0,1:T(4,128)} %param.17) | copy-start | bytes 122884
  3.7 3.7 %copy-start.1 = (bf16[16,2560]{1,0:T(8,128)(2,1)S(1)}, bf16[16,2560]{1,0:T(8,128)(2,1)}, u32[]{:S(2)}) copy-start(bf16[16,2560]{1,0:T(8,128)(2,1)} %image_ref.1) | copy-start | bytes 245764
  4.3 11.0 %collective-permute-start.2 = (bf16[64,2560]{1,0:T(8,128)(2,1)S(1)}, bf16[64,2560]{1,0:T(8,128)(2,1)S(1)}, u32[]{:S(2)}, u32[]{:S(2)}) collective-permute-start(bf16[64,2560]{1,0:T(8,128)(2,1)S(1)} %fusion.1.refs_0_), channel_id=1, source_target_pairs={{0,2},{1,3},{2,0},{3,1},{4,6},{5,7},{6,4},{7,5},{8,10},{9,11},{10,... | collective-permute-start | bytes 983048 | tf_op jit(solution)/shard_map/ppermute | solution.py:41
  8.2 11.7 %collective-permute-start.5 = (bf16[48,640]{1,0:T(8,128)(2,1)S(1)}, bf16[48,640]{1,0:T(8,128)(2,1)S(1)}, u32[]{:S(2)}, u32[]{:S(2)}) collective-permute-start(bf16[48,640]{1,0:T(8,128)(2,1)S(1)} %get-tuple-element.27), channel_id=1, source_target_pairs={{0,12},{1,13},{2,14},{3,15},{4,8},{5,9},{6,10},{7,11},{8,4},{9,5},... | collective-permute-start | bytes 184328 | tf_op jit(solution)/shard_map/ppermute | solution.py:41
  11.8 8.2 %collective-permute-start.4 = (bf16[48,640]{1,0:T(8,128)(2,1)S(1)}, bf16[48,640]{1,0:T(8,128)(2,1)S(1)}, u32[]{:S(2)}, u32[]{:S(2)}) collective-permute-start(bf16[48,640]{1,0:T(8,128)(2,1)S(1)} %get-tuple-element.26), channel_id=1, source_target_pairs={{0,8},{1,9},{2,10},{3,11},{4,12},{5,13},{6,14},{7,15},{8,0},{9,1},... | collective-permute-start | bytes 184328 | tf_op jit(solution)/shard_map/ppermute | solution.py:41
  11.8 8.2 %collective-permute-start.3 = (bf16[48,640]{1,0:T(8,128)(2,1)S(1)}, bf16[48,640]{1,0:T(8,128)(2,1)S(1)}, u32[]{:S(2)}, u32[]{:S(2)}) collective-permute-start(bf16[48,640]{1,0:T(8,128)(2,1)S(1)} %get-tuple-element.25.refs_1_), channel_id=1, source_target_pairs={{0,4},{1,5},{2,6},{3,7},{4,0},{5,1},{6,2},{7,3},{8,12},{9,13},{10,... | collective-permute-start | bytes 184328 | tf_op jit(solution)/shard_map/ppermute | solution.py:41
  15.5 6.4 %collective-permute-start.7 = (bf16[16,2560]{1,0:T(8,128)(2,1)S(1)}, bf16[16,2560]{1,0:T(8,128)(2,1)S(1)}, u32[]{:S(2)}, u32[]{:S(2)}) collective-permute-start(bf16[16,2560]{1,0:T(8,128)(2,1)S(1)} %get-tuple-element.48.refs_1_), channel_id=1, source_target_pairs={{0,4},{1,5},{2,6},{3,7},{4,0},{5,1},{6,2},{7,3},{8,12},{9,13},{10,... | collective-permute-start | bytes 245768 | tf_op jit(solution)/shard_map/ppermute | solution.py:41
  17.4 7.8 %collective-permute-start.8 = (bf16[16,2560]{1,0:T(8,128)(2,1)S(1)}, bf16[16,2560]{1,0:T(8,128)(2,1)S(1)}, u32[]{:S(2)}, u32[]{:S(2)}) collective-permute-start(bf16[16,2560]{1,0:T(8,128)(2,1)S(1)} %get-tuple-element.47.refs_2_), channel_id=1, source_target_pairs={{0,8},{1,9},{2,10},{3,11},{4,12},{5,13},{6,14},{7,15},{8,0},{9,1},... | collective-permute-start | bytes 245768 | tf_op jit(solution)/shard_map/ppermute | solution.py:41
  19.9 6.4 %collective-permute-start.9 = (bf16[16,2560]{1,0:T(8,128)(2,1)S(1)}, bf16[16,2560]{1,0:T(8,128)(2,1)S(1)}, u32[]{:S(2)}, u32[]{:S(2)}) collective-permute-start(bf16[16,2560]{1,0:T(8,128)(2,1)S(1)} %get-tuple-element.46.refs_3_), channel_id=1, source_target_pairs={{0,12},{1,13},{2,14},{3,15},{4,8},{5,9},{6,10},{7,11},{8,4},{9,5},... | collective-permute-start | bytes 245768 | tf_op jit(solution)/shard_map/ppermute | solution.py:41
  20.1 11.4 %collective-permute-start.6 = (bf16[192,640]{1,0:T(8,128)(2,1)S(1)}, bf16[192,640]{1,0:T(8,128)(2,1)S(1)}, u32[]{:S(2)}, u32[]{:S(2)}) collective-permute-start(bf16[192,640]{1,0:T(8,128)(2,1)S(1)} %pad_maximum_fusion.refs_0_), channel_id=1, source_target_pairs={{0,2},{1,3},{2,0},{3,1},{4,6},{5,7},{6,4},{7,5},{8,10},{9,11},{10,... | collective-permute-start | bytes 737288 | tf_op jit(solution)/shard_map/ppermute | solution.py:41
  21.9 15.3 %collective-permute-start.10 = (bf16[192,640]{1,0:T(8,128)(2,1)S(1)}, bf16[192,640]{1,0:T(8,128)(2,1)S(1)}, u32[]{:S(2)}, u32[]{:S(2)}) collective-permute-start(bf16[192,640]{1,0:T(8,128)(2,1)S(1)} %pad_maximum_fusion.refs_0_), channel_id=1, source_target_pairs={{0,1},{1,0},{2,3},{3,2},{4,5},{5,4},{6,7},{7,6},{8,9},{9,8},{10,11... | collective-permute-start | bytes 737288 | tf_op jit(solution)/shard_map/ppermute | solution.py:41
  27.0 4.6 %collective-permute-start.12 = (bf16[48,512]{1,0:T(8,128)(2,1)S(1)}, bf16[48,512]{1,0:T(8,128)(2,1)S(1)}, u32[]{:S(2)}, u32[]{:S(2)}) collective-permute-start(bf16[48,512]{1,0:T(8,128)(2,1)S(1)} %get-tuple-element.29.refs_1_), channel_id=1, source_target_pairs={{0,4},{1,5},{2,6},{3,7},{4,0},{5,1},{6,2},{7,3},{8,12},{9,13},{10,... | collective-permute-start | bytes 147464 | tf_op jit(solution)/shard_map/ppermute | solution.py:41
  28.2 5.7 %collective-permute-start.13 = (bf16[48,512]{1,0:T(8,128)(2,1)S(1)}, bf16[48,512]{1,0:T(8,128)(2,1)S(1)}, u32[]{:S(2)}, u32[]{:S(2)}) collective-permute-start(bf16[48,512]{1,0:T(8,128)(2,1)S(1)} %get-tuple-element.31), channel_id=1, source_target_pairs={{0,8},{1,9},{2,10},{3,11},{4,12},{5,13},{6,14},{7,15},{8,0},{9,1},... | collective-permute-start | bytes 147464 | tf_op jit(solution)/shard_map/ppermute | solution.py:41
  29.7 5.9 %collective-permute-start.14 = (bf16[48,512]{1,0:T(8,128)(2,1)S(1)}, bf16[48,512]{1,0:T(8,128)(2,1)S(1)}, u32[]{:S(2)}, u32[]{:S(2)}) collective-permute-start(bf16[48,512]{1,0:T(8,128)(2,1)S(1)} %get-tuple-element.32), channel_id=1, source_target_pairs={{0,12},{1,13},{2,14},{3,15},{4,8},{5,9},{6,10},{7,11},{8,4},{9,5},... | collective-permute-start | bytes 147464 | tf_op jit(solution)/shard_map/ppermute | solution.py:41
  31.5 5.7 %collective-permute-start.11 = (bf16[192,640]{1,0:T(8,128)(2,1)S(1)}, bf16[192,640]{1,0:T(8,128)(2,1)S(1)}, u32[]{:S(2)}, u32[]{:S(2)}) collective-permute-start(bf16[192,640]{1,0:T(8,128)(2,1)S(1)} %tie.12.refs_1_), channel_id=1, source_target_pairs={{0,1},{1,0},{2,3},{3,2},{4,5},{5,4},{6,7},{7,6},{8,9},{9,8},{10,11... | collective-permute-start | bytes 737288 | tf_op jit(solution)/shard_map/ppermute | solution.py:41
  35.6 13.7 %collective-permute-start.15 = (bf16[192,512]{1,0:T(8,128)(2,1)S(1)}, bf16[192,512]{1,0:T(8,128)(2,1)S(1)}, u32[]{:S(2)}, u32[]{:S(2)}) collective-permute-start(bf16[192,512]{1,0:T(8,128)(2,1)S(1)} %constant_dynamic-update-slice_fusion.refs_7_.refs_0_), channel_id=1, source_target_pairs={{0,2},{1,3},{2,0},{3,1},{4,6},{5,7},{6,4},{7,5},{8,10},{9,11},{10,... | collective-permute-start | bytes 589832 | tf_op jit(solution)/shard_map/ppermute | solution.py:41
  49.4 1.6 %collective-permute-start.17 = (bf16[192,640]{1,0:T(8,128)(2,1)S(1)}, bf16[192,640]{1,0:T(8,128)(2,1)S(1)}, u32[]{:S(2)}, u32[]{:S(2)}) collective-permute-start(bf16[192,640]{1,0:T(8,128)(2,1)S(1)} %tie.15), channel_id=1, source_target_pairs={{0,1},{1,0},{2,3},{3,2},{4,5},{5,4},{6,7},{7,6},{8,9},{9,8},{10,11... | collective-permute-start | bytes 737288 | tf_op jit(solution)/shard_map/ppermute | solution.py:41
  49.7 1.9 %collective-permute-start.19 = (bf16[192,512]{1,0:T(8,128)(2,1)S(1)}, bf16[192,512]{1,0:T(8,128)(2,1)S(1)}, u32[]{:S(2)}, u32[]{:S(2)}) collective-permute-start(bf16[192,512]{1,0:T(8,128)(2,1)S(1)} %constant_dynamic-update-slice_fusion.refs_7_.refs_0_), channel_id=1, source_target_pairs={{0,1},{1,0},{2,3},{3,2},{4,5},{5,4},{6,7},{7,6},{8,9},{9,8},{10,11... | collective-permute-start | bytes 589832 | tf_op jit(solution)/shard_map/ppermute | solution.py:41
  50.2 1.4 %collective-permute-start.20 = (bf16[192,512]{1,0:T(8,128)(2,1)S(1)}, bf16[192,512]{1,0:T(8,128)(2,1)S(1)}, u32[]{:S(2)}, u32[]{:S(2)}) collective-permute-start(bf16[192,512]{1,0:T(8,128)(2,1)S(1)} %tie.13.refs_1_), channel_id=1, source_target_pairs={{0,1},{1,0},{2,3},{3,2},{4,5},{5,4},{6,7},{7,6},{8,9},{9,8},{10,11... | collective-permute-start | bytes 589832 | tf_op jit(solution)/shard_map/ppermute | solution.py:41
  51.0 12.4 %collective-permute-start.18 = (bf16[192,640]{1,0:T(8,128)(2,1)S(1)}, bf16[192,640]{1,0:T(8,128)(2,1)S(1)}, u32[]{:S(2)}, u32[]{:S(2)}) collective-permute-start(bf16[192,640]{1,0:T(8,128)(2,1)S(1)} %add_convert_fusion.1.refs_7_), channel_id=1, source_target_pairs={{0,2},{1,3},{2,0},{3,1},{4,6},{5,7},{6,4},{7,5},{8,10},{9,11},{10,... | collective-permute-start | bytes 737288 | tf_op jit(solution)/shard_map/ppermute | solution.py:41
  63.5 1.5 %collective-permute-start.21 = (bf16[192,512]{1,0:T(8,128)(2,1)S(1)}, bf16[192,512]{1,0:T(8,128)(2,1)S(1)}, u32[]{:S(2)}, u32[]{:S(2)}) collective-permute-start(bf16[192,512]{1,0:T(8,128)(2,1)S(1)} %tie.17), channel_id=1, source_target_pairs={{0,1},{1,0},{2,3},{3,2},{4,5},{5,4},{6,7},{7,6},{8,9},{9,8},{10,11... | collective-permute-start | bytes 589832 | tf_op jit(solution)/shard_map/ppermute | solution.py:41
  63.9 2.7 %collective-permute-start.16 = (bf16[192,640]{1,0:T(8,128)(2,1)S(1)}, bf16[192,640]{1,0:T(8,128)(2,1)S(1)}, u32[]{:S(2)}, u32[]{:S(2)}) collective-permute-start(bf16[192,640]{1,0:T(8,128)(2,1)S(1)} %tie.14), channel_id=1, source_target_pairs={{0,1},{1,0},{2,3},{3,2},{4,5},{5,4},{6,7},{7,6},{8,9},{9,8},{10,11... | collective-permute-start | bytes 737288 | tf_op jit(solution)/shard_map/ppermute | solution.py:41
  64.2 7.0 %collective-permute-start.25 = (bf16[192,512]{1,0:T(8,128)(2,1)S(1)}, bf16[192,512]{1,0:T(8,128)(2,1)S(1)}, u32[]{:S(2)}, u32[]{:S(2)}) collective-permute-start(bf16[192,512]{1,0:T(8,128)(2,1)S(1)} %tie.19), channel_id=1, source_target_pairs={{0,1},{1,0},{2,3},{3,2},{4,5},{5,4},{6,7},{7,6},{8,9},{9,8},{10,11... | collective-permute-start | bytes 589832 | tf_op jit(solution)/shard_map/ppermute | solution.py:41
  65.1 7.2 %collective-permute-start.26 = (bf16[192,512]{1,0:T(8,128)(2,1)S(1)}, bf16[192,512]{1,0:T(8,128)(2,1)S(1)}, u32[]{:S(2)}, u32[]{:S(2)}) collective-permute-start(bf16[192,512]{1,0:T(8,128)(2,1)S(1)} %add_convert_fusion.3.refs_1_), channel_id=1, source_target_pairs={{0,2},{1,3},{2,0},{3,1},{4,6},{5,7},{6,4},{7,5},{8,10},{9,11},{10,... | collective-permute-start | bytes 589832 | tf_op jit(solution)/shard_map/ppermute | solution.py:41
  66.7 7.9 %collective-permute-start.22 = (bf16[48,640]{1,0:T(8,128)(2,1)S(1)}, bf16[48,640]{1,0:T(8,128)(2,1)S(1)}, u32[]{:S(2)}, u32[]{:S(2)}) collective-permute-start(bf16[48,640]{1,0:T(8,128)(2,1)S(1)} %get-tuple-element.51), channel_id=1, source_target_pairs={{0,4},{1,5},{2,6},{3,7},{4,0},{5,1},{6,2},{7,3},{8,12},{9,13},{10,... | collective-permute-start | bytes 184328 | tf_op jit(solution)/shard_map/ppermute | solution.py:41
  66.8 10.0 %collective-permute-start.23 = (bf16[48,640]{1,0:T(8,128)(2,1)S(1)}, bf16[48,640]{1,0:T(8,128)(2,1)S(1)}, u32[]{:S(2)}, u32[]{:S(2)}) collective-permute-start(bf16[48,640]{1,0:T(8,128)(2,1)S(1)} %get-tuple-element.50), channel_id=1, source_target_pairs={{0,8},{1,9},{2,10},{3,11},{4,12},{5,13},{6,14},{7,15},{8,0},{9,1},... | collective-permute-start | bytes 184328 | tf_op jit(solution)/shard_map/ppermute | solution.py:41
  69.0 7.8 %collective-permute-start.24 = (bf16[48,640]{1,0:T(8,128)(2,1)S(1)}, bf16[48,640]{1,0:T(8,128)(2,1)S(1)}, u32[]{:S(2)}, u32[]{:S(2)}) collective-permute-start(bf16[48,640]{1,0:T(8,128)(2,1)S(1)} %get-tuple-element.49), channel_id=1, source_target_pairs={{0,12},{1,13},{2,14},{3,15},{4,8},{5,9},{6,10},{7,11},{8,4},{9,5},... | collective-permute-start | bytes 184328 | tf_op jit(solution)/shard_map/ppermute | solution.py:41
  72.3 5.4 %collective-permute-start.27 = (bf16[48,512]{1,0:T(8,128)(2,1)S(1)}, bf16[48,512]{1,0:T(8,128)(2,1)S(1)}, u32[]{:S(2)}, u32[]{:S(2)}) collective-permute-start(bf16[48,512]{1,0:T(8,128)(2,1)S(1)} %get-tuple-element.55), channel_id=1, source_target_pairs={{0,4},{1,5},{2,6},{3,7},{4,0},{5,1},{6,2},{7,3},{8,12},{9,13},{10,... | collective-permute-start | bytes 147464 | tf_op jit(solution)/shard_map/ppermute | solution.py:41
  72.4 5.3 %collective-permute-start.28 = (bf16[48,512]{1,0:T(8,128)(2,1)S(1)}, bf16[48,512]{1,0:T(8,128)(2,1)S(1)}, u32[]{:S(2)}, u32[]{:S(2)}) collective-permute-start(bf16[48,512]{1,0:T(8,128)(2,1)S(1)} %get-tuple-element.54), channel_id=1, source_target_pairs={{0,8},{1,9},{2,10},{3,11},{4,12},{5,13},{6,14},{7,15},{8,0},{9,1},... | collective-permute-start | bytes 147464 | tf_op jit(solution)/shard_map/ppermute | solution.py:41
  74.7 5.9 %collective-permute-start.29 = (bf16[48,512]{1,0:T(8,128)(2,1)S(1)}, bf16[48,512]{1,0:T(8,128)(2,1)S(1)}, u32[]{:S(2)}, u32[]{:S(2)}) collective-permute-start(bf16[48,512]{1,0:T(8,128)(2,1)S(1)} %get-tuple-element.53), channel_id=1, source_target_pairs={{0,12},{1,13},{2,14},{3,15},{4,8},{5,9},{6,10},{7,11},{8,4},{9,5},... | collective-permute-start | bytes 147464 | tf_op jit(solution)/shard_map/ppermute | solution.py:41

commit v12 on v11

--- a/solution.py
+++ b/solution.py
@@ -210,6 +210,8 @@
 
 def cuts(units):
     edges = [0] + list(range(256, units - 255, 512)) + [units]
+    if edges[-1] - edges[-2] > 256 and len(edges) > 2:
+        edges.insert(-1, edges[-2] + 256)
     return list(zip(edges[:-1], edges[1:]))
 
 
@@ -229,7 +231,7 @@
                     source.at[lo:hi], target.at[lo:hi], sems.at[3 * i + t]
                 )
             )
-    for copy in copies[:6]:
+    for copy in copies[:2]:
         copy.start()
 
     cap, chunks, width, high = packing.cap, packing.chunks, packing.width, packing.rows
@@ -249,6 +251,8 @@
                 total_ref[j * lanes + c, pl.ds(slot, blocks, stride=cap), :] = packed_ref[
                     c, pl.ds(j * cap + slot, blocks, stride=high), :
                 ]
+    for copy in copies[2:6]:
+        copy.start()
     for c in range(chunks * lanes):
         part = total_ref[c, 0:rows, :]
         if spare:

time: 81.6 us -> 81.7 us (level)
  no operation moved by 1% of the time
where the time goes in v12:
time: 81.7 us; the launch traced here: 81.5 us
  starting transfers between devices  33 us (40%)
  Pallas kernels  27.9 us (34%)
  waiting for transfers between devices  16.6 us (20%)
  other arithmetic  1.93 us (2%)
  between operations  1.14 us (1%)
    ppermute x30, starting transfers between devices, swap(): return lax.ppermute(value, 'dev', moves)  33 us
    pallas_call x2, Pallas kernels, expert_rows(): pl.pallas_call(functools.partial(expert_kernel, packing, unit_cuts, len(a...  23.9 us
    ppermute x30, waiting for transfers between devices, swap(): return lax.ppermute(value, 'dev', moves)  16.6 us
    pallas_call x2, Pallas kernels, combine(): pl.pallas_call(functools.partial(combine_kernel, packing), out_shape=jax....  1.77 us
  transfers between devices with their start and end apart: 30, of which 11 were waited for; matrix products, arithmetic and copies ran while one was open for 1% of the time, Pallas kernels for 33%

profile of v12, /device:TPU:0, one launch (start us, length us, event | category | flops | bytes accessed | tf_op | source)
XLA Modules:
  0.0 81.5 jit_solution(11771559034419648283)
XLA Ops:
  0.6 0.0 copy-start
  0.7 1.1 %fusion.5 = bf16[2,2,2,2,16,256]{5,4,3,2,1,0:T(8,128)(2,1)S(1)} fusion(s32[]{:T(128)S(6)} %select_n.80, bf16[2,2,2,2,16,256]{5,4,3,2,1,0:T(8,128)(2,1)} %bitcast.29), kind=kLoop, calls=%fused_computation.21 | loop fusion | flops 65536 | bytes 262148 | tf_op jit(solution)/shard_map/jit(_roll_dynamic)/concatenate | solution.py:389
  1.8 0.1 fusion.3
  1.9 0.1 fusion.2
  2.0 0.0 copy-start.7
  2.0 0.0 copy-start.5
  2.1 0.0 copy-start.6
  2.1 0.0 copy-start.4
  2.1 0.3 convolution_convert_fusion
  2.5 0.5 collective-permute-start
  3.0 0.1 collective-permute-start.1
  3.1 0.1 fusion.7
  3.3 0.3 fusion.16
  3.7 0.6 collective-permute-done
  4.3 0.1 fusion.1.refs_0_
  4.3 3.0 %collective-permute-start.2 = (bf16[64,2560]{1,0:T(8,128)(2,1)S(1)}, bf16[64,2560]{1,0:T(8,128)(2,1)S(1)}, u32[]{:S(2)}, u32[]{:S(2)}) collective-permute-start(bf16[64,2560]{1,0:T(8,128)(2,1)S(1)} %fusion.1.refs_0_), channel_id=1, source_target_pairs={{0,2},{1,3},{2,0},{3,1},{4,6},{5,7},{6,4},{7,5},{8,10},{9,11},{10,... | collective-permute-start | bytes 983048 | tf_op jit(solution)/shard_map/ppermute | solution.py:41
  7.3 0.8 %prepare.1 = (f32[16,4]{1,0:T(8,128)S(1)}, f32[16,4]{1,0:T(8,128)S(1)}, bf16[16,2560]{1,0:T(8,128)(2,1)S(1)}, bf16[48,640]{1,0:T(8,128)(2,1)S(1)}, bf16[48,640]{...) custom-call(s32[4,16]{1,0:T(4,128)S(1)} %pad_add_fusion.ids_ref, ...), custom_call_target="tpu_custom_call" | custom-call | tf_op jit(solution)/shard_map/prepare/pallas_call | solution.py:123
  8.2 3.6 %collective-permute-start.5 = (bf16[48,640]{1,0:T(8,128)(2,1)S(1)}, bf16[48,640]{1,0:T(8,128)(2,1)S(1)}, u32[]{:S(2)}, u32[]{:S(2)}) collective-permute-start(bf16[48,640]{1,0:T(8,128)(2,1)S(1)} %get-tuple-element.27), channel_id=1, source_target_pairs={{0,12},{1,13},{2,14},{3,15},{4,8},{5,9},{6,10},{7,11},{8,4},{9,5},... | collective-permute-start | bytes 184328 | tf_op jit(solution)/shard_map/ppermute | solution.py:41
  11.8 0.8 collective-permute-start.3
  12.6 0.3 route.2.refs_8_.weight_ref
  12.9 2.4 %collective-permute-done.2.refs_0_ = bf16[64,2560]{1,0:T(8,128)(2,1)S(1)} collective-permute-done((bf16[64,2560]{1,0:T(8,128)(2,1)S(1)}, bf16[64,2560]{1,0:T(8,128)(2,1)S(1)}, u32[]{:S(2)}, u32[]{:S(2)}) %collective-permute-start.2) | collective-permute-done | bytes 327712 | tf_op jit(solution)/shard_map/ppermute | solution.py:41
  15.3 0.1 fusion.9
  15.5 1.9 %collective-permute-start.7 = (bf16[16,2560]{1,0:T(8,128)(2,1)S(1)}, bf16[16,2560]{1,0:T(8,128)(2,1)S(1)}, u32[]{:S(2)}, u32[]{:S(2)}) collective-permute-start(bf16[16,2560]{1,0:T(8,128)(2,1)S(1)} %get-tuple-element.48.refs_1_), channel_id=1, source_target_pairs={{0,4},{1,5},{2,6},{3,7},{4,0},{5,1},{6,2},{7,3},{8,12},{9,13},{10,... | collective-permute-start | bytes 245768 | tf_op jit(solution)/shard_map/ppermute | solution.py:41
  17.4 2.5 %collective-permute-start.8 = (bf16[16,2560]{1,0:T(8,128)(2,1)S(1)}, bf16[16,2560]{1,0:T(8,128)(2,1)S(1)}, u32[]{:S(2)}, u32[]{:S(2)}) collective-permute-start(bf16[16,2560]{1,0:T(8,128)(2,1)S(1)} %get-tuple-element.47.refs_2_), channel_id=1, source_target_pairs={{0,8},{1,9},{2,10},{3,11},{4,12},{5,13},{6,14},{7,15},{8,0},{9,1},... | collective-permute-start | bytes 245768 | tf_op jit(solution)/shard_map/ppermute | solution.py:41
  19.9 0.1 collective-permute-start.9
  20.1 1.8 %collective-permute-start.6 = (bf16[192,640]{1,0:T(8,128)(2,1)S(1)}, bf16[192,640]{1,0:T(8,128)(2,1)S(1)}, u32[]{:S(2)}, u32[]{:S(2)}) collective-permute-start(bf16[192,640]{1,0:T(8,128)(2,1)S(1)} %pad_maximum_fusion.refs_0_), channel_id=1, source_target_pairs={{0,2},{1,3},{2,0},{3,1},{4,6},{5,7},{6,4},{7,5},{8,10},{9,11},{10,... | collective-permute-start | bytes 737288 | tf_op jit(solution)/shard_map/ppermute | solution.py:41
  21.9 3.3 %collective-permute-done.8.refs_2_ = bf16[16,2560]{1,0:T(8,128)(2,1)S(1)} collective-permute-done((bf16[16,2560]{1,0:T(8,128)(2,1)S(1)}, bf16[16,2560]{1,0:T(8,128)(2,1)S(1)}, u32[]{:S(2)}, u32[]{:S(2)}) %collective-permute-start.8) | collective-permute-done | bytes 81952 | tf_op jit(solution)/shard_map/ppermute | solution.py:41
  25.1 1.2 %collective-permute-done.9.refs_3_ = bf16[16,2560]{1,0:T(8,128)(2,1)S(1)} collective-permute-done((bf16[16,2560]{1,0:T(8,128)(2,1)S(1)}, bf16[16,2560]{1,0:T(8,128)(2,1)S(1)}, u32[]{:S(2)}, u32[]{:S(2)}) %collective-permute-start.9) | collective-permute-done | bytes 81952 | tf_op jit(solution)/shard_map/ppermute | solution.py:41
  26.3 0.6 modulate.1
  27.0 1.2 %collective-permute-start.12 = (bf16[48,512]{1,0:T(8,128)(2,1)S(1)}, bf16[48,512]{1,0:T(8,128)(2,1)S(1)}, u32[]{:S(2)}, u32[]{:S(2)}) collective-permute-start(bf16[48,512]{1,0:T(8,128)(2,1)S(1)} %get-tuple-element.29.refs_1_), channel_id=1, source_target_pairs={{0,4},{1,5},{2,6},{3,7},{4,0},{5,1},{6,2},{7,3},{8,12},{9,13},{10,... | collective-permute-start | bytes 147464 | tf_op jit(solution)/shard_map/ppermute | solution.py:41
  28.2 1.6 %collective-permute-start.13 = (bf16[48,512]{1,0:T(8,128)(2,1)S(1)}, bf16[48,512]{1,0:T(8,128)(2,1)S(1)}, u32[]{:S(2)}, u32[]{:S(2)}) collective-permute-start(bf16[48,512]{1,0:T(8,128)(2,1)S(1)} %get-tuple-element.31), channel_id=1, source_target_pairs={{0,8},{1,9},{2,10},{3,11},{4,12},{5,13},{6,14},{7,15},{8,0},{9,1},... | collective-permute-start | bytes 147464 | tf_op jit(solution)/shard_map/ppermute | solution.py:41
  29.7 1.7 %collective-permute-start.14 = (bf16[48,512]{1,0:T(8,128)(2,1)S(1)}, bf16[48,512]{1,0:T(8,128)(2,1)S(1)}, u32[]{:S(2)}, u32[]{:S(2)}) collective-permute-start(bf16[48,512]{1,0:T(8,128)(2,1)S(1)} %get-tuple-element.32), channel_id=1, source_target_pairs={{0,12},{1,13},{2,14},{3,15},{4,8},{5,9},{6,10},{7,11},{8,4},{9,5},... | collective-permute-start | bytes 147464 | tf_op jit(solution)/shard_map/ppermute | solution.py:41
  31.5 0.1 collective-permute-start.11
  31.6 2.4 %collective-permute-done.13 = bf16[48,512]{1,0:T(8,128)(2,1)S(1)} collective-permute-done((bf16[48,512]{1,0:T(8,128)(2,1)S(1)}, bf16[48,512]{1,0:T(8,128)(2,1)S(1)}, u32[]{:S(2)}, u32[]{:S(2)}) %collective-permute-start.13) | collective-permute-done | bytes 49184 | tf_op jit(solution)/shard_map/ppermute | solution.py:41
  33.9 1.7 %collective-permute-done.14 = bf16[48,512]{1,0:T(8,128)(2,1)S(1)} collective-permute-done((bf16[48,512]{1,0:T(8,128)(2,1)S(1)}, bf16[48,512]{1,0:T(8,128)(2,1)S(1)}, u32[]{:S(2)}, u32[]{:S(2)}) %collective-permute-start.14) | collective-permute-done | bytes 49184 | tf_op jit(solution)/shard_map/ppermute | solution.py:41
  35.6 1.5 %collective-permute-start.15 = (bf16[192,512]{1,0:T(8,128)(2,1)S(1)}, bf16[192,512]{1,0:T(8,128)(2,1)S(1)}, u32[]{:S(2)}, u32[]{:S(2)}) collective-permute-start(bf16[192,512]{1,0:T(8,128)(2,1)S(1)} %constant_dynamic-update-slice_fusion.refs_7_.refs_0_), channel_id=1, source_target_pairs={{0,2},{1,3},{2,0},{3,1},{4,6},{5,7},{6,4},{7,5},{8,10},{9,11},{10,... | collective-permute-start | bytes 589832 | tf_op jit(solution)/shard_map/ppermute | solution.py:41
  37.2 12.2 %experts.2 = (bf16[192,640]{1,0:T(8,128)(2,1)S(1)}, bf16[192,640]{1,0:T(8,128)(2,1)S(1)}, bf16[192,640]{1,0:T(8,128)(2,1)S(1)}, bf16[192,640]{1,0:T(8,128)(2,1)S(1)}) custom-call(bf16[192,640]{1,0:T(8,128)(2,1)S(1)} %pad_maximum_fusion.refs_0_, bf16[192,640]{1,0:T(8,128)(2,1)S(1)} %tie.12.refs_1_, bf16[192,640]{1,0:T(8,128)(2,1)S(1)} %collective-permute-done.10.refs_2_, ...), custom_call_target="tpu_custom_call" | custom-call | flops 5096079360 | bytes 26542080 | tf_op jit(solution)/shard_map/experts/pallas_call | solution.py:320
  49.5 0.1 collective-permute-start.17
  49.6 0.3 route.3.refs_8_.weight_ref
  49.8 0.5 collective-permute-start.19
  50.3 0.1 collective-permute-start.20
  50.4 0.6 collective-permute-done.17
  51.1 0.1 add_convert_fusion.1.refs_7_
  51.1 0.6 collective-permute-start.18
  51.7 0.1 collective-permute-done.20.refs_3_
  51.8 11.7 %experts.3 = (bf16[192,512]{1,0:T(8,128)(2,1)S(1)}, bf16[192,512]{1,0:T(8,128)(2,1)S(1)}, bf16[192,512]{1,0:T(8,128)(2,1)S(1)}, bf16[192,512]{1,0:T(8,128)(2,1)S(1)}) custom-call(bf16[192,512]{1,0:T(8,128)(2,1)S(1)} %constant_dynamic-update-slice_fusion.refs_7_.refs_0_, bf16[192,512]{1,0:T(8,128)(2,1)S(1)} %tie.13.refs_1_, ...), custom_call_target="tpu_custom_call" | custom-call | flops 3822059520 | bytes 26542080 | tf_op jit(solution)/shard_map/experts/pallas_call | solution.py:320
  63.5 0.4 collective-permute-start.21
  63.9 0.3 collective-permute-start.16
  64.2 0.4 collective-permute-start.25
  64.6 0.5 collective-permute-done.21
  65.1 0.1 add_convert_fusion.3.refs_1_
  65.1 1.5 %collective-permute-start.26 = (bf16[192,512]{1,0:T(8,128)(2,1)S(1)}, bf16[192,512]{1,0:T(8,128)(2,1)S(1)}, u32[]{:S(2)}, u32[]{:S(2)}) collective-permute-start(bf16[192,512]{1,0:T(8,128)(2,1)S(1)} %add_convert_fusion.3.refs_1_), channel_id=1, source_target_pairs={{0,2},{1,3},{2,0},{3,1},{4,6},{5,7},{6,4},{7,5},{8,10},{9,11},{10,... | collective-permute-start | bytes 589832 | tf_op jit(solution)/shard_map/ppermute | solution.py:41
  66.6 0.1 add_convert_fusion
  66.8 0.1 collective-permute-start.22
  66.9 2.2 %collective-permute-start.23 = (bf16[48,640]{1,0:T(8,128)(2,1)S(1)}, bf16[48,640]{1,0:T(8,128)(2,1)S(1)}, u32[]{:S(2)}, u32[]{:S(2)}) collective-permute-start(bf16[48,640]{1,0:T(8,128)(2,1)S(1)} %get-tuple-element.50), channel_id=1, source_target_pairs={{0,8},{1,9},{2,10},{3,11},{4,12},{5,13},{6,14},{7,15},{8,0},{9,1},... | collective-permute-start | bytes 184328 | tf_op jit(solution)/shard_map/ppermute | solution.py:41
  69.1 2.1 %collective-permute-start.24 = (bf16[48,640]{1,0:T(8,128)(2,1)S(1)}, bf16[48,640]{1,0:T(8,128)(2,1)S(1)}, u32[]{:S(2)}, u32[]{:S(2)}) collective-permute-start(bf16[48,640]{1,0:T(8,128)(2,1)S(1)} %get-tuple-element.49), channel_id=1, source_target_pairs={{0,12},{1,13},{2,14},{3,15},{4,8},{5,9},{6,10},{7,11},{8,4},{9,5},... | collective-permute-start | bytes 184328 | tf_op jit(solution)/shard_map/ppermute | solution.py:41
  71.2 1.1 %collective-permute-done.26 = bf16[192,512]{1,0:T(8,128)(2,1)S(1)} collective-permute-done((bf16[192,512]{1,0:T(8,128)(2,1)S(1)}, bf16[192,512]{1,0:T(8,128)(2,1)S(1)}, u32[]{:S(2)}, u32[]{:S(2)}) %collective-permute-start.26) | collective-permute-done | bytes 196640 | tf_op jit(solution)/shard_map/ppermute | solution.py:41
  72.3 0.1 add_convert_fusion.2
  72.4 0.1 collective-permute-start.27
  72.5 2.2 %collective-permute-start.28 = (bf16[48,512]{1,0:T(8,128)(2,1)S(1)}, bf16[48,512]{1,0:T(8,128)(2,1)S(1)}, u32[]{:S(2)}, u32[]{:S(2)}) collective-permute-start(bf16[48,512]{1,0:T(8,128)(2,1)S(1)} %get-tuple-element.54), channel_id=1, source_target_pairs={{0,8},{1,9},{2,10},{3,11},{4,12},{5,13},{6,14},{7,15},{8,0},{9,1},... | collective-permute-start | bytes 147464 | tf_op jit(solution)/shard_map/ppermute | solution.py:41
  74.7 2.1 %collective-permute-start.29 = (bf16[48,512]{1,0:T(8,128)(2,1)S(1)}, bf16[48,512]{1,0:T(8,128)(2,1)S(1)}, u32[]{:S(2)}, u32[]{:S(2)}) collective-permute-start(bf16[48,512]{1,0:T(8,128)(2,1)S(1)} %get-tuple-element.53), channel_id=1, source_target_pairs={{0,12},{1,13},{2,14},{3,15},{4,8},{5,9},{6,10},{7,11},{8,4},{9,5},... | collective-permute-start | bytes 147464 | tf_op jit(solution)/shard_map/ppermute | solution.py:41
  76.9 0.9 %combine.2 = bf16[16,2560]{1,0:T(8,128)(2,1)} custom-call(f32[16,4]{1,0:T(8,128)S(1)} %get-tuple-element.22.spot_ref, f32[16,2]{1,0:T(8,128)S(1)} %route.2.refs_8_.weight_ref, bf16[48,640]{1,0:T(8,128)(2,1)S(1)} %get-tuple-element.52.refs_0_, bf16[48,640]{1,0:T(8,128)(2,1)S(1)} %collective-permute-done.22.refs_1_, ...), custom_call_target="tpu_custom_call" | custom-call | tf_op jit(solution)/shard_map/combine/pallas_call | solution.py:373
  77.8 2.9 %collective-permute-done.29.refs_3_ = bf16[48,512]{1,0:T(8,128)(2,1)S(1)} collective-permute-done((bf16[48,512]{1,0:T(8,128)(2,1)S(1)}, bf16[48,512]{1,0:T(8,128)(2,1)S(1)}, u32[]{:S(2)}, u32[]{:S(2)}) %collective-permute-start.29) | collective-permute-done | bytes 49184 | tf_op jit(solution)/shard_map/ppermute | solution.py:41
  80.6 0.9 %combine.3 = bf16[16,2560]{1,0:T(8,128)(2,1)} custom-call(f32[16,4]{1,0:T(8,128)S(1)} %get-tuple-element.28.spot_ref, f32[16,2]{1,0:T(8,128)S(1)} %route.3.refs_8_.weight_ref, bf16[48,512]{1,0:T(8,128)(2,1)S(1)} %get-tuple-element.56.refs_0_, bf16[48,512]{1,0:T(8,128)(2,1)S(1)} %collective-permute-done.27.refs_1_, ...), custom_call_target="tpu_custom_call" | custom-call | tf_op jit(solution)/shard_map/combine/pallas_call | solution.py:373
  (61 shorter events, 0.5 us)
Async XLA Ops:
  0.6 1.4 %copy-start = (bf16[256,2560]{1,0:T(8,128)(2,1)S(1)}, bf16[256,2560]{1,0:T(8,128)(2,1)}, u32[]{:S(2)}) copy-start(bf16[256,2560]{1,0:T(8,128)(2,1)} %param.14) | copy-start | bytes 3932164
  2.0 1.1 %copy-start.7 = (s32[2]{0:T(128)S(1)}, s32[2]{0:T(128)}, u32[]{:S(2)}) copy-start(s32[2]{0:T(128)} %param.20) | copy-start | bytes 28
  2.0 1.2 %copy-start.5 = (s32[16,2]{0,1:T(2,128)S(1)}, s32[16,2]{0,1:T(2,128)}, u32[]{:S(2)}) copy-start(s32[16,2]{0,1:T(2,128)} %param.19) | copy-start | bytes 388
  2.1 1.2 %copy-start.6 = (s32[16,2]{0,1:T(2,128)S(1)}, s32[16,2]{0,1:T(2,128)}, u32[]{:S(2)}) copy-start(s32[16,2]{0,1:T(2,128)} %param.18) | copy-start | bytes 388
  2.1 1.2 %copy-start.3 = (f32[2560]{0:T(1024)S(1)}, f32[2560]{0:T(1024)}, u32[]{:S(2)}) copy-start(f32[2560]{0:T(1024)} %param.16) | copy-start | bytes 30724
  2.1 1.2 %copy-start.4 = (f32[2560]{0:T(1024)S(1)}, f32[2560]{0:T(1024)}, u32[]{:S(2)}) copy-start(f32[2560]{0:T(1024)} %param.15) | copy-start | bytes 30724
  2.5 1.8 %collective-permute-start = (bf16[64,2560]{1,0:T(8,128)(2,1)S(1)}, bf16[64,2560]{1,0:T(8,128)(2,1)S(1)}, u32[]{:S(2)}, u32[]{:S(2)}) collective-permute-start(bf16[64,2560]{1,0:T(8,128)(2,1)S(1)} %get-tuple-element.45), channel_id=1, source_target_pairs={{0,1},{1,0},{2,3},{3,2},{4,5},{5,4},{6,7},{7,6},{8,9},{9,8},{10,11... | collective-permute-start | bytes 983048 | tf_op jit(solution)/shard_map/ppermute | solution.py:41
  3.0 12.3 %collective-permute-start.1 = (bf16[64,2560]{1,0:T(8,128)(2,1)S(1)}, bf16[64,2560]{1,0:T(8,128)(2,1)S(1)}, u32[]{:S(2)}, u32[]{:S(2)}) collective-permute-start(bf16[64,2560]{1,0:T(8,128)(2,1)S(1)} %get-tuple-element.44), channel_id=1, source_target_pairs={{0,1},{1,0},{2,3},{3,2},{4,5},{5,4},{6,7},{7,6},{8,9},{9,8},{10,11... | collective-permute-start | bytes 983048 | tf_op jit(solution)/shard_map/ppermute | solution.py:41
  3.7 3.6 %copy-start.2 = (f32[2560,4]{0,1:T(4,128)S(1)}, f32[2560,4]{0,1:T(4,128)}, u32[]{:S(2)}) copy-start(f32[2560,4]{0,1:T(4,128)} %param.17) | copy-start | bytes 122884
  3.7 3.7 %copy-start.1 = (bf16[16,2560]{1,0:T(8,128)(2,1)S(1)}, bf16[16,2560]{1,0:T(8,128)(2,1)}, u32[]{:S(2)}) copy-start(bf16[16,2560]{1,0:T(8,128)(2,1)} %image_ref.1) | copy-start | bytes 245764
  4.3 11.0 %collective-permute-start.2 = (bf16[64,2560]{1,0:T(8,128)(2,1)S(1)}, bf16[64,2560]{1,0:T(8,128)(2,1)S(1)}, u32[]{:S(2)}, u32[]{:S(2)}) collective-permute-start(bf16[64,2560]{1,0:T(8,128)(2,1)S(1)} %fusion.1.refs_0_), channel_id=1, source_target_pairs={{0,2},{1,3},{2,0},{3,1},{4,6},{5,7},{6,4},{7,5},{8,10},{9,11},{10,... | collective-permute-start | bytes 983048 | tf_op jit(solution)/shard_map/ppermute | solution.py:41
  8.2 11.7 %collective-permute-start.5 = (bf16[48,640]{1,0:T(8,128)(2,1)S(1)}, bf16[48,640]{1,0:T(8,128)(2,1)S(1)}, u32[]{:S(2)}, u32[]{:S(2)}) collective-permute-start(bf16[48,640]{1,0:T(8,128)(2,1)S(1)} %get-tuple-element.27), channel_id=1, source_target_pairs={{0,12},{1,13},{2,14},{3,15},{4,8},{5,9},{6,10},{7,11},{8,4},{9,5},... | collective-permute-start | bytes 184328 | tf_op jit(solution)/shard_map/ppermute | solution.py:41
  11.8 8.2 %collective-permute-start.4 = (bf16[48,640]{1,0:T(8,128)(2,1)S(1)}, bf16[48,640]{1,0:T(8,128)(2,1)S(1)}, u32[]{:S(2)}, u32[]{:S(2)}) collective-permute-start(bf16[48,640]{1,0:T(8,128)(2,1)S(1)} %get-tuple-element.26), channel_id=1, source_target_pairs={{0,8},{1,9},{2,10},{3,11},{4,12},{5,13},{6,14},{7,15},{8,0},{9,1},... | collective-permute-start | bytes 184328 | tf_op jit(solution)/shard_map/ppermute | solution.py:41
  11.8 8.2 %collective-permute-start.3 = (bf16[48,640]{1,0:T(8,128)(2,1)S(1)}, bf16[48,640]{1,0:T(8,128)(2,1)S(1)}, u32[]{:S(2)}, u32[]{:S(2)}) collective-permute-start(bf16[48,640]{1,0:T(8,128)(2,1)S(1)} %get-tuple-element.25.refs_1_), channel_id=1, source_target_pairs={{0,4},{1,5},{2,6},{3,7},{4,0},{5,1},{6,2},{7,3},{8,12},{9,13},{10,... | collective-permute-start | bytes 184328 | tf_op jit(solution)/shard_map/ppermute | solution.py:41
  15.5 6.4 %collective-permute-start.7 = (bf16[16,2560]{1,0:T(8,128)(2,1)S(1)}, bf16[16,2560]{1,0:T(8,128)(2,1)S(1)}, u32[]{:S(2)}, u32[]{:S(2)}) collective-permute-start(bf16[16,2560]{1,0:T(8,128)(2,1)S(1)} %get-tuple-element.48.refs_1_), channel_id=1, source_target_pairs={{0,4},{1,5},{2,6},{3,7},{4,0},{5,1},{6,2},{7,3},{8,12},{9,13},{10,... | collective-permute-start | bytes 245768 | tf_op jit(solution)/shard_map/ppermute | solution.py:41
  17.4 7.8 %collective-permute-start.8 = (bf16[16,2560]{1,0:T(8,128)(2,1)S(1)}, bf16[16,2560]{1,0:T(8,128)(2,1)S(1)}, u32[]{:S(2)}, u32[]{:S(2)}) collective-permute-start(bf16[16,2560]{1,0:T(8,128)(2,1)S(1)} %get-tuple-element.47.refs_2_), channel_id=1, source_target_pairs={{0,8},{1,9},{2,10},{3,11},{4,12},{5,13},{6,14},{7,15},{8,0},{9,1},... | collective-permute-start | bytes 245768 | tf_op jit(solution)/shard_map/ppermute | solution.py:41
  19.9 6.4 %collective-permute-start.9 = (bf16[16,2560]{1,0:T(8,128)(2,1)S(1)}, bf16[16,2560]{1,0:T(8,128)(2,1)S(1)}, u32[]{:S(2)}, u32[]{:S(2)}) collective-permute-start(bf16[16,2560]{1,0:T(8,128)(2,1)S(1)} %get-tuple-element.46.refs_3_), channel_id=1, source_target_pairs={{0,12},{1,13},{2,14},{3,15},{4,8},{5,9},{6,10},{7,11},{8,4},{9,5},... | collective-permute-start | bytes 245768 | tf_op jit(solution)/shard_map/ppermute | solution.py:41
  20.1 11.4 %collective-permute-start.6 = (bf16[192,640]{1,0:T(8,128)(2,1)S(1)}, bf16[192,640]{1,0:T(8,128)(2,1)S(1)}, u32[]{:S(2)}, u32[]{:S(2)}) collective-permute-start(bf16[192,640]{1,0:T(8,128)(2,1)S(1)} %pad_maximum_fusion.refs_0_), channel_id=1, source_target_pairs={{0,2},{1,3},{2,0},{3,1},{4,6},{5,7},{6,4},{7,5},{8,10},{9,11},{10,... | collective-permute-start | bytes 737288 | tf_op jit(solution)/shard_map/ppermute | solution.py:41
  21.9 15.3 %collective-permute-start.10 = (bf16[192,640]{1,0:T(8,128)(2,1)S(1)}, bf16[192,640]{1,0:T(8,128)(2,1)S(1)}, u32[]{:S(2)}, u32[]{:S(2)}) collective-permute-start(bf16[192,640]{1,0:T(8,128)(2,1)S(1)} %pad_maximum_fusion.refs_0_), channel_id=1, source_target_pairs={{0,1},{1,0},{2,3},{3,2},{4,5},{5,4},{6,7},{7,6},{8,9},{9,8},{10,11... | collective-permute-start | bytes 737288 | tf_op jit(solution)/shard_map/ppermute | solution.py:41
  27.0 4.6 %collective-permute-start.12 = (bf16[48,512]{1,0:T(8,128)(2,1)S(1)}, bf16[48,512]{1,0:T(8,128)(2,1)S(1)}, u32[]{:S(2)}, u32[]{:S(2)}) collective-permute-start(bf16[48,512]{1,0:T(8,128)(2,1)S(1)} %get-tuple-element.29.refs_1_), channel_id=1, source_target_pairs={{0,4},{1,5},{2,6},{3,7},{4,0},{5,1},{6,2},{7,3},{8,12},{9,13},{10,... | collective-permute-start | bytes 147464 | tf_op jit(solution)/shard_map/ppermute | solution.py:41
  28.2 5.7 %collective-permute-start.13 = (bf16[48,512]{1,0:T(8,128)(2,1)S(1)}, bf16[48,512]{1,0:T(8,128)(2,1)S(1)}, u32[]{:S(2)}, u32[]{:S(2)}) collective-permute-start(bf16[48,512]{1,0:T(8,128)(2,1)S(1)} %get-tuple-element.31), channel_id=1, source_target_pairs={{0,8},{1,9},{2,10},{3,11},{4,12},{5,13},{6,14},{7,15},{8,0},{9,1},... | collective-permute-start | bytes 147464 | tf_op jit(solution)/shard_map/ppermute | solution.py:41
  29.7 5.9 %collective-permute-start.14 = (bf16[48,512]{1,0:T(8,128)(2,1)S(1)}, bf16[48,512]{1,0:T(8,128)(2,1)S(1)}, u32[]{:S(2)}, u32[]{:S(2)}) collective-permute-start(bf16[48,512]{1,0:T(8,128)(2,1)S(1)} %get-tuple-element.32), channel_id=1, source_target_pairs={{0,12},{1,13},{2,14},{3,15},{4,8},{5,9},{6,10},{7,11},{8,4},{9,5},... | collective-permute-start | bytes 147464 | tf_op jit(solution)/shard_map/ppermute | solution.py:41
  31.5 5.7 %collective-permute-start.11 = (bf16[192,640]{1,0:T(8,128)(2,1)S(1)}, bf16[192,640]{1,0:T(8,128)(2,1)S(1)}, u32[]{:S(2)}, u32[]{:S(2)}) collective-permute-start(bf16[192,640]{1,0:T(8,128)(2,1)S(1)} %tie.12.refs_1_), channel_id=1, source_target_pairs={{0,1},{1,0},{2,3},{3,2},{4,5},{5,4},{6,7},{7,6},{8,9},{9,8},{10,11... | collective-permute-start | bytes 737288 | tf_op jit(solution)/shard_map/ppermute | solution.py:41
  35.6 13.8 %collective-permute-start.15 = (bf16[192,512]{1,0:T(8,128)(2,1)S(1)}, bf16[192,512]{1,0:T(8,128)(2,1)S(1)}, u32[]{:S(2)}, u32[]{:S(2)}) collective-permute-start(bf16[192,512]{1,0:T(8,128)(2,1)S(1)} %constant_dynamic-update-slice_fusion.refs_7_.refs_0_), channel_id=1, source_target_pairs={{0,2},{1,3},{2,0},{3,1},{4,6},{5,7},{6,4},{7,5},{8,10},{9,11},{10,... | collective-permute-start | bytes 589832 | tf_op jit(solution)/shard_map/ppermute | solution.py:41
  49.5 1.6 %collective-permute-start.17 = (bf16[192,640]{1,0:T(8,128)(2,1)S(1)}, bf16[192,640]{1,0:T(8,128)(2,1)S(1)}, u32[]{:S(2)}, u32[]{:S(2)}) collective-permute-start(bf16[192,640]{1,0:T(8,128)(2,1)S(1)} %tie.15), channel_id=1, source_target_pairs={{0,1},{1,0},{2,3},{3,2},{4,5},{5,4},{6,7},{7,6},{8,9},{9,8},{10,11... | collective-permute-start | bytes 737288 | tf_op jit(solution)/shard_map/ppermute | solution.py:41
  49.8 1.9 %collective-permute-start.19 = (bf16[192,512]{1,0:T(8,128)(2,1)S(1)}, bf16[192,512]{1,0:T(8,128)(2,1)S(1)}, u32[]{:S(2)}, u32[]{:S(2)}) collective-permute-start(bf16[192,512]{1,0:T(8,128)(2,1)S(1)} %constant_dynamic-update-slice_fusion.refs_7_.refs_0_), channel_id=1, source_target_pairs={{0,1},{1,0},{2,3},{3,2},{4,5},{5,4},{6,7},{7,6},{8,9},{9,8},{10,11... | collective-permute-start | bytes 589832 | tf_op jit(solution)/shard_map/ppermute | solution.py:41
  50.3 1.4 %collective-permute-start.20 = (bf16[192,512]{1,0:T(8,128)(2,1)S(1)}, bf16[192,512]{1,0:T(8,128)(2,1)S(1)}, u32[]{:S(2)}, u32[]{:S(2)}) collective-permute-start(bf16[192,512]{1,0:T(8,128)(2,1)S(1)} %tie.13.refs_1_), channel_id=1, source_target_pairs={{0,1},{1,0},{2,3},{3,2},{4,5},{5,4},{6,7},{7,6},{8,9},{9,8},{10,11... | collective-permute-start | bytes 589832 | tf_op jit(solution)/shard_map/ppermute | solution.py:41
  51.1 12.4 %collective-permute-start.18 = (bf16[192,640]{1,0:T(8,128)(2,1)S(1)}, bf16[192,640]{1,0:T(8,128)(2,1)S(1)}, u32[]{:S(2)}, u32[]{:S(2)}) collective-permute-start(bf16[192,640]{1,0:T(8,128)(2,1)S(1)} %add_convert_fusion.1.refs_7_), channel_id=1, source_target_pairs={{0,2},{1,3},{2,0},{3,1},{4,6},{5,7},{6,4},{7,5},{8,10},{9,11},{10,... | collective-permute-start | bytes 737288 | tf_op jit(solution)/shard_map/ppermute | solution.py:41
  63.5 1.5 %collective-permute-start.21 = (bf16[192,512]{1,0:T(8,128)(2,1)S(1)}, bf16[192,512]{1,0:T(8,128)(2,1)S(1)}, u32[]{:S(2)}, u32[]{:S(2)}) collective-permute-start(bf16[192,512]{1,0:T(8,128)(2,1)S(1)} %tie.17), channel_id=1, source_target_pairs={{0,1},{1,0},{2,3},{3,2},{4,5},{5,4},{6,7},{7,6},{8,9},{9,8},{10,11... | collective-permute-start | bytes 589832 | tf_op jit(solution)/shard_map/ppermute | solution.py:41
  63.9 2.7 %collective-permute-start.16 = (bf16[192,640]{1,0:T(8,128)(2,1)S(1)}, bf16[192,640]{1,0:T(8,128)(2,1)S(1)}, u32[]{:S(2)}, u32[]{:S(2)}) collective-permute-start(bf16[192,640]{1,0:T(8,128)(2,1)S(1)} %tie.14), channel_id=1, source_target_pairs={{0,1},{1,0},{2,3},{3,2},{4,5},{5,4},{6,7},{7,6},{8,9},{9,8},{10,11... | collective-permute-start | bytes 737288 | tf_op jit(solution)/shard_map/ppermute | solution.py:41
  64.2 7.0 %collective-permute-start.25 = (bf16[192,512]{1,0:T(8,128)(2,1)S(1)}, bf16[192,512]{1,0:T(8,128)(2,1)S(1)}, u32[]{:S(2)}, u32[]{:S(2)}) collective-permute-start(bf16[192,512]{1,0:T(8,128)(2,1)S(1)} %tie.19), channel_id=1, source_target_pairs={{0,1},{1,0},{2,3},{3,2},{4,5},{5,4},{6,7},{7,6},{8,9},{9,8},{10,11... | collective-permute-start | bytes 589832 | tf_op jit(solution)/shard_map/ppermute | solution.py:41
  65.1 7.2 %collective-permute-start.26 = (bf16[192,512]{1,0:T(8,128)(2,1)S(1)}, bf16[192,512]{1,0:T(8,128)(2,1)S(1)}, u32[]{:S(2)}, u32[]{:S(2)}) collective-permute-start(bf16[192,512]{1,0:T(8,128)(2,1)S(1)} %add_convert_fusion.3.refs_1_), channel_id=1, source_target_pairs={{0,2},{1,3},{2,0},{3,1},{4,6},{5,7},{6,4},{7,5},{8,10},{9,11},{10,... | collective-permute-start | bytes 589832 | tf_op jit(solution)/shard_map/ppermute | solution.py:41
  66.8 7.9 %collective-permute-start.22 = (bf16[48,640]{1,0:T(8,128)(2,1)S(1)}, bf16[48,640]{1,0:T(8,128)(2,1)S(1)}, u32[]{:S(2)}, u32[]{:S(2)}) collective-permute-start(bf16[48,640]{1,0:T(8,128)(2,1)S(1)} %get-tuple-element.51), channel_id=1, source_target_pairs={{0,4},{1,5},{2,6},{3,7},{4,0},{5,1},{6,2},{7,3},{8,12},{9,13},{10,... | collective-permute-start | bytes 184328 | tf_op jit(solution)/shard_map/ppermute | solution.py:41
  66.9 10.0 %collective-permute-start.23 = (bf16[48,640]{1,0:T(8,128)(2,1)S(1)}, bf16[48,640]{1,0:T(8,128)(2,1)S(1)}, u32[]{:S(2)}, u32[]{:S(2)}) collective-permute-start(bf16[48,640]{1,0:T(8,128)(2,1)S(1)} %get-tuple-element.50), channel_id=1, source_target_pairs={{0,8},{1,9},{2,10},{3,11},{4,12},{5,13},{6,14},{7,15},{8,0},{9,1},... | collective-permute-start | bytes 184328 | tf_op jit(solution)/shard_map/ppermute | solution.py:41
  69.1 7.8 %collective-permute-start.24 = (bf16[48,640]{1,0:T(8,128)(2,1)S(1)}, bf16[48,640]{1,0:T(8,128)(2,1)S(1)}, u32[]{:S(2)}, u32[]{:S(2)}) collective-permute-start(bf16[48,640]{1,0:T(8,128)(2,1)S(1)} %get-tuple-element.49), channel_id=1, source_target_pairs={{0,12},{1,13},{2,14},{3,15},{4,8},{5,9},{6,10},{7,11},{8,4},{9,5},... | collective-permute-start | bytes 184328 | tf_op jit(solution)/shard_map/ppermute | solution.py:41
  72.4 5.4 %collective-permute-start.27 = (bf16[48,512]{1,0:T(8,128)(2,1)S(1)}, bf16[48,512]{1,0:T(8,128)(2,1)S(1)}, u32[]{:S(2)}, u32[]{:S(2)}) collective-permute-start(bf16[48,512]{1,0:T(8,128)(2,1)S(1)} %get-tuple-element.55), channel_id=1, source_target_pairs={{0,4},{1,5},{2,6},{3,7},{4,0},{5,1},{6,2},{7,3},{8,12},{9,13},{10,... | collective-permute-start | bytes 147464 | tf_op jit(solution)/shard_map/ppermute | solution.py:41
  72.5 5.3 %collective-permute-start.28 = (bf16[48,512]{1,0:T(8,128)(2,1)S(1)}, bf16[48,512]{1,0:T(8,128)(2,1)S(1)}, u32[]{:S(2)}, u32[]{:S(2)}) collective-permute-start(bf16[48,512]{1,0:T(8,128)(2,1)S(1)} %get-tuple-element.54), channel_id=1, source_target_pairs={{0,8},{1,9},{2,10},{3,11},{4,12},{5,13},{6,14},{7,15},{8,0},{9,1},... | collective-permute-start | bytes 147464 | tf_op jit(solution)/shard_map/ppermute | solution.py:41
  74.7 5.9 %collective-permute-start.29 = (bf16[48,512]{1,0:T(8,128)(2,1)S(1)}, bf16[48,512]{1,0:T(8,128)(2,1)S(1)}, u32[]{:S(2)}, u32[]{:S(2)}) collective-permute-start(bf16[48,512]{1,0:T(8,128)(2,1)S(1)} %get-tuple-element.53), channel_id=1, source_target_pairs={{0,12},{1,13},{2,14},{3,15},{4,8},{5,9},{6,10},{7,11},{8,4},{9,5},... | collective-permute-start | bytes 147464 | tf_op jit(solution)/shard_map/ppermute | solution.py:41

commit v13 on v12

--- a/solution.py
+++ b/solution.py
@@ -9,6 +9,7 @@
 
 PLEN = 128
 HINT = 1 << 33
+STRIP = 512
 VMEM = pl.BlockSpec(memory_space=pltpu.VMEM)
 SMEM = pl.BlockSpec(memory_space=pltpu.SMEM)
 ANY = pl.BlockSpec(memory_space=pl.ANY)
@@ -210,8 +211,6 @@
 
 def cuts(units):
     edges = [0] + list(range(256, units - 255, 512)) + [units]
-    if edges[-1] - edges[-2] > 256 and len(edges) > 2:
-        edges.insert(-1, edges[-2] + 256)
     return list(zip(edges[:-1], edges[1:]))
 
 
@@ -269,14 +268,17 @@
                 total_ref[c, 0:rows, :] += term[:, c * 128 : (c + 1) * 128]
 
     features = gate_hbm.shape[1]
-    middle = features // 256 * 128
 
     def product(weight_ref, lo, hi):
-        return jnp.dot(
-            weight_ref[lo:hi, :middle], rows_ref[:middle, :], preferred_element_type=jnp.float32
-        ) + jnp.dot(
-            weight_ref[lo:hi, middle:], rows_ref[middle:, :], preferred_element_type=jnp.float32
-        )
+        terms = [
+            jnp.dot(
+                weight_ref[lo:hi, strip : strip + STRIP],
+                rows_ref[strip : strip + STRIP, :],
+                preferred_element_type=jnp.float32,
+            )
+            for strip in range(0, features, STRIP)
+        ]
+        return functools.reduce(jnp.add, terms)
 
     def gated(gate, up):
         return (gate * jax.nn.sigmoid(gate) * up).astype(jnp.bfloat16).T[0:rows]

time: 81.7 us -> 81.6 us (level)
  no operation moved by 1% of the time
where the time goes in v13:
time: 81.6 us; the launch traced here: 81.4 us
  starting transfers between devices  33 us (40%)
  Pallas kernels  27.8 us (34%)
  waiting for transfers between devices  16.7 us (20%)
  other arithmetic  1.93 us (2%)
  between operations  1.14 us (1%)
    ppermute x30, starting transfers between devices, swap(): return lax.ppermute(value, 'dev', moves)  33 us
    pallas_call x2, Pallas kernels, expert_rows(): pl.pallas_call(functools.partial(expert_kernel, packing, unit_cuts, len(a...  23.9 us
    ppermute x30, waiting for transfers between devices, swap(): return lax.ppermute(value, 'dev', moves)  16.7 us
    pallas_call x2, Pallas kernels, combine(): pl.pallas_call(functools.partial(combine_kernel, packing), out_shape=jax....  1.77 us
  transfers between devices with their start and end apart: 30, of which 11 were waited for; matrix products, arithmetic and copies ran while one was open for 1% of the time, Pallas kernels for 33%

profile of v13, /device:TPU:0, one launch (start us, length us, event | category | flops | bytes accessed | tf_op | source)
XLA Modules:
  0.0 81.4 jit_solution(15225555167285992981)
XLA Ops:
  0.6 0.0 copy-start
  0.7 1.1 %fusion.5 = bf16[2,2,2,2,16,256]{5,4,3,2,1,0:T(8,128)(2,1)S(1)} fusion(s32[]{:T(128)S(6)} %select_n.80, bf16[2,2,2,2,16,256]{5,4,3,2,1,0:T(8,128)(2,1)} %bitcast.29), kind=kLoop, calls=%fused_computation.21 | loop fusion | flops 65536 | bytes 262148 | tf_op jit(solution)/shard_map/jit(_roll_dynamic)/concatenate | solution.py:391
  1.8 0.1 fusion.3
  1.9 0.1 fusion.2
  2.0 0.0 copy-start.7
  2.0 0.0 copy-start.5
  2.1 0.0 copy-start.6
  2.1 0.0 copy-start.4
  2.1 0.3 convolution_convert_fusion
  2.5 0.5 collective-permute-start
  3.0 0.1 collective-permute-start.1
  3.1 0.1 fusion.7
  3.3 0.3 fusion.16
  3.7 0.6 collective-permute-done
  4.3 0.1 fusion.1.refs_0_
  4.3 3.0 %collective-permute-start.2 = (bf16[64,2560]{1,0:T(8,128)(2,1)S(1)}, bf16[64,2560]{1,0:T(8,128)(2,1)S(1)}, u32[]{:S(2)}, u32[]{:S(2)}) collective-permute-start(bf16[64,2560]{1,0:T(8,128)(2,1)S(1)} %fusion.1.refs_0_), channel_id=1, source_target_pairs={{0,2},{1,3},{2,0},{3,1},{4,6},{5,7},{6,4},{7,5},{8,10},{9,11},{10,... | collective-permute-start | bytes 983048 | tf_op jit(solution)/shard_map/ppermute | solution.py:42
  7.3 0.8 %prepare.1 = (f32[16,4]{1,0:T(8,128)S(1)}, f32[16,4]{1,0:T(8,128)S(1)}, bf16[16,2560]{1,0:T(8,128)(2,1)S(1)}, bf16[48,640]{1,0:T(8,128)(2,1)S(1)}, bf16[48,640]{...) custom-call(s32[4,16]{1,0:T(4,128)S(1)} %pad_add_fusion.ids_ref, ...), custom_call_target="tpu_custom_call" | custom-call | tf_op jit(solution)/shard_map/prepare/pallas_call | solution.py:124
  8.2 3.6 %collective-permute-start.5 = (bf16[48,640]{1,0:T(8,128)(2,1)S(1)}, bf16[48,640]{1,0:T(8,128)(2,1)S(1)}, u32[]{:S(2)}, u32[]{:S(2)}) collective-permute-start(bf16[48,640]{1,0:T(8,128)(2,1)S(1)} %get-tuple-element.27), channel_id=1, source_target_pairs={{0,12},{1,13},{2,14},{3,15},{4,8},{5,9},{6,10},{7,11},{8,4},{9,5},... | collective-permute-start | bytes 184328 | tf_op jit(solution)/shard_map/ppermute | solution.py:42
  11.8 0.8 collective-permute-start.3
  12.6 0.3 route.2.refs_8_.weight_ref
  12.9 2.4 %collective-permute-done.2.refs_0_ = bf16[64,2560]{1,0:T(8,128)(2,1)S(1)} collective-permute-done((bf16[64,2560]{1,0:T(8,128)(2,1)S(1)}, bf16[64,2560]{1,0:T(8,128)(2,1)S(1)}, u32[]{:S(2)}, u32[]{:S(2)}) %collective-permute-start.2) | collective-permute-done | bytes 327712 | tf_op jit(solution)/shard_map/ppermute | solution.py:42
  15.3 0.1 fusion.9
  15.5 1.9 %collective-permute-start.7 = (bf16[16,2560]{1,0:T(8,128)(2,1)S(1)}, bf16[16,2560]{1,0:T(8,128)(2,1)S(1)}, u32[]{:S(2)}, u32[]{:S(2)}) collective-permute-start(bf16[16,2560]{1,0:T(8,128)(2,1)S(1)} %get-tuple-element.48.refs_1_), channel_id=1, source_target_pairs={{0,4},{1,5},{2,6},{3,7},{4,0},{5,1},{6,2},{7,3},{8,12},{9,13},{10,... | collective-permute-start | bytes 245768 | tf_op jit(solution)/shard_map/ppermute | solution.py:42
  17.4 2.5 %collective-permute-start.8 = (bf16[16,2560]{1,0:T(8,128)(2,1)S(1)}, bf16[16,2560]{1,0:T(8,128)(2,1)S(1)}, u32[]{:S(2)}, u32[]{:S(2)}) collective-permute-start(bf16[16,2560]{1,0:T(8,128)(2,1)S(1)} %get-tuple-element.47.refs_2_), channel_id=1, source_target_pairs={{0,8},{1,9},{2,10},{3,11},{4,12},{5,13},{6,14},{7,15},{8,0},{9,1},... | collective-permute-start | bytes 245768 | tf_op jit(solution)/shard_map/ppermute | solution.py:42
  19.9 0.1 collective-permute-start.9
  20.1 1.8 %collective-permute-start.6 = (bf16[192,640]{1,0:T(8,128)(2,1)S(1)}, bf16[192,640]{1,0:T(8,128)(2,1)S(1)}, u32[]{:S(2)}, u32[]{:S(2)}) collective-permute-start(bf16[192,640]{1,0:T(8,128)(2,1)S(1)} %pad_maximum_fusion.refs_0_), channel_id=1, source_target_pairs={{0,2},{1,3},{2,0},{3,1},{4,6},{5,7},{6,4},{7,5},{8,10},{9,11},{10,... | collective-permute-start | bytes 737288 | tf_op jit(solution)/shard_map/ppermute | solution.py:42
  21.9 3.3 %collective-permute-done.8.refs_2_ = bf16[16,2560]{1,0:T(8,128)(2,1)S(1)} collective-permute-done((bf16[16,2560]{1,0:T(8,128)(2,1)S(1)}, bf16[16,2560]{1,0:T(8,128)(2,1)S(1)}, u32[]{:S(2)}, u32[]{:S(2)}) %collective-permute-start.8) | collective-permute-done | bytes 81952 | tf_op jit(solution)/shard_map/ppermute | solution.py:42
  25.1 1.2 %collective-permute-done.9.refs_3_ = bf16[16,2560]{1,0:T(8,128)(2,1)S(1)} collective-permute-done((bf16[16,2560]{1,0:T(8,128)(2,1)S(1)}, bf16[16,2560]{1,0:T(8,128)(2,1)S(1)}, u32[]{:S(2)}, u32[]{:S(2)}) %collective-permute-start.9) | collective-permute-done | bytes 81952 | tf_op jit(solution)/shard_map/ppermute | solution.py:42
  26.3 0.6 modulate.1
  27.0 1.2 %collective-permute-start.12 = (bf16[48,512]{1,0:T(8,128)(2,1)S(1)}, bf16[48,512]{1,0:T(8,128)(2,1)S(1)}, u32[]{:S(2)}, u32[]{:S(2)}) collective-permute-start(bf16[48,512]{1,0:T(8,128)(2,1)S(1)} %get-tuple-element.29.refs_1_), channel_id=1, source_target_pairs={{0,4},{1,5},{2,6},{3,7},{4,0},{5,1},{6,2},{7,3},{8,12},{9,13},{10,... | collective-permute-start | bytes 147464 | tf_op jit(solution)/shard_map/ppermute | solution.py:42
  28.2 1.6 %collective-permute-start.13 = (bf16[48,512]{1,0:T(8,128)(2,1)S(1)}, bf16[48,512]{1,0:T(8,128)(2,1)S(1)}, u32[]{:S(2)}, u32[]{:S(2)}) collective-permute-start(bf16[48,512]{1,0:T(8,128)(2,1)S(1)} %get-tuple-element.31), channel_id=1, source_target_pairs={{0,8},{1,9},{2,10},{3,11},{4,12},{5,13},{6,14},{7,15},{8,0},{9,1},... | collective-permute-start | bytes 147464 | tf_op jit(solution)/shard_map/ppermute | solution.py:42
  29.7 1.7 %collective-permute-start.14 = (bf16[48,512]{1,0:T(8,128)(2,1)S(1)}, bf16[48,512]{1,0:T(8,128)(2,1)S(1)}, u32[]{:S(2)}, u32[]{:S(2)}) collective-permute-start(bf16[48,512]{1,0:T(8,128)(2,1)S(1)} %get-tuple-element.32), channel_id=1, source_target_pairs={{0,12},{1,13},{2,14},{3,15},{4,8},{5,9},{6,10},{7,11},{8,4},{9,5},... | collective-permute-start | bytes 147464 | tf_op jit(solution)/shard_map/ppermute | solution.py:42
  31.5 0.1 collective-permute-start.11
  31.6 2.4 %collective-permute-done.13 = bf16[48,512]{1,0:T(8,128)(2,1)S(1)} collective-permute-done((bf16[48,512]{1,0:T(8,128)(2,1)S(1)}, bf16[48,512]{1,0:T(8,128)(2,1)S(1)}, u32[]{:S(2)}, u32[]{:S(2)}) %collective-permute-start.13) | collective-permute-done | bytes 49184 | tf_op jit(solution)/shard_map/ppermute | solution.py:42
  33.9 1.7 %collective-permute-done.14 = bf16[48,512]{1,0:T(8,128)(2,1)S(1)} collective-permute-done((bf16[48,512]{1,0:T(8,128)(2,1)S(1)}, bf16[48,512]{1,0:T(8,128)(2,1)S(1)}, u32[]{:S(2)}, u32[]{:S(2)}) %collective-permute-start.14) | collective-permute-done | bytes 49184 | tf_op jit(solution)/shard_map/ppermute | solution.py:42
  35.6 1.5 %collective-permute-start.15 = (bf16[192,512]{1,0:T(8,128)(2,1)S(1)}, bf16[192,512]{1,0:T(8,128)(2,1)S(1)}, u32[]{:S(2)}, u32[]{:S(2)}) collective-permute-start(bf16[192,512]{1,0:T(8,128)(2,1)S(1)} %constant_dynamic-update-slice_fusion.refs_7_.refs_0_), channel_id=1, source_target_pairs={{0,2},{1,3},{2,0},{3,1},{4,6},{5,7},{6,4},{7,5},{8,10},{9,11},{10,... | collective-permute-start | bytes 589832 | tf_op jit(solution)/shard_map/ppermute | solution.py:42
  37.2 12.1 %experts.2 = (bf16[192,640]{1,0:T(8,128)(2,1)S(1)}, bf16[192,640]{1,0:T(8,128)(2,1)S(1)}, bf16[192,640]{1,0:T(8,128)(2,1)S(1)}, bf16[192,640]{1,0:T(8,128)(2,1)S(1)}) custom-call(bf16[192,640]{1,0:T(8,128)(2,1)S(1)} %pad_maximum_fusion.refs_0_, bf16[192,640]{1,0:T(8,128)(2,1)S(1)} %tie.12.refs_1_, bf16[192,640]{1,0:T(8,128)(2,1)S(1)} %collective-permute-done.10.refs_2_, ...), custom_call_target="tpu_custom_call" | custom-call | flops 5096079360 | bytes 26542080 | tf_op jit(solution)/shard_map/experts/pallas_call | solution.py:322
  49.4 0.1 collective-permute-start.17
  49.4 0.3 route.3.refs_8_.weight_ref
  49.7 0.5 collective-permute-start.19
  50.2 0.1 collective-permute-start.20
  50.3 0.6 collective-permute-done.17
  50.9 0.1 add_convert_fusion.1.refs_7_
  51.0 0.6 collective-permute-start.18
  51.6 0.1 collective-permute-done.20.refs_3_
  51.7 11.7 %experts.3 = (bf16[192,512]{1,0:T(8,128)(2,1)S(1)}, bf16[192,512]{1,0:T(8,128)(2,1)S(1)}, bf16[192,512]{1,0:T(8,128)(2,1)S(1)}, bf16[192,512]{1,0:T(8,128)(2,1)S(1)}) custom-call(bf16[192,512]{1,0:T(8,128)(2,1)S(1)} %constant_dynamic-update-slice_fusion.refs_7_.refs_0_, bf16[192,512]{1,0:T(8,128)(2,1)S(1)} %tie.13.refs_1_, ...), custom_call_target="tpu_custom_call" | custom-call | flops 3822059520 | bytes 26542080 | tf_op jit(solution)/shard_map/experts/pallas_call | solution.py:322
  63.5 0.3 collective-permute-start.21
  63.8 0.3 collective-permute-start.16
  64.2 0.3 collective-permute-start.25
  64.5 0.5 collective-permute-done.21
  65.0 0.1 add_convert_fusion.3.refs_1_
  65.1 1.5 %collective-permute-start.26 = (bf16[192,512]{1,0:T(8,128)(2,1)S(1)}, bf16[192,512]{1,0:T(8,128)(2,1)S(1)}, u32[]{:S(2)}, u32[]{:S(2)}) collective-permute-start(bf16[192,512]{1,0:T(8,128)(2,1)S(1)} %add_convert_fusion.3.refs_1_), channel_id=1, source_target_pairs={{0,2},{1,3},{2,0},{3,1},{4,6},{5,7},{6,4},{7,5},{8,10},{9,11},{10,... | collective-permute-start | bytes 589832 | tf_op jit(solution)/shard_map/ppermute | solution.py:42
  66.6 0.1 add_convert_fusion
  66.7 0.1 collective-permute-start.22
  66.8 2.2 %collective-permute-start.23 = (bf16[48,640]{1,0:T(8,128)(2,1)S(1)}, bf16[48,640]{1,0:T(8,128)(2,1)S(1)}, u32[]{:S(2)}, u32[]{:S(2)}) collective-permute-start(bf16[48,640]{1,0:T(8,128)(2,1)S(1)} %get-tuple-element.50), channel_id=1, source_target_pairs={{0,8},{1,9},{2,10},{3,11},{4,12},{5,13},{6,14},{7,15},{8,0},{9,1},... | collective-permute-start | bytes 184328 | tf_op jit(solution)/shard_map/ppermute | solution.py:42
  69.0 2.1 %collective-permute-start.24 = (bf16[48,640]{1,0:T(8,128)(2,1)S(1)}, bf16[48,640]{1,0:T(8,128)(2,1)S(1)}, u32[]{:S(2)}, u32[]{:S(2)}) collective-permute-start(bf16[48,640]{1,0:T(8,128)(2,1)S(1)} %get-tuple-element.49), channel_id=1, source_target_pairs={{0,12},{1,13},{2,14},{3,15},{4,8},{5,9},{6,10},{7,11},{8,4},{9,5},... | collective-permute-start | bytes 184328 | tf_op jit(solution)/shard_map/ppermute | solution.py:42
  71.2 1.0 %collective-permute-done.26 = bf16[192,512]{1,0:T(8,128)(2,1)S(1)} collective-permute-done((bf16[192,512]{1,0:T(8,128)(2,1)S(1)}, bf16[192,512]{1,0:T(8,128)(2,1)S(1)}, u32[]{:S(2)}, u32[]{:S(2)}) %collective-permute-start.26) | collective-permute-done | bytes 196640 | tf_op jit(solution)/shard_map/ppermute | solution.py:42
  72.2 0.1 add_convert_fusion.2
  72.3 0.1 collective-permute-start.27
  72.4 2.3 %collective-permute-start.28 = (bf16[48,512]{1,0:T(8,128)(2,1)S(1)}, bf16[48,512]{1,0:T(8,128)(2,1)S(1)}, u32[]{:S(2)}, u32[]{:S(2)}) collective-permute-start(bf16[48,512]{1,0:T(8,128)(2,1)S(1)} %get-tuple-element.54), channel_id=1, source_target_pairs={{0,8},{1,9},{2,10},{3,11},{4,12},{5,13},{6,14},{7,15},{8,0},{9,1},... | collective-permute-start | bytes 147464 | tf_op jit(solution)/shard_map/ppermute | solution.py:42
  74.7 2.1 %collective-permute-start.29 = (bf16[48,512]{1,0:T(8,128)(2,1)S(1)}, bf16[48,512]{1,0:T(8,128)(2,1)S(1)}, u32[]{:S(2)}, u32[]{:S(2)}) collective-permute-start(bf16[48,512]{1,0:T(8,128)(2,1)S(1)} %get-tuple-element.53), channel_id=1, source_target_pairs={{0,12},{1,13},{2,14},{3,15},{4,8},{5,9},{6,10},{7,11},{8,4},{9,5},... | collective-permute-start | bytes 147464 | tf_op jit(solution)/shard_map/ppermute | solution.py:42
  76.8 0.9 %combine.2 = bf16[16,2560]{1,0:T(8,128)(2,1)} custom-call(f32[16,4]{1,0:T(8,128)S(1)} %get-tuple-element.22.spot_ref, f32[16,2]{1,0:T(8,128)S(1)} %route.2.refs_8_.weight_ref, bf16[48,640]{1,0:T(8,128)(2,1)S(1)} %get-tuple-element.52.refs_0_, bf16[48,640]{1,0:T(8,128)(2,1)S(1)} %collective-permute-done.22.refs_1_, ...), custom_call_target="tpu_custom_call" | custom-call | tf_op jit(solution)/shard_map/combine/pallas_call | solution.py:375
  77.7 2.9 %collective-permute-done.29.refs_3_ = bf16[48,512]{1,0:T(8,128)(2,1)S(1)} collective-permute-done((bf16[48,512]{1,0:T(8,128)(2,1)S(1)}, bf16[48,512]{1,0:T(8,128)(2,1)S(1)}, u32[]{:S(2)}, u32[]{:S(2)}) %collective-permute-start.29) | collective-permute-done | bytes 49184 | tf_op jit(solution)/shard_map/ppermute | solution.py:42
  80.6 0.9 %combine.3 = bf16[16,2560]{1,0:T(8,128)(2,1)} custom-call(f32[16,4]{1,0:T(8,128)S(1)} %get-tuple-element.28.spot_ref, f32[16,2]{1,0:T(8,128)S(1)} %route.3.refs_8_.weight_ref, bf16[48,512]{1,0:T(8,128)(2,1)S(1)} %get-tuple-element.56.refs_0_, bf16[48,512]{1,0:T(8,128)(2,1)S(1)} %collective-permute-done.27.refs_1_, ...), custom_call_target="tpu_custom_call" | custom-call | tf_op jit(solution)/shard_map/combine/pallas_call | solution.py:375
  (61 shorter events, 0.5 us)
Async XLA Ops:
  0.6 1.4 %copy-start = (bf16[256,2560]{1,0:T(8,128)(2,1)S(1)}, bf16[256,2560]{1,0:T(8,128)(2,1)}, u32[]{:S(2)}) copy-start(bf16[256,2560]{1,0:T(8,128)(2,1)} %param.14) | copy-start | bytes 3932164
  2.0 1.1 %copy-start.7 = (s32[2]{0:T(128)S(1)}, s32[2]{0:T(128)}, u32[]{:S(2)}) copy-start(s32[2]{0:T(128)} %param.20) | copy-start | bytes 28
  2.0 1.2 %copy-start.5 = (s32[16,2]{0,1:T(2,128)S(1)}, s32[16,2]{0,1:T(2,128)}, u32[]{:S(2)}) copy-start(s32[16,2]{0,1:T(2,128)} %param.19) | copy-start | bytes 388
  2.1 1.2 %copy-start.6 = (s32[16,2]{0,1:T(2,128)S(1)}, s32[16,2]{0,1:T(2,128)}, u32[]{:S(2)}) copy-start(s32[16,2]{0,1:T(2,128)} %param.18) | copy-start | bytes 388
  2.1 1.2 %copy-start.3 = (f32[2560]{0:T(1024)S(1)}, f32[2560]{0:T(1024)}, u32[]{:S(2)}) copy-start(f32[2560]{0:T(1024)} %param.16) | copy-start | bytes 30724
  2.1 1.2 %copy-start.4 = (f32[2560]{0:T(1024)S(1)}, f32[2560]{0:T(1024)}, u32[]{:S(2)}) copy-start(f32[2560]{0:T(1024)} %param.15) | copy-start | bytes 30724
  2.5 1.8 %collective-permute-start = (bf16[64,2560]{1,0:T(8,128)(2,1)S(1)}, bf16[64,2560]{1,0:T(8,128)(2,1)S(1)}, u32[]{:S(2)}, u32[]{:S(2)}) collective-permute-start(bf16[64,2560]{1,0:T(8,128)(2,1)S(1)} %get-tuple-element.45), channel_id=1, source_target_pairs={{0,1},{1,0},{2,3},{3,2},{4,5},{5,4},{6,7},{7,6},{8,9},{9,8},{10,11... | collective-permute-start | bytes 983048 | tf_op jit(solution)/shard_map/ppermute | solution.py:42
  3.0 12.3 %collective-permute-start.1 = (bf16[64,2560]{1,0:T(8,128)(2,1)S(1)}, bf16[64,2560]{1,0:T(8,128)(2,1)S(1)}, u32[]{:S(2)}, u32[]{:S(2)}) collective-permute-start(bf16[64,2560]{1,0:T(8,128)(2,1)S(1)} %get-tuple-element.44), channel_id=1, source_target_pairs={{0,1},{1,0},{2,3},{3,2},{4,5},{5,4},{6,7},{7,6},{8,9},{9,8},{10,11... | collective-permute-start | bytes 983048 | tf_op jit(solution)/shard_map/ppermute | solution.py:42
  3.7 3.6 %copy-start.2 = (f32[2560,4]{0,1:T(4,128)S(1)}, f32[2560,4]{0,1:T(4,128)}, u32[]{:S(2)}) copy-start(f32[2560,4]{0,1:T(4,128)} %param.17) | copy-start | bytes 122884
  3.7 3.7 %copy-start.1 = (bf16[16,2560]{1,0:T(8,128)(2,1)S(1)}, bf16[16,2560]{1,0:T(8,128)(2,1)}, u32[]{:S(2)}) copy-start(bf16[16,2560]{1,0:T(8,128)(2,1)} %image_ref.1) | copy-start | bytes 245764
  4.3 11.0 %collective-permute-start.2 = (bf16[64,2560]{1,0:T(8,128)(2,1)S(1)}, bf16[64,2560]{1,0:T(8,128)(2,1)S(1)}, u32[]{:S(2)}, u32[]{:S(2)}) collective-permute-start(bf16[64,2560]{1,0:T(8,128)(2,1)S(1)} %fusion.1.refs_0_), channel_id=1, source_target_pairs={{0,2},{1,3},{2,0},{3,1},{4,6},{5,7},{6,4},{7,5},{8,10},{9,11},{10,... | collective-permute-start | bytes 983048 | tf_op jit(solution)/shard_map/ppermute | solution.py:42
  8.2 11.7 %collective-permute-start.5 = (bf16[48,640]{1,0:T(8,128)(2,1)S(1)}, bf16[48,640]{1,0:T(8,128)(2,1)S(1)}, u32[]{:S(2)}, u32[]{:S(2)}) collective-permute-start(bf16[48,640]{1,0:T(8,128)(2,1)S(1)} %get-tuple-element.27), channel_id=1, source_target_pairs={{0,12},{1,13},{2,14},{3,15},{4,8},{5,9},{6,10},{7,11},{8,4},{9,5},... | collective-permute-start | bytes 184328 | tf_op jit(solution)/shard_map/ppermute | solution.py:42
  11.8 8.2 %collective-permute-start.4 = (bf16[48,640]{1,0:T(8,128)(2,1)S(1)}, bf16[48,640]{1,0:T(8,128)(2,1)S(1)}, u32[]{:S(2)}, u32[]{:S(2)}) collective-permute-start(bf16[48,640]{1,0:T(8,128)(2,1)S(1)} %get-tuple-element.26), channel_id=1, source_target_pairs={{0,8},{1,9},{2,10},{3,11},{4,12},{5,13},{6,14},{7,15},{8,0},{9,1},... | collective-permute-start | bytes 184328 | tf_op jit(solution)/shard_map/ppermute | solution.py:42
  11.8 8.2 %collective-permute-start.3 = (bf16[48,640]{1,0:T(8,128)(2,1)S(1)}, bf16[48,640]{1,0:T(8,128)(2,1)S(1)}, u32[]{:S(2)}, u32[]{:S(2)}) collective-permute-start(bf16[48,640]{1,0:T(8,128)(2,1)S(1)} %get-tuple-element.25.refs_1_), channel_id=1, source_target_pairs={{0,4},{1,5},{2,6},{3,7},{4,0},{5,1},{6,2},{7,3},{8,12},{9,13},{10,... | collective-permute-start | bytes 184328 | tf_op jit(solution)/shard_map/ppermute | solution.py:42
  15.5 6.4 %collective-permute-start.7 = (bf16[16,2560]{1,0:T(8,128)(2,1)S(1)}, bf16[16,2560]{1,0:T(8,128)(2,1)S(1)}, u32[]{:S(2)}, u32[]{:S(2)}) collective-permute-start(bf16[16,2560]{1,0:T(8,128)(2,1)S(1)} %get-tuple-element.48.refs_1_), channel_id=1, source_target_pairs={{0,4},{1,5},{2,6},{3,7},{4,0},{5,1},{6,2},{7,3},{8,12},{9,13},{10,... | collective-permute-start | bytes 245768 | tf_op jit(solution)/shard_map/ppermute | solution.py:42
  17.4 7.8 %collective-permute-start.8 = (bf16[16,2560]{1,0:T(8,128)(2,1)S(1)}, bf16[16,2560]{1,0:T(8,128)(2,1)S(1)}, u32[]{:S(2)}, u32[]{:S(2)}) collective-permute-start(bf16[16,2560]{1,0:T(8,128)(2,1)S(1)} %get-tuple-element.47.refs_2_), channel_id=1, source_target_pairs={{0,8},{1,9},{2,10},{3,11},{4,12},{5,13},{6,14},{7,15},{8,0},{9,1},... | collective-permute-start | bytes 245768 | tf_op jit(solution)/shard_map/ppermute | solution.py:42
  19.9 6.4 %collective-permute-start.9 = (bf16[16,2560]{1,0:T(8,128)(2,1)S(1)}, bf16[16,2560]{1,0:T(8,128)(2,1)S(1)}, u32[]{:S(2)}, u32[]{:S(2)}) collective-permute-start(bf16[16,2560]{1,0:T(8,128)(2,1)S(1)} %get-tuple-element.46.refs_3_), channel_id=1, source_target_pairs={{0,12},{1,13},{2,14},{3,15},{4,8},{5,9},{6,10},{7,11},{8,4},{9,5},... | collective-permute-start | bytes 245768 | tf_op jit(solution)/shard_map/ppermute | solution.py:42
  20.1 11.4 %collective-permute-start.6 = (bf16[192,640]{1,0:T(8,128)(2,1)S(1)}, bf16[192,640]{1,0:T(8,128)(2,1)S(1)}, u32[]{:S(2)}, u32[]{:S(2)}) collective-permute-start(bf16[192,640]{1,0:T(8,128)(2,1)S(1)} %pad_maximum_fusion.refs_0_), channel_id=1, source_target_pairs={{0,2},{1,3},{2,0},{3,1},{4,6},{5,7},{6,4},{7,5},{8,10},{9,11},{10,... | collective-permute-start | bytes 737288 | tf_op jit(solution)/shard_map/ppermute | solution.py:42
  21.9 15.3 %collective-permute-start.10 = (bf16[192,640]{1,0:T(8,128)(2,1)S(1)}, bf16[192,640]{1,0:T(8,128)(2,1)S(1)}, u32[]{:S(2)}, u32[]{:S(2)}) collective-permute-start(bf16[192,640]{1,0:T(8,128)(2,1)S(1)} %pad_maximum_fusion.refs_0_), channel_id=1, source_target_pairs={{0,1},{1,0},{2,3},{3,2},{4,5},{5,4},{6,7},{7,6},{8,9},{9,8},{10,11... | collective-permute-start | bytes 737288 | tf_op jit(solution)/shard_map/ppermute | solution.py:42
  27.0 4.6 %collective-permute-start.12 = (bf16[48,512]{1,0:T(8,128)(2,1)S(1)}, bf16[48,512]{1,0:T(8,128)(2,1)S(1)}, u32[]{:S(2)}, u32[]{:S(2)}) collective-permute-start(bf16[48,512]{1,0:T(8,128)(2,1)S(1)} %get-tuple-element.29.refs_1_), channel_id=1, source_target_pairs={{0,4},{1,5},{2,6},{3,7},{4,0},{5,1},{6,2},{7,3},{8,12},{9,13},{10,... | collective-permute-start | bytes 147464 | tf_op jit(solution)/shard_map/ppermute | solution.py:42
  28.2 5.7 %collective-permute-start.13 = (bf16[48,512]{1,0:T(8,128)(2,1)S(1)}, bf16[48,512]{1,0:T(8,128)(2,1)S(1)}, u32[]{:S(2)}, u32[]{:S(2)}) collective-permute-start(bf16[48,512]{1,0:T(8,128)(2,1)S(1)} %get-tuple-element.31), channel_id=1, source_target_pairs={{0,8},{1,9},{2,10},{3,11},{4,12},{5,13},{6,14},{7,15},{8,0},{9,1},... | collective-permute-start | bytes 147464 | tf_op jit(solution)/shard_map/ppermute | solution.py:42
  29.7 5.9 %collective-permute-start.14 = (bf16[48,512]{1,0:T(8,128)(2,1)S(1)}, bf16[48,512]{1,0:T(8,128)(2,1)S(1)}, u32[]{:S(2)}, u32[]{:S(2)}) collective-permute-start(bf16[48,512]{1,0:T(8,128)(2,1)S(1)} %get-tuple-element.32), channel_id=1, source_target_pairs={{0,12},{1,13},{2,14},{3,15},{4,8},{5,9},{6,10},{7,11},{8,4},{9,5},... | collective-permute-start | bytes 147464 | tf_op jit(solution)/shard_map/ppermute | solution.py:42
  31.5 5.7 %collective-permute-start.11 = (bf16[192,640]{1,0:T(8,128)(2,1)S(1)}, bf16[192,640]{1,0:T(8,128)(2,1)S(1)}, u32[]{:S(2)}, u32[]{:S(2)}) collective-permute-start(bf16[192,640]{1,0:T(8,128)(2,1)S(1)} %tie.12.refs_1_), channel_id=1, source_target_pairs={{0,1},{1,0},{2,3},{3,2},{4,5},{5,4},{6,7},{7,6},{8,9},{9,8},{10,11... | collective-permute-start | bytes 737288 | tf_op jit(solution)/shard_map/ppermute | solution.py:42
  35.6 13.7 %collective-permute-start.15 = (bf16[192,512]{1,0:T(8,128)(2,1)S(1)}, bf16[192,512]{1,0:T(8,128)(2,1)S(1)}, u32[]{:S(2)}, u32[]{:S(2)}) collective-permute-start(bf16[192,512]{1,0:T(8,128)(2,1)S(1)} %constant_dynamic-update-slice_fusion.refs_7_.refs_0_), channel_id=1, source_target_pairs={{0,2},{1,3},{2,0},{3,1},{4,6},{5,7},{6,4},{7,5},{8,10},{9,11},{10,... | collective-permute-start | bytes 589832 | tf_op jit(solution)/shard_map/ppermute | solution.py:42
  49.4 1.6 %collective-permute-start.17 = (bf16[192,640]{1,0:T(8,128)(2,1)S(1)}, bf16[192,640]{1,0:T(8,128)(2,1)S(1)}, u32[]{:S(2)}, u32[]{:S(2)}) collective-permute-start(bf16[192,640]{1,0:T(8,128)(2,1)S(1)} %tie.15), channel_id=1, source_target_pairs={{0,1},{1,0},{2,3},{3,2},{4,5},{5,4},{6,7},{7,6},{8,9},{9,8},{10,11... | collective-permute-start | bytes 737288 | tf_op jit(solution)/shard_map/ppermute | solution.py:42
  49.7 1.9 %collective-permute-start.19 = (bf16[192,512]{1,0:T(8,128)(2,1)S(1)}, bf16[192,512]{1,0:T(8,128)(2,1)S(1)}, u32[]{:S(2)}, u32[]{:S(2)}) collective-permute-start(bf16[192,512]{1,0:T(8,128)(2,1)S(1)} %constant_dynamic-update-slice_fusion.refs_7_.refs_0_), channel_id=1, source_target_pairs={{0,1},{1,0},{2,3},{3,2},{4,5},{5,4},{6,7},{7,6},{8,9},{9,8},{10,11... | collective-permute-start | bytes 589832 | tf_op jit(solution)/shard_map/ppermute | solution.py:42
  50.2 1.4 %collective-permute-start.20 = (bf16[192,512]{1,0:T(8,128)(2,1)S(1)}, bf16[192,512]{1,0:T(8,128)(2,1)S(1)}, u32[]{:S(2)}, u32[]{:S(2)}) collective-permute-start(bf16[192,512]{1,0:T(8,128)(2,1)S(1)} %tie.13.refs_1_), channel_id=1, source_target_pairs={{0,1},{1,0},{2,3},{3,2},{4,5},{5,4},{6,7},{7,6},{8,9},{9,8},{10,11... | collective-permute-start | bytes 589832 | tf_op jit(solution)/shard_map/ppermute | solution.py:42
  51.0 12.4 %collective-permute-start.18 = (bf16[192,640]{1,0:T(8,128)(2,1)S(1)}, bf16[192,640]{1,0:T(8,128)(2,1)S(1)}, u32[]{:S(2)}, u32[]{:S(2)}) collective-permute-start(bf16[192,640]{1,0:T(8,128)(2,1)S(1)} %add_convert_fusion.1.refs_7_), channel_id=1, source_target_pairs={{0,2},{1,3},{2,0},{3,1},{4,6},{5,7},{6,4},{7,5},{8,10},{9,11},{10,... | collective-permute-start | bytes 737288 | tf_op jit(solution)/shard_map/ppermute | solution.py:42
  63.5 1.5 %collective-permute-start.21 = (bf16[192,512]{1,0:T(8,128)(2,1)S(1)}, bf16[192,512]{1,0:T(8,128)(2,1)S(1)}, u32[]{:S(2)}, u32[]{:S(2)}) collective-permute-start(bf16[192,512]{1,0:T(8,128)(2,1)S(1)} %tie.17), channel_id=1, source_target_pairs={{0,1},{1,0},{2,3},{3,2},{4,5},{5,4},{6,7},{7,6},{8,9},{9,8},{10,11... | collective-permute-start | bytes 589832 | tf_op jit(solution)/shard_map/ppermute | solution.py:42
  63.8 2.7 %collective-permute-start.16 = (bf16[192,640]{1,0:T(8,128)(2,1)S(1)}, bf16[192,640]{1,0:T(8,128)(2,1)S(1)}, u32[]{:S(2)}, u32[]{:S(2)}) collective-permute-start(bf16[192,640]{1,0:T(8,128)(2,1)S(1)} %tie.14), channel_id=1, source_target_pairs={{0,1},{1,0},{2,3},{3,2},{4,5},{5,4},{6,7},{7,6},{8,9},{9,8},{10,11... | collective-permute-start | bytes 737288 | tf_op jit(solution)/shard_map/ppermute | solution.py:42
  64.2 7.0 %collective-permute-start.25 = (bf16[192,512]{1,0:T(8,128)(2,1)S(1)}, bf16[192,512]{1,0:T(8,128)(2,1)S(1)}, u32[]{:S(2)}, u32[]{:S(2)}) collective-permute-start(bf16[192,512]{1,0:T(8,128)(2,1)S(1)} %tie.19), channel_id=1, source_target_pairs={{0,1},{1,0},{2,3},{3,2},{4,5},{5,4},{6,7},{7,6},{8,9},{9,8},{10,11... | collective-permute-start | bytes 589832 | tf_op jit(solution)/shard_map/ppermute | solution.py:42
  65.1 7.1 %collective-permute-start.26 = (bf16[192,512]{1,0:T(8,128)(2,1)S(1)}, bf16[192,512]{1,0:T(8,128)(2,1)S(1)}, u32[]{:S(2)}, u32[]{:S(2)}) collective-permute-start(bf16[192,512]{1,0:T(8,128)(2,1)S(1)} %add_convert_fusion.3.refs_1_), channel_id=1, source_target_pairs={{0,2},{1,3},{2,0},{3,1},{4,6},{5,7},{6,4},{7,5},{8,10},{9,11},{10,... | collective-permute-start | bytes 589832 | tf_op jit(solution)/shard_map/ppermute | solution.py:42
  66.7 8.0 %collective-permute-start.22 = (bf16[48,640]{1,0:T(8,128)(2,1)S(1)}, bf16[48,640]{1,0:T(8,128)(2,1)S(1)}, u32[]{:S(2)}, u32[]{:S(2)}) collective-permute-start(bf16[48,640]{1,0:T(8,128)(2,1)S(1)} %get-tuple-element.51), channel_id=1, source_target_pairs={{0,4},{1,5},{2,6},{3,7},{4,0},{5,1},{6,2},{7,3},{8,12},{9,13},{10,... | collective-permute-start | bytes 184328 | tf_op jit(solution)/shard_map/ppermute | solution.py:42
  66.8 10.0 %collective-permute-start.23 = (bf16[48,640]{1,0:T(8,128)(2,1)S(1)}, bf16[48,640]{1,0:T(8,128)(2,1)S(1)}, u32[]{:S(2)}, u32[]{:S(2)}) collective-permute-start(bf16[48,640]{1,0:T(8,128)(2,1)S(1)} %get-tuple-element.50), channel_id=1, source_target_pairs={{0,8},{1,9},{2,10},{3,11},{4,12},{5,13},{6,14},{7,15},{8,0},{9,1},... | collective-permute-start | bytes 184328 | tf_op jit(solution)/shard_map/ppermute | solution.py:42
  69.0 7.7 %collective-permute-start.24 = (bf16[48,640]{1,0:T(8,128)(2,1)S(1)}, bf16[48,640]{1,0:T(8,128)(2,1)S(1)}, u32[]{:S(2)}, u32[]{:S(2)}) collective-permute-start(bf16[48,640]{1,0:T(8,128)(2,1)S(1)} %get-tuple-element.49), channel_id=1, source_target_pairs={{0,12},{1,13},{2,14},{3,15},{4,8},{5,9},{6,10},{7,11},{8,4},{9,5},... | collective-permute-start | bytes 184328 | tf_op jit(solution)/shard_map/ppermute | solution.py:42
  72.3 5.4 %collective-permute-start.27 = (bf16[48,512]{1,0:T(8,128)(2,1)S(1)}, bf16[48,512]{1,0:T(8,128)(2,1)S(1)}, u32[]{:S(2)}, u32[]{:S(2)}) collective-permute-start(bf16[48,512]{1,0:T(8,128)(2,1)S(1)} %get-tuple-element.55), channel_id=1, source_target_pairs={{0,4},{1,5},{2,6},{3,7},{4,0},{5,1},{6,2},{7,3},{8,12},{9,13},{10,... | collective-permute-start | bytes 147464 | tf_op jit(solution)/shard_map/ppermute | solution.py:42
  72.4 5.3 %collective-permute-start.28 = (bf16[48,512]{1,0:T(8,128)(2,1)S(1)}, bf16[48,512]{1,0:T(8,128)(2,1)S(1)}, u32[]{:S(2)}, u32[]{:S(2)}) collective-permute-start(bf16[48,512]{1,0:T(8,128)(2,1)S(1)} %get-tuple-element.54), channel_id=1, source_target_pairs={{0,8},{1,9},{2,10},{3,11},{4,12},{5,13},{6,14},{7,15},{8,0},{9,1},... | collective-permute-start | bytes 147464 | tf_op jit(solution)/shard_map/ppermute | solution.py:42
  74.7 5.9 %collective-permute-start.29 = (bf16[48,512]{1,0:T(8,128)(2,1)S(1)}, bf16[48,512]{1,0:T(8,128)(2,1)S(1)}, u32[]{:S(2)}, u32[]{:S(2)}) collective-permute-start(bf16[48,512]{1,0:T(8,128)(2,1)S(1)} %get-tuple-element.53), channel_id=1, source_target_pairs={{0,12},{1,13},{2,14},{3,15},{4,8},{5,9},{6,10},{7,11},{8,4},{9,5},... | collective-permute-start | bytes 147464 | tf_op jit(solution)/shard_map/ppermute | solution.py:42

commit v14 on v13

--- a/solution.py
+++ b/solution.py
@@ -10,6 +10,7 @@
 PLEN = 128
 HINT = 1 << 33
 STRIP = 512
+LIMIT = 24 << 20
 VMEM = pl.BlockSpec(memory_space=pltpu.VMEM)
 SMEM = pl.BlockSpec(memory_space=pltpu.SMEM)
 ANY = pl.BlockSpec(memory_space=pl.ANY)
@@ -141,11 +142,11 @@
     value = refs[0][...]
     for ref in refs[1:count]:
         value = value.astype(jnp.float32) + ref[...].astype(jnp.float32)
-    refs[-1][...] = value
-
-
-def tie(values, after, cost=0):
-    kind = values[0].dtype if len(values) == 1 else jnp.float32
+    refs[-1][...] = value.astype(refs[-1].dtype)
+
+
+def tie(values, after, cost=0, kind=None):
+    kind = kind or values[0].dtype
     return pl.pallas_call(
         functools.partial(tie_kernel, len(values)),
         out_shape=jax.ShapeDtypeStruct(values[0].shape, kind),
@@ -214,22 +215,25 @@
     return list(zip(edges[:-1], edges[1:]))
 
 
-def expert_kernel(packing, unit_cuts, count, after, *refs):
+def expert_kernel(packing, unit_cuts, count, after, fetch, *refs):
     row_refs = refs[:count]
     gate_hbm, up_hbm, down_hbm = refs[count : count + 3]
     place = count + 3 + after
     out_refs = refs[place : place + count]
-    gate_ref, up_ref, down_ref, rows_ref, total_ref, packed_ref, sems = refs[place + count :]
+    if fetch:
+        gate_ref, up_ref, down_ref, rows_ref, total_ref, packed_ref, sems = refs[place + count :]
+    else:
+        gate_ref, up_ref, down_ref = gate_hbm, up_hbm, down_hbm
+        rows_ref, total_ref, packed_ref = refs[place + count :]
     copies = []
     for i, (lo, hi) in enumerate(unit_cuts):
         for t, (source, target) in enumerate(
             ((gate_hbm, gate_ref), (up_hbm, up_ref), (down_hbm, down_ref))
         ):
-            copies.append(
-                pltpu.make_async_copy(
-                    source.at[lo:hi], target.at[lo:hi], sems.at[3 * i + t]
+            if fetch:
+                copies.append(
+                    pltpu.make_async_copy(source.at[lo:hi], target.at[lo:hi], sems.at[3 * i + t])
                 )
-            )
     for copy in copies[:2]:
         copy.start()
 
@@ -285,17 +289,16 @@
 
     inner = None
     for i, (lo, hi) in enumerate(unit_cuts):
-        if i > 0:
-            copies[3 * i - 1].wait()
-        copies[3 * i].wait()
-        copies[3 * i + 1].wait()
+        for copy in copies[max(3 * i - 1, 0) : 3 * i + 2]:
+            copy.wait()
         for copy in copies[3 * (i + 2) : 3 * (i + 3)]:
             copy.start()
         following = product(gate_ref, lo, hi), product(up_ref, lo, hi)
         if i > 0:
             down(i - 1, gated(*inner))
         inner = following
-    copies[-1].wait()
+    for copy in copies[-1:]:
+        copy.wait()
     down(len(unit_cuts) - 1, gated(*inner))
 
     for c in range(lanes):
@@ -315,35 +318,36 @@
             ref[:, columns] = part.astype(jnp.bfloat16)
 
 
-def expert_rows(arrays, w_gate, w_up, w_down, packing, after):
-    features, units = w_gate.shape
+def expert_rows(arrays, w_gate, w_up, w_down, packing, after, fetch):
+    units, features = w_down.shape
     rows = len(arrays) * (arrays[0].shape[0] // packing.rows) * packing.cap
     unit_cuts = cuts(units)
-    return pl.pallas_call(
-        functools.partial(expert_kernel, packing, unit_cuts, len(arrays), len(after)),
-        out_shape=[jax.ShapeDtypeStruct(arrays[0].shape, jnp.bfloat16)] * len(arrays),
-        in_specs=[VMEM] * len(arrays) + [HBM] * 3 + [ANY] * len(after),
-        out_specs=[VMEM] * len(arrays),
+    weight = jax.ShapeDtypeStruct((units, features), jnp.bfloat16)
+    kept = 3 if fetch else 0
+    results = pl.pallas_call(
+        functools.partial(expert_kernel, packing, unit_cuts, len(arrays), len(after), fetch),
+        out_shape=[jax.ShapeDtypeStruct(arrays[0].shape, jnp.bfloat16)] * len(arrays)
+        + [weight] * kept,
+        in_specs=[VMEM] * len(arrays) + [HBM if fetch else VMEM] * 3 + [ANY] * len(after),
+        out_specs=[VMEM] * (len(arrays) + kept),
         scratch_shapes=[
-            pltpu.VMEM((units, features), jnp.bfloat16),
-            pltpu.VMEM((units, features), jnp.bfloat16),
-            pltpu.VMEM((units, features), jnp.bfloat16),
             pltpu.VMEM((features, -(-rows // 128) * 128), jnp.bfloat16),
             pltpu.VMEM((features // 128, rows + 16, 128), jnp.float32),
             pltpu.VMEM(
                 (packing.width // 128, len(arrays) * arrays[0].shape[0] + packing.rows, 128),
                 jnp.float32,
             ),
-            pltpu.SemaphoreType.DMA((3 * len(unit_cuts),)),
-        ],
-        compiler_params=pltpu.CompilerParams(vmem_limit_bytes=48 << 20),
+        ]
+        + [pltpu.SemaphoreType.DMA((3 * len(unit_cuts),))] * (kept // 3),
+        compiler_params=pltpu.CompilerParams(vmem_limit_bytes=LIMIT),
         cost_estimate=pl.CostEstimate(
             flops=6 * rows * features * units,
             bytes_accessed=6 * features * units,
             transcendentals=rows * units,
         ),
         name="experts",
-    )(*arrays, w_gate.T, w_up.T, w_down, *after)
+    )(*arrays, w_gate, w_up, w_down, *after)
+    return list(results[: len(arrays)]), list(results[len(arrays) :])
 
 
 def combine_kernel(packing, spot_ref, weight_ref, *refs):
@@ -442,10 +446,10 @@
 
     def join_cores(results):
         own, other = results[:pairs], results[pairs:]
-        sums = [None] * pairs
-        for k in list(range(1, pairs)) + [0]:
-            sums[k] = own[k].astype(wide) + grid.swap(other[k], 2, 1).astype(wide)
-        return sums[0], [value.astype(narrow) for value in sums[1:]]
+        crossing = [
+            tie([own[k], grid.swap(other[k], 2, 1)], [], 0, narrow) for k in range(1, pairs)
+        ]
+        return own[0].astype(wide) + grid.swap(other[0], 2, 1).astype(wide), crossing
 
     def from_pairs(crossing):
         return [grid.swap(value, 1, k) for k, value in enumerate(crossing, 1)]
@@ -486,7 +490,7 @@
     terms = parts[:1] + [grid.swap(part, 0, k) for k, part in enumerate(sent, 1)]
     image_first = jnp.concatenate([tie([image_first[0]], sent)] + image_first[1:], axis=0)
     image_own = to_pairs(image_first)
-    weights = (w_gate, w_up, w_down)
+    weights = (w_gate.T, w_up.T, w_down)
 
     caption_normed, blocks = modulate(terms, caption_spot, small, caption_packing, experts)
     received = to_experts(blocks)
@@ -497,24 +501,25 @@
 
     image_weights = route(image_normed, image_spot, small)
     caption_weights = route(caption_normed, caption_spot, small)
-    image_results = expert_rows(
-        image_arrays, *weights, image_packing, [caption_first, image_weights]
+    image_results, weights = expert_rows(
+        image_arrays, *weights, image_packing, [caption_first, image_weights], True
     )
     caption_own = caption_own[:1] + [tie([value], image_results[:1]) for value in caption_own[1:]]
-    image_results = list(image_results[:pairs]) + [
+    image_results = image_results[:pairs] + [
         tie([value], caption_own[1:2]) for value in image_results[pairs:]
     ]
     image_kept, image_crossing = join_cores(image_results)
-    caption_results = expert_rows(
+    caption_results, _ = expert_rows(
         caption_own + over_cores(caption_own),
         *weights,
         caption_packing,
         image_crossing[:1] + [caption_weights],
+        False,
     )
     image_received = [
         tie([value], caption_results[:1]) for value in from_pairs(image_crossing)
     ]
-    caption_results = list(caption_results[:pairs]) + [
+    caption_results = caption_results[:pairs] + [
         tie([value], image_received[:1]) for value in caption_results[pairs:]
     ]
     caption_kept, caption_crossing = join_cores(caption_results)

time: 81.6 us -> 76.3 us (0.935)
  Pallas kernels: 27.8 us -> 22.5 us
    pallas_call x2, Pallas kernels: 23.9 us -> 18.5 us  [expert_rows(): pl.pallas_call(functools.partial(expert_kernel, packing, unit_cuts, len(a...]
  transfers between devices with their start and end apart: 30 -> 30, of which waited for: 11 -> 11; matrix products, arithmetic and copies ran while one was open for 1% -> 1% of each run, Pallas kernels for 33% -> 28%
where the time goes in v14:
time: 76.3 us; the launch traced here: 76.2 us
  starting transfers between devices  32.8 us (43%)
  Pallas kernels  22.5 us (29%)
  waiting for transfers between devices  16.9 us (22%)
  other arithmetic  1.84 us (2%)
  between operations  1.17 us (2%)
    ppermute x30, starting transfers between devices, swap(): return lax.ppermute(value, 'dev', moves)  32.8 us
    pallas_call x2, Pallas kernels, expert_rows(): pl.pallas_call(functools.partial(expert_kernel, packing, unit_cuts, len(a...  18.5 us
    ppermute x30, waiting for transfers between devices, swap(): return lax.ppermute(value, 'dev', moves)  16.9 us
    pallas_call x2, Pallas kernels, combine(): pl.pallas_call(functools.partial(combine_kernel, packing), out_shape=jax....  1.77 us
  transfers between devices with their start and end apart: 30, of which 11 were waited for; matrix products, arithmetic and copies ran while one was open for 1% of the time, Pallas kernels for 28%

profile of v14, /device:TPU:0, one launch (start us, length us, event | category | flops | bytes accessed | tf_op | source)
XLA Modules:
  0.0 76.2 jit_solution(11503595312062546085)
XLA Ops:
  0.6 0.0 copy-start
  0.7 1.1 %fusion.5 = bf16[2,2,2,2,16,256]{5,4,3,2,1,0:T(8,128)(2,1)S(1)} fusion(s32[]{:T(128)S(6)} %select_n.80, bf16[2,2,2,2,16,256]{5,4,3,2,1,0:T(8,128)(2,1)} %bitcast.27), kind=kLoop, calls=%fused_computation.19 | loop fusion | flops 65536 | bytes 262148 | tf_op jit(solution)/shard_map/jit(_roll_dynamic)/concatenate | solution.py:395
  1.8 0.1 fusion.3
  1.9 0.1 fusion.2
  2.1 0.0 copy-start.8
  2.1 0.0 copy-start.6
  2.1 0.0 copy-start.5
  2.1 0.3 convolution_convert_fusion
  2.5 0.5 collective-permute-start
  3.0 0.1 collective-permute-start.1
  3.1 0.1 fusion.7
  3.3 0.3 fusion.16
  3.7 0.0 copy-start.3
  3.7 0.6 collective-permute-done
  4.3 0.1 fusion.1.refs_0_
  4.4 3.0 %collective-permute-start.2 = (bf16[64,2560]{1,0:T(8,128)(2,1)S(1)}, bf16[64,2560]{1,0:T(8,128)(2,1)S(1)}, u32[]{:S(2)}, u32[]{:S(2)}) collective-permute-start(bf16[64,2560]{1,0:T(8,128)(2,1)S(1)} %fusion.1.refs_0_), channel_id=1, source_target_pairs={{0,2},{1,3},{2,0},{3,1},{4,6},{5,7},{6,4},{7,5},{8,10},{9,11},{10,... | collective-permute-start | bytes 983048 | tf_op jit(solution)/shard_map/ppermute | solution.py:43
  7.4 0.8 %prepare.1 = (f32[16,4]{1,0:T(8,128)S(1)}, f32[16,4]{1,0:T(8,128)S(1)}, bf16[16,2560]{1,0:T(8,128)(2,1)S(1)}, bf16[48,640]{1,0:T(8,128)(2,1)S(1)}, bf16[48,640]{...) custom-call(s32[4,16]{1,0:T(4,128)S(1)} %pad_add_fusion.ids_ref, ...), custom_call_target="tpu_custom_call" | custom-call | tf_op jit(solution)/shard_map/prepare/pallas_call | solution.py:125
  8.2 1.6 %collective-permute-start.3 = (bf16[48,640]{1,0:T(8,128)(2,1)S(1)}, bf16[48,640]{1,0:T(8,128)(2,1)S(1)}, u32[]{:S(2)}, u32[]{:S(2)}) collective-permute-start(bf16[48,640]{1,0:T(8,128)(2,1)S(1)} %get-tuple-element.28.refs_1_), channel_id=1, source_target_pairs={{0,4},{1,5},{2,6},{3,7},{4,0},{5,1},{6,2},{7,3},{8,12},{9,13},{10,... | collective-permute-start | bytes 184328 | tf_op jit(solution)/shard_map/ppermute | solution.py:43
  9.8 2.6 %collective-permute-start.4 = (bf16[48,640]{1,0:T(8,128)(2,1)S(1)}, bf16[48,640]{1,0:T(8,128)(2,1)S(1)}, u32[]{:S(2)}, u32[]{:S(2)}) collective-permute-start(bf16[48,640]{1,0:T(8,128)(2,1)S(1)} %get-tuple-element.29), channel_id=1, source_target_pairs={{0,8},{1,9},{2,10},{3,11},{4,12},{5,13},{6,14},{7,15},{8,0},{9,1},... | collective-permute-start | bytes 184328 | tf_op jit(solution)/shard_map/ppermute | solution.py:43
  12.4 0.2 collective-permute-start.5
  12.6 0.3 route.2.refs_8_.weight_ref
  12.9 2.4 %collective-permute-done.2.refs_0_ = bf16[64,2560]{1,0:T(8,128)(2,1)S(1)} collective-permute-done((bf16[64,2560]{1,0:T(8,128)(2,1)S(1)}, bf16[64,2560]{1,0:T(8,128)(2,1)S(1)}, u32[]{:S(2)}, u32[]{:S(2)}) %collective-permute-start.2) | collective-permute-done | bytes 327712 | tf_op jit(solution)/shard_map/ppermute | solution.py:43
  15.4 0.1 fusion.9
  15.5 1.9 %collective-permute-start.7 = (bf16[16,2560]{1,0:T(8,128)(2,1)S(1)}, bf16[16,2560]{1,0:T(8,128)(2,1)S(1)}, u32[]{:S(2)}, u32[]{:S(2)}) collective-permute-start(bf16[16,2560]{1,0:T(8,128)(2,1)S(1)} %get-tuple-element.54.refs_1_), channel_id=1, source_target_pairs={{0,4},{1,5},{2,6},{3,7},{4,0},{5,1},{6,2},{7,3},{8,12},{9,13},{10,... | collective-permute-start | bytes 245768 | tf_op jit(solution)/shard_map/ppermute | solution.py:43
  17.4 2.5 %collective-permute-start.8 = (bf16[16,2560]{1,0:T(8,128)(2,1)S(1)}, bf16[16,2560]{1,0:T(8,128)(2,1)S(1)}, u32[]{:S(2)}, u32[]{:S(2)}) collective-permute-start(bf16[16,2560]{1,0:T(8,128)(2,1)S(1)} %get-tuple-element.53.refs_2_), channel_id=1, source_target_pairs={{0,8},{1,9},{2,10},{3,11},{4,12},{5,13},{6,14},{7,15},{8,0},{9,1},... | collective-permute-start | bytes 245768 | tf_op jit(solution)/shard_map/ppermute | solution.py:43
  19.9 0.1 collective-permute-start.9
  20.1 1.8 %collective-permute-start.6 = (bf16[192,640]{1,0:T(8,128)(2,1)S(1)}, bf16[192,640]{1,0:T(8,128)(2,1)S(1)}, u32[]{:S(2)}, u32[]{:S(2)}) collective-permute-start(bf16[192,640]{1,0:T(8,128)(2,1)S(1)} %pad_maximum_fusion.refs_0_), channel_id=1, source_target_pairs={{0,2},{1,3},{2,0},{3,1},{4,6},{5,7},{6,4},{7,5},{8,10},{9,11},{10,... | collective-permute-start | bytes 737288 | tf_op jit(solution)/shard_map/ppermute | solution.py:43
  21.9 3.3 %collective-permute-done.8.refs_2_ = bf16[16,2560]{1,0:T(8,128)(2,1)S(1)} collective-permute-done((bf16[16,2560]{1,0:T(8,128)(2,1)S(1)}, bf16[16,2560]{1,0:T(8,128)(2,1)S(1)}, u32[]{:S(2)}, u32[]{:S(2)}) %collective-permute-start.8) | collective-permute-done | bytes 81952 | tf_op jit(solution)/shard_map/ppermute | solution.py:43
  25.2 1.2 %collective-permute-done.9.refs_3_ = bf16[16,2560]{1,0:T(8,128)(2,1)S(1)} collective-permute-done((bf16[16,2560]{1,0:T(8,128)(2,1)S(1)}, bf16[16,2560]{1,0:T(8,128)(2,1)S(1)}, u32[]{:S(2)}, u32[]{:S(2)}) %collective-permute-start.9) | collective-permute-done | bytes 81952 | tf_op jit(solution)/shard_map/ppermute | solution.py:43
  26.4 0.6 modulate.1
  27.0 1.2 %collective-permute-start.12 = (bf16[48,512]{1,0:T(8,128)(2,1)S(1)}, bf16[48,512]{1,0:T(8,128)(2,1)S(1)}, u32[]{:S(2)}, u32[]{:S(2)}) collective-permute-start(bf16[48,512]{1,0:T(8,128)(2,1)S(1)} %get-tuple-element.32.refs_1_), channel_id=1, source_target_pairs={{0,4},{1,5},{2,6},{3,7},{4,0},{5,1},{6,2},{7,3},{8,12},{9,13},{10,... | collective-permute-start | bytes 147464 | tf_op jit(solution)/shard_map/ppermute | solution.py:43
  28.2 1.6 %collective-permute-start.13 = (bf16[48,512]{1,0:T(8,128)(2,1)S(1)}, bf16[48,512]{1,0:T(8,128)(2,1)S(1)}, u32[]{:S(2)}, u32[]{:S(2)}) collective-permute-start(bf16[48,512]{1,0:T(8,128)(2,1)S(1)} %get-tuple-element.34), channel_id=1, source_target_pairs={{0,8},{1,9},{2,10},{3,11},{4,12},{5,13},{6,14},{7,15},{8,0},{9,1},... | collective-permute-start | bytes 147464 | tf_op jit(solution)/shard_map/ppermute | solution.py:43
  29.8 1.7 %collective-permute-start.14 = (bf16[48,512]{1,0:T(8,128)(2,1)S(1)}, bf16[48,512]{1,0:T(8,128)(2,1)S(1)}, u32[]{:S(2)}, u32[]{:S(2)}) collective-permute-start(bf16[48,512]{1,0:T(8,128)(2,1)S(1)} %get-tuple-element.35), channel_id=1, source_target_pairs={{0,12},{1,13},{2,14},{3,15},{4,8},{5,9},{6,10},{7,11},{8,4},{9,5},... | collective-permute-start | bytes 147464 | tf_op jit(solution)/shard_map/ppermute | solution.py:43
  31.5 0.1 collective-permute-start.11
  31.6 2.4 %collective-permute-done.13 = bf16[48,512]{1,0:T(8,128)(2,1)S(1)} collective-permute-done((bf16[48,512]{1,0:T(8,128)(2,1)S(1)}, bf16[48,512]{1,0:T(8,128)(2,1)S(1)}, u32[]{:S(2)}, u32[]{:S(2)}) %collective-permute-start.13) | collective-permute-done | bytes 49184 | tf_op jit(solution)/shard_map/ppermute | solution.py:43
  34.0 1.7 %collective-permute-done.14 = bf16[48,512]{1,0:T(8,128)(2,1)S(1)} collective-permute-done((bf16[48,512]{1,0:T(8,128)(2,1)S(1)}, bf16[48,512]{1,0:T(8,128)(2,1)S(1)}, u32[]{:S(2)}, u32[]{:S(2)}) %collective-permute-start.14) | collective-permute-done | bytes 49184 | tf_op jit(solution)/shard_map/ppermute | solution.py:43
  35.7 1.5 %collective-permute-start.15 = (bf16[192,512]{1,0:T(8,128)(2,1)S(1)}, bf16[192,512]{1,0:T(8,128)(2,1)S(1)}, u32[]{:S(2)}, u32[]{:S(2)}) collective-permute-start(bf16[192,512]{1,0:T(8,128)(2,1)S(1)} %constant_dynamic-update-slice_fusion.refs_7_.refs_0_), channel_id=1, source_target_pairs={{0,2},{1,3},{2,0},{3,1},{4,6},{5,7},{6,4},{7,5},{8,10},{9,11},{10,... | collective-permute-start | bytes 589832 | tf_op jit(solution)/shard_map/ppermute | solution.py:43
  37.2 11.4 %experts.2 = (bf16[192,640]{1,0:T(8,128)(2,1)S(1)}, bf16[192,640]{1,0:T(8,128)(2,1)S(1)}, bf16[192,640]{1,0:T(8,128)(2,1)S(1)}, bf16[192,640]{1,0:T(8,128)(2,1)S...) custom-call(bf16[192,640]{1,0:T(8,128)(2,1)S(1)} %pad_maximum_fusion.refs_0_, ...), custom_call_target="tpu_custom_call" | custom-call | flops 5096079360 | bytes 26542080 | tf_op jit(solution)/shard_map/experts/pallas_call | solution.py:327
  48.6 0.1 collective-permute-start.17
  48.7 0.5 collective-permute-start.19
  49.2 0.1 collective-permute-start.20
  49.3 0.3 route.3.refs_8_.weight_ref
  49.6 0.5 collective-permute-start.16
  50.1 0.1 collective-permute-done.17.refs_1_
  50.2 0.1 tie.18.refs_7_
  50.3 0.6 collective-permute-start.18
  50.9 7.1 %experts.3 = (bf16[192,512]{1,0:T(8,128)(2,1)S(1)}, bf16[192,512]{1,0:T(8,128)(2,1)S(1)}, bf16[192,512]{1,0:T(8,128)(2,1)S(1)}, bf16[192,512]{1,0:T(8,128)(2,1)S(1)}) custom-call(bf16[192,512]{1,0:T(8,128)(2,1)S(1)} %constant_dynamic-update-slice_fusion.refs_7_.refs_0_, bf16[192,512]{1,0:T(8,128)(2,1)S(1)} %tie.15.refs_1_, ...), custom_call_target="tpu_custom_call" | custom-call | flops 3822059520 | bytes 26542080 | tf_op jit(solution)/shard_map/experts/pallas_call | solution.py:327
  58.0 0.4 collective-permute-done.18.refs_0_
  58.4 0.1 collective-permute-start.21
  58.5 0.6 collective-permute-start.25
  59.0 0.8 %collective-permute-done.21.refs_1_ = bf16[192,512]{1,0:T(8,128)(2,1)S(1)} collective-permute-done((bf16[192,512]{1,0:T(8,128)(2,1)S(1)}, bf16[192,512]{1,0:T(8,128)(2,1)S(1)}, u32[]{:S(2)}, u32[]{:S(2)}) %collective-permute-start.21) | collective-permute-done | bytes 196640 | tf_op jit(solution)/shard_map/ppermute | solution.py:43
  59.9 1.2 %collective-permute-start.26 = (bf16[192,512]{1,0:T(8,128)(2,1)S(1)}, bf16[192,512]{1,0:T(8,128)(2,1)S(1)}, u32[]{:S(2)}, u32[]{:S(2)}) collective-permute-start(bf16[192,512]{1,0:T(8,128)(2,1)S(1)} %tie.21.refs_1_), channel_id=1, source_target_pairs={{0,2},{1,3},{2,0},{3,1},{4,6},{5,7},{6,4},{7,5},{8,10},{9,11},{10,... | collective-permute-start | bytes 589832 | tf_op jit(solution)/shard_map/ppermute | solution.py:43
  61.2 0.1 add_convert_fusion
  61.3 0.1 collective-permute-start.22
  61.4 2.3 %collective-permute-start.23 = (bf16[48,640]{1,0:T(8,128)(2,1)S(1)}, bf16[48,640]{1,0:T(8,128)(2,1)S(1)}, u32[]{:S(2)}, u32[]{:S(2)}) collective-permute-start(bf16[48,640]{1,0:T(8,128)(2,1)S(1)} %get-tuple-element.56), channel_id=1, source_target_pairs={{0,8},{1,9},{2,10},{3,11},{4,12},{5,13},{6,14},{7,15},{8,0},{9,1},... | collective-permute-start | bytes 184328 | tf_op jit(solution)/shard_map/ppermute | solution.py:43
  63.7 2.1 %collective-permute-start.24 = (bf16[48,640]{1,0:T(8,128)(2,1)S(1)}, bf16[48,640]{1,0:T(8,128)(2,1)S(1)}, u32[]{:S(2)}, u32[]{:S(2)}) collective-permute-start(bf16[48,640]{1,0:T(8,128)(2,1)S(1)} %get-tuple-element.55), channel_id=1, source_target_pairs={{0,12},{1,13},{2,14},{3,15},{4,8},{5,9},{6,10},{7,11},{8,4},{9,5},... | collective-permute-start | bytes 184328 | tf_op jit(solution)/shard_map/ppermute | solution.py:43
  65.8 1.1 %collective-permute-done.26 = bf16[192,512]{1,0:T(8,128)(2,1)S(1)} collective-permute-done((bf16[192,512]{1,0:T(8,128)(2,1)S(1)}, bf16[192,512]{1,0:T(8,128)(2,1)S(1)}, u32[]{:S(2)}, u32[]{:S(2)}) %collective-permute-start.26) | collective-permute-done | bytes 196640 | tf_op jit(solution)/shard_map/ppermute | solution.py:43
  67.0 0.1 add_convert_fusion.1
  67.1 0.1 collective-permute-start.27
  67.1 2.3 %collective-permute-start.28 = (bf16[48,512]{1,0:T(8,128)(2,1)S(1)}, bf16[48,512]{1,0:T(8,128)(2,1)S(1)}, u32[]{:S(2)}, u32[]{:S(2)}) collective-permute-start(bf16[48,512]{1,0:T(8,128)(2,1)S(1)} %get-tuple-element.60), channel_id=1, source_target_pairs={{0,8},{1,9},{2,10},{3,11},{4,12},{5,13},{6,14},{7,15},{8,0},{9,1},... | collective-permute-start | bytes 147464 | tf_op jit(solution)/shard_map/ppermute | solution.py:43
  69.4 2.1 %collective-permute-start.29 = (bf16[48,512]{1,0:T(8,128)(2,1)S(1)}, bf16[48,512]{1,0:T(8,128)(2,1)S(1)}, u32[]{:S(2)}, u32[]{:S(2)}) collective-permute-start(bf16[48,512]{1,0:T(8,128)(2,1)S(1)} %get-tuple-element.59), channel_id=1, source_target_pairs={{0,12},{1,13},{2,14},{3,15},{4,8},{5,9},{6,10},{7,11},{8,4},{9,5},... | collective-permute-start | bytes 147464 | tf_op jit(solution)/shard_map/ppermute | solution.py:43
  71.5 0.9 %combine.2 = bf16[16,2560]{1,0:T(8,128)(2,1)} custom-call(f32[16,4]{1,0:T(8,128)S(1)} %get-tuple-element.25.spot_ref, f32[16,2]{1,0:T(8,128)S(1)} %route.2.refs_8_.weight_ref, bf16[48,640]{1,0:T(8,128)(2,1)S(1)} %get-tuple-element.58.refs_0_, bf16[48,640]{1,0:T(8,128)(2,1)S(1)} %collective-permute-done.22.refs_1_, ...), custom_call_target="tpu_custom_call" | custom-call | tf_op jit(solution)/shard_map/combine/pallas_call | solution.py:379
  72.4 2.9 %collective-permute-done.29.refs_3_ = bf16[48,512]{1,0:T(8,128)(2,1)S(1)} collective-permute-done((bf16[48,512]{1,0:T(8,128)(2,1)S(1)}, bf16[48,512]{1,0:T(8,128)(2,1)S(1)}, u32[]{:S(2)}, u32[]{:S(2)}) %collective-permute-start.29) | collective-permute-done | bytes 49184 | tf_op jit(solution)/shard_map/ppermute | solution.py:43
  75.3 0.9 %combine.3 = bf16[16,2560]{1,0:T(8,128)(2,1)} custom-call(f32[16,4]{1,0:T(8,128)S(1)} %get-tuple-element.31.spot_ref, f32[16,2]{1,0:T(8,128)S(1)} %route.3.refs_8_.weight_ref, bf16[48,512]{1,0:T(8,128)(2,1)S(1)} %get-tuple-element.62.refs_0_, bf16[48,512]{1,0:T(8,128)(2,1)S(1)} %collective-permute-done.27.refs_1_, ...), custom_call_target="tpu_custom_call" | custom-call | tf_op jit(solution)/shard_map/combine/pallas_call | solution.py:379
  (63 shorter events, 0.6 us)
Async XLA Ops:
  0.6 1.4 %copy-start = (bf16[256,2560]{1,0:T(8,128)(2,1)S(1)}, bf16[256,2560]{1,0:T(8,128)(2,1)}, u32[]{:S(2)}) copy-start(bf16[256,2560]{1,0:T(8,128)(2,1)} %param.14) | copy-start | bytes 3932164
  2.1 1.1 %copy-start.8 = (s32[2]{0:T(128)S(1)}, s32[2]{0:T(128)}, u32[]{:S(2)}) copy-start(s32[2]{0:T(128)} %param.20) | copy-start | bytes 28
  2.1 1.2 %copy-start.6 = (s32[16,2]{0,1:T(2,128)S(1)}, s32[16,2]{0,1:T(2,128)}, u32[]{:S(2)}) copy-start(s32[16,2]{0,1:T(2,128)} %param.19) | copy-start | bytes 388
  2.1 1.2 %copy-start.7 = (s32[16,2]{0,1:T(2,128)S(1)}, s32[16,2]{0,1:T(2,128)}, u32[]{:S(2)}) copy-start(s32[16,2]{0,1:T(2,128)} %param.18) | copy-start | bytes 388
  2.1 1.2 %copy-start.4 = (f32[2560]{0:T(1024)S(1)}, f32[2560]{0:T(1024)}, u32[]{:S(2)}) copy-start(f32[2560]{0:T(1024)} %param.15) | copy-start | bytes 30724
  2.1 1.2 %copy-start.5 = (f32[2560]{0:T(1024)S(1)}, f32[2560]{0:T(1024)}, u32[]{:S(2)}) copy-start(f32[2560]{0:T(1024)} %param.16) | copy-start | bytes 30724
  2.5 1.8 %collective-permute-start = (bf16[64,2560]{1,0:T(8,128)(2,1)S(1)}, bf16[64,2560]{1,0:T(8,128)(2,1)S(1)}, u32[]{:S(2)}, u32[]{:S(2)}) collective-permute-start(bf16[64,2560]{1,0:T(8,128)(2,1)S(1)} %get-tuple-element.51), channel_id=1, source_target_pairs={{0,1},{1,0},{2,3},{3,2},{4,5},{5,4},{6,7},{7,6},{8,9},{9,8},{10,11... | collective-permute-start | bytes 983048 | tf_op jit(solution)/shard_map/ppermute | solution.py:43
  3.0 12.3 %collective-permute-start.1 = (bf16[64,2560]{1,0:T(8,128)(2,1)S(1)}, bf16[64,2560]{1,0:T(8,128)(2,1)S(1)}, u32[]{:S(2)}, u32[]{:S(2)}) collective-permute-start(bf16[64,2560]{1,0:T(8,128)(2,1)S(1)} %get-tuple-element.50), channel_id=1, source_target_pairs={{0,1},{1,0},{2,3},{3,2},{4,5},{5,4},{6,7},{7,6},{8,9},{9,8},{10,11... | collective-permute-start | bytes 983048 | tf_op jit(solution)/shard_map/ppermute | solution.py:43
  3.7 3.6 %copy-start.3 = (f32[2560,4]{0,1:T(4,128)S(1)}, f32[2560,4]{0,1:T(4,128)}, u32[]{:S(2)}) copy-start(f32[2560,4]{0,1:T(4,128)} %param.17) | copy-start | bytes 122884
  3.7 3.7 %copy-start.2 = (bf16[16,2560]{1,0:T(8,128)(2,1)S(1)}, bf16[16,2560]{1,0:T(8,128)(2,1)}, u32[]{:S(2)}) copy-start(bf16[16,2560]{1,0:T(8,128)(2,1)} %image_ref.1) | copy-start | bytes 245764
  4.4 11.0 %collective-permute-start.2 = (bf16[64,2560]{1,0:T(8,128)(2,1)S(1)}, bf16[64,2560]{1,0:T(8,128)(2,1)S(1)}, u32[]{:S(2)}, u32[]{:S(2)}) collective-permute-start(bf16[64,2560]{1,0:T(8,128)(2,1)S(1)} %fusion.1.refs_0_), channel_id=1, source_target_pairs={{0,2},{1,3},{2,0},{3,1},{4,6},{5,7},{6,4},{7,5},{8,10},{9,11},{10,... | collective-permute-start | bytes 983048 | tf_op jit(solution)/shard_map/ppermute | solution.py:43
  8.2 11.8 %collective-permute-start.3 = (bf16[48,640]{1,0:T(8,128)(2,1)S(1)}, bf16[48,640]{1,0:T(8,128)(2,1)S(1)}, u32[]{:S(2)}, u32[]{:S(2)}) collective-permute-start(bf16[48,640]{1,0:T(8,128)(2,1)S(1)} %get-tuple-element.28.refs_1_), channel_id=1, source_target_pairs={{0,4},{1,5},{2,6},{3,7},{4,0},{5,1},{6,2},{7,3},{8,12},{9,13},{10,... | collective-permute-start | bytes 184328 | tf_op jit(solution)/shard_map/ppermute | solution.py:43
  9.8 10.2 %collective-permute-start.4 = (bf16[48,640]{1,0:T(8,128)(2,1)S(1)}, bf16[48,640]{1,0:T(8,128)(2,1)S(1)}, u32[]{:S(2)}, u32[]{:S(2)}) collective-permute-start(bf16[48,640]{1,0:T(8,128)(2,1)S(1)} %get-tuple-element.29), channel_id=1, source_target_pairs={{0,8},{1,9},{2,10},{3,11},{4,12},{5,13},{6,14},{7,15},{8,0},{9,1},... | collective-permute-start | bytes 184328 | tf_op jit(solution)/shard_map/ppermute | solution.py:43
  12.4 7.7 %collective-permute-start.5 = (bf16[48,640]{1,0:T(8,128)(2,1)S(1)}, bf16[48,640]{1,0:T(8,128)(2,1)S(1)}, u32[]{:S(2)}, u32[]{:S(2)}) collective-permute-start(bf16[48,640]{1,0:T(8,128)(2,1)S(1)} %get-tuple-element.30), channel_id=1, source_target_pairs={{0,12},{1,13},{2,14},{3,15},{4,8},{5,9},{6,10},{7,11},{8,4},{9,5},... | collective-permute-start | bytes 184328 | tf_op jit(solution)/shard_map/ppermute | solution.py:43
  15.5 6.4 %collective-permute-start.7 = (bf16[16,2560]{1,0:T(8,128)(2,1)S(1)}, bf16[16,2560]{1,0:T(8,128)(2,1)S(1)}, u32[]{:S(2)}, u32[]{:S(2)}) collective-permute-start(bf16[16,2560]{1,0:T(8,128)(2,1)S(1)} %get-tuple-element.54.refs_1_), channel_id=1, source_target_pairs={{0,4},{1,5},{2,6},{3,7},{4,0},{5,1},{6,2},{7,3},{8,12},{9,13},{10,... | collective-permute-start | bytes 245768 | tf_op jit(solution)/shard_map/ppermute | solution.py:43
  17.4 7.8 %collective-permute-start.8 = (bf16[16,2560]{1,0:T(8,128)(2,1)S(1)}, bf16[16,2560]{1,0:T(8,128)(2,1)S(1)}, u32[]{:S(2)}, u32[]{:S(2)}) collective-permute-start(bf16[16,2560]{1,0:T(8,128)(2,1)S(1)} %get-tuple-element.53.refs_2_), channel_id=1, source_target_pairs={{0,8},{1,9},{2,10},{3,11},{4,12},{5,13},{6,14},{7,15},{8,0},{9,1},... | collective-permute-start | bytes 245768 | tf_op jit(solution)/shard_map/ppermute | solution.py:43
  19.9 6.4 %collective-permute-start.9 = (bf16[16,2560]{1,0:T(8,128)(2,1)S(1)}, bf16[16,2560]{1,0:T(8,128)(2,1)S(1)}, u32[]{:S(2)}, u32[]{:S(2)}) collective-permute-start(bf16[16,2560]{1,0:T(8,128)(2,1)S(1)} %get-tuple-element.52.refs_3_), channel_id=1, source_target_pairs={{0,12},{1,13},{2,14},{3,15},{4,8},{5,9},{6,10},{7,11},{8,4},{9,5},... | collective-permute-start | bytes 245768 | tf_op jit(solution)/shard_map/ppermute | solution.py:43
  20.1 11.4 %collective-permute-start.6 = (bf16[192,640]{1,0:T(8,128)(2,1)S(1)}, bf16[192,640]{1,0:T(8,128)(2,1)S(1)}, u32[]{:S(2)}, u32[]{:S(2)}) collective-permute-start(bf16[192,640]{1,0:T(8,128)(2,1)S(1)} %pad_maximum_fusion.refs_0_), channel_id=1, source_target_pairs={{0,2},{1,3},{2,0},{3,1},{4,6},{5,7},{6,4},{7,5},{8,10},{9,11},{10,... | collective-permute-start | bytes 737288 | tf_op jit(solution)/shard_map/ppermute | solution.py:43
  21.9 15.3 %collective-permute-start.10 = (bf16[192,640]{1,0:T(8,128)(2,1)S(1)}, bf16[192,640]{1,0:T(8,128)(2,1)S(1)}, u32[]{:S(2)}, u32[]{:S(2)}) collective-permute-start(bf16[192,640]{1,0:T(8,128)(2,1)S(1)} %pad_maximum_fusion.refs_0_), channel_id=1, source_target_pairs={{0,1},{1,0},{2,3},{3,2},{4,5},{5,4},{6,7},{7,6},{8,9},{9,8},{10,11... | collective-permute-start | bytes 737288 | tf_op jit(solution)/shard_map/ppermute | solution.py:43
  27.0 4.6 %collective-permute-start.12 = (bf16[48,512]{1,0:T(8,128)(2,1)S(1)}, bf16[48,512]{1,0:T(8,128)(2,1)S(1)}, u32[]{:S(2)}, u32[]{:S(2)}) collective-permute-start(bf16[48,512]{1,0:T(8,128)(2,1)S(1)} %get-tuple-element.32.refs_1_), channel_id=1, source_target_pairs={{0,4},{1,5},{2,6},{3,7},{4,0},{5,1},{6,2},{7,3},{8,12},{9,13},{10,... | collective-permute-start | bytes 147464 | tf_op jit(solution)/shard_map/ppermute | solution.py:43
  28.2 5.7 %collective-permute-start.13 = (bf16[48,512]{1,0:T(8,128)(2,1)S(1)}, bf16[48,512]{1,0:T(8,128)(2,1)S(1)}, u32[]{:S(2)}, u32[]{:S(2)}) collective-permute-start(bf16[48,512]{1,0:T(8,128)(2,1)S(1)} %get-tuple-element.34), channel_id=1, source_target_pairs={{0,8},{1,9},{2,10},{3,11},{4,12},{5,13},{6,14},{7,15},{8,0},{9,1},... | collective-permute-start | bytes 147464 | tf_op jit(solution)/shard_map/ppermute | solution.py:43
  29.8 5.9 %collective-permute-start.14 = (bf16[48,512]{1,0:T(8,128)(2,1)S(1)}, bf16[48,512]{1,0:T(8,128)(2,1)S(1)}, u32[]{:S(2)}, u32[]{:S(2)}) collective-permute-start(bf16[48,512]{1,0:T(8,128)(2,1)S(1)} %get-tuple-element.35), channel_id=1, source_target_pairs={{0,12},{1,13},{2,14},{3,15},{4,8},{5,9},{6,10},{7,11},{8,4},{9,5},... | collective-permute-start | bytes 147464 | tf_op jit(solution)/shard_map/ppermute | solution.py:43
  31.5 5.7 %collective-permute-start.11 = (bf16[192,640]{1,0:T(8,128)(2,1)S(1)}, bf16[192,640]{1,0:T(8,128)(2,1)S(1)}, u32[]{:S(2)}, u32[]{:S(2)}) collective-permute-start(bf16[192,640]{1,0:T(8,128)(2,1)S(1)} %tie.14.refs_1_), channel_id=1, source_target_pairs={{0,1},{1,0},{2,3},{3,2},{4,5},{5,4},{6,7},{7,6},{8,9},{9,8},{10,11... | collective-permute-start | bytes 737288 | tf_op jit(solution)/shard_map/ppermute | solution.py:43
  35.7 12.9 %collective-permute-start.15 = (bf16[192,512]{1,0:T(8,128)(2,1)S(1)}, bf16[192,512]{1,0:T(8,128)(2,1)S(1)}, u32[]{:S(2)}, u32[]{:S(2)}) collective-permute-start(bf16[192,512]{1,0:T(8,128)(2,1)S(1)} %constant_dynamic-update-slice_fusion.refs_7_.refs_0_), channel_id=1, source_target_pairs={{0,2},{1,3},{2,0},{3,1},{4,6},{5,7},{6,4},{7,5},{8,10},{9,11},{10,... | collective-permute-start | bytes 589832 | tf_op jit(solution)/shard_map/ppermute | solution.py:43
  48.6 1.6 %collective-permute-start.17 = (bf16[192,640]{1,0:T(8,128)(2,1)S(1)}, bf16[192,640]{1,0:T(8,128)(2,1)S(1)}, u32[]{:S(2)}, u32[]{:S(2)}) collective-permute-start(bf16[192,640]{1,0:T(8,128)(2,1)S(1)} %tie.17), channel_id=1, source_target_pairs={{0,1},{1,0},{2,3},{3,2},{4,5},{5,4},{6,7},{7,6},{8,9},{9,8},{10,11... | collective-permute-start | bytes 737288 | tf_op jit(solution)/shard_map/ppermute | solution.py:43
  48.7 2.2 %collective-permute-start.19 = (bf16[192,512]{1,0:T(8,128)(2,1)S(1)}, bf16[192,512]{1,0:T(8,128)(2,1)S(1)}, u32[]{:S(2)}, u32[]{:S(2)}) collective-permute-start(bf16[192,512]{1,0:T(8,128)(2,1)S(1)} %constant_dynamic-update-slice_fusion.refs_7_.refs_0_), channel_id=1, source_target_pairs={{0,1},{1,0},{2,3},{3,2},{4,5},{5,4},{6,7},{7,6},{8,9},{9,8},{10,11... | collective-permute-start | bytes 589832 | tf_op jit(solution)/shard_map/ppermute | solution.py:43
  49.2 1.7 %collective-permute-start.20 = (bf16[192,512]{1,0:T(8,128)(2,1)S(1)}, bf16[192,512]{1,0:T(8,128)(2,1)S(1)}, u32[]{:S(2)}, u32[]{:S(2)}) collective-permute-start(bf16[192,512]{1,0:T(8,128)(2,1)S(1)} %tie.15.refs_1_), channel_id=1, source_target_pairs={{0,1},{1,0},{2,3},{3,2},{4,5},{5,4},{6,7},{7,6},{8,9},{9,8},{10,11... | collective-permute-start | bytes 589832 | tf_op jit(solution)/shard_map/ppermute | solution.py:43
  49.6 11.6 %collective-permute-start.16 = (bf16[192,640]{1,0:T(8,128)(2,1)S(1)}, bf16[192,640]{1,0:T(8,128)(2,1)S(1)}, u32[]{:S(2)}, u32[]{:S(2)}) collective-permute-start(bf16[192,640]{1,0:T(8,128)(2,1)S(1)} %tie.16), channel_id=1, source_target_pairs={{0,1},{1,0},{2,3},{3,2},{4,5},{5,4},{6,7},{7,6},{8,9},{9,8},{10,11... | collective-permute-start | bytes 737288 | tf_op jit(solution)/shard_map/ppermute | solution.py:43
  50.3 8.1 %collective-permute-start.18 = (bf16[192,640]{1,0:T(8,128)(2,1)S(1)}, bf16[192,640]{1,0:T(8,128)(2,1)S(1)}, u32[]{:S(2)}, u32[]{:S(2)}) collective-permute-start(bf16[192,640]{1,0:T(8,128)(2,1)S(1)} %tie.18.refs_7_), channel_id=1, source_target_pairs={{0,2},{1,3},{2,0},{3,1},{4,6},{5,7},{6,4},{7,5},{8,10},{9,11},{10,... | collective-permute-start | bytes 737288 | tf_op jit(solution)/shard_map/ppermute | solution.py:43
  58.4 1.5 %collective-permute-start.21 = (bf16[192,512]{1,0:T(8,128)(2,1)S(1)}, bf16[192,512]{1,0:T(8,128)(2,1)S(1)}, u32[]{:S(2)}, u32[]{:S(2)}) collective-permute-start(bf16[192,512]{1,0:T(8,128)(2,1)S(1)} %tie.20), channel_id=1, source_target_pairs={{0,1},{1,0},{2,3},{3,2},{4,5},{5,4},{6,7},{7,6},{8,9},{9,8},{10,11... | collective-permute-start | bytes 589832 | tf_op jit(solution)/shard_map/ppermute | solution.py:43
  58.5 7.3 %collective-permute-start.25 = (bf16[192,512]{1,0:T(8,128)(2,1)S(1)}, bf16[192,512]{1,0:T(8,128)(2,1)S(1)}, u32[]{:S(2)}, u32[]{:S(2)}) collective-permute-start(bf16[192,512]{1,0:T(8,128)(2,1)S(1)} %tie.23), channel_id=1, source_target_pairs={{0,1},{1,0},{2,3},{3,2},{4,5},{5,4},{6,7},{7,6},{8,9},{9,8},{10,11... | collective-permute-start | bytes 589832 | tf_op jit(solution)/shard_map/ppermute | solution.py:43
  59.9 7.0 %collective-permute-start.26 = (bf16[192,512]{1,0:T(8,128)(2,1)S(1)}, bf16[192,512]{1,0:T(8,128)(2,1)S(1)}, u32[]{:S(2)}, u32[]{:S(2)}) collective-permute-start(bf16[192,512]{1,0:T(8,128)(2,1)S(1)} %tie.21.refs_1_), channel_id=1, source_target_pairs={{0,2},{1,3},{2,0},{3,1},{4,6},{5,7},{6,4},{7,5},{8,10},{9,11},{10,... | collective-permute-start | bytes 589832 | tf_op jit(solution)/shard_map/ppermute | solution.py:43
  61.2 15.0 %copy-start.1 = (bf16[256,2560]{1,0:T(8,128)(2,1)S(1)}, bf16[256,2560]{1,0:T(8,128)(2,1)}, u32[]{:S(2)}) copy-start(bf16[256,2560]{1,0:T(8,128)(2,1)} %param.14) | copy-start | bytes 3932164
  61.3 8.0 %collective-permute-start.22 = (bf16[48,640]{1,0:T(8,128)(2,1)S(1)}, bf16[48,640]{1,0:T(8,128)(2,1)S(1)}, u32[]{:S(2)}, u32[]{:S(2)}) collective-permute-start(bf16[48,640]{1,0:T(8,128)(2,1)S(1)} %get-tuple-element.57), channel_id=1, source_target_pairs={{0,4},{1,5},{2,6},{3,7},{4,0},{5,1},{6,2},{7,3},{8,12},{9,13},{10,... | collective-permute-start | bytes 184328 | tf_op jit(solution)/shard_map/ppermute | solution.py:43
  61.4 10.1 %collective-permute-start.23 = (bf16[48,640]{1,0:T(8,128)(2,1)S(1)}, bf16[48,640]{1,0:T(8,128)(2,1)S(1)}, u32[]{:S(2)}, u32[]{:S(2)}) collective-permute-start(bf16[48,640]{1,0:T(8,128)(2,1)S(1)} %get-tuple-element.56), channel_id=1, source_target_pairs={{0,8},{1,9},{2,10},{3,11},{4,12},{5,13},{6,14},{7,15},{8,0},{9,1},... | collective-permute-start | bytes 184328 | tf_op jit(solution)/shard_map/ppermute | solution.py:43
  63.7 7.8 %collective-permute-start.24 = (bf16[48,640]{1,0:T(8,128)(2,1)S(1)}, bf16[48,640]{1,0:T(8,128)(2,1)S(1)}, u32[]{:S(2)}, u32[]{:S(2)}) collective-permute-start(bf16[48,640]{1,0:T(8,128)(2,1)S(1)} %get-tuple-element.55), channel_id=1, source_target_pairs={{0,12},{1,13},{2,14},{3,15},{4,8},{5,9},{6,10},{7,11},{8,4},{9,5},... | collective-permute-start | bytes 184328 | tf_op jit(solution)/shard_map/ppermute | solution.py:43
  67.1 5.4 %collective-permute-start.27 = (bf16[48,512]{1,0:T(8,128)(2,1)S(1)}, bf16[48,512]{1,0:T(8,128)(2,1)S(1)}, u32[]{:S(2)}, u32[]{:S(2)}) collective-permute-start(bf16[48,512]{1,0:T(8,128)(2,1)S(1)} %get-tuple-element.61), channel_id=1, source_target_pairs={{0,4},{1,5},{2,6},{3,7},{4,0},{5,1},{6,2},{7,3},{8,12},{9,13},{10,... | collective-permute-start | bytes 147464 | tf_op jit(solution)/shard_map/ppermute | solution.py:43
  67.1 5.3 %collective-permute-start.28 = (bf16[48,512]{1,0:T(8,128)(2,1)S(1)}, bf16[48,512]{1,0:T(8,128)(2,1)S(1)}, u32[]{:S(2)}, u32[]{:S(2)}) collective-permute-start(bf16[48,512]{1,0:T(8,128)(2,1)S(1)} %get-tuple-element.60), channel_id=1, source_target_pairs={{0,8},{1,9},{2,10},{3,11},{4,12},{5,13},{6,14},{7,15},{8,0},{9,1},... | collective-permute-start | bytes 147464 | tf_op jit(solution)/shard_map/ppermute | solution.py:43
  69.4 5.9 %collective-permute-start.29 = (bf16[48,512]{1,0:T(8,128)(2,1)S(1)}, bf16[48,512]{1,0:T(8,128)(2,1)S(1)}, u32[]{:S(2)}, u32[]{:S(2)}) collective-permute-start(bf16[48,512]{1,0:T(8,128)(2,1)S(1)} %get-tuple-element.59), channel_id=1, source_target_pairs={{0,12},{1,13},{2,14},{3,15},{4,8},{5,9},{6,10},{7,11},{8,4},{9,5},... | collective-permute-start | bytes 147464 | tf_op jit(solution)/shard_map/ppermute | solution.py:43

commit v15 on v14

--- a/solution.py
+++ b/solution.py
@@ -10,7 +10,7 @@
 PLEN = 128
 HINT = 1 << 33
 STRIP = 512
-LIMIT = 24 << 20
+LIMIT = 8 << 20
 VMEM = pl.BlockSpec(memory_space=pltpu.VMEM)
 SMEM = pl.BlockSpec(memory_space=pltpu.SMEM)
 ANY = pl.BlockSpec(memory_space=pl.ANY)
@@ -215,27 +215,43 @@
     return list(zip(edges[:-1], edges[1:]))
 
 
-def expert_kernel(packing, unit_cuts, count, after, fetch, *refs):
-    row_refs = refs[:count]
-    gate_hbm, up_hbm, down_hbm = refs[count : count + 3]
+def concat_kernel(count, *refs):
+    refs[-1][...] = jnp.concatenate([ref[...] for ref in refs[:count]], axis=0)
+
+
+def concat(values, after):
+    rows, columns = values[0].shape
+    return pl.pallas_call(
+        functools.partial(concat_kernel, len(values)),
+        out_shape=jax.ShapeDtypeStruct((rows * len(values), columns), values[0].dtype),
+        in_specs=[VMEM] * len(values) + [ANY] * len(after),
+        out_specs=VMEM,
+        compiler_params=pltpu.CompilerParams(vmem_limit_bytes=8 << 20),
+        name="concat",
+    )(*values, *after)
+
+
+def expert_kernel(packing, unit_cuts, count, after, held, *refs):
+    row_refs, sources = refs[:count], refs[count : count + 3]
     place = count + 3 + after
-    out_refs = refs[place : place + count]
-    if fetch:
-        gate_ref, up_ref, down_ref, rows_ref, total_ref, packed_ref, sems = refs[place + count :]
-    else:
-        gate_ref, up_ref, down_ref = gate_hbm, up_hbm, down_hbm
-        rows_ref, total_ref, packed_ref = refs[place + count :]
-    copies = []
+    out_refs, refs = refs[place : place + count], refs[place + count :]
+    weight_refs = sources[:held] + refs[: 3 - held]
+    gate_ref, up_ref, down_ref = weight_refs
+    rows_ref, total_ref, packed_ref = refs[3 - held : 6 - held]
+    copies = [[] for _ in unit_cuts]
     for i, (lo, hi) in enumerate(unit_cuts):
-        for t, (source, target) in enumerate(
-            ((gate_hbm, gate_ref), (up_hbm, up_ref), (down_hbm, down_ref))
-        ):
-            if fetch:
-                copies.append(
-                    pltpu.make_async_copy(source.at[lo:hi], target.at[lo:hi], sems.at[3 * i + t])
+        for t in range(held, 3):
+            copies[i].append(
+                pltpu.make_async_copy(
+                    sources[t].at[lo:hi], weight_refs[t].at[lo:hi], refs[-1].at[3 * i + t]
                 )
-    for copy in copies[:2]:
-        copy.start()
+            )
+
+    def start(i):
+        for copy in copies[i] if i < len(copies) else []:
+            copy.start()
+
+    start(0)
 
     cap, chunks, width, high = packing.cap, packing.chunks, packing.width, packing.rows
     per_ref = row_refs[0].shape[0] // high
@@ -254,8 +270,7 @@
                 total_ref[j * lanes + c, pl.ds(slot, blocks, stride=cap), :] = packed_ref[
                     c, pl.ds(j * cap + slot, blocks, stride=high), :
                 ]
-    for copy in copies[2:6]:
-        copy.start()
+    start(1)
     for c in range(chunks * lanes):
         part = total_ref[c, 0:rows, :]
         if spare:
@@ -271,7 +286,7 @@
             else:
                 total_ref[c, 0:rows, :] += term[:, c * 128 : (c + 1) * 128]
 
-    features = gate_hbm.shape[1]
+    features = gate_ref.shape[1]
 
     def product(weight_ref, lo, hi):
         terms = [
@@ -289,15 +304,16 @@
 
     inner = None
     for i, (lo, hi) in enumerate(unit_cuts):
-        for copy in copies[max(3 * i - 1, 0) : 3 * i + 2]:
+        for copy in copies[i - 1][-1:] if i > 0 else []:
             copy.wait()
-        for copy in copies[3 * (i + 2) : 3 * (i + 3)]:
-            copy.start()
+        for copy in copies[i][:-1]:
+            copy.wait()
+        start(i + 2)
         following = product(gate_ref, lo, hi), product(up_ref, lo, hi)
         if i > 0:
             down(i - 1, gated(*inner))
         inner = following
-    for copy in copies[-1:]:
+    for copy in copies[-1][-1:]:
         copy.wait()
     down(len(unit_cuts) - 1, gated(*inner))
 
@@ -318,17 +334,17 @@
             ref[:, columns] = part.astype(jnp.bfloat16)
 
 
-def expert_rows(arrays, w_gate, w_up, w_down, packing, after, fetch):
-    units, features = w_down.shape
+def expert_rows(arrays, weights, packing, after, held):
+    units, features = weights[2].shape
     rows = len(arrays) * (arrays[0].shape[0] // packing.rows) * packing.cap
     unit_cuts = cuts(units)
     weight = jax.ShapeDtypeStruct((units, features), jnp.bfloat16)
-    kept = 3 if fetch else 0
+    kept = 3 - held
     results = pl.pallas_call(
-        functools.partial(expert_kernel, packing, unit_cuts, len(arrays), len(after), fetch),
+        functools.partial(expert_kernel, packing, unit_cuts, len(arrays), len(after), held),
         out_shape=[jax.ShapeDtypeStruct(arrays[0].shape, jnp.bfloat16)] * len(arrays)
         + [weight] * kept,
-        in_specs=[VMEM] * len(arrays) + [HBM if fetch else VMEM] * 3 + [ANY] * len(after),
+        in_specs=[VMEM] * (len(arrays) + held) + [HBM] * kept + [ANY] * len(after),
         out_specs=[VMEM] * (len(arrays) + kept),
         scratch_shapes=[
             pltpu.VMEM((features, -(-rows // 128) * 128), jnp.bfloat16),
@@ -338,16 +354,17 @@
                 jnp.float32,
             ),
         ]
-        + [pltpu.SemaphoreType.DMA((3 * len(unit_cuts),))] * (kept // 3),
-        compiler_params=pltpu.CompilerParams(vmem_limit_bytes=LIMIT),
+        + [pltpu.SemaphoreType.DMA((3 * len(unit_cuts),))] * (kept > 0),
+        compiler_params=pltpu.CompilerParams(vmem_limit_bytes=(8 << 20) + 12 * rows * features),
         cost_estimate=pl.CostEstimate(
             flops=6 * rows * features * units,
             bytes_accessed=6 * features * units,
             transcendentals=rows * units,
         ),
         name="experts",
-    )(*arrays, w_gate, w_up, w_down, *after)
-    return list(results[: len(arrays)]), list(results[len(arrays) :])
+    )(*arrays, *weights, *after)
+    results = list(results)
+    return results[: len(arrays)], list(weights[:held]) + results[len(arrays) :]
 
 
 def combine_kernel(packing, spot_ref, weight_ref, *refs):
@@ -496,13 +513,13 @@
     received = to_experts(blocks)
     image_own = image_own[:1] + [tie([value], blocks[1:2]) for value in image_own[1:]]
     image_arrays = image_own + over_cores(image_own)
-    caption_first = jnp.concatenate([blocks[0]] + received, axis=0)
+    caption_first = concat([blocks[0]] + received, [])
     caption_own = to_pairs(caption_first)
 
     image_weights = route(image_normed, image_spot, small)
     caption_weights = route(caption_normed, caption_spot, small)
     image_results, weights = expert_rows(
-        image_arrays, *weights, image_packing, [caption_first, image_weights], True
+        image_arrays, weights, image_packing, [caption_first, image_weights], 3
     )
     caption_own = caption_own[:1] + [tie([value], image_results[:1]) for value in caption_own[1:]]
     image_results = image_results[:pairs] + [
@@ -511,10 +528,10 @@
     image_kept, image_crossing = join_cores(image_results)
     caption_results, _ = expert_rows(
         caption_own + over_cores(caption_own),
-        *weights,
+        weights,
         caption_packing,
         image_crossing[:1] + [caption_weights],
-        False,
+        3,
     )
     image_received = [
         tie([value], caption_results[:1]) for value in from_pairs(image_crossing)

time: 76.3 us -> 73.7 us (0.966)
  Pallas kernels: 22.5 us -> 19 us
  waiting for transfers between devices: 16.9 us -> 17.7 us
    pallas_call x2, Pallas kernels: 18.5 us -> 14.9 us  [expert_rows(): pl.pallas_call(functools.partial(expert_kernel, packing, unit_cuts, len(a...]
    ppermute x30, waiting for transfers between devices: 16.9 us -> 17.7 us  [swap(): return lax.ppermute(value, 'dev', moves)]
  transfers between devices with their start and end apart: 30 -> 30, of which waited for: 11 -> 12; matrix products, arithmetic and copies ran while one was open for 1% -> 1% of each run, Pallas kernels for 28% -> 25%
where the time goes in v15:
time: 73.7 us; the launch traced here: 73.6 us
  starting transfers between devices  32.9 us (45%)
  Pallas kernels  19 us (26%)
  waiting for transfers between devices  17.7 us (24%)
  other arithmetic  1.83 us (2%)
  between operations  1.27 us (2%)
    ppermute x30, starting transfers between devices, swap(): return lax.ppermute(value, 'dev', moves)  32.9 us
    ppermute x30, waiting for transfers between devices, swap(): return lax.ppermute(value, 'dev', moves)  17.7 us
    pallas_call x2, Pallas kernels, expert_rows(): pl.pallas_call(functools.partial(expert_kernel, packing, unit_cuts, len(a...  14.9 us
    pallas_call x2, Pallas kernels, combine(): pl.pallas_call(functools.partial(combine_kernel, packing), out_shape=jax....  1.77 us
  transfers between devices with their start and end apart: 30, of which 12 were waited for; matrix products, arithmetic and copies ran while one was open for 1% of the time, Pallas kernels for 25%

profile of v15, /device:TPU:0, one launch (start us, length us, event | category | flops | bytes accessed | tf_op | source)
XLA Modules:
  0.0 73.6 jit_solution(15403862966000000875)
XLA Ops:
  0.6 0.0 copy-start
  0.7 1.1 %fusion.5 = bf16[2,2,2,2,16,256]{5,4,3,2,1,0:T(8,128)(2,1)S(1)} fusion(s32[]{:T(128)S(6)} %select_n.80, bf16[2,2,2,2,16,256]{5,4,3,2,1,0:T(8,128)(2,1)} %bitcast.35), kind=kLoop, calls=%fused_computation.19 | loop fusion | flops 65536 | bytes 262148 | tf_op jit(solution)/shard_map/jit(_roll_dynamic)/concatenate | solution.py:412
  1.8 0.1 fusion.3
  1.9 0.1 fusion.2
  2.0 0.0 copy-start.5
  2.1 0.0 copy-start.6
  2.1 0.3 convolution_convert_fusion
  2.5 0.5 collective-permute-start
  3.0 0.1 collective-permute-start.1
  3.1 0.1 fusion.7
  3.3 0.3 fusion.16
  3.7 0.0 copy-start.2
  3.7 0.6 collective-permute-done
  4.3 0.1 fusion.1.refs_0_
  4.3 3.0 %collective-permute-start.2 = (bf16[64,2560]{1,0:T(8,128)(2,1)S(1)}, bf16[64,2560]{1,0:T(8,128)(2,1)S(1)}, u32[]{:S(2)}, u32[]{:S(2)}) collective-permute-start(bf16[64,2560]{1,0:T(8,128)(2,1)S(1)} %fusion.1.refs_0_), channel_id=1, source_target_pairs={{0,2},{1,3},{2,0},{3,1},{4,6},{5,7},{6,4},{7,5},{8,10},{9,11},{10,... | collective-permute-start | bytes 983048 | tf_op jit(solution)/shard_map/ppermute | solution.py:43
  7.3 0.8 %prepare.1 = (f32[16,4]{1,0:T(8,128)S(1)}, f32[16,4]{1,0:T(8,128)S(1)}, bf16[16,2560]{1,0:T(8,128)(2,1)S(1)}, bf16[48,640]{1,0:T(8,128)(2,1)S(1)}, bf16[48,640]{...) custom-call(s32[4,16]{1,0:T(4,128)S(1)} %pad_add_fusion.ids_ref, ...), custom_call_target="tpu_custom_call" | custom-call | tf_op jit(solution)/shard_map/prepare/pallas_call | solution.py:125
  8.2 3.6 %collective-permute-start.5 = (bf16[48,640]{1,0:T(8,128)(2,1)S(1)}, bf16[48,640]{1,0:T(8,128)(2,1)S(1)}, u32[]{:S(2)}, u32[]{:S(2)}) collective-permute-start(bf16[48,640]{1,0:T(8,128)(2,1)S(1)} %get-tuple-element.27), channel_id=1, source_target_pairs={{0,12},{1,13},{2,14},{3,15},{4,8},{5,9},{6,10},{7,11},{8,4},{9,5},... | collective-permute-start | bytes 184328 | tf_op jit(solution)/shard_map/ppermute | solution.py:43
  11.8 0.8 %collective-permute-start.3 = (bf16[48,640]{1,0:T(8,128)(2,1)S(1)}, bf16[48,640]{1,0:T(8,128)(2,1)S(1)}, u32[]{:S(2)}, u32[]{:S(2)}) collective-permute-start(bf16[48,640]{1,0:T(8,128)(2,1)S(1)} %get-tuple-element.25.refs_1_), channel_id=1, source_target_pairs={{0,4},{1,5},{2,6},{3,7},{4,0},{5,1},{6,2},{7,3},{8,12},{9,13},{10,... | collective-permute-start | bytes 184328 | tf_op jit(solution)/shard_map/ppermute | solution.py:43
  12.6 2.7 %collective-permute-done.2.refs_0_ = bf16[64,2560]{1,0:T(8,128)(2,1)S(1)} collective-permute-done((bf16[64,2560]{1,0:T(8,128)(2,1)S(1)}, bf16[64,2560]{1,0:T(8,128)(2,1)S(1)}, u32[]{:S(2)}, u32[]{:S(2)}) %collective-permute-start.2) | collective-permute-done | bytes 327712 | tf_op jit(solution)/shard_map/ppermute | solution.py:43
  15.3 0.1 fusion.9
  15.5 1.9 %collective-permute-start.7 = (bf16[16,2560]{1,0:T(8,128)(2,1)S(1)}, bf16[16,2560]{1,0:T(8,128)(2,1)S(1)}, u32[]{:S(2)}, u32[]{:S(2)}) collective-permute-start(bf16[16,2560]{1,0:T(8,128)(2,1)S(1)} %get-tuple-element.48.refs_1_), channel_id=1, source_target_pairs={{0,4},{1,5},{2,6},{3,7},{4,0},{5,1},{6,2},{7,3},{8,12},{9,13},{10,... | collective-permute-start | bytes 245768 | tf_op jit(solution)/shard_map/ppermute | solution.py:43
  17.4 2.5 %collective-permute-start.8 = (bf16[16,2560]{1,0:T(8,128)(2,1)S(1)}, bf16[16,2560]{1,0:T(8,128)(2,1)S(1)}, u32[]{:S(2)}, u32[]{:S(2)}) collective-permute-start(bf16[16,2560]{1,0:T(8,128)(2,1)S(1)} %get-tuple-element.47.refs_2_), channel_id=1, source_target_pairs={{0,8},{1,9},{2,10},{3,11},{4,12},{5,13},{6,14},{7,15},{8,0},{9,1},... | collective-permute-start | bytes 245768 | tf_op jit(solution)/shard_map/ppermute | solution.py:43
  19.9 0.1 collective-permute-start.9
  20.1 1.8 %collective-permute-start.6 = (bf16[192,640]{1,0:T(8,128)(2,1)S(1)}, bf16[192,640]{1,0:T(8,128)(2,1)S(1)}, u32[]{:S(2)}, u32[]{:S(2)}) collective-permute-start(bf16[192,640]{1,0:T(8,128)(2,1)S(1)} %pad_maximum_fusion.refs_0_), channel_id=1, source_target_pairs={{0,2},{1,3},{2,0},{3,1},{4,6},{5,7},{6,4},{7,5},{8,10},{9,11},{10,... | collective-permute-start | bytes 737288 | tf_op jit(solution)/shard_map/ppermute | solution.py:43
  21.9 3.2 %collective-permute-done.8.refs_2_ = bf16[16,2560]{1,0:T(8,128)(2,1)S(1)} collective-permute-done((bf16[16,2560]{1,0:T(8,128)(2,1)S(1)}, bf16[16,2560]{1,0:T(8,128)(2,1)S(1)}, u32[]{:S(2)}, u32[]{:S(2)}) %collective-permute-start.8) | collective-permute-done | bytes 81952 | tf_op jit(solution)/shard_map/ppermute | solution.py:43
  25.1 1.2 %collective-permute-done.9.refs_3_ = bf16[16,2560]{1,0:T(8,128)(2,1)S(1)} collective-permute-done((bf16[16,2560]{1,0:T(8,128)(2,1)S(1)}, bf16[16,2560]{1,0:T(8,128)(2,1)S(1)}, u32[]{:S(2)}, u32[]{:S(2)}) %collective-permute-start.9) | collective-permute-done | bytes 81952 | tf_op jit(solution)/shard_map/ppermute | solution.py:43
  26.4 0.0 slice-start.7
  26.4 0.6 modulate.1
  27.1 0.1 collective-permute-start.11
  27.2 1.2 %collective-permute-start.12 = (bf16[48,512]{1,0:T(8,128)(2,1)S(1)}, bf16[48,512]{1,0:T(8,128)(2,1)S(1)}, u32[]{:S(2)}, u32[]{:S(2)}) collective-permute-start(bf16[48,512]{1,0:T(8,128)(2,1)S(1)} %get-tuple-element.29.refs_1_), channel_id=1, source_target_pairs={{0,4},{1,5},{2,6},{3,7},{4,0},{5,1},{6,2},{7,3},{8,12},{9,13},{10,... | collective-permute-start | bytes 147464 | tf_op jit(solution)/shard_map/ppermute | solution.py:43
  28.4 2.6 %collective-permute-start.13 = (bf16[48,512]{1,0:T(8,128)(2,1)S(1)}, bf16[48,512]{1,0:T(8,128)(2,1)S(1)}, u32[]{:S(2)}, u32[]{:S(2)}) collective-permute-start(bf16[48,512]{1,0:T(8,128)(2,1)S(1)} %get-tuple-element.31), channel_id=1, source_target_pairs={{0,8},{1,9},{2,10},{3,11},{4,12},{5,13},{6,14},{7,15},{8,0},{9,1},... | collective-permute-start | bytes 147464 | tf_op jit(solution)/shard_map/ppermute | solution.py:43
  31.0 0.6 collective-permute-start.14
  31.6 0.3 route.2.refs_8_.weight_ref
  31.9 2.6 %collective-permute-done.13.refs_2_ = bf16[48,512]{1,0:T(8,128)(2,1)S(1)} collective-permute-done((bf16[48,512]{1,0:T(8,128)(2,1)S(1)}, bf16[48,512]{1,0:T(8,128)(2,1)S(1)}, u32[]{:S(2)}, u32[]{:S(2)}) %collective-permute-start.13) | collective-permute-done | bytes 49184 | tf_op jit(solution)/shard_map/ppermute | solution.py:43
  34.5 2.4 %collective-permute-done.14.refs_3_ = bf16[48,512]{1,0:T(8,128)(2,1)S(1)} collective-permute-done((bf16[48,512]{1,0:T(8,128)(2,1)S(1)}, bf16[48,512]{1,0:T(8,128)(2,1)S(1)}, u32[]{:S(2)}, u32[]{:S(2)}) %collective-permute-start.14) | collective-permute-done | bytes 49184 | tf_op jit(solution)/shard_map/ppermute | solution.py:43
  36.9 1.6 %collective-permute-start.15 = (bf16[192,512]{1,0:T(8,128)(2,1)S(1)}, bf16[192,512]{1,0:T(8,128)(2,1)S(1)}, u32[]{:S(2)}, u32[]{:S(2)}) collective-permute-start(bf16[192,512]{1,0:T(8,128)(2,1)S(1)} %concat.1.refs_7_.refs_0_), channel_id=1, source_target_pairs={{0,2},{1,3},{2,0},{3,1},{4,6},{5,7},{6,4},{7,5},{8,10},{9,11},{10,... | collective-permute-start | bytes 589832 | tf_op jit(solution)/shard_map/ppermute | solution.py:43
  38.6 7.8 %experts.2 = (bf16[192,640]{1,0:T(8,128)(2,1)S(1)}, bf16[192,640]{1,0:T(8,128)(2,1)S(1)}, bf16[192,640]{1,0:T(8,128)(2,1)S(1)}, bf16[192,640]{1,0:T(8,128)(2,1)S(1)}) custom-call(bf16[192,640]{1,0:T(8,128)(2,1)S(1)} %pad_maximum_fusion.refs_0_, bf16[192,640]{1,0:T(8,128)(2,1)S(1)} %tie.14.refs_1_, bf16[192,640]{1,0:T(8,128)(2,1)S(1)} %collective-permute-done.10.refs_2_, ...), custom_call_target="tpu_custom_call" | custom-call | flops 5096079360 | bytes 26542080 | tf_op jit(solution)/shard_map/experts/pallas_call | solution.py:343
  46.4 0.1 collective-permute-start.17
  46.5 0.5 collective-permute-start.19
  47.0 0.1 collective-permute-start.20
  47.1 0.3 route.3.refs_8_.weight_ref
  47.4 0.5 collective-permute-start.16
  47.9 0.1 collective-permute-done.17.refs_1_
  48.0 0.1 tie.18.refs_7_
  48.1 0.6 collective-permute-start.18
  48.6 7.1 %experts.3 = (bf16[192,512]{1,0:T(8,128)(2,1)S(1)}, bf16[192,512]{1,0:T(8,128)(2,1)S(1)}, bf16[192,512]{1,0:T(8,128)(2,1)S(1)}, bf16[192,512]{1,0:T(8,128)(2,1)S(1)}) custom-call(bf16[192,512]{1,0:T(8,128)(2,1)S(1)} %concat.1.refs_7_.refs_0_, bf16[192,512]{1,0:T(8,128)(2,1)S(1)} %tie.15.refs_1_, bf16[192,512]{1,0:T(8,128)(2,1)S(1)} %collective-permute-done.19.refs_2_, ...), custom_call_target="tpu_custom_call" | custom-call | flops 3822059520 | bytes 26542080 | tf_op jit(solution)/shard_map/experts/pallas_call | solution.py:343
  55.7 0.4 collective-permute-done.18.refs_0_
  56.2 0.1 collective-permute-start.21
  56.3 0.6 collective-permute-start.25
  56.8 0.8 %collective-permute-done.21.refs_1_ = bf16[192,512]{1,0:T(8,128)(2,1)S(1)} collective-permute-done((bf16[192,512]{1,0:T(8,128)(2,1)S(1)}, bf16[192,512]{1,0:T(8,128)(2,1)S(1)}, u32[]{:S(2)}, u32[]{:S(2)}) %collective-permute-start.21) | collective-permute-done | bytes 196640 | tf_op jit(solution)/shard_map/ppermute | solution.py:43
  57.8 1.2 %collective-permute-start.26 = (bf16[192,512]{1,0:T(8,128)(2,1)S(1)}, bf16[192,512]{1,0:T(8,128)(2,1)S(1)}, u32[]{:S(2)}, u32[]{:S(2)}) collective-permute-start(bf16[192,512]{1,0:T(8,128)(2,1)S(1)} %tie.21.refs_1_), channel_id=1, source_target_pairs={{0,2},{1,3},{2,0},{3,1},{4,6},{5,7},{6,4},{7,5},{8,10},{9,11},{10,... | collective-permute-start | bytes 589832 | tf_op jit(solution)/shard_map/ppermute | solution.py:43
  59.0 0.1 add_convert_fusion
  59.1 0.1 collective-permute-start.22
  59.2 1.8 %collective-permute-start.23 = (bf16[48,640]{1,0:T(8,128)(2,1)S(1)}, bf16[48,640]{1,0:T(8,128)(2,1)S(1)}, u32[]{:S(2)}, u32[]{:S(2)}) collective-permute-start(bf16[48,640]{1,0:T(8,128)(2,1)S(1)} %get-tuple-element.50), channel_id=1, source_target_pairs={{0,8},{1,9},{2,10},{3,11},{4,12},{5,13},{6,14},{7,15},{8,0},{9,1},... | collective-permute-start | bytes 184328 | tf_op jit(solution)/shard_map/ppermute | solution.py:43
  61.0 2.6 %collective-permute-start.24 = (bf16[48,640]{1,0:T(8,128)(2,1)S(1)}, bf16[48,640]{1,0:T(8,128)(2,1)S(1)}, u32[]{:S(2)}, u32[]{:S(2)}) collective-permute-start(bf16[48,640]{1,0:T(8,128)(2,1)S(1)} %get-tuple-element.49), channel_id=1, source_target_pairs={{0,12},{1,13},{2,14},{3,15},{4,8},{5,9},{6,10},{7,11},{8,4},{9,5},... | collective-permute-start | bytes 184328 | tf_op jit(solution)/shard_map/ppermute | solution.py:43
  63.6 1.2 %collective-permute-done.26 = bf16[192,512]{1,0:T(8,128)(2,1)S(1)} collective-permute-done((bf16[192,512]{1,0:T(8,128)(2,1)S(1)}, bf16[192,512]{1,0:T(8,128)(2,1)S(1)}, u32[]{:S(2)}, u32[]{:S(2)}) %collective-permute-start.26) | collective-permute-done | bytes 196640 | tf_op jit(solution)/shard_map/ppermute | solution.py:43
  64.8 0.1 add_convert_fusion.1
  64.9 0.1 collective-permute-start.27
  65.0 1.8 %collective-permute-start.28 = (bf16[48,512]{1,0:T(8,128)(2,1)S(1)}, bf16[48,512]{1,0:T(8,128)(2,1)S(1)}, u32[]{:S(2)}, u32[]{:S(2)}) collective-permute-start(bf16[48,512]{1,0:T(8,128)(2,1)S(1)} %get-tuple-element.54), channel_id=1, source_target_pairs={{0,8},{1,9},{2,10},{3,11},{4,12},{5,13},{6,14},{7,15},{8,0},{9,1},... | collective-permute-start | bytes 147464 | tf_op jit(solution)/shard_map/ppermute | solution.py:43
  66.8 2.6 %collective-permute-start.29 = (bf16[48,512]{1,0:T(8,128)(2,1)S(1)}, bf16[48,512]{1,0:T(8,128)(2,1)S(1)}, u32[]{:S(2)}, u32[]{:S(2)}) collective-permute-start(bf16[48,512]{1,0:T(8,128)(2,1)S(1)} %get-tuple-element.53), channel_id=1, source_target_pairs={{0,12},{1,13},{2,14},{3,15},{4,8},{5,9},{6,10},{7,11},{8,4},{9,5},... | collective-permute-start | bytes 147464 | tf_op jit(solution)/shard_map/ppermute | solution.py:43
  69.3 0.9 %combine.2 = bf16[16,2560]{1,0:T(8,128)(2,1)} custom-call(f32[16,4]{1,0:T(8,128)S(1)} %get-tuple-element.22.spot_ref, f32[16,2]{1,0:T(8,128)S(1)} %route.2.refs_8_.weight_ref, bf16[48,640]{1,0:T(8,128)(2,1)S(1)} %get-tuple-element.52.refs_0_, bf16[48,640]{1,0:T(8,128)(2,1)S(1)} %collective-permute-done.22.refs_1_, ...), custom_call_target="tpu_custom_call" | custom-call | tf_op jit(solution)/shard_map/combine/pallas_call | solution.py:396
  70.2 0.5 collective-permute-done.28.refs_2_
  70.8 1.9 %collective-permute-done.29.refs_3_ = bf16[48,512]{1,0:T(8,128)(2,1)S(1)} collective-permute-done((bf16[48,512]{1,0:T(8,128)(2,1)S(1)}, bf16[48,512]{1,0:T(8,128)(2,1)S(1)}, u32[]{:S(2)}, u32[]{:S(2)}) %collective-permute-start.29) | collective-permute-done | bytes 49184 | tf_op jit(solution)/shard_map/ppermute | solution.py:43
  72.7 0.9 %combine.3 = bf16[16,2560]{1,0:T(8,128)(2,1)} custom-call(f32[16,4]{1,0:T(8,128)S(1)} %get-tuple-element.28.spot_ref, f32[16,2]{1,0:T(8,128)S(1)} %route.3.refs_8_.weight_ref, bf16[48,512]{1,0:T(8,128)(2,1)S(1)} %get-tuple-element.56.refs_0_, bf16[48,512]{1,0:T(8,128)(2,1)S(1)} %collective-permute-done.27.refs_1_, ...), custom_call_target="tpu_custom_call" | custom-call | tf_op jit(solution)/shard_map/combine/pallas_call | solution.py:396
  (79 shorter events, 0.6 us)
Async XLA Ops:
  0.6 1.4 %copy-start = (bf16[256,2560]{1,0:T(8,128)(2,1)S(1)}, bf16[256,2560]{1,0:T(8,128)(2,1)}, u32[]{:S(2)}) copy-start(bf16[256,2560]{1,0:T(8,128)(2,1)} %param.14) | copy-start | bytes 3932164
  2.0 1.1 %copy-start.7 = (s32[2]{0:T(128)S(1)}, s32[2]{0:T(128)}, u32[]{:S(2)}) copy-start(s32[2]{0:T(128)} %param.20) | copy-start | bytes 28
  2.0 1.2 %copy-start.5 = (s32[16,2]{0,1:T(2,128)S(1)}, s32[16,2]{0,1:T(2,128)}, u32[]{:S(2)}) copy-start(s32[16,2]{0,1:T(2,128)} %param.19) | copy-start | bytes 388
  2.1 1.2 %copy-start.6 = (s32[16,2]{0,1:T(2,128)S(1)}, s32[16,2]{0,1:T(2,128)}, u32[]{:S(2)}) copy-start(s32[16,2]{0,1:T(2,128)} %param.18) | copy-start | bytes 388
  2.1 1.2 %copy-start.3 = (f32[2560]{0:T(1024)S(1)}, f32[2560]{0:T(1024)}, u32[]{:S(2)}) copy-start(f32[2560]{0:T(1024)} %param.16) | copy-start | bytes 30724
  2.1 1.2 %copy-start.4 = (f32[2560]{0:T(1024)S(1)}, f32[2560]{0:T(1024)}, u32[]{:S(2)}) copy-start(f32[2560]{0:T(1024)} %param.15) | copy-start | bytes 30724
  2.5 1.8 %collective-permute-start = (bf16[64,2560]{1,0:T(8,128)(2,1)S(1)}, bf16[64,2560]{1,0:T(8,128)(2,1)S(1)}, u32[]{:S(2)}, u32[]{:S(2)}) collective-permute-start(bf16[64,2560]{1,0:T(8,128)(2,1)S(1)} %get-tuple-element.45), channel_id=1, source_target_pairs={{0,1},{1,0},{2,3},{3,2},{4,5},{5,4},{6,7},{7,6},{8,9},{9,8},{10,11... | collective-permute-start | bytes 983048 | tf_op jit(solution)/shard_map/ppermute | solution.py:43
  3.0 12.3 %collective-permute-start.1 = (bf16[64,2560]{1,0:T(8,128)(2,1)S(1)}, bf16[64,2560]{1,0:T(8,128)(2,1)S(1)}, u32[]{:S(2)}, u32[]{:S(2)}) collective-permute-start(bf16[64,2560]{1,0:T(8,128)(2,1)S(1)} %get-tuple-element.44), channel_id=1, source_target_pairs={{0,1},{1,0},{2,3},{3,2},{4,5},{5,4},{6,7},{7,6},{8,9},{9,8},{10,11... | collective-permute-start | bytes 983048 | tf_op jit(solution)/shard_map/ppermute | solution.py:43
  3.7 3.6 %copy-start.2 = (f32[2560,4]{0,1:T(4,128)S(1)}, f32[2560,4]{0,1:T(4,128)}, u32[]{:S(2)}) copy-start(f32[2560,4]{0,1:T(4,128)} %param.17) | copy-start | bytes 122884
  3.7 3.7 %copy-start.1 = (bf16[16,2560]{1,0:T(8,128)(2,1)S(1)}, bf16[16,2560]{1,0:T(8,128)(2,1)}, u32[]{:S(2)}) copy-start(bf16[16,2560]{1,0:T(8,128)(2,1)} %image_ref.1) | copy-start | bytes 245764
  4.3 11.0 %collective-permute-start.2 = (bf16[64,2560]{1,0:T(8,128)(2,1)S(1)}, bf16[64,2560]{1,0:T(8,128)(2,1)S(1)}, u32[]{:S(2)}, u32[]{:S(2)}) collective-permute-start(bf16[64,2560]{1,0:T(8,128)(2,1)S(1)} %fusion.1.refs_0_), channel_id=1, source_target_pairs={{0,2},{1,3},{2,0},{3,1},{4,6},{5,7},{6,4},{7,5},{8,10},{9,11},{10,... | collective-permute-start | bytes 983048 | tf_op jit(solution)/shard_map/ppermute | solution.py:43
  8.2 11.7 %collective-permute-start.5 = (bf16[48,640]{1,0:T(8,128)(2,1)S(1)}, bf16[48,640]{1,0:T(8,128)(2,1)S(1)}, u32[]{:S(2)}, u32[]{:S(2)}) collective-permute-start(bf16[48,640]{1,0:T(8,128)(2,1)S(1)} %get-tuple-element.27), channel_id=1, source_target_pairs={{0,12},{1,13},{2,14},{3,15},{4,8},{5,9},{6,10},{7,11},{8,4},{9,5},... | collective-permute-start | bytes 184328 | tf_op jit(solution)/shard_map/ppermute | solution.py:43
  11.8 8.2 %collective-permute-start.4 = (bf16[48,640]{1,0:T(8,128)(2,1)S(1)}, bf16[48,640]{1,0:T(8,128)(2,1)S(1)}, u32[]{:S(2)}, u32[]{:S(2)}) collective-permute-start(bf16[48,640]{1,0:T(8,128)(2,1)S(1)} %get-tuple-element.26), channel_id=1, source_target_pairs={{0,8},{1,9},{2,10},{3,11},{4,12},{5,13},{6,14},{7,15},{8,0},{9,1},... | collective-permute-start | bytes 184328 | tf_op jit(solution)/shard_map/ppermute | solution.py:43
  11.8 8.2 %collective-permute-start.3 = (bf16[48,640]{1,0:T(8,128)(2,1)S(1)}, bf16[48,640]{1,0:T(8,128)(2,1)S(1)}, u32[]{:S(2)}, u32[]{:S(2)}) collective-permute-start(bf16[48,640]{1,0:T(8,128)(2,1)S(1)} %get-tuple-element.25.refs_1_), channel_id=1, source_target_pairs={{0,4},{1,5},{2,6},{3,7},{4,0},{5,1},{6,2},{7,3},{8,12},{9,13},{10,... | collective-permute-start | bytes 184328 | tf_op jit(solution)/shard_map/ppermute | solution.py:43
  15.5 6.4 %collective-permute-start.7 = (bf16[16,2560]{1,0:T(8,128)(2,1)S(1)}, bf16[16,2560]{1,0:T(8,128)(2,1)S(1)}, u32[]{:S(2)}, u32[]{:S(2)}) collective-permute-start(bf16[16,2560]{1,0:T(8,128)(2,1)S(1)} %get-tuple-element.48.refs_1_), channel_id=1, source_target_pairs={{0,4},{1,5},{2,6},{3,7},{4,0},{5,1},{6,2},{7,3},{8,12},{9,13},{10,... | collective-permute-start | bytes 245768 | tf_op jit(solution)/shard_map/ppermute | solution.py:43
  17.4 7.8 %collective-permute-start.8 = (bf16[16,2560]{1,0:T(8,128)(2,1)S(1)}, bf16[16,2560]{1,0:T(8,128)(2,1)S(1)}, u32[]{:S(2)}, u32[]{:S(2)}) collective-permute-start(bf16[16,2560]{1,0:T(8,128)(2,1)S(1)} %get-tuple-element.47.refs_2_), channel_id=1, source_target_pairs={{0,8},{1,9},{2,10},{3,11},{4,12},{5,13},{6,14},{7,15},{8,0},{9,1},... | collective-permute-start | bytes 245768 | tf_op jit(solution)/shard_map/ppermute | solution.py:43
  19.9 6.4 %collective-permute-start.9 = (bf16[16,2560]{1,0:T(8,128)(2,1)S(1)}, bf16[16,2560]{1,0:T(8,128)(2,1)S(1)}, u32[]{:S(2)}, u32[]{:S(2)}) collective-permute-start(bf16[16,2560]{1,0:T(8,128)(2,1)S(1)} %get-tuple-element.46.refs_3_), channel_id=1, source_target_pairs={{0,12},{1,13},{2,14},{3,15},{4,8},{5,9},{6,10},{7,11},{8,4},{9,5},... | collective-permute-start | bytes 245768 | tf_op jit(solution)/shard_map/ppermute | solution.py:43
  20.0 18.5 %slice-start.6 = ((s8[8847360]{0:T(1024)(128)(4,1)}), s8[4194304]{0:T(1024)(128)(4,1)S(1)}, s32[]{:S(2)}) async-start(s8[8847360]{0:T(1024)(128)(4,1)} %bitcast.30), calls=%async_computation.6 | async-start | bytes 8388608
  20.1 7.0 %collective-permute-start.6 = (bf16[192,640]{1,0:T(8,128)(2,1)S(1)}, bf16[192,640]{1,0:T(8,128)(2,1)S(1)}, u32[]{:S(2)}, u32[]{:S(2)}) collective-permute-start(bf16[192,640]{1,0:T(8,128)(2,1)S(1)} %pad_maximum_fusion.refs_0_), channel_id=1, source_target_pairs={{0,2},{1,3},{2,0},{3,1},{4,6},{5,7},{6,4},{7,5},{8,10},{9,11},{10,... | collective-permute-start | bytes 737288 | tf_op jit(solution)/shard_map/ppermute | solution.py:43
  21.9 16.6 %collective-permute-start.10 = (bf16[192,640]{1,0:T(8,128)(2,1)S(1)}, bf16[192,640]{1,0:T(8,128)(2,1)S(1)}, u32[]{:S(2)}, u32[]{:S(2)}) collective-permute-start(bf16[192,640]{1,0:T(8,128)(2,1)S(1)} %pad_maximum_fusion.refs_0_), channel_id=1, source_target_pairs={{0,1},{1,0},{2,3},{3,2},{4,5},{5,4},{6,7},{7,6},{8,9},{9,8},{10,11... | collective-permute-start | bytes 737288 | tf_op jit(solution)/shard_map/ppermute | solution.py:43
  26.3 12.2 %slice-start = ((s8[8847360]{0:T(1024)(128)(4,1)}), s8[4194304]{0:T(1024)(128)(4,1)S(1)}, s32[]{:S(2)}) async-start(s8[8847360]{0:T(1024)(128)(4,1)} %bitcast.22), calls=%async_computation | async-start | bytes 8388608
  26.3 12.2 %slice-start.3 = ((s8[8847360]{0:T(1024)(128)(4,1)}), s8[4194304]{0:T(1024)(128)(4,1)S(1)}, s32[]{:S(2)}) async-start(s8[8847360]{0:T(1024)(128)(4,1)} %bitcast.26), calls=%async_computation.3 | async-start | bytes 8388608
  26.3 12.2 %slice-start.1 = ((s8[8847360]{0:T(1024)(128)(4,1)}), s8[4194304]{0:T(1024)(128)(4,1)S(1)}, s32[]{:S(2)}) async-start(s8[8847360]{0:T(1024)(128)(4,1)} %bitcast.22), calls=%async_computation.1 | async-start | bytes 8388608
  26.3 12.2 %slice-start.2 = ((s8[8847360]{0:T(1024)(128)(4,1)}), s8[458752]{0:T(1024)(128)(4,1)S(1)}, s32[]{:S(2)}) async-start(s8[8847360]{0:T(1024)(128)(4,1)} %bitcast.22), calls=%async_computation.2 | async-start | bytes 917504
  26.3 12.2 %slice-start.4 = ((s8[8847360]{0:T(1024)(128)(4,1)}), s8[4194304]{0:T(1024)(128)(4,1)S(1)}, s32[]{:S(2)}) async-start(s8[8847360]{0:T(1024)(128)(4,1)} %bitcast.26), calls=%async_computation.4 | async-start | bytes 8388608
  26.3 12.2 %slice-start.5 = ((s8[8847360]{0:T(1024)(128)(4,1)}), s8[458752]{0:T(1024)(128)(4,1)S(1)}, s32[]{:S(2)}) async-start(s8[8847360]{0:T(1024)(128)(4,1)} %bitcast.26), calls=%async_computation.5 | async-start | bytes 917504
  26.4 12.2 %slice-start.7 = ((s8[8847360]{0:T(1024)(128)(4,1)}), s8[4194304]{0:T(1024)(128)(4,1)S(1)}, s32[]{:S(2)}) async-start(s8[8847360]{0:T(1024)(128)(4,1)} %bitcast.30), calls=%async_computation.7 | async-start | bytes 8388608
  26.4 12.2 %slice-start.8 = ((s8[8847360]{0:T(1024)(128)(4,1)}), s8[458752]{0:T(1024)(128)(4,1)S(1)}, s32[]{:S(2)}) async-start(s8[8847360]{0:T(1024)(128)(4,1)} %bitcast.30), calls=%async_computation.8 | async-start | bytes 917504
  27.1 11.4 %collective-permute-start.11 = (bf16[192,640]{1,0:T(8,128)(2,1)S(1)}, bf16[192,640]{1,0:T(8,128)(2,1)S(1)}, u32[]{:S(2)}, u32[]{:S(2)}) collective-permute-start(bf16[192,640]{1,0:T(8,128)(2,1)S(1)} %tie.14.refs_1_), channel_id=1, source_target_pairs={{0,1},{1,0},{2,3},{3,2},{4,5},{5,4},{6,7},{7,6},{8,9},{9,8},{10,11... | collective-permute-start | bytes 737288 | tf_op jit(solution)/shard_map/ppermute | solution.py:43
  27.2 4.7 %collective-permute-start.12 = (bf16[48,512]{1,0:T(8,128)(2,1)S(1)}, bf16[48,512]{1,0:T(8,128)(2,1)S(1)}, u32[]{:S(2)}, u32[]{:S(2)}) collective-permute-start(bf16[48,512]{1,0:T(8,128)(2,1)S(1)} %get-tuple-element.29.refs_1_), channel_id=1, source_target_pairs={{0,4},{1,5},{2,6},{3,7},{4,0},{5,1},{6,2},{7,3},{8,12},{9,13},{10,... | collective-permute-start | bytes 147464 | tf_op jit(solution)/shard_map/ppermute | solution.py:43
  28.4 6.1 %collective-permute-start.13 = (bf16[48,512]{1,0:T(8,128)(2,1)S(1)}, bf16[48,512]{1,0:T(8,128)(2,1)S(1)}, u32[]{:S(2)}, u32[]{:S(2)}) collective-permute-start(bf16[48,512]{1,0:T(8,128)(2,1)S(1)} %get-tuple-element.31), channel_id=1, source_target_pairs={{0,8},{1,9},{2,10},{3,11},{4,12},{5,13},{6,14},{7,15},{8,0},{9,1},... | collective-permute-start | bytes 147464 | tf_op jit(solution)/shard_map/ppermute | solution.py:43
  31.0 5.9 %collective-permute-start.14 = (bf16[48,512]{1,0:T(8,128)(2,1)S(1)}, bf16[48,512]{1,0:T(8,128)(2,1)S(1)}, u32[]{:S(2)}, u32[]{:S(2)}) collective-permute-start(bf16[48,512]{1,0:T(8,128)(2,1)S(1)} %get-tuple-element.32), channel_id=1, source_target_pairs={{0,12},{1,13},{2,14},{3,15},{4,8},{5,9},{6,10},{7,11},{8,4},{9,5},... | collective-permute-start | bytes 147464 | tf_op jit(solution)/shard_map/ppermute | solution.py:43
  36.9 9.5 %collective-permute-start.15 = (bf16[192,512]{1,0:T(8,128)(2,1)S(1)}, bf16[192,512]{1,0:T(8,128)(2,1)S(1)}, u32[]{:S(2)}, u32[]{:S(2)}) collective-permute-start(bf16[192,512]{1,0:T(8,128)(2,1)S(1)} %concat.1.refs_7_.refs_0_), channel_id=1, source_target_pairs={{0,2},{1,3},{2,0},{3,1},{4,6},{5,7},{6,4},{7,5},{8,10},{9,11},{10,... | collective-permute-start | bytes 589832 | tf_op jit(solution)/shard_map/ppermute | solution.py:43
  46.4 1.6 %collective-permute-start.17 = (bf16[192,640]{1,0:T(8,128)(2,1)S(1)}, bf16[192,640]{1,0:T(8,128)(2,1)S(1)}, u32[]{:S(2)}, u32[]{:S(2)}) collective-permute-start(bf16[192,640]{1,0:T(8,128)(2,1)S(1)} %tie.17), channel_id=1, source_target_pairs={{0,1},{1,0},{2,3},{3,2},{4,5},{5,4},{6,7},{7,6},{8,9},{9,8},{10,11... | collective-permute-start | bytes 737288 | tf_op jit(solution)/shard_map/ppermute | solution.py:43
  46.5 2.1 %collective-permute-start.19 = (bf16[192,512]{1,0:T(8,128)(2,1)S(1)}, bf16[192,512]{1,0:T(8,128)(2,1)S(1)}, u32[]{:S(2)}, u32[]{:S(2)}) collective-permute-start(bf16[192,512]{1,0:T(8,128)(2,1)S(1)} %concat.1.refs_7_.refs_0_), channel_id=1, source_target_pairs={{0,1},{1,0},{2,3},{3,2},{4,5},{5,4},{6,7},{7,6},{8,9},{9,8},{10,11... | collective-permute-start | bytes 589832 | tf_op jit(solution)/shard_map/ppermute | solution.py:43
  47.0 1.6 %collective-permute-start.20 = (bf16[192,512]{1,0:T(8,128)(2,1)S(1)}, bf16[192,512]{1,0:T(8,128)(2,1)S(1)}, u32[]{:S(2)}, u32[]{:S(2)}) collective-permute-start(bf16[192,512]{1,0:T(8,128)(2,1)S(1)} %tie.15.refs_1_), channel_id=1, source_target_pairs={{0,1},{1,0},{2,3},{3,2},{4,5},{5,4},{6,7},{7,6},{8,9},{9,8},{10,11... | collective-permute-start | bytes 589832 | tf_op jit(solution)/shard_map/ppermute | solution.py:43
  47.4 11.6 %collective-permute-start.16 = (bf16[192,640]{1,0:T(8,128)(2,1)S(1)}, bf16[192,640]{1,0:T(8,128)(2,1)S(1)}, u32[]{:S(2)}, u32[]{:S(2)}) collective-permute-start(bf16[192,640]{1,0:T(8,128)(2,1)S(1)} %tie.16), channel_id=1, source_target_pairs={{0,1},{1,0},{2,3},{3,2},{4,5},{5,4},{6,7},{7,6},{8,9},{9,8},{10,11... | collective-permute-start | bytes 737288 | tf_op jit(solution)/shard_map/ppermute | solution.py:43
  48.1 8.1 %collective-permute-start.18 = (bf16[192,640]{1,0:T(8,128)(2,1)S(1)}, bf16[192,640]{1,0:T(8,128)(2,1)S(1)}, u32[]{:S(2)}, u32[]{:S(2)}) collective-permute-start(bf16[192,640]{1,0:T(8,128)(2,1)S(1)} %tie.18.refs_7_), channel_id=1, source_target_pairs={{0,2},{1,3},{2,0},{3,1},{4,6},{5,7},{6,4},{7,5},{8,10},{9,11},{10,... | collective-permute-start | bytes 737288 | tf_op jit(solution)/shard_map/ppermute | solution.py:43
  56.2 1.5 %collective-permute-start.21 = (bf16[192,512]{1,0:T(8,128)(2,1)S(1)}, bf16[192,512]{1,0:T(8,128)(2,1)S(1)}, u32[]{:S(2)}, u32[]{:S(2)}) collective-permute-start(bf16[192,512]{1,0:T(8,128)(2,1)S(1)} %tie.20), channel_id=1, source_target_pairs={{0,1},{1,0},{2,3},{3,2},{4,5},{5,4},{6,7},{7,6},{8,9},{9,8},{10,11... | collective-permute-start | bytes 589832 | tf_op jit(solution)/shard_map/ppermute | solution.py:43
  56.3 7.3 %collective-permute-start.25 = (bf16[192,512]{1,0:T(8,128)(2,1)S(1)}, bf16[192,512]{1,0:T(8,128)(2,1)S(1)}, u32[]{:S(2)}, u32[]{:S(2)}) collective-permute-start(bf16[192,512]{1,0:T(8,128)(2,1)S(1)} %tie.23), channel_id=1, source_target_pairs={{0,1},{1,0},{2,3},{3,2},{4,5},{5,4},{6,7},{7,6},{8,9},{9,8},{10,11... | collective-permute-start | bytes 589832 | tf_op jit(solution)/shard_map/ppermute | solution.py:43
  57.8 7.0 %collective-permute-start.26 = (bf16[192,512]{1,0:T(8,128)(2,1)S(1)}, bf16[192,512]{1,0:T(8,128)(2,1)S(1)}, u32[]{:S(2)}, u32[]{:S(2)}) collective-permute-start(bf16[192,512]{1,0:T(8,128)(2,1)S(1)} %tie.21.refs_1_), channel_id=1, source_target_pairs={{0,2},{1,3},{2,0},{3,1},{4,6},{5,7},{6,4},{7,5},{8,10},{9,11},{10,... | collective-permute-start | bytes 589832 | tf_op jit(solution)/shard_map/ppermute | solution.py:43
  59.1 7.7 %collective-permute-start.22 = (bf16[48,640]{1,0:T(8,128)(2,1)S(1)}, bf16[48,640]{1,0:T(8,128)(2,1)S(1)}, u32[]{:S(2)}, u32[]{:S(2)}) collective-permute-start(bf16[48,640]{1,0:T(8,128)(2,1)S(1)} %get-tuple-element.51), channel_id=1, source_target_pairs={{0,4},{1,5},{2,6},{3,7},{4,0},{5,1},{6,2},{7,3},{8,12},{9,13},{10,... | collective-permute-start | bytes 184328 | tf_op jit(solution)/shard_map/ppermute | solution.py:43
  59.2 10.1 %collective-permute-start.23 = (bf16[48,640]{1,0:T(8,128)(2,1)S(1)}, bf16[48,640]{1,0:T(8,128)(2,1)S(1)}, u32[]{:S(2)}, u32[]{:S(2)}) collective-permute-start(bf16[48,640]{1,0:T(8,128)(2,1)S(1)} %get-tuple-element.50), channel_id=1, source_target_pairs={{0,8},{1,9},{2,10},{3,11},{4,12},{5,13},{6,14},{7,15},{8,0},{9,1},... | collective-permute-start | bytes 184328 | tf_op jit(solution)/shard_map/ppermute | solution.py:43
  61.0 8.3 %collective-permute-start.24 = (bf16[48,640]{1,0:T(8,128)(2,1)S(1)}, bf16[48,640]{1,0:T(8,128)(2,1)S(1)}, u32[]{:S(2)}, u32[]{:S(2)}) collective-permute-start(bf16[48,640]{1,0:T(8,128)(2,1)S(1)} %get-tuple-element.49), channel_id=1, source_target_pairs={{0,12},{1,13},{2,14},{3,15},{4,8},{5,9},{6,10},{7,11},{8,4},{9,5},... | collective-permute-start | bytes 184328 | tf_op jit(solution)/shard_map/ppermute | solution.py:43
  64.9 5.4 %collective-permute-start.27 = (bf16[48,512]{1,0:T(8,128)(2,1)S(1)}, bf16[48,512]{1,0:T(8,128)(2,1)S(1)}, u32[]{:S(2)}, u32[]{:S(2)}) collective-permute-start(bf16[48,512]{1,0:T(8,128)(2,1)S(1)} %get-tuple-element.55), channel_id=1, source_target_pairs={{0,4},{1,5},{2,6},{3,7},{4,0},{5,1},{6,2},{7,3},{8,12},{9,13},{10,... | collective-permute-start | bytes 147464 | tf_op jit(solution)/shard_map/ppermute | solution.py:43
  65.0 5.8 %collective-permute-start.28 = (bf16[48,512]{1,0:T(8,128)(2,1)S(1)}, bf16[48,512]{1,0:T(8,128)(2,1)S(1)}, u32[]{:S(2)}, u32[]{:S(2)}) collective-permute-start(bf16[48,512]{1,0:T(8,128)(2,1)S(1)} %get-tuple-element.54), channel_id=1, source_target_pairs={{0,8},{1,9},{2,10},{3,11},{4,12},{5,13},{6,14},{7,15},{8,0},{9,1},... | collective-permute-start | bytes 147464 | tf_op jit(solution)/shard_map/ppermute | solution.py:43
  66.8 5.9 %collective-permute-start.29 = (bf16[48,512]{1,0:T(8,128)(2,1)S(1)}, bf16[48,512]{1,0:T(8,128)(2,1)S(1)}, u32[]{:S(2)}, u32[]{:S(2)}) collective-permute-start(bf16[48,512]{1,0:T(8,128)(2,1)S(1)} %get-tuple-element.53), channel_id=1, source_target_pairs={{0,12},{1,13},{2,14},{3,15},{4,8},{5,9},{6,10},{7,11},{8,4},{9,5},... | collective-permute-start | bytes 147464 | tf_op jit(solution)/shard_map/ppermute | solution.py:43
